TPU v7x, 128 devices: a whole 4x4x4 slice. The times are simulated.
128 devices in a mesh: expert: 16 (over z, x), shard: 8 (over y, core).
Axes of the slice: x: 4, y: 4, z: 4, core: 2. Of those that a mesh axis runs over, the one named last changes fastest.
Arguments:
- block_input: bfloat16 [16384, 2048], P(('expert', 'shard')), may hold values from -6 to 6
- out_grad: bfloat16 [16384, 2048], P(('expert', 'shard')), may hold values from -6 to 6
- norm1_gain: bfloat16 [2048], replicated, may hold values from 0.5 to 1.5
- w_query: bfloat16 [2048, 4096], P(None, 'shard'), may hold values from -0.125 to 0.125
- w_key: bfloat16 [2048, 512], P(None, 'shard'), may hold values from -0.125 to 0.125
- w_value: bfloat16 [2048, 512], P(None, 'shard'), may hold values from -0.125 to 0.125
- query_gain: bfloat16 [128], replicated, may hold values from 0.25 to 1.75
- key_gain: bfloat16 [128], replicated, may hold values from 0.25 to 1.75
- w_out: bfloat16 [4096, 2048], P('shard'), may hold values from -0.375 to 0.375
- norm2_gain: bfloat16 [2048], replicated, may hold values from 0.5 to 1.5
- w_router: bfloat16 [2048, 128], replicated, may hold values from -0.0625 to 0.0625
- w_gate: bfloat16 [128, 2048, 768], P(('expert', 'shard')), may hold values from -0.125 to 0.125
- w_up: bfloat16 [128, 2048, 768], P(('expert', 'shard')), may hold values from -0.125 to 0.125
- w_down: bfloat16 [128, 768, 2048], P(('expert', 'shard')), may hold values from -0.4375 to 0.4375
- seq_lengths: int32 [16, 4], P('expert'), may hold values from 1 to 768, 1024 in all within a row
- token_places: int32 [16, 1024], P('expert'), may hold values from 0 to 1023, each once within a row
- expert_routes: int32 [16384, 4], P(('expert', 'shard')), may hold values from 0 to 127, all different within a row; in each aligned block of 128 rows (0 to 127, 128 to 255, ...) at most 5 rows name the same one
Outputs:
- result: bfloat16 [16384, 2048], P(('expert', 'shard'))
- grad_input: float32 [16384, 2048], P(('expert', 'shard'))
- grad_norm1_gain: float32 [2048], replicated
- grad_w_query: float32 [2048, 4096], P(None, 'shard')
- grad_w_key: float32 [2048, 512], P(None, 'shard')
- grad_w_value: float32 [2048, 512], P(None, 'shard')
- grad_query_gain: float32 [128], replicated
- grad_key_gain: float32 [128], replicated
- grad_w_out: float32 [4096, 2048], P('shard')
- grad_norm2_gain: float32 [2048], replicated
- grad_w_router: float32 [2048, 128], replicated
- grad_w_gate: float32 [128, 2048, 768], P(('expert', 'shard'))
- grad_w_up: float32 [128, 2048, 768], P(('expert', 'shard'))
- grad_w_down: float32 [128, 768, 2048], P(('expert', 'shard'))
Inputs may be any that keep to these rules, and one draw needn't show every extreme that they name: `seq_lengths`: each group's 4 lengths sum to 1024, and the longest is exactly 768. `token_places`: each row is a permutation of the 1024 places of its group. `expert_routes`: each token names 4 different experts; among the rows of one device no expert is named more than 5 times, a bound that some block reaches.
All inputs are finite; a program needn't handle non-finite values.
Results may differ from a plain program's by a relative error of at most 0.025.
Values may be sent and summed in bfloat16 or wider, within the bound.
No kernel may reach another device: no remote copies, remote signals or barrier semaphores. Data moves between devices by JAX's collectives and lax.ppermute only.
A program may use at most 192 MiB of HBM per device.

v0:
```python
import jax
import jax.numpy as jnp
from jax import lax
from jax.sharding import PartitionSpec as P

norm_eps = 1e-06
rope_base = 1000000.0
masked_score = -1e30


def partner(shard, axis, stride):
    return lax.ppermute(shard, axis, [(i, i ^ 1 << stride) for i in range(lax.axis_size(axis))])


def rms_gain(values, gain):
    return values * lax.rsqrt(jnp.mean(values * values, axis=-1, keepdims=True) + norm_eps) * gain


def rotate(values, cosine, sine):
    half_size = values.shape[-1] // 2
    turned = jnp.concatenate([-values[..., half_size:], values[..., :half_size]], axis=-1)
    return values * cosine + turned * sine


def rope_tables(positions, head_size):
    inverse_freq = rope_base ** (-jnp.arange(0, head_size, 2).astype(jnp.float32) / head_size)
    angles = positions.astype(jnp.float32)[:, None] * inverse_freq[None, :]
    angles = jnp.concatenate([angles, angles], axis=-1)
    return (jnp.cos(angles), jnp.sin(angles))


def place_info(lengths_row, group_tokens):
    position_ids = jnp.arange(group_tokens, dtype=jnp.int32)
    seq_ends = jnp.cumsum(lengths_row)
    passed = position_ids[:, None] >= seq_ends[None, :]
    starts = jnp.sum(jnp.where(passed, lengths_row[None, :], 0), axis=1)
    documents = jnp.sum(passed.astype(jnp.int32), axis=1)
    return (documents, position_ids - starts)


def slot_table(route_block, experts, capacity):
    flattened = route_block.reshape(-1)
    assignments = flattened.shape[0]
    one_hot = (flattened[:, None] == jnp.arange(experts, dtype=jnp.int32)[None, :]).astype(
        jnp.int32
    )
    before = jnp.cumsum(one_hot, axis=0) - one_hot
    slot_ids = jnp.sum(before * one_hot, axis=1)
    targets = flattened * capacity + slot_ids
    owner_table = (
        jnp.full((experts * capacity,), assignments, jnp.int32)
        .at[targets]
        .set(jnp.arange(assignments, dtype=jnp.int32))
    )
    return (slot_ids, owner_table)


def head_path(raw, gain, cosine, sine, factor):
    return rotate(rms_gain(raw, gain), cosine[:, None, :], sine[:, None, :]) * factor


def on_device(
    block_input,
    out_grad,
    norm1_gain,
    w_query,
    w_key,
    w_value,
    query_gain,
    key_gain,
    w_out,
    norm2_gain,
    w_router,
    w_gate,
    w_up,
    w_down,
    seq_lengths,
    token_places,
    expert_routes,
):
    tok_rows, width = block_input.shape
    shards = lax.axis_size("shard")
    group_tokens = tok_rows * shards
    head_size = query_gain.shape[0]
    local_heads = w_query.shape[1] // head_size
    key_cols = w_key.shape[1]
    experts = w_router.shape[1]
    top_count = expert_routes.shape[1]
    capacity = 5 * tok_rows * top_count // (4 * experts)
    gain_one = norm1_gain.astype(jnp.float32)
    gain_two = norm2_gain.astype(jnp.float32)
    gain_query = query_gain.astype(jnp.float32)
    gain_key = key_gain.astype(jnp.float32)
    input_float = block_input.astype(jnp.float32)
    normed1 = rms_gain(input_float, gain_one).astype(jnp.bfloat16)
    group_rows = lax.all_gather(normed1, "shard", axis=0, tiled=True)
    places = token_places[0]
    position_ids = jnp.arange(group_tokens, dtype=jnp.int32)
    inverse = jnp.zeros((group_tokens,), jnp.int32).at[places].set(position_ids)
    stream = group_rows[inverse]
    query_raw = jnp.dot(stream, w_query, preferred_element_type=jnp.float32).reshape(
        group_tokens, local_heads, head_size
    )
    key_local = jnp.dot(stream, w_key, preferred_element_type=jnp.float32).astype(jnp.bfloat16)
    value_local = jnp.dot(stream, w_value, preferred_element_type=jnp.float32).astype(jnp.bfloat16)
    upper_half = lax.axis_index("shard") % 2 == 1
    key_other, value_other = partner((key_local, value_local), "shard", 0)
    key_full = jnp.where(
        upper_half,
        jnp.concatenate([key_other, key_local], axis=1),
        jnp.concatenate([key_local, key_other], axis=1),
    )
    value_full = jnp.where(
        upper_half,
        jnp.concatenate([value_other, value_local], axis=1),
        jnp.concatenate([value_local, value_other], axis=1),
    )
    documents, positions = place_info(seq_lengths[0], group_tokens)
    cosine, sine = rope_tables(positions, head_size)

    def query_fn(raw, gain):
        return head_path(raw, gain, cosine, sine, head_size ** (-0.5))

    def key_fn(raw, gain):
        return head_path(raw, gain, cosine, sine, 1.0)

    key_float = key_full.astype(jnp.float32).reshape(group_tokens, 1, head_size)
    query_use = query_fn(query_raw, gain_query).astype(jnp.bfloat16)
    key_use = key_fn(key_float, gain_key)[:, 0, :].astype(jnp.bfloat16)
    span = min(512, group_tokens)
    block_count = group_tokens // span

    def allowed_mask(first_row, last_key):
        query_docs = documents[first_row : first_row + span]
        query_ids = position_ids[first_row : first_row + span]
        return (query_docs[:, None] == documents[None, :last_key]) & (
            position_ids[None, :last_key] <= query_ids[:, None]
        )

    out_pieces = []
    lse_pieces = []
    for block_number in range(block_count):
        first_row = block_number * span
        last_key = first_row + span
        allowed = allowed_mask(first_row, last_key)
        scores = jnp.einsum(
            "qhd,kd->hqk",
            query_use[first_row:last_key],
            key_use[:last_key],
            preferred_element_type=jnp.float32,
        )
        masked = jnp.where(allowed[None], scores, masked_score)
        peak = jnp.max(masked, axis=-1, keepdims=True)
        expo = jnp.exp(masked - peak)
        denominator = jnp.sum(expo, axis=-1, keepdims=True)
        lse_pieces.append(peak + jnp.log(denominator))
        weights_low = (expo / denominator).astype(jnp.bfloat16)
        out_pieces.append(
            jnp.einsum(
                "hqk,kd->qhd",
                weights_low,
                value_full[:last_key],
                preferred_element_type=jnp.float32,
            )
        )
    attn_low = (
        jnp.concatenate(out_pieces, axis=0)
        .reshape(group_tokens, local_heads * head_size)
        .astype(jnp.bfloat16)
    )
    log_sums = jnp.concatenate(lse_pieces, axis=1)
    picked = places
    attention = lax.psum_scatter(
        jnp.dot(attn_low[picked], w_out, preferred_element_type=jnp.float32),
        "shard",
        scatter_dimension=0,
        tiled=True,
    )
    hidden_in = input_float + attention
    normed2 = rms_gain(hidden_in, gain_two).astype(jnp.bfloat16)
    logits = jnp.dot(normed2, w_router, preferred_element_type=jnp.float32)
    router_probs = jax.nn.softmax(logits, axis=-1)
    chosen = jnp.take_along_axis(router_probs, expert_routes, axis=1)
    chosen_sum = jnp.sum(chosen, axis=1, keepdims=True)
    gates = chosen / chosen_sum
    slot_ids, owner_table = slot_table(expert_routes, experts, capacity)
    padded_rows = jnp.concatenate([normed2, jnp.zeros((1, width), jnp.bfloat16)], axis=0)
    send_rows = padded_rows[owner_table // top_count].reshape(experts, capacity, width)
    received = lax.all_to_all(
        send_rows, ("expert", "shard"), split_axis=0, concat_axis=0, tiled=True
    )
    flattened = received.reshape(-1, width)
    gate_pre = jnp.dot(flattened, w_gate[0], preferred_element_type=jnp.float32)
    up_pre = jnp.dot(flattened, w_up[0], preferred_element_type=jnp.float32)
    activated = (jax.nn.silu(gate_pre) * up_pre).astype(jnp.bfloat16)
    produced = (
        jnp.dot(activated, w_down[0], preferred_element_type=jnp.float32)
        .astype(jnp.bfloat16)
        .reshape(received.shape)
    )
    returned = lax.all_to_all(
        produced, ("expert", "shard"), split_axis=0, concat_axis=0, tiled=True
    )
    hidden_shape = received.shape[:2] + (gate_pre.shape[1],)
    returned, kept_rows, kept_gate, kept_up, kept_act = (
        returned,
        received,
        gate_pre.reshape(hidden_shape),
        up_pre.reshape(hidden_shape),
        activated.reshape(hidden_shape),
    )
    assign_ids = expert_routes.reshape(-1) * capacity + slot_ids
    copies = returned.reshape(-1, width)[assign_ids].reshape(tok_rows, top_count, width)
    mixture = jnp.einsum("tk,tkd->td", gates, copies.astype(jnp.float32))
    result = (hidden_in + mixture).astype(jnp.bfloat16)
    grad_top = out_grad.astype(jnp.float32)
    grad_gates = jnp.einsum("tkd,td->tk", copies.astype(jnp.float32), grad_top)
    grad_copies_out = (
        (gates[:, :, None] * grad_top[:, None, :]).astype(jnp.bfloat16).reshape(-1, width)
    )
    padded_grads = jnp.concatenate([grad_copies_out, jnp.zeros((1, width), jnp.bfloat16)], axis=0)
    send_grads = padded_grads[owner_table].reshape(experts, capacity, width)
    got_grads = lax.all_to_all(
        send_grads, ("expert", "shard"), split_axis=0, concat_axis=0, tiled=True
    )
    flat_grads = got_grads.reshape(-1, width)
    flat_rows = kept_rows.reshape(-1, width)
    flat_gate = kept_gate.reshape(flat_grads.shape[0], -1)
    flat_up = kept_up.reshape(flat_grads.shape[0], -1)
    flat_act = kept_act.reshape(flat_grads.shape[0], -1)
    grad_act = lax.dot_general(
        flat_grads, w_down[0], (((1,), (1,)), ((), ())), preferred_element_type=jnp.float32
    )
    grad_down = lax.dot_general(
        flat_act, flat_grads, (((0,), (0,)), ((), ())), preferred_element_type=jnp.float32
    )
    sigmoid_gate = jax.nn.sigmoid(flat_gate)
    grad_gate_pre = (
        grad_act * flat_up * sigmoid_gate * (1.0 + flat_gate * (1.0 - sigmoid_gate))
    ).astype(jnp.bfloat16)
    grad_up_pre = (grad_act * flat_gate * sigmoid_gate).astype(jnp.bfloat16)
    grad_wgate = lax.dot_general(
        flat_rows, grad_gate_pre, (((0,), (0,)), ((), ())), preferred_element_type=jnp.float32
    )
    grad_wup = lax.dot_general(
        flat_rows, grad_up_pre, (((0,), (0,)), ((), ())), preferred_element_type=jnp.float32
    )
    grad_in = lax.dot_general(
        grad_gate_pre, w_gate[0], (((1,), (1,)), ((), ())), preferred_element_type=jnp.float32
    )
    grad_in = grad_in + lax.dot_general(
        grad_up_pre, w_up[0], (((1,), (1,)), ((), ())), preferred_element_type=jnp.float32
    )
    grad_in = grad_in.astype(jnp.bfloat16).reshape(got_grads.shape)
    back_grads = lax.all_to_all(
        grad_in, ("expert", "shard"), split_axis=0, concat_axis=0, tiled=True
    )
    grad_copy = (
        back_grads.reshape(-1, width)[assign_ids]
        .astype(jnp.float32)
        .reshape(tok_rows, top_count, width)
    )
    grad_normed2 = jnp.sum(grad_copy, axis=1)
    grad_chosen = (grad_gates - jnp.sum(grad_gates * gates, axis=1, keepdims=True)) / chosen_sum
    route_hot = (
        expert_routes[:, :, None] == jnp.arange(experts, dtype=jnp.int32)[None, None, :]
    ).astype(jnp.float32)
    grad_probs = jnp.einsum("tk,tke->te", grad_chosen, route_hot)
    grad_logits = (
        router_probs * (grad_probs - jnp.sum(router_probs * grad_probs, axis=1, keepdims=True))
    ).astype(jnp.bfloat16)
    grad_router = lax.dot_general(
        normed2, grad_logits, (((0,), (0,)), ((), ())), preferred_element_type=jnp.float32
    )
    grad_normed2 = grad_normed2 + lax.dot_general(
        grad_logits, w_router, (((1,), (1,)), ((), ())), preferred_element_type=jnp.float32
    )
    unused_two, norm2_pull = jax.vjp(rms_gain, hidden_in, gain_two)
    grad_from_norm2, grad_gain_two = norm2_pull(grad_normed2)
    grad_hidden = grad_top + grad_from_norm2
    grad_attention = grad_hidden.astype(jnp.bfloat16)
    group_grads = lax.all_gather(grad_attention, "shard", axis=0, tiled=True)
    stream_grads = group_grads[inverse]
    grad_wout = lax.dot_general(
        attn_low, stream_grads, (((0,), (0,)), ((), ())), preferred_element_type=jnp.float32
    )
    grad_heads = lax.dot_general(
        stream_grads, w_out, (((1,), (1,)), ((), ())), preferred_element_type=jnp.float32
    )
    grad_heads = grad_heads.astype(jnp.bfloat16).reshape(group_tokens, local_heads, head_size)
    query_grad_pieces = []
    grad_key_use = jnp.zeros((group_tokens, head_size), jnp.float32)
    grad_value = jnp.zeros((group_tokens, head_size), jnp.float32)
    for block_number in range(block_count):
        first_row = block_number * span
        last_key = first_row + span
        allowed = allowed_mask(first_row, last_key)
        query_block = query_use[first_row:last_key]
        key_block = key_use[:last_key]
        head_grads = grad_heads[first_row:last_key]
        scores = jnp.einsum(
            "qhd,kd->hqk", query_block, key_block, preferred_element_type=jnp.float32
        )
        soft_weights = jnp.where(
            allowed[None], jnp.exp(scores - log_sums[:, first_row:last_key]), 0.0
        )
        grad_soft = jnp.einsum(
            "qhd,kd->hqk", head_grads, value_full[:last_key], preferred_element_type=jnp.float32
        )
        delta = jnp.sum(soft_weights * grad_soft, axis=-1, keepdims=True)
        grad_scores = (soft_weights * (grad_soft - delta)).astype(jnp.bfloat16)
        query_grad_pieces.append(
            jnp.einsum("hqk,kd->qhd", grad_scores, key_block, preferred_element_type=jnp.float32)
        )
        grad_key_use = grad_key_use.at[:last_key].add(
            jnp.einsum("hqk,qhd->kd", grad_scores, query_block, preferred_element_type=jnp.float32)
        )
        grad_value = grad_value.at[:last_key].add(
            jnp.einsum(
                "hqk,qhd->kd",
                soft_weights.astype(jnp.bfloat16),
                head_grads,
                preferred_element_type=jnp.float32,
            )
        )
    grad_query_use = jnp.concatenate(query_grad_pieces, axis=0)
    unused_query, query_pull = jax.vjp(query_fn, query_raw, gain_query)
    grad_query_raw, grad_gain_query = query_pull(grad_query_use)
    unused_key, key_pull = jax.vjp(key_fn, key_float, gain_key)
    grad_key_float, grad_gain_key = key_pull(grad_key_use[:, None, :])
    grad_key_full = grad_key_float[:, 0, :]
    key_grad_other, value_grad_other = (
        partner(grad_key_full.astype(jnp.bfloat16), "shard", 0).astype(grad_key_full.dtype),
        partner(grad_value.astype(jnp.bfloat16), "shard", 0).astype(grad_value.dtype),
    )
    key_total = grad_key_full + key_grad_other
    value_total = grad_value + value_grad_other
    grad_key_own = jnp.where(upper_half, key_total[:, key_cols:], key_total[:, :key_cols])
    grad_value_own = jnp.where(upper_half, value_total[:, key_cols:], value_total[:, :key_cols])
    grad_query_low = grad_query_raw.reshape(group_tokens, local_heads * head_size).astype(
        jnp.bfloat16
    )
    grad_key_low = grad_key_own.astype(jnp.bfloat16)
    grad_value_low = grad_value_own.astype(jnp.bfloat16)
    grad_wquery = lax.dot_general(
        stream, grad_query_low, (((0,), (0,)), ((), ())), preferred_element_type=jnp.float32
    )
    grad_wkey = lax.dot_general(
        stream, grad_key_low, (((0,), (0,)), ((), ())), preferred_element_type=jnp.float32
    )
    grad_wvalue = lax.dot_general(
        stream, grad_value_low, (((0,), (0,)), ((), ())), preferred_element_type=jnp.float32
    )
    picked = places
    summed = lax.dot_general(
        grad_query_low[picked],
        w_query,
        (((1,), (1,)), ((), ())),
        preferred_element_type=jnp.float32,
    )
    summed = summed + lax.dot_general(
        grad_key_low[picked], w_key, (((1,), (1,)), ((), ())), preferred_element_type=jnp.float32
    )
    grad_normed1 = lax.psum_scatter(
        (
            summed
            + lax.dot_general(
                grad_value_low[picked],
                w_value,
                (((1,), (1,)), ((), ())),
                preferred_element_type=jnp.float32,
            )
        ).astype(jnp.bfloat16),
        "shard",
        scatter_dimension=0,
        tiled=True,
    ).astype(jnp.float32)
    unused_one, norm1_pull = jax.vjp(rms_gain, input_float, gain_one)
    grad_from_norm1, grad_gain_one = norm1_pull(grad_normed1)
    grad_input = grad_hidden + grad_from_norm1
    grad_wquery, grad_wkey, grad_wvalue, grad_wout = (
        lax.psum(grad_wquery.astype(jnp.bfloat16), "expert").astype(jnp.float32),
        lax.psum(grad_wkey.astype(jnp.bfloat16), "expert").astype(jnp.float32),
        lax.psum(grad_wvalue.astype(jnp.bfloat16), "expert").astype(jnp.float32),
        lax.psum(grad_wout.astype(jnp.bfloat16), "expert").astype(jnp.float32),
    )
    grad_gain_one, grad_gain_two, grad_gain_query, grad_gain_key, grad_router = lax.psum(
        (grad_gain_one, grad_gain_two, grad_gain_query, grad_gain_key, grad_router),
        ("expert", "shard"),
    )
    return (
        result,
        grad_input,
        grad_gain_one,
        grad_wquery,
        grad_wkey,
        grad_wvalue,
        grad_gain_query,
        grad_gain_key,
        grad_wout,
        grad_gain_two,
        grad_router,
        grad_wgate[None],
        grad_wup[None],
        grad_down[None],
    )


def solution(mesh):
    return jax.shard_map(
        on_device,
        mesh=mesh,
        in_specs=(
            P(("expert", "shard"), None),
            P(("expert", "shard"), None),
            P(),
            P(None, "shard"),
            P(None, "shard"),
            P(None, "shard"),
            P(),
            P(),
            P("shard", None),
            P(),
            P(),
            P(("expert", "shard"), None, None),
            P(("expert", "shard"), None, None),
            P(("expert", "shard"), None, None),
            P("expert", None),
            P("expert", None),
            P(("expert", "shard"), None),
        ),
        out_specs=(
            P(("expert", "shard"), None),
            P(("expert", "shard"), None),
            P(),
            P(None, "shard"),
            P(None, "shard"),
            P(None, "shard"),
            P(),
            P(),
            P("shard", None),
            P(),
            P(),
            P(("expert", "shard"), None, None),
            P(("expert", "shard"), None, None),
            P(("expert", "shard"), None, None),
        ),
        check_vma=False,
    )
```

profile of v0, /device:TPU:1, one launch (start us, length us, event | category | flops | bytes accessed | tf_op | source)
XLA Modules:
  0.0 944.8 jit_solution(955864034650449809)
XLA Ops:
  16.5 4.3 scatter_custom_fusion
  24.5 23.9 %all-gather.3.cloned.1.call-done = bf16[1024,2048]{1,0:T(8,128)(2,1)} async-done(((bf16[128,2048]{1,0:T(8,128)(2,1)}), bf16[1024,2048]{1,0:T(8,128)(2,1)}) %all-gather.3.cloned.1.call-update) | async-done | bytes 4194320 | tf_op jit(solution)/shard_map/all_gather | solution.py:96
  48.5 11.5 %gather_fusion = bf16[1024,2048]{1,0:T(8,128)(2,1)} fusion(bf16[1024,2048]{1,0:T(8,128)(2,1)} %all-gather.3.cloned.1.call-done, s32[1024]{0:T(1024)S(1)} %fusion.103), kind=kCustom, calls=%fused_computation | custom fusion | bytes 8392704 | tf_op jit(solution)/shard_map/gather | solution.py:100
  60.0 3.7 convolution_convert_fusion.6
  64.1 5.4 multiply_reduce_fusion.2
  70.1 2.9 copy.142
  83.2 4.5 fusion.76
  91.8 3.8 fusion.35
  109.9 6.5 gather_fusion.1
  116.4 7.5 fusion.127
  130.3 2.8 scatter_custom_fusion.1
  133.2 42.3 %reduce-scatter.3.cloned.1.call-done = f32[128,2048]{1,0:T(8,128)} async-done(((f32[1024,2048]{1,0:T(8,128)}), f32[128,2048]{1,0:T(8,128)}) %reduce-scatter.3.cloned.1.call-update) | async-done | bytes 1048592 | tf_op jit(solution)/shard_map/reduce_scatter | solution.py:173
  179.9 8.0 gather_fusion.2
  187.9 5.4 reshape.841
  193.4 61.7 %all_to_all.20 = bf16[128,5,2048]{2,1,0:T(8,128)(2,1)} all-to-all(bf16[128,5,2048]{2,1,0:T(8,128)(2,1)} %reshape.841), channel_id=1, replica_groups=mesh['expert'=16,'shard'=8] {'expert','shard'}, dimensions={0} | all-to-all | bytes 5242880 | tf_op jit(solution)/shard_map/all_to_all | solution.py:189
  255.0 5.6 reshape.842
  260.6 5.0 fusion.27
  265.7 3.6 multiply_convert_fusion.3
  270.2 3.8 convolution_convert_fusion
  274.0 5.4 reshape.843
  279.4 5.9 all-to-all-start.1
  285.6 4.2 mul.506
  289.8 5.3 mul.507
  296.7 3.7 gather_fusion.10
  300.6 37.5 %all-to-all-done.1 = bf16[128,5,2048]{2,1,0:T(8,128)(2,1)} async-done(((bf16[128,5,2048]{2,1,0:T(8,128)(2,1)}), bf16[128,5,2048]{2,1,0:T(8,128)(2,1)}, u32[]{:S(2)}, u32[]{:S(2)}) %all-to-all-start.1) | async-done | bytes 2621472 | tf_op jit(solution)/shard_map/all_to_all | solution.py:201
  338.1 5.6 reshape.844
  343.7 7.3 gather_fusion.3
  351.0 4.1 reshape.845
  355.1 4.5 fusion.65
  363.9 8.8 gather_fusion.4
  372.7 5.4 reshape.846
  378.2 58.8 %all_to_all.21 = bf16[128,5,2048]{2,1,0:T(8,128)(2,1)} all-to-all(bf16[128,5,2048]{2,1,0:T(8,128)(2,1)} %reshape.846), channel_id=1, replica_groups=mesh['expert'=16,'shard'=8] {'expert','shard'}, dimensions={0} | all-to-all | bytes 5242880 | tf_op jit(solution)/shard_map/all_to_all | solution.py:223
  437.0 5.6 reshape.847
  442.6 5.8 multiply_convert_fusion.1
  453.2 2.8 reshape.848
  456.0 5.4 all-to-all-start.3
  462.1 52.2 %all-to-all-done.3 = bf16[128,5,2048]{2,1,0:T(8,128)(2,1)} async-done(((bf16[128,5,2048]{2,1,0:T(8,128)(2,1)}), bf16[128,5,2048]{2,1,0:T(8,128)(2,1)}, u32[]{:S(2)}, u32[]{:S(2)}) %all-to-all-start.3) | async-done | bytes 2621472 | tf_op jit(solution)/shard_map/all_to_all | solution.py:255
  514.3 4.2 reshape.849
  518.5 3.3 gather_fusion.5
  521.8 4.7 reshape.850
  526.5 5.9 reduce_sum.233
  535.6 28.1 %all-gather.5.cloned.1.call-done = bf16[1024,2048]{1,0:T(8,128)(2,1)} async-done(((bf16[128,2048]{1,0:T(8,128)(2,1)}), bf16[1024,2048]{1,0:T(8,128)(2,1)}) %all-gather.5.cloned.1.call-update) | async-done | bytes 4194320 | tf_op jit(solution)/shard_map/all_gather | solution.py:282
  563.8 11.9 %gather_fusion.6 = bf16[1024,2048]{1,0:T(8,128)(2,1)} fusion(bf16[1024,2048]{1,0:T(8,128)(2,1)} %all-gather.5.cloned.1.call-done, s32[1024]{0:T(1024)S(1)} %copy-done.63), kind=kCustom, calls=%fused_computation.6 | custom fusion | bytes 8392704 | tf_op jit(solution)/shard_map/gather | solution.py:283
  575.7 5.4 convolution_convert_fusion.5
  587.7 3.7 convolution_convert_fusion.1
  594.1 2.9 fusion.126
  606.0 3.0 fusion.69
  617.5 3.9 multiply_reduce_fusion
  623.4 6.1 convolution_convert_fusion.2
  635.6 4.0 gather_fusion.7
  639.6 7.2 fusion.129
  647.2 3.2 gather_fusion.9
  650.4 3.2 gather_fusion.8
  654.9 6.8 add_convert_fusion
  664.1 4.0 fusion.128
  668.1 5.9 convolution_bitcast_fusion
  674.0 4.6 convolution_bitcast_fusion.1
  678.6 4.6 convolution_bitcast_fusion.2
  683.2 60.3 %all-reduce.15.cloned.1.call-done = (bf16[2048,512]{1,0:T(8,128)(2,1)}, bf16[2048,64]{0,1:T(8,128)(2,1)}, bf16[2048,64]{0,1:T(8,128)(2,1)}, bf16[512,2048]{1,0:T(8,128)(2,1)}) async-done(((bf16[2048,512]{1,0:T(8,128)(2,1)}, bf16[2048,64]{0,1:T(8,128)(2,1)}, bf16[2048,64]{0,1:T(8,128)(2,1)}, bf16[512,2048]{1,0:T(8,128)(2,1)}), (bf16[2048,512]{1,0:T(8,128)(2,1)}, bf16[2048,64]{0,1:T(8,128)(2,1)}, ...) | async-done | bytes 4718608 | tf_op jit(solution)/shard_map/psum | solution.py:382
  743.5 4.3 convert_element_type.256
  752.1 28.3 %reduce-scatter.5.cloned.1.call-done = bf16[128,2048]{1,0:T(8,128)(2,1)} async-done(((bf16[1024,2048]{1,0:T(8,128)(2,1)}), bf16[128,2048]{1,0:T(8,128)(2,1)}) %reduce-scatter.5.cloned.1.call-update) | async-done | bytes 524304 | tf_op jit(solution)/shard_map/reduce_scatter | solution.py:364
  782.1 68.3 %all-reduce.8 = (f32[2048]{0:T(1024)}, f32[128]{0:T(128)}, f32[128]{0:T(128)}, f32[2048]{0:T(1024)}) all-reduce(f32[2048]{0:T(1024)S(1)} %get-tuple-element.82, f32[128]{0:T(128)S(1)} %get-tuple-element.78, f32[128]{0:T(128)S(1)} %get-tuple-element.84, ...), channel_id=1, replica_groups=mesh['expert'=16,'shard'=8] {'expert','shard'}, use_global_device_ids=true, to_apply=%region_31.32 | all-reduce | flops 4352 | bytes 34816 | tf_op jit(solution)/shard_map/psum | solution.py:387
  850.4 4.3 fusion.61
  854.7 80.6 %all-reduce.13.cloned.1.call-done = f32[2048,128]{1,0:T(8,128)} async-done(((f32[2048,128]{1,0:T(8,128)}), f32[2048,128]{1,0:T(8,128)}) %all-reduce.13.cloned.1.call-update) | async-done | bytes 1048592 | tf_op jit(solution)/shard_map/psum | solution.py:387
  (334 shorter events, 115.4 us)
Async XLA Ops:
  7.2 263.1 %copy-start = (bf16[1,768,2048]{2,1,0:T(8,128)(2,1)S(1)}, bf16[1,768,2048]{2,1,0:T(8,128)(2,1)}, u32[]{:S(2)}) copy-start(bf16[1,768,2048]{2,1,0:T(8,128)(2,1)} %param.42) | copy-start | bytes 9437188
  7.2 41.3 %all-gather.3.cloned.1.call-start = ((), (), s32[]{:S(2)}) async-start(), calls=%async_computation.6 | async-start | bytes 4718592 | tf_op jit(solution)/shard_map/all_gather | solution.py:96
  12.5 163.0 %reduce-scatter.3.cloned.1.call-start = ((), (), s32[]{:S(2)}) async-start(), calls=%async_computation.7 | async-start | bytes 9437184 | tf_op jit(solution)/shard_map/reduce_scatter | solution.py:173
  22.2 26.3 %copy-start.62 = (s32[1024]{0:T(1024)}, s32[1024]{0:T(1024)S(1)}, u32[]{:S(2)}) copy-start(s32[1024]{0:T(1024)S(1)} %fusion.103) | copy-start | bytes 12292
  23.3 77.9 %copy-start.24 = (pred[512,512]{0,1:T(8,128)(4,1)}, pred[512,512]{0,1:T(8,128)(4,1)S(1)}, u32[]{:S(2)}) copy-start(pred[512,512]{0,1:T(8,128)(4,1)S(1)} %compare_and_fusion) | copy-start | bytes 786436
  60.0 4.1 copy-start.3
  63.8 19.5 %copy-start.22 = (bf16[1024,64]{0,1:T(8,128)(2,1)}, bf16[1024,64]{0,1:T(8,128)(2,1)S(1)}, u32[]{:S(2)}) copy-start(bf16[1024,64]{0,1:T(8,128)(2,1)S(1)} %convolution_convert_fusion.6) | copy-start | bytes 393220
  63.8 17.2 %collective-permute-start.1 = (bf16[1024,64]{0,1:T(8,128)(2,1)S(1)}, bf16[1024,64]{0,1:T(8,128)(2,1)}, u32[]{:S(2)}, u32[]{:S(2)}) collective-permute-start(bf16[1024,64]{0,1:T(8,128)(2,1)S(1)} %convolution_convert_fusion.6), channel_id=1, source_target_pairs={{0,1},{1,0},{2,3},{3,2},{4,5},{5,4},{6,7},{7,6},{8,9},{9,8},{10,11... | collective-permute-start | bytes 393224 | tf_op jit(solution)/shard_map/ppermute | solution.py:12
  70.1 21.7 %copy-start.46 = (f32[1024,4]{0,1:T(4,128)}, f32[1024,4]{0,1:T(4,128)S(1)}, u32[]{:S(2)}) copy-start(f32[1024,4]{0,1:T(4,128)S(1)} %fusion.101) | copy-start | bytes 49156
  74.9 3.6 copy-start.4
  74.9 3.7 copy-start.41
  78.7 4.6 copy-start.30
  80.7 18.7 %collective-permute-start = (bf16[1024,64]{0,1:T(8,128)(2,1)}, bf16[1024,64]{0,1:T(8,128)(2,1)}, u32[]{:S(2)}, u32[]{:S(2)}) collective-permute-start(bf16[1024,64]{0,1:T(8,128)(2,1)} %convolution_convert_fusion.7), channel_id=1, source_target_pairs={{0,1},{1,0},{2,3},{3,2},{4,5},{5,4},{6,7},{7,6},{8,9},{9,8},{10,11... | collective-permute-start | bytes 393224 | tf_op jit(solution)/shard_map/ppermute | solution.py:12
  82.0 5.7 copy-start.64
  82.1 5.6 copy-start.50
  91.8 3.9 copy-start.33
  97.1 4.1 copy-start.6
  98.5 5.5 copy-start.2
  98.6 5.5 copy-start.56
  177.1 357.2 %copy-start.72 = (f32[128]{0:T(128)}, f32[128]{0:T(128)S(1)}, u32[]{:S(2)}) copy-start(f32[128]{0:T(128)S(1)} %fusion.113) | copy-start | bytes 1540
  260.6 5.0 copy-start.35
  260.6 5.0 copy-start.81
  265.7 3.6 copy-start.85
  279.4 5.9 copy-start.61
  279.4 58.7 %all-to-all-start.1 = ((bf16[128,5,2048]{2,1,0:T(8,128)(2,1)}), bf16[128,5,2048]{2,1,0:T(8,128)(2,1)}, u32[]{:S(2)}, u32[]{:S(2)}) async-start(bf16[128,5,2048]{2,1,0:T(8,128)(2,1)} %reshape.843), calls=%async_computation.2 | async-start | bytes 8388608 | tf_op jit(solution)/shard_map/all_to_all | solution.py:201
  442.6 5.8 copy-start.80
  456.0 58.3 %all-to-all-start.3 = ((bf16[128,5,2048]{2,1,0:T(8,128)(2,1)}), bf16[128,5,2048]{2,1,0:T(8,128)(2,1)}, u32[]{:S(2)}, u32[]{:S(2)}) async-start(bf16[128,5,2048]{2,1,0:T(8,128)(2,1)} %reshape.848), calls=%async_computation.4 | async-start | bytes 8388608 | tf_op jit(solution)/shard_map/all_to_all | solution.py:255
  461.4 102.4 %all-gather.5.cloned.1.call-start = ((), (), s32[]{:S(2)}) async-start(), calls=%async_computation.8 | async-start | bytes 4718592 | tf_op jit(solution)/shard_map/all_gather | solution.py:282
  526.5 5.9 copy-start.10
  526.5 5.9 copy-start.38
  534.3 41.4 %copy-start.17 = (f32[128,2048]{1,0:T(8,128)}, f32[128,2048]{1,0:T(8,128)S(1)}, u32[]{:S(2)}) copy-start(f32[128,2048]{1,0:T(8,128)S(1)} %get-tuple-element.136) | copy-start | bytes 3145732
  534.3 29.5 %copy-start.63 = (s32[1024]{0:T(1024)S(1)}, s32[1024]{0:T(1024)}, u32[]{:S(2)}) copy-start(s32[1024]{0:T(1024)} %copy-done.62) | copy-start | bytes 12292
  535.5 208.0 %all-reduce.15.cloned.1.call-start = ((), (), s32[]{:S(2)}) async-start(), calls=%async_computation.11 | async-start | bytes 9437184 | tf_op jit(solution)/shard_map/psum | solution.py:382
  575.7 5.5 copy-start.7
  575.7 5.5 copy-start.25
  585.8 5.7 slice-start
  587.7 3.8 slice-start.1
  587.7 3.8 copy-start.12
  597.0 32.5 %collective-permute-start.3 = (bf16[1024,128]{0,1:T(8,128)(2,1)}, bf16[1024,128]{0,1:T(8,128)(2,1)}, u32[]{:S(2)}, u32[]{:S(2)}) collective-permute-start(bf16[1024,128]{0,1:T(8,128)(2,1)} %get-tuple-element.141), channel_id=1, source_target_pairs={{0,1},{1,0},{2,3},{3,2},{4,5},{5,4},{6,7},{7,6},{8,9},{9,8},{10,11... | collective-permute-start | bytes 786440 | tf_op jit(solution)/shard_map/ppermute | solution.py:12
  601.7 10.9 %copy-start.19 = (f32[512,4,128]{2,0,1:T(8,128)}, f32[512,4,128]{2,0,1:T(8,128)S(1)}, u32[]{:S(2)}) copy-start(f32[512,4,128]{2,0,1:T(8,128)S(1)} %convolution_bitcast_fusion.3) | copy-start | bytes 3145732
  603.2 5.8 copy-start.65
  606.0 6.6 copy-start.18
  609.0 3.5 copy-start.27
  611.0 21.0 %collective-permute-start.2 = (bf16[1024,128]{0,1:T(8,128)(2,1)}, bf16[1024,128]{0,1:T(8,128)(2,1)}, u32[]{:S(2)}, u32[]{:S(2)}) collective-permute-start(bf16[1024,128]{0,1:T(8,128)(2,1)} %fusion.97), channel_id=1, source_target_pairs={{0,1},{1,0},{2,3},{3,2},{4,5},{5,4},{6,7},{7,6},{8,9},{9,8},{10,11... | collective-permute-start | bytes 786440 | tf_op jit(solution)/shard_map/ppermute | solution.py:12
  612.7 4.8 copy-start.8
  612.7 4.8 copy-start.47
  612.7 4.7 copy-start.74
  617.5 3.9 copy-start.59
  623.4 6.1 copy-start.45
  623.4 7.1 copy-start.5
  634.9 145.5 %reduce-scatter.5.cloned.1.call-start = ((), (), s32[]{:S(2)}) async-start(), calls=%async_computation.9 | async-start | bytes 4718592 | tf_op jit(solution)/shard_map/reduce_scatter | solution.py:364
  647.0 6.6 copy-start.43
  661.7 273.6 %all-reduce.13.cloned.1.call-start = ((), (), s32[]{:S(2)}) async-start(), calls=%async_computation.10 | async-start | bytes 2097152 | tf_op jit(solution)/shard_map/psum | solution.py:387
  664.1 4.0 copy-start.14
  668.1 5.9 copy-start.36
  668.1 5.9 copy-start.87
  674.0 4.6 copy-start.84
  743.5 4.4 copy-start.37
  747.9 32.6 %copy-start.13 = (bf16[128,2048]{1,0:T(8,128)(2,1)S(1)}, bf16[128,2048]{1,0:T(8,128)(2,1)}, u32[]{:S(2)}) copy-start(bf16[128,2048]{1,0:T(8,128)(2,1)} %param.29) | copy-start | bytes 1572868
  747.9 32.5 %copy-start.53 = (f32[2048]{0:T(1024)S(1)}, f32[2048]{0:T(1024)}, u32[]{:S(2)}) copy-start(f32[2048]{0:T(1024)} %copy-done.52) | copy-start | bytes 24580
  747.9 32.5 %copy-start.76 = (f32[128]{0:T(128)S(1)}, f32[128]{0:T(128)}, u32[]{:S(2)}) copy-start(f32[128]{0:T(128)} %copy-done.75) | copy-start | bytes 1540
  750.5 31.6 %copy-start.79 = (f32[128]{0:T(128)S(1)}, f32[128]{0:T(128)}, u32[]{:S(2)}) copy-start(f32[128]{0:T(128)} %copy-done.78) | copy-start | bytes 1540
  750.5 99.9 %copy-start.73 = (f32[128]{0:T(128)S(1)}, f32[128]{0:T(128)}, u32[]{:S(2)}) copy-start(f32[128]{0:T(128)} %copy-done.72) | copy-start | bytes 1540
  850.4 87.2 %copy-start.1 = (bf16[1,768,2048]{2,1,0:T(8,128)(2,1)S(1)}, bf16[1,768,2048]{2,1,0:T(8,128)(2,1)}, u32[]{:S(2)}) copy-start(bf16[1,768,2048]{2,1,0:T(8,128)(2,1)} %param.42) | copy-start | bytes 9437188
  (38 other events, 70.6 us)
Sparse Core Ops, SparseCore 0:
  12.7 35.7 all-gather.2
  124.1 51.3 reduce-scatter.2
  535.6 28.0 all-gather.4
  635.1 108.4 all-reduce.14
  745.9 34.4 reduce-scatter.4
  785.8 149.3 all-reduce.12
where the time goes:
time: 955 us; the launch traced here: 945 us
  waiting for transfers between devices  353 us (37%)
  blocking collectives  189 us (20%)
  local copies, waits for them, and re-layouts  167 us (17%)
  matrix products  123 us (13%)
  other arithmetic  83.6 us (9%)
  between operations  16 us (2%)
  starting transfers between devices  12.9 us (1%)
    psum x1, waiting for transfers between devices, on_device(): lax.psum((grad_gain_one, grad_gain_two, grad_gain_query, grad_gain_key, g...  80.6 us
    psum x1, blocking collectives, on_device(): lax.psum((grad_gain_one, grad_gain_two, grad_gain_query, grad_gain_key, g...  68.3 us
    all_to_all x1, blocking collectives, on_device(): lax.all_to_all(send_rows, ('expert', 'shard'), split_axis=0, concat_axis=...  61.7 us
    psum x1, waiting for transfers between devices, on_device(): lax.psum(grad_wquery.astype(jnp.bfloat16), 'expert').astype(jnp.float32)  60.3 us
    all_to_all x1, blocking collectives, on_device(): lax.all_to_all(send_grads, ('expert', 'shard'), split_axis=0, concat_axis...  58.8 us
    all_to_all x1, waiting for transfers between devices, on_device(): lax.all_to_all(grad_in, ('expert', 'shard'), split_axis=0, concat_axis=0,...  52.2 us
    reduce_scatter x1, waiting for transfers between devices, on_device(): lax.psum_scatter(jnp.dot(attn_low[picked], w_out, preferred_element_type=...  42.3 us
    all_to_all x1, waiting for transfers between devices, on_device(): lax.all_to_all(produced, ('expert', 'shard'), split_axis=0, concat_axis=0...  37.5 us
  transfers between devices with their start and end apart: 12, of which 8 were waited for; matrix products, arithmetic and copies ran while one was open for 17% of the time, Pallas kernels for 0%

commit v1 on v0

v1 whole, which is shorter than its diff:
```python
import functools

import jax
import jax.numpy as jnp
from jax import lax
from jax.experimental import pallas as pl
from jax.experimental.pallas import tpu as pltpu
from jax.sharding import PartitionSpec as P

EPS = 1e-06
ROPE_BASE = 1000000.0
LOG2E = 1.4426950408889634
T = 128
D = 2048
HEAD = 128
LH = 4
E = 128
CAP = 5
SLOTS = E * CAP
SEG = D // 128
ROWS = 1024
HALF = 512
F = 768
bf16 = jnp.bfloat16
f32 = jnp.float32
ALL = ("expert", "shard")


def dot(a, b):
    return jnp.dot(a, b, preferred_element_type=f32)


def dot_t(a, b):
    return lax.dot_general(a, b, (((1,), (1,)), ((), ())), preferred_element_type=f32)


def call(kernel, name, outs, scratch, args, flops=0, smem=()):
    in_specs = [
        pl.BlockSpec(memory_space=pltpu.SMEM if i in smem else pltpu.VMEM)
        for i in range(len(args))
    ]
    bytes_accessed = sum(a.size * a.dtype.itemsize for a in args) + sum(
        s.size * s.dtype.itemsize for s in outs
    )
    return pl.pallas_call(
        kernel,
        out_shape=outs,
        in_specs=in_specs,
        out_specs=[pl.BlockSpec(memory_space=pltpu.VMEM) for _ in outs],
        scratch_shapes=scratch,
        compiler_params=pltpu.CompilerParams(vmem_limit_bytes=56 * 1024 * 1024),
        cost_estimate=pl.CostEstimate(
            flops=flops, bytes_accessed=bytes_accessed, transcendentals=0
        ),
        name=name,
    )(*args)


def sds(shape, dtype):
    return jax.ShapeDtypeStruct(shape, dtype)


def load_rows(payload_ref, buf):
    def body(i, carry):
        rows = pl.ds(pl.multiple_of(i * SLOTS, SLOTS), SLOTS)
        buf[rows, :] = payload_ref[rows, :].astype(f32)
        return carry

    lax.fori_loop(0, SEG, body, 0)


def rows_chunk(buf, j):
    low = buf[pl.ds(2 * j, SLOTS, stride=SEG), :]
    high = buf[pl.ds(2 * j + 1, SLOTS, stride=SEG), :]
    return jnp.concatenate([low, high], axis=1).astype(bf16)


def put_chunk(buf, j, values):
    buf[pl.ds(2 * j, SLOTS, stride=SEG), :] = values[:, :128]
    buf[pl.ds(2 * j + 1, SLOTS, stride=SEG), :] = values[:, 128:]


def store_rows(payload_ref, buf):
    def body(i, carry):
        rows = pl.ds(pl.multiple_of(i * SLOTS, SLOTS), SLOTS)
        payload_ref[rows, :] = buf[rows, :].astype(bf16)
        return carry

    lax.fori_loop(0, SEG, body, 0)


def pack_body(x_ref, at_ref, out_ref, buf):
    slot = lax.broadcasted_iota(jnp.int32, (SLOTS, T), 0)
    hit = slot == at_ref[0:1, :]
    for k in range(1, 4):
        hit = hit | (slot == at_ref[k : k + 1, :])
    pick = jnp.where(hit, 1.0, 0.0).astype(bf16)
    for j in range(SEG // 2):
        put_chunk(buf, j, dot(pick, x_ref[:, j * 256 : (j + 1) * 256]))
    store_rows(out_ref, buf)


def pack(x, assign_t):
    return call(
        pack_body,
        "pack_rows",
        [sds((SLOTS * SEG, 128), bf16)],
        [pltpu.VMEM((SLOTS * SEG, 128), f32)],
        (x, assign_t),
        flops=2 * SLOTS * T * D,
    )[0]


def gate_matrix(assign_ref, gates_ref):
    lane = lax.broadcasted_iota(jnp.int32, (T, SLOTS), 1)
    total = jnp.where(lane == assign_ref[:, 0:1], gates_ref[:, 0:1], 0.0)
    for k in range(1, 4):
        total = total + jnp.where(lane == assign_ref[:, k : k + 1], gates_ref[:, k : k + 1], 0.0)
    high = total.astype(bf16)
    return high, (total - high.astype(f32)).astype(bf16)


def qkv_body(piece, xa, xb, g1, wt, gq, gk, cos, sin, qraw, qt, kraw, kt, vt, n1):
    for half, ref in ((0, xa), (1, xb)):
        x = ref[...].astype(f32)
        r = lax.rsqrt(jnp.mean(x * x, axis=-1, keepdims=True) + EPS)
        n1[half * T : (half + 1) * T, :] = (x * r * g1[...]).astype(bf16)
    raw = dot_t(wt[...], n1[...])
    first, second = piece * T, HALF + piece * T
    c = jnp.concatenate([cos[:, first : first + T], cos[:, second : second + T]], axis=1)
    s = jnp.concatenate([sin[:, first : first + T], sin[:, second : second + T]], axis=1)

    def path(v, gain, factor):
        v = v * lax.rsqrt(jnp.mean(v * v, axis=0, keepdims=True) + EPS) * gain
        low, high = v[:64], v[64:]
        return (
            ((low * c - high * s) * factor).astype(bf16),
            ((high * c + low * s) * factor).astype(bf16),
        )

    qraw[...] = raw[: LH * HEAD]
    for h in range(LH):
        low, high = path(raw[h * HEAD : (h + 1) * HEAD], gq[...], HEAD ** (-0.5))
        qt[h * HEAD : h * HEAD + 64, :] = low
        qt[h * HEAD + 64 : (h + 1) * HEAD, :] = high
    key = raw[LH * HEAD : (LH + 1) * HEAD].astype(bf16)
    kraw[...] = key
    low, high = path(key.astype(f32), gk[...], 1.0)
    kt[:64, :] = low
    kt[64:, :] = high
    vt[...] = raw[(LH + 1) * HEAD :].astype(bf16)


def qkv(piece, xa, xb, g1, wt, gq, gk, cos, sin):
    return call(
        functools.partial(qkv_body, piece),
        f"qkv{piece}",
        [
            sds((LH * HEAD, 2 * T), f32),
            sds((LH * HEAD, 2 * T), bf16),
            sds((HEAD, 2 * T), bf16),
            sds((HEAD, 2 * T), bf16),
            sds((HEAD, 2 * T), bf16),
            sds((2 * T, D), bf16),
        ],
        [],
        (xa, xb, g1, wt, gq, gk, cos, sin),
        flops=2 * 2 * T * D * 768,
    )


def build_mask(info, mask):
    for b in range(8):
        keys = jnp.broadcast_to(info[0:1, b * T : (b + 1) * T], (T, T)).T
        for j in range(8):
            cols = slice(j * T, (j + 1) * T)
            inside = (keys >= info[1:2, cols]) & (keys <= info[0:1, cols])
            mask[b * T : (b + 1) * T, cols] = jnp.where(inside, 1.0, 0.0)


def attend_body(*refs):
    q, k, v = refs[0:4], refs[4:8], refs[8:12]
    info, ot0, ot1, linv, qt, kt, kn, vn, mask, vt = refs[12:]
    for dy in range(4):
        for dc in range(2):
            to = slice(dc * HALF + dy * T, dc * HALF + (dy + 1) * T)
            src = slice(dc * T, (dc + 1) * T)
            qt[:, to] = q[dy][:, src]
            kt[:, to] = k[dy][:, src]
            vt[:, to] = v[dy][:, src]
    for b in range(8):
        rows = slice(b * T, (b + 1) * T)
        kn[rows, :] = kt[:, rows].astype(f32).T.astype(bf16)
        vn[rows, :] = vt[:, rows].astype(f32).T.astype(bf16)
    build_mask(info, mask)
    for half, out in ((1, ot1), (0, ot0)):

        def body(i, carry):
            local = pl.ds(pl.multiple_of(i * 256, 256), 256)
            cols = pl.ds(pl.multiple_of(half * HALF + i * 256, 256), 256)
            for h in range(LH):
                heads = slice(h * HEAD, (h + 1) * HEAD)
                scores = dot(kn[...], qt[heads, cols])
                weights = jnp.exp2(scores * LOG2E) * mask[:, cols]
                inverse = 1.0 / jnp.sum(weights, axis=0, keepdims=True)
                out[heads, local] = (dot(vt[...], weights.astype(bf16)) * inverse).astype(bf16)
                linv[h : h + 1, cols] = inverse
            return carry

        lax.fori_loop(0, 2, body, 0)


def attend(q, k, v, info):
    return call(
        attend_body,
        "attend",
        [
            sds((LH * HEAD, HALF), bf16),
            sds((LH * HEAD, HALF), bf16),
            sds((8, ROWS), f32),
            sds((LH * HEAD, ROWS), bf16),
            sds((HEAD, ROWS), bf16),
            sds((ROWS, HEAD), bf16),
            sds((ROWS, HEAD), bf16),
        ],
        [pltpu.VMEM((ROWS, ROWS), f32), pltpu.VMEM((HEAD, ROWS), bf16)],
        (*q, *k, *v, info),
        flops=4 * LH * ROWS * ROWS * HEAD,
    )


def outproj_body(ot0, otr, wa, wb, b0, b1, b2, b3):
    def body(i, carry):
        rows = pl.ds(pl.multiple_of(i * 512, 512), 512)
        total = dot(wa[rows, :], ot0[...]) + dot(wb[rows, :], otr[...])
        for dy, out in enumerate((b0, b1, b2, b3)):
            out[rows, :] = total[:, dy * T : (dy + 1) * T].astype(bf16)
        return carry

    lax.fori_loop(0, 4, body, 0)


def outproj(ot0, otr, wa, wb):
    return call(
        outproj_body,
        "out_projection",
        [sds((D, T), bf16)] * 4,
        [],
        (ot0, otr, wa, wb),
        flops=2 * D * 1024 * HALF,
    )


def router_body(
    b0, b1, b2, b3, x0, g2, wr, routes, at, hidden, n2, probs, gates, payload, buf
):
    for j in range(SEG):
        rows = slice(j * 128, (j + 1) * 128)
        total = (
            b0[rows, :].astype(f32)
            + b1[rows, :].astype(f32)
            + b2[rows, :].astype(f32)
            + b3[rows, :].astype(f32)
        )
        hidden[:, rows] = x0[:, rows].astype(f32) + total.T
    v = hidden[...]
    r = lax.rsqrt(jnp.mean(v * v, axis=-1, keepdims=True) + EPS)
    n2[...] = (v * r * g2[...]).astype(bf16)
    pack_body(n2, at, payload, buf)
    logits = dot(n2[...], wr[...])
    expo = jnp.exp(logits - jnp.max(logits, axis=-1, keepdims=True))
    p = expo / jnp.sum(expo, axis=-1, keepdims=True)
    probs[...] = p
    lane = lax.broadcasted_iota(jnp.int32, (T, E), 1)
    chosen = [
        jnp.sum(jnp.where(lane == routes[:, k : k + 1], p, 0.0), axis=-1, keepdims=True)
        for k in range(4)
    ]
    total = chosen[0] + chosen[1] + chosen[2] + chosen[3]
    packed = jnp.where(lane == 4, total, 0.0)
    for k in range(4):
        packed = jnp.where(lane == k, chosen[k] / total, packed)
    gates[...] = packed


def router(b, x0, g2, wr, routes, assign_t):
    return call(
        router_body,
        "router",
        [
            sds((T, D), f32),
            sds((T, D), bf16),
            sds((T, E), f32),
            sds((T, E), f32),
            sds((SLOTS * SEG, 128), bf16),
        ],
        [pltpu.VMEM((SLOTS * SEG, 128), f32)],
        (*b, x0, g2, wr, routes, assign_t),
        flops=2 * SLOTS * T * D,
    )


def expert_grad_body(payload, wd, gr, ga, buf):
    load_rows(payload, buf)
    for j in range(SEG // 2):
        gr[:, j * 256 : (j + 1) * 256] = rows_chunk(buf, j)

    def body(i, carry):
        cols = pl.ds(pl.multiple_of(i * 256, 256), 256)
        ga[:, cols] = dot_t(gr[...], wd[cols, :])
        return carry

    lax.fori_loop(0, F // 256, body, 0)


def expert_grad(payload, wd):
    return call(
        expert_grad_body,
        "expert_grad_rows",
        [sds((SLOTS, D), bf16), sds((SLOTS, F), f32)],
        [pltpu.VMEM((SLOTS * SEG, 128), f32)],
        (payload, wd),
        flops=2 * SLOTS * D * F,
    )


def expert_main_body(payload, wg, wu, ga, back, xr, act, dg, du, sc, buf):
    load_rows(payload, buf)
    for j in range(SEG // 2):
        xr[:, j * 256 : (j + 1) * 256] = rows_chunk(buf, j)
    sc[...] = jnp.zeros_like(sc)

    def forward(i, carry):
        cols = pl.ds(pl.multiple_of(i * 256, 256), 256)
        gate = dot(xr[...], wg[:, cols])
        up = dot(xr[...], wu[:, cols])
        grad = ga[:, cols]
        s = 1.0 / (1.0 + jnp.exp(-gate))
        silu = gate * s
        a = (silu * up).astype(bf16)
        act[:, cols] = a
        dg[:, cols] = (grad * up * s * (1.0 + gate * (1.0 - s))).astype(bf16)
        du[:, cols] = (grad * silu).astype(bf16)
        sc[...] += jnp.sum(a.astype(f32) * grad, axis=1, keepdims=True)
        return carry

    lax.fori_loop(0, F // 256, forward, 0)
    for j in range(SEG // 2):
        rows = slice(j * 256, (j + 1) * 256)
        put_chunk(buf, j, dot_t(dg[...], wg[rows, :]) + dot_t(du[...], wu[rows, :]))
    store_rows(back, buf)


def expert_main(payload, wg, wu, ga):
    return call(
        expert_main_body,
        "expert_main",
        [
            sds((SLOTS * SEG, 128), bf16),
            sds((SLOTS, D), bf16),
            sds((SLOTS, F), bf16),
            sds((SLOTS, F), bf16),
            sds((SLOTS, F), bf16),
            sds((SLOTS, 1), f32),
        ],
        [pltpu.VMEM((SLOTS * SEG, 128), f32)],
        (payload, wg, wu, ga),
        flops=8 * SLOTS * D * F,
    )


def expert_out_body(act, wd, payload, buf):
    for j in range(SEG // 2):
        put_chunk(buf, j, dot(act[...], wd[:, j * 256 : (j + 1) * 256]))
    store_rows(payload, buf)


def expert_out(act, wd):
    return call(
        expert_out_body,
        "expert_out",
        [sds((SLOTS * SEG, 128), bf16)],
        [pltpu.VMEM((SLOTS * SEG, 128), f32)],
        (act, wd),
        flops=2 * SLOTS * D * F,
    )[0]


def combine_body(
    payload, scin, hidden, n2, probs, gates, routes, slots, assign, og, g2, wr,
    ghid, gatt, grouter, gg2, buf, gn2,
):
    load_rows(payload, buf)
    high, low = gate_matrix(assign, gates)
    lane = lax.broadcasted_iota(jnp.int32, (T, E), 1)
    grads = []
    for k in range(4):
        hot = jnp.where(lane == routes[:, k : k + 1], 1.0, 0.0)
        rows = lax.dot_general(
            hot, scin[...], (((1,), (0,)), ((), ())),
            precision=lax.Precision.HIGHEST, preferred_element_type=f32,
        )
        picked = jnp.where(lane == slots[:, k : k + 1], rows, 0.0)
        grads.append(jnp.sum(picked, axis=-1, keepdims=True))
    inner = sum(grads[k] * gates[:, k : k + 1] for k in range(4))
    inverse = 1.0 / gates[:, 4:5]
    grad_probs = jnp.zeros((T, E), f32)
    for k in range(4):
        grad_probs = jnp.where(
            lane == routes[:, k : k + 1], (grads[k] - inner) * inverse, grad_probs
        )
    p = probs[...]
    gl = (p * (grad_probs - jnp.sum(p * grad_probs, axis=-1, keepdims=True))).astype(bf16)
    for j in range(SEG // 2):
        cols = slice(j * 256, (j + 1) * 256)
        rows = rows_chunk(buf, j)
        gn2[:, cols] = dot(high, rows) + dot(low, rows) + dot_t(gl, wr[cols, :])
    c = gn2[...]
    v = hidden[...]
    r = lax.rsqrt(jnp.mean(v * v, axis=-1, keepdims=True) + EPS)
    u = c * g2[...]
    m = jnp.mean(u * v, axis=-1, keepdims=True)
    total = og[...].astype(f32) + r * u - v * (r * r * r * m)
    ghid[...] = total
    gatt[...] = total.astype(bf16)
    gg2[...] = jnp.sum(c * (v * r), axis=0, keepdims=True)
    for j in range(SEG):
        cols = slice(j * 128, (j + 1) * 128)
        grouter[cols, :] = dot(n2[:, cols].astype(f32).T.astype(bf16), gl).astype(bf16)


def combine(payload, scin, hidden, n2, probs, gates, routes, slots, assign, og, g2, wr):
    return call(
        combine_body,
        "combine_grads",
        [sds((T, D), f32), sds((T, D), bf16), sds((D, E), bf16), sds((1, D), f32)],
        [pltpu.VMEM((SLOTS * SEG, 128), f32), pltpu.VMEM((T, D), f32)],
        (payload, scin, hidden, n2, probs, gates, routes, slots, assign, og, g2, wr),
        flops=4 * SLOTS * T * D,
    )


def result_body(payload, hidden, gates, assign, out, buf):
    load_rows(payload, buf)
    high, low = gate_matrix(assign, gates)
    for j in range(SEG // 2):
        cols = slice(j * 256, (j + 1) * 256)
        rows = rows_chunk(buf, j)
        out[:, cols] = (hidden[:, cols] + dot(high, rows) + dot(low, rows)).astype(bf16)


def result_rows(payload, hidden, gates, assign):
    return call(
        result_body,
        "result",
        [sds((T, D), bf16)],
        [pltpu.VMEM((SLOTS * SEG, 128), f32)],
        (payload, hidden, gates, assign),
        flops=4 * SLOTS * T * D,
    )[0]


def pre_body(*refs):
    blocks, (ot0, ot1, wo, gw, dt, rows_all) = refs[:8], refs[8:]
    for b in range(8):
        rows_all[b * T : (b + 1) * T, :] = blocks[b][...]

    def weight(i, carry):
        cols = pl.ds(pl.multiple_of(i * 256, 256), 256)
        gw[:, cols] = (
            dot(ot0[...], rows_all[:HALF, cols]) + dot(ot1[...], rows_all[HALF:, cols])
        ).astype(bf16)
        return carry

    lax.fori_loop(0, 8, weight, 0)

    def heads(i, carry):
        tokens = pl.ds(pl.multiple_of(i * 256, 256), 256)
        dt[:, tokens] = dot_t(wo[...], rows_all[tokens, :]).astype(bf16)
        return carry

    lax.fori_loop(0, 4, heads, 0)


def pre(blocks, ot0, ot1, wo):
    return call(
        pre_body,
        "out_projection_grad",
        [sds((LH * HEAD, D), bf16), sds((LH * HEAD, ROWS), bf16)],
        [pltpu.VMEM((ROWS, D), bf16)],
        (*blocks, ot0, ot1, wo),
        flops=4 * 512 * ROWS * D,
    )


def bwd_body(*refs):
    qr, kr = refs[0:4], refs[4:8]
    (qt, kt, kn, vn, dt, ot0, ot1, linv, info, cos, sin, gq, gk) = refs[8:21]
    dq0, dq1, dkv, ggq, ggk, mask, wb, sb, dqt, dk, dv, raw = refs[21:]
    build_mask(info, mask)
    dk[...] = jnp.zeros_like(dk)
    dv[...] = jnp.zeros_like(dv)
    for half, out in ((0, ot0), (1, ot1)):

        def body(i, carry):
            local = pl.ds(pl.multiple_of(i * 256, 256), 256)
            cols = pl.ds(pl.multiple_of(half * HALF + i * 256, 256), 256)
            for h in range(LH):
                heads = slice(h * HEAD, (h + 1) * HEAD)
                part = slice(h * 256, (h + 1) * 256)
                scores = dot(kn[...], qt[heads, cols])
                weights = jnp.exp2(scores * LOG2E) * (mask[:, cols] * linv[h : h + 1, cols])
                grad = dt[heads, cols]
                delta = jnp.sum(
                    grad.astype(f32) * out[heads, local].astype(f32), axis=0, keepdims=True
                )
                wb[:, part] = weights.astype(bf16)
                sb[:, part] = (weights * (dot(vn[...], grad) - delta)).astype(bf16)
                dqt[heads, cols] = dot(kt[...], sb[:, part])
            grads = jnp.concatenate(
                [dt[h * HEAD : (h + 1) * HEAD, cols] for h in range(LH)], axis=1
            )
            queries = jnp.concatenate(
                [qt[h * HEAD : (h + 1) * HEAD, cols] for h in range(LH)], axis=1
            )
            dv[...] += dot_t(wb[...], grads)
            dk[...] += dot_t(sb[...], queries)
            return carry

        lax.fori_loop(0, 2, body, 0)

    def unrope(v):
        low, high = v[:64], v[64:]
        c, s = cos[...], sin[...]
        return jnp.concatenate([low * c + high * s, high * c - low * s], axis=0)

    def norm_back(v, grad, gain):
        r = lax.rsqrt(jnp.mean(v * v, axis=0, keepdims=True) + EPS)
        n = v * r
        gain_grad = jnp.sum(grad * n, axis=1, keepdims=True)
        u = grad * gain
        return r * (u - n * jnp.mean(u * n, axis=0, keepdims=True)), gain_grad

    total = jnp.zeros((HEAD, 1), f32)
    for h in range(LH):
        heads = slice(h * HEAD, (h + 1) * HEAD)
        for dy in range(4):
            for dc in range(2):
                to = slice(dc * HALF + dy * T, dc * HALF + (dy + 1) * T)
                raw[:, to] = qr[dy][heads, dc * T : (dc + 1) * T]
        grad, part = norm_back(raw[...], unrope(dqt[heads, :] * (HEAD ** (-0.5))), gq[...])
        total = total + part
        dq0[heads, :] = grad[:, :HALF].astype(bf16)
        dq1[heads, :] = grad[:, HALF:].astype(bf16)
    ggq[...] = total
    for dy in range(4):
        for dc in range(2):
            to = slice(dc * HALF + dy * T, dc * HALF + (dy + 1) * T)
            raw[:, to] = kr[dy][:, dc * T : (dc + 1) * T].astype(f32)
    grad, part = norm_back(raw[...], unrope(dk[...].T), gk[...])
    ggk[...] = part
    dkv[:HEAD, :] = grad.astype(bf16)
    dkv[HEAD:, :] = dv[...].T.astype(bf16)


def bwd(qr, kr, *rest):
    return call(
        bwd_body,
        "attend_grad",
        [
            sds((LH * HEAD, HALF), bf16),
            sds((LH * HEAD, HALF), bf16),
            sds((2 * HEAD, ROWS), bf16),
            sds((HEAD, 1), f32),
            sds((HEAD, 1), f32),
        ],
        [
            pltpu.VMEM((ROWS, ROWS), f32),
            pltpu.VMEM((ROWS, LH * 256), bf16),
            pltpu.VMEM((ROWS, LH * 256), bf16),
            pltpu.VMEM((LH * HEAD, ROWS), f32),
            pltpu.VMEM((ROWS, HEAD), f32),
            pltpu.VMEM((ROWS, HEAD), f32),
            pltpu.VMEM((HEAD, ROWS), f32),
        ],
        (*qr, *kr, *rest),
        flops=10 * LH * ROWS * ROWS * HEAD,
    )


def qkv_grad_body(core, n1t, dq0, dq1, own, sib, out, tot, dt):
    tot[:, :HALF] = (own[:, :HALF].astype(f32) + sib[:, HALF:].astype(f32)).astype(bf16)
    tot[:, HALF:] = (own[:, HALF:].astype(f32) + sib[:, :HALF].astype(f32)).astype(bf16)
    dt[:512, :HALF] = dq0[...]
    dt[:512, HALF:] = dq1[...]
    upper = core[0] == 1
    dt[512:576, :] = jnp.where(upper, tot[64:128, :], tot[:64, :])
    dt[576:, :] = jnp.where(upper, tot[192:, :], tot[128:192, :])

    def body(i, carry):
        rows = pl.ds(pl.multiple_of(i * 512, 512), 512)
        out[rows, :] = dot_t(n1t[rows, :], dt[...]).astype(bf16)
        return carry

    lax.fori_loop(0, 4, body, 0)


def qkv_grad(core, n1t, dq0, dq1, own, sib):
    return call(
        qkv_grad_body,
        "qkv_weight_grad",
        [sds((D, 640), bf16), sds((2 * HEAD, ROWS), bf16)],
        [pltpu.VMEM((640, ROWS), bf16)],
        (core, n1t, dq0, dq1, own, sib),
        flops=2 * D * 640 * ROWS,
        smem=(0,),
    )


def normed_grad_body(wa, wb, wkv, dq0, dqr, tot, n1t, g1, b0, b1, b2, b3, gg1):
    def body(i, carry):
        rows = pl.ds(pl.multiple_of(i * 512, 512), 512)
        total = (
            dot(wa[rows, :], dq0[...])
            + dot(wb[rows, :], dqr[...])
            + dot(wkv[rows, :], tot[:, :HALF])
        )
        for dy, out in enumerate((b0, b1, b2, b3)):
            out[rows, :] = total[:, dy * T : (dy + 1) * T].astype(bf16)
        gain = jnp.sum(total * n1t[rows, :HALF].astype(f32), axis=1, keepdims=True)
        gg1[rows, :] = gain / g1[rows, :]
        return carry

    lax.fori_loop(0, 4, body, 0)


def normed_grad(wa, wb, wkv, dq0, dqr, tot, n1t, g1):
    return call(
        normed_grad_body,
        "normed_grad",
        [sds((D, T), bf16)] * 4 + [sds((D, 1), f32)],
        [],
        (wa, wb, wkv, dq0, dqr, tot, n1t, g1),
        flops=2 * D * 1280 * HALF,
    )


def final_body(b0, b1, b2, b3, x0, ghid, g1, out, c):
    for j in range(SEG):
        rows = slice(j * 128, (j + 1) * 128)
        total = (
            b0[rows, :].astype(f32)
            + b1[rows, :].astype(f32)
            + b2[rows, :].astype(f32)
            + b3[rows, :].astype(f32)
        )
        c[:, rows] = total.T
    v = x0[...].astype(f32)
    r = lax.rsqrt(jnp.mean(v * v, axis=-1, keepdims=True) + EPS)
    u = c[...] * g1[...]
    m = jnp.mean(u * v, axis=-1, keepdims=True)
    out[...] = ghid[...] + r * u - v * (r * r * r * m)


def final(b, x0, ghid, g1):
    return call(
        final_body,
        "input_grad",
        [sds((T, D), f32)],
        [pltpu.VMEM((T, D), f32)],
        (*b, x0, ghid, g1),
        flops=T * D * 10,
    )[0]


def sibling(x):
    return lax.ppermute(x, "shard", [(i, i ^ 1) for i in range(8)])


def from_chip(x, dy):
    return lax.ppermute(x, "shard", [(i, (i - 2 * dy) % 8) for i in range(8)])


def to_chip(x, dy):
    return lax.ppermute(x, "shard", [(i, (i + 2 * dy) % 8) for i in range(8)])


def gather_blocks(x):
    first = [x] + [from_chip(x, dy) for dy in (1, 2, 3)]
    return first, [sibling(b) for b in first]


def exchange(x):
    return lax.all_to_all(x, ALL, split_axis=0, concat_axis=0, tiled=True)


def exchange_rows(payload):
    return exchange(payload.reshape(E, CAP * SEG, 128)).reshape(SLOTS * SEG, 128)


def exchange_slots(values):
    wide = jnp.pad(values.reshape(E, CAP), ((0, 0), (0, 128 - CAP)))
    return exchange(wide.reshape(E, 1, 128)).reshape(E, 128)


def on_device(
    block_input, out_grad, norm1_gain, w_query, w_key, w_value, query_gain, key_gain, w_out,
    norm2_gain, w_router, w_gate, w_up, w_down, seq_lengths, token_places, expert_routes,
):
    shard = lax.axis_index("shard")
    chip, core = shard // 2, shard % 2
    g1 = norm1_gain.astype(f32).reshape(1, D)
    g2 = norm2_gain.astype(f32).reshape(1, D)
    g1_col = norm1_gain.astype(f32).reshape(D, 1)
    gq = query_gain.astype(f32).reshape(HEAD, 1)
    gk = key_gain.astype(f32).reshape(HEAD, 1)

    x_own, x_sib = gather_blocks(block_input)

    chips = (chip + jnp.arange(4)) % 4
    order = jnp.concatenate([chips * 2 + core, chips * 2 + 1 - core])
    places = token_places[0].reshape(8, T)[order].reshape(ROWS)
    lengths = seq_lengths[0]
    ends = jnp.cumsum(lengths)
    starts = jnp.sum(
        jnp.where(places[:, None] >= ends[None, :], lengths[None, :], 0), axis=1
    )
    positions = (places - starts).astype(f32)
    info = jnp.concatenate(
        [places[None].astype(f32), starts[None].astype(f32), jnp.zeros((6, ROWS), f32)], axis=0
    )
    inverse_freq = ROPE_BASE ** (-jnp.arange(0, HEAD, 2).astype(f32) / HEAD)
    angles = inverse_freq[:, None] * positions[None, :]
    cos, sin = jnp.cos(angles), jnp.sin(angles)

    routes = expert_routes
    hot = (routes[:, :, None] == jnp.arange(E, dtype=jnp.int32)).astype(f32)
    earlier = jnp.tril(jnp.ones((T, T), bf16), -1)
    before = dot(earlier, jnp.sum(hot, axis=1).astype(bf16))
    slots = jnp.sum(before[:, None, :] * hot, axis=2).astype(jnp.int32)
    assign = routes * CAP + slots
    assign_t = assign.T

    wkv_t = jnp.concatenate([w_key.T, w_value.T], axis=0)
    wkv_ts = sibling(wkv_t)
    lower = core == 0
    wkv_low = jnp.where(lower, wkv_t, wkv_ts)
    wkv_high = jnp.where(lower, wkv_ts, wkv_t)
    wkv_ft = jnp.concatenate([wkv_low[:64], wkv_high[:64], wkv_low[64:], wkv_high[64:]], axis=0)
    w_t = jnp.concatenate([w_query.T, wkv_ft], axis=0)
    wo_t = w_out.T
    wo_ts = sibling(wo_t)
    wq_s = sibling(w_query)

    pieces = [qkv(dy, x_own[dy], x_sib[dy], g1, w_t, gq, gk, cos, sin) for dy in range(4)]
    q_raw, q, k_raw, k, v, n1 = zip(*pieces)
    og_payload = pack(out_grad, assign_t)
    og_payload, _ = lax.optimization_barrier((og_payload, x_own[2]))
    got_grads = exchange_rows(og_payload)
    ot0, ot1, linv, qt, kt, kn, vn = attend(q, k, v, info)
    blocks = outproj(ot0, sibling(ot1), wo_t, wo_ts)
    blocks = [blocks[0]] + [to_chip(blocks[dy], dy) for dy in (1, 2, 3)]
    hidden, n2, probs, gates, payload = router(blocks, block_input, g2, w_router, routes, assign_t)
    got_rows = exchange_rows(payload)

    n1, wkv_ft, gates_late, _ = lax.optimization_barrier((n1, wkv_ft, gates, payload))
    slot_ids = jnp.arange(SLOTS, dtype=jnp.int32)
    slot_gates = jnp.sum(
        jnp.where(
            assign.reshape(-1)[:, None] == slot_ids[None, :],
            gates_late[:, :4].reshape(-1)[:, None],
            0.0,
        ),
        axis=0,
    )
    got_gates = exchange_slots(slot_gates)
    n1_t = jnp.concatenate([p[:T] for p in n1] + [p[T:] for p in n1], axis=0).T
    wkv_full = wkv_ft.T
    grad_rows, grad_act = expert_grad(got_grads, w_down[0])

    back, rows, act, dg, du, sc = expert_main(got_rows, w_gate[0], w_up[0], grad_act)
    back_sc = exchange_slots(sc)
    back_grads = exchange_rows(back)

    out_payload = expert_out(act, w_down[0])
    gate_col = got_gates[:, :CAP].reshape(SLOTS, 1)
    scaled_rows = (rows.astype(f32) * gate_col).astype(bf16)
    scaled_act = (act.astype(f32) * gate_col).astype(bf16)

    def weight_grad(a, b):
        return lax.dot_general(a, b, (((0,), (0,)), ((), ())), preferred_element_type=f32)

    grad_wgate = weight_grad(scaled_rows, dg)
    grad_wup = weight_grad(scaled_rows, du)
    grad_wdown = weight_grad(scaled_act, grad_rows)

    ghid, gatt, grouter, gg2 = combine(
        back_grads, back_sc, hidden, n2, probs, gates, routes, slots, assign, out_grad, g2, w_router
    )
    g_own, g_sib = gather_blocks(gatt)
    out_payload, grouter, _ = lax.optimization_barrier((out_payload, grouter, g_own[2]))
    returned = exchange_rows(out_payload)
    result = result_rows(returned, hidden, gates, assign)

    gwout, dt = pre(g_own + g_sib, ot0, ot1, w_out)
    grad_wout = lax.psum(gwout, "expert").astype(f32)
    router_parts = exchange(grouter.reshape(E, SEG, 128))
    router_sum = jnp.sum(router_parts.astype(f32), axis=0).astype(bf16)
    grad_router = exchange(jnp.broadcast_to(router_sum[None], (E, SEG, 128)))
    grad_router = grad_router.reshape(D, E).astype(f32)

    dq0, dq1, dkv, ggq, ggk = bwd(
        q_raw, k_raw, qt, kt, kn, vn, dt, ot0, ot1, linv, info, cos, sin, gq, gk
    )
    dq_sib, dkv_sib = sibling(dq1), sibling(dkv)
    gw, dkv_total = qkv_grad(core.reshape(1), n1_t, dq0, dq1, dkv, dkv_sib)
    gw = lax.psum(gw, "expert").astype(f32)
    blocks = normed_grad(w_query, wq_s, wkv_full, dq0, dq_sib, dkv_total, n1_t, g1_col)
    gg1 = blocks[4]
    blocks = [blocks[0]] + [to_chip(blocks[dy], dy) for dy in (1, 2, 3)]
    grad_input = final(blocks, block_input, ghid, g1)

    vector = jnp.concatenate([gg1.reshape(-1), gg2.reshape(-1), ggq.reshape(-1), ggk.reshape(-1)])
    per = vector.shape[0] // E
    wide = jnp.pad(vector.reshape(E, per), ((0, 0), (0, 128 - per))).reshape(E, 1, 128)
    mine = jnp.sum(exchange(wide), axis=0, keepdims=True)
    vector = exchange(jnp.broadcast_to(mine, (E, 1, 128)))[:, 0, :per].reshape(-1)
    return (
        result,
        grad_input,
        vector[:D],
        gw[:, :512],
        gw[:, 512:576],
        gw[:, 576:],
        vector[2 * D : 2 * D + HEAD],
        vector[2 * D + HEAD :],
        grad_wout,
        vector[D : 2 * D],
        grad_router,
        grad_wgate[None],
        grad_wup[None],
        grad_wdown[None],
    )


def solution(mesh):
    rows = P(("expert", "shard"), None)
    experts = P(("expert", "shard"), None, None)
    columns = P(None, "shard")
    return jax.shard_map(
        on_device,
        mesh=mesh,
        in_specs=(
            rows, rows, P(), columns, columns, columns, P(), P(), P("shard", None), P(), P(),
            experts, experts, experts, P("expert", None), P("expert", None), rows,
        ),
        out_specs=(
            rows, rows, P(), columns, columns, columns, P(), P(), P("shard", None), P(), P(),
            experts, experts, experts,
        ),
        check_vma=False,
    )
```

time: 955 us -> 534 us (0.56)
  waiting for transfers between devices: 353 us -> 150 us
  blocking collectives: 189 us -> 28.1 us
  Pallas kernels: 0 us -> 151 us
  matrix products: 123 us -> 17.5 us
  local copies, waits for them, and re-layouts: 167 us -> 64.8 us
  starting transfers between devices: 12.9 us -> 79.7 us
  other arithmetic: 83.6 us -> 19.4 us
    pallas_call x0 -> x18, Pallas kernels: none -> 151 us  [call(): pl.pallas_call(kernel, out_shape=outs, in_specs=in_specs, out_specs=[pl.B...]
    psum x2 -> x1, waiting for transfers between devices: 141 us -> 0.01 us  [on_device(): gw = lax.psum(gw, 'expert').astype(f32)]
    dot_general x38 -> x4, matrix products: 123 us -> 17.5 us  [the longest x3 17.3 us: weight_grad(): lax.dot_general(a, b, (((0,), (0,)), ((), ())), preferred_element_type=f32)]
    all_to_all x2, blocking collectives: 120 us -> 28.1 us  [exchange(): return lax.all_to_all(x, ALL, split_axis=0, concat_axis=0, tiled=True)]
    ppermute x4 -> x26, waiting for transfers between devices: 0.01 us -> 73.7 us  [the longest x6 52.9 us: to_chip(): return lax.ppermute(x, 'shard', [(i, (i + 2 * dy) % 8) for i in range(8)])]
    gather x15 -> x1, local copies, waits for them, and re-layouts: 71.9 us -> 0.55 us  [on_device(): places = token_places[0].reshape(8, T)[order].reshape(ROWS)]
    reduce_scatter x2 -> x0, waiting for transfers between devices: 70.6 us -> none  [the longest x1 42.3 us: on_device(): lax.psum_scatter(jnp.dot(attn_low[picked], w_out, preferred_element_type=...]
    psum x1 -> x0, blocking collectives: 68.3 us -> none  [on_device(): lax.psum((grad_gain_one, grad_gain_two, grad_gain_query, grad_gain_key, g...]
  transfers between devices with their start and end apart: 12 -> 35, of which waited for: 8 -> 13; matrix products, arithmetic and copies ran while one was open for 17% -> 15% of each run, Pallas kernels for 0% -> 25%
where the time goes in v1:
time: 534 us; the launch traced here: 526 us
  Pallas kernels  151 us (28%)
  waiting for transfers between devices  150 us (28%)
  starting transfers between devices  79.7 us (15%)
  local copies, waits for them, and re-layouts  64.8 us (12%)
  blocking collectives  28.1 us (5%)
  other arithmetic  19.4 us (4%)
  matrix products  17.5 us (3%)
  between operations  15.2 us (3%)
    pallas_call x18, Pallas kernels, call(): pl.pallas_call(kernel, out_shape=outs, in_specs=in_specs, out_specs=[pl.B...  151 us
    all_to_all x8, waiting for transfers between devices, exchange(): return lax.all_to_all(x, ALL, split_axis=0, concat_axis=0, tiled=True)  76 us
    all_to_all x8, starting transfers between devices, exchange(): return lax.all_to_all(x, ALL, split_axis=0, concat_axis=0, tiled=True)  53.8 us
    ppermute x6, waiting for transfers between devices, to_chip(): return lax.ppermute(x, 'shard', [(i, (i + 2 * dy) % 8) for i in range(8)])  52.9 us
    unnamed x110, local copies, waits for them, and re-layouts  35 us
    all_to_all x2, blocking collectives, exchange(): return lax.all_to_all(x, ALL, split_axis=0, concat_axis=0, tiled=True)  28.1 us
    ppermute x6, waiting for transfers between devices, from_chip(): return lax.ppermute(x, 'shard', [(i, (i - 2 * dy) % 8) for i in range(8)])  18.3 us
    dot_general x3, matrix products, weight_grad(): lax.dot_general(a, b, (((0,), (0,)), ((), ())), preferred_element_type=f32)  17.3 us
  transfers between devices with their start and end apart: 35, of which 13 were waited for; matrix products, arithmetic and copies ran while one was open for 15% of the time, Pallas kernels for 25%

profile of v1, /device:TPU:1, one launch (start us, length us, event | category | flops | bytes accessed | tf_op | source)
XLA Modules:
  0.0 525.6 jit_solution(14564528985845260108)
XLA Ops:
  8.7 2.8 collective-permute-start.2
  18.1 2.4 copy.180
  22.9 3.9 copy.195
  28.2 1.8 multiply_sine_fusion
  30.1 4.8 pack_rows.1
  35.6 1.7 bitcast_dynamic-update-slice_fusion
  38.9 1.6 fusion.14
  40.6 1.9 copy.183
  43.7 10.0 %all-to-all-start.1 = ((bf16[128,80,128]{2,1,0:T(8,128)(2,1)}), bf16[128,80,128]{2,1,0:T(8,128)(2,1)}, u32[]{:S(2)}, u32[]{:S(2)}) async-start(bf16[128,80,128]{2,1,0:T(8,128)(2,1)} %bitcast.72), calls=%async_computation.1 | async-start | bytes 5242880 | tf_op jit(solution)/shard_map/all_to_all | solution.py:694
  59.1 1.6 copy-done.2
  60.8 4.9 qkv0.1
  65.7 4.9 qkv1.1
  70.5 4.9 qkv2.1
  75.4 4.9 qkv3.1
  80.3 10.9 %attend.1 = (bf16[512,512]{1,0:T(8,128)(2,1)}, bf16[512,512]{1,0:T(8,128)(2,1)}, f32[8,1024]{1,0:T(8,128)}, bf16[512,1024]{1,0:T(8,128)(2,1)}, bf16[128,1024]{1,...) custom-call(bf16[512,256]{1,0:T(8,128)(2,1)} %get-tuple-element.89.refs_0_, ...), custom_call_target="tpu_custom_call" | custom-call | flops 2147483648 | bytes 4521984 | tf_op jit(solution)/shard_map/attend/pallas_call | solution.py:45
  91.3 2.0 collective-permute-done.8.otr
  94.2 6.7 %out_projection.1 = (bf16[2048,128]{1,0:T(8,128)(2,1)}, bf16[2048,128]{1,0:T(8,128)(2,1)}, bf16[2048,128]{1,0:T(8,128)(2,1)}, bf16[2048,128]{1,0:T(8,128)(2,1)}) custom-call(bf16[512,512]{1,0:T(8,128)(2,1)} %get-tuple-element.101.ot0.refs_8_.refs_13_, bf16[512,512]{1,0:T(8,128)(2,1)} %copy-done.39, bf16[2048,512]{1,0:T(8,128)(2,1)} %bitcast.18.wa, ...), custom_call_target="tpu_custom_call" | custom-call | flops 2147483648 | bytes 7340032 | tf_op jit(solution)/shard_map/out_projection/pallas_call | solution.py:45
  101.5 2.4 collective-permute-start.11
  106.6 9.1 %collective-permute-done.10.b1 = bf16[2048,128]{1,0:T(8,128)(2,1)S(1)} collective-permute-done((bf16[2048,128]{1,0:T(8,128)(2,1)}, bf16[2048,128]{1,0:T(8,128)(2,1)S(1)}, u32[]{:S(2)}, u32[]{:S(2)}) %collective-permute-start.10) | collective-permute-done | bytes 524320 | tf_op jit(solution)/shard_map/ppermute | solution.py:685
  115.7 11.6 %collective-permute-done.11.b2 = bf16[2048,128]{1,0:T(8,128)(2,1)S(1)} collective-permute-done((bf16[2048,128]{1,0:T(8,128)(2,1)}, bf16[2048,128]{1,0:T(8,128)(2,1)S(1)}, u32[]{:S(2)}, u32[]{:S(2)}) %collective-permute-start.11) | collective-permute-done | bytes 524320 | tf_op jit(solution)/shard_map/ppermute | solution.py:685
  128.3 6.7 %router.1 = (f32[128,2048]{1,0:T(8,128)}, bf16[128,2048]{1,0:T(8,128)(2,1)}, f32[128,128]{1,0:T(8,128)}, f32[128,128]{1,0:T(8,128)}, bf16[10240,128]{1,0:T(8,128)(2,1)}) custom-call(bf16[2048,128]{1,0:T(8,128)(2,1)} %get-tuple-element.103.b0, bf16[2048,128]{1,0:T(8,128)(2,1)} %copy-done.22, bf16[2048,128]{1,0:T(8,128)(2,1)} %copy-done.23, ...), custom_call_target="tpu_custom_call" | custom-call | flops 335544320 | bytes 7483392 | tf_op jit(solution)/shard_map/router/pallas_call | solution.py:45
  135.0 9.7 %all-to-all-start = ((bf16[128,80,128]{2,1,0:T(8,128)(2,1)}), bf16[128,80,128]{2,1,0:T(8,128)(2,1)S(1)}, u32[]{:S(2)}, u32[]{:S(2)}) async-start(bf16[128,80,128]{2,1,0:T(8,128)(2,1)} %bitcast.82), calls=%async_computation | async-start | bytes 5242880 | tf_op jit(solution)/shard_map/all_to_all | solution.py:694
  144.6 8.5 %expert_grad_rows.1 = (bf16[640,2048]{1,0:T(8,128)(2,1)}, f32[640,768]{1,0:T(8,128)}) custom-call(bf16[10240,128]{1,0:T(8,128)(2,1)} %bitcast.26.payload, bf16[768,2048]{1,0:T(8,128)(2,1)} %bitcast.106), custom_call_target="tpu_custom_call" | custom-call | flops 2013265920 | bytes 10354688 | tf_op jit(solution)/shard_map/expert_grad_rows/pallas_call | solution.py:45
  153.2 27.6 %all-to-all-done = bf16[128,80,128]{2,1,0:T(8,128)(2,1)S(1)} async-done(((bf16[128,80,128]{2,1,0:T(8,128)(2,1)}), bf16[128,80,128]{2,1,0:T(8,128)(2,1)S(1)}, u32[]{:S(2)}, u32[]{:S(2)}) %all-to-all-start) | async-done | bytes 2621472 | tf_op jit(solution)/shard_map/all_to_all | solution.py:694
  182.2 20.5 %expert_main.1 = (bf16[10240,128]{1,0:T(8,128)(2,1)}, bf16[640,2048]{1,0:T(8,128)(2,1)}, bf16[640,768]{1,0:T(8,128)(2,1)}, bf16[640,768]{1,0:T(8,128)(2,1)}, bf16[640,768]{1,0:T(8,128)(2,1)}, /*index=5*/f32[640,1]{1,0:T(8,128)}) custom-call(bf16[10240,128]{1,0:T(8,128)(2,1)} %bitcast.83, bf16[2048,768]{1,0:T(8,128)(2,1)} %bitcast.104, ...), custom_call_target="tpu_custom_call" | custom-call | flops 8053063680 | bytes 19073536 | tf_op jit(solution)/shard_map/expert_main/pallas_call | solution.py:45
  204.2 14.4 %all_to_all.50 = f32[128,1,128]{2,1,0:T(1,128)} all-to-all(f32[128,1,128]{2,1,0:T(1,128)S(1)} %bitcast.94), channel_id=1, replica_groups=mesh['expert'=16,'shard'=8] {'expert','shard'}, dimensions={0} | all-to-all | bytes 131072 | tf_op jit(solution)/shard_map/all_to_all | solution.py:694
  218.5 4.5 all-to-all-start.2
  225.3 3.0 pad_maximum_fusion
  228.3 2.3 copy.205
  230.5 2.3 copy.206
  232.8 2.3 copy.207
  235.1 1.9 slice_dynamic-update-slice_fusion.7
  236.9 1.9 slice_dynamic-update-slice_fusion.6
  238.8 20.4 %all-to-all-done.2 = bf16[128,80,128]{2,1,0:T(8,128)(2,1)S(1)} async-done(((bf16[128,80,128]{2,1,0:T(8,128)(2,1)}), bf16[128,80,128]{2,1,0:T(8,128)(2,1)S(1)}, u32[]{:S(2)}, u32[]{:S(2)}) %all-to-all-start.2) | async-done | bytes 2621472 | tf_op jit(solution)/shard_map/all_to_all | solution.py:694
  260.7 8.7 %combine_grads.1 = (f32[128,2048]{1,0:T(8,128)}, bf16[128,2048]{1,0:T(8,128)(2,1)}, bf16[2048,128]{1,0:T(8,128)(2,1)}, f32[1,2048]{1,0:T(1,128)}) custom-call(bf16[10240,128]{1,0:T(8,128)(2,1)} %bitcast.74, f32[128,128]{1,0:T(8,128)} %bitcast.92, f32[128,2048]{1,0:T(8,128)} %get-tuple-element.113.hidden, bf16[128,2048]{1,0:T(8,128)(2,1)} %get-tuple-element.114.n2, ...), custom_call_target="tpu_custom_call" | custom-call | flops 671088640 | bytes 7559168 | tf_op jit(solution)/shard_map/combine_grads/pallas_call | solution.py:45
  269.4 2.1 collective-permute-start.15
  274.7 1.8 collective-permute-start.17
  276.5 16.2 %collective-permute-done.15.refs_1_ = bf16[128,2048]{1,0:T(8,128)(2,1)} collective-permute-done((bf16[128,2048]{1,0:T(8,128)(2,1)}, bf16[128,2048]{1,0:T(8,128)(2,1)}, u32[]{:S(2)}, u32[]{:S(2)}) %collective-permute-start.15) | collective-permute-done | bytes 524320 | tf_op jit(solution)/shard_map/ppermute | solution.py:681
  294.2 2.1 collective-permute-done.16.refs_3_
  300.6 11.1 %out_projection_grad.1 = (bf16[512,2048]{1,0:T(8,128)(2,1)}, bf16[512,1024]{1,0:T(8,128)(2,1)}) custom-call(bf16[128,2048]{1,0:T(8,128)(2,1)} %get-tuple-element.118.refs_0_, bf16[128,2048]{1,0:T(8,128)(2,1)} %collective-permute-done.15.refs_1_, bf16[128,2048]{1,0:T(8,128)(2,1)} %collective-permute-done.13.refs_2_, ...), custom_call_target="tpu_custom_call" | custom-call | flops 4294967296 | bytes 10485760 | tf_op jit(solution)/shard_map/out_projection_grad/pallas_call | solution.py:45
  311.6 19.0 %attend_grad.1 = (bf16[512,512]{1,0:T(8,128)(2,1)}, bf16[512,512]{1,0:T(8,128)(2,1)}, bf16[256,1024]{1,0:T(8,128)(2,1)}, f32[128,1]{1,0:T(8,128)}, f32[128,1]{1,0:T(8,128)}) custom-call(f32[512,256]{1,0:T(8,128)} %get-tuple-element.125.refs_0_, f32[512,256]{1,0:T(8,128)} %get-tuple-element.126.refs_1_, f32[512,256]{1,0:T(8,128)} %get-tuple-element.127.refs_2_, ...), custom_call_target="tpu_custom_call" | custom-call | flops 5368709120 | bytes 8456192 | tf_op jit(solution)/shard_map/attend_grad/pallas_call | solution.py:45
  333.6 8.7 %qkv_weight_grad.1 = (bf16[2048,640]{1,0:T(8,128)(2,1)}, bf16[256,1024]{1,0:T(8,128)(2,1)}) custom-call(s32[1]{0:T(128)} %bitcast.36.core, bf16[2048,1024]{1,0:T(8,128)(2,1)} %bitcast.37.n1t, bf16[512,512]{1,0:T(8,128)(2,1)} %get-tuple-element.139.dq0, bf16[512,512]{1,0:T(8,128)(2,1)} %get-tuple-element.140.dq1, bf16[256,1024]{1,0:T(8,128)(2,1)} %get-tuple-element.145.own, ...), custom_call_target="tpu_custom_call" | custom-call | flops 2684354560 | bytes 9437188 | tf_op jit(solution)/shard_map/qkv_weight_grad/pallas_call | solution.py:45
  344.9 3.8 all-to-all-start.9
  348.7 7.1 %expert_out.1 = bf16[10240,128]{1,0:T(8,128)(2,1)} custom-call(bf16[640,768]{1,0:T(8,128)(2,1)} %get-tuple-element.110.act, bf16[768,2048]{1,0:T(8,128)(2,1)} %bitcast.107), custom_call_target="tpu_custom_call" | custom-call | flops 2013265920 | bytes 6750208 | tf_op jit(solution)/shard_map/expert_out/pallas_call | solution.py:45
  355.8 2.9 all-to-all-done.9
  358.7 7.1 %all-to-all-start.7 = ((bf16[128,16,128]{2,1,0:T(8,128)(2,1)}), bf16[128,16,128]{2,1,0:T(8,128)(2,1)S(1)}, u32[]{:S(2)}, u32[]{:S(2)}) async-start(bf16[128,16,128]{2,1,0:T(8,128)(2,1)} %bitcast.42), calls=%async_computation.7 | async-start | bytes 1048576 | tf_op jit(solution)/shard_map/all_to_all | solution.py:694
  368.2 9.8 %normed_grad.1 = (bf16[2048,128]{1,0:T(8,128)(2,1)}, bf16[2048,128]{1,0:T(8,128)(2,1)}, bf16[2048,128]{1,0:T(8,128)(2,1)}, bf16[2048,128]{1,0:T(8,128)(2,1)}, f32[2048,1]{1,0:T(8,128)}) custom-call(bf16[2048,512]{1,0:T(8,128)(2,1)} %wa.1, bf16[2048,512]{1,0:T(8,128)(2,1)} %collective-permute-done.14.wb, bf16[2048,256]{1,0:T(8,128)(2,1)} %bitcast.79, ...), custom_call_target="tpu_custom_call" | custom-call | flops 2684354560 | bytes 13123584 | tf_op jit(solution)/shard_map/normed_grad/pallas_call | solution.py:45
  378.0 1.6 reduce.3
  380.4 9.7 %all-to-all-start.5 = ((f32[128,1,128]{2,1,0:T(1,128)}), f32[128,1,128]{2,1,0:T(1,128)S(1)}, u32[]{:S(2)}, u32[]{:S(2)}) async-start(f32[128,1,128]{2,1,0:T(1,128)} %bitcast.41), calls=%async_computation.5 | async-start | bytes 131072 | tf_op jit(solution)/shard_map/all_to_all | solution.py:694
  390.2 9.4 %all-to-all-done.5 = f32[128,1,128]{2,1,0:T(1,128)S(1)} async-done(((f32[128,1,128]{2,1,0:T(1,128)}), f32[128,1,128]{2,1,0:T(1,128)S(1)}, u32[]{:S(2)}, u32[]{:S(2)}) %all-to-all-start.5) | async-done | bytes 65568 | tf_op jit(solution)/shard_map/all_to_all | solution.py:694
  400.5 4.4 all-to-all-start.8
  405.0 15.7 %all-to-all-done.8 = bf16[128,16,128]{2,1,0:T(8,128)(2,1)S(1)} async-done(((bf16[128,16,128]{2,1,0:T(8,128)(2,1)}), bf16[128,16,128]{2,1,0:T(8,128)(2,1)S(1)}, u32[]{:S(2)}, u32[]{:S(2)}) %all-to-all-start.8) | async-done | bytes 524320 | tf_op jit(solution)/shard_map/all_to_all | solution.py:694
  420.8 13.7 %all_to_all.51 = f32[128,1,128]{2,1,0:T(1,128)S(1)} all-to-all(f32[128,1,128]{2,1,0:T(1,128)S(1)} %broadcast_in_dim.74), channel_id=1, replica_groups=mesh['expert'=16,'shard'=8] {'expert','shard'}, dimensions={0} | all-to-all | bytes 131072 | tf_op jit(solution)/shard_map/all_to_all | solution.py:694
  434.5 4.8 all-to-all-start.4
  439.5 7.7 %convolution_bitcast_fusion.2 = f32[1,2048,768]{2,1,0:T(8,128)} fusion(bf16[640,768]{1,0:T(8,128)(2,1)} %get-tuple-element.161, bf16[640,2048]{1,0:T(8,128)(2,1)} %get-tuple-element.159, f32[640]{0:T(1024)S(1)} %mul.93), kind=kOutput, calls=%fused_computation.4 | convolution fusion | flops 2017198080 | bytes 9898496 | tf_op jit(solution)/shard_map/dot_general | solution.py:791
  447.2 4.9 convolution_bitcast_fusion.1
  452.1 4.7 convolution_bitcast_fusion
  459.3 2.4 collective-permute-start.24
  464.3 20.2 %collective-permute-done.23.b1 = bf16[2048,128]{1,0:T(8,128)(2,1)S(1)} collective-permute-done((bf16[2048,128]{1,0:T(8,128)(2,1)}, bf16[2048,128]{1,0:T(8,128)(2,1)S(1)}, u32[]{:S(2)}, u32[]{:S(2)}) %collective-permute-start.23) | collective-permute-done | bytes 524320 | tf_op jit(solution)/shard_map/ppermute | solution.py:685
  484.5 12.0 %collective-permute-done.24.b2 = bf16[2048,128]{1,0:T(8,128)(2,1)} collective-permute-done((bf16[2048,128]{1,0:T(8,128)(2,1)}, bf16[2048,128]{1,0:T(8,128)(2,1)}, u32[]{:S(2)}, u32[]{:S(2)}) %collective-permute-start.24) | collective-permute-done | bytes 524320 | tf_op jit(solution)/shard_map/ppermute | solution.py:685
  496.5 3.6 input_grad.1
  501.7 5.7 %result.1 = bf16[128,2048]{1,0:T(8,128)(2,1)} custom-call(bf16[10240,128]{1,0:T(8,128)(2,1)} %bitcast.73, f32[128,2048]{1,0:T(8,128)} %get-tuple-element.113.hidden, f32[128,128]{1,0:T(8,128)} %get-tuple-element.160.gates, s32[128,4]{1,0:T(8,128)} %copy-done.17), custom_call_target="tpu_custom_call" | custom-call | flops 671088640 | bytes 4261888 | tf_op jit(solution)/shard_map/result/pallas_call | solution.py:45
  507.4 4.3 slice.104
  514.2 4.1 convert_element_type.100
  (211 shorter events, 60.6 us)
Async XLA Ops:
  7.2 15.0 %copy-start = (s32[1,1024]{1,0:T(1,128)S(1)}, s32[1,1024]{1,0:T(1,128)}, u32[]{:S(2)}) copy-start(s32[1,1024]{1,0:T(1,128)} %param.32) | copy-start | bytes 12292
  7.2 10.1 %copy-start.28 = (s32[128,4]{0,1:T(4,128)S(1)}, s32[128,4]{0,1:T(4,128)}, u32[]{:S(2)}) copy-start(s32[128,4]{0,1:T(4,128)} %param.33) | copy-start | bytes 6148
  7.2 10.3 %copy-start.30 = (bf16[2048]{0:T(1024)(128)(2,1)S(1)}, bf16[2048]{0:T(1024)(128)(2,1)}, u32[]{:S(2)}) copy-start(bf16[2048]{0:T(1024)(128)(2,1)} %param.19) | copy-start | bytes 12292
  7.2 10.9 %copy-start.6 = (bf16[2048,512]{1,0:T(8,128)(2,1)S(1)}, bf16[2048,512]{1,0:T(8,128)(2,1)}, u32[]{:S(2)}) copy-start(bf16[2048,512]{1,0:T(8,128)(2,1)} %wa.1) | copy-start | bytes 6291460
  7.2 51.9 %collective-permute-start = (bf16[128,2048]{1,0:T(8,128)(2,1)}, bf16[128,2048]{1,0:T(8,128)(2,1)}, u32[]{:S(2)}, u32[]{:S(2)}) collective-permute-start(bf16[128,2048]{1,0:T(8,128)(2,1)} %x0.3), channel_id=1, source_target_pairs={{0,1},{1,0},{2,3},{3,2},{4,5},{5,4},{6,7},{7,6},{8,9},{9,8},{10,11... | collective-permute-start | bytes 1572872 | tf_op jit(solution)/shard_map/ppermute | solution.py:677
  8.7 48.4 %collective-permute-start.2 = (bf16[128,2048]{1,0:T(8,128)(2,1)}, bf16[128,2048]{1,0:T(8,128)(2,1)}, u32[]{:S(2)}, u32[]{:S(2)}) collective-permute-start(bf16[128,2048]{1,0:T(8,128)(2,1)} %x0.3), channel_id=1, source_target_pairs={{0,6},{1,7},{2,0},{3,1},{4,2},{5,3},{6,4},{7,5},{8,14},{9,15},{10,... | collective-permute-start | bytes 1572872 | tf_op jit(solution)/shard_map/ppermute | solution.py:681
  11.6 32.2 %collective-permute-start.4 = (bf16[128,2048]{1,0:T(8,128)(2,1)}, bf16[128,2048]{1,0:T(8,128)(2,1)}, u32[]{:S(2)}, u32[]{:S(2)}) collective-permute-start(bf16[128,2048]{1,0:T(8,128)(2,1)} %x0.3), channel_id=1, source_target_pairs={{0,4},{1,5},{2,6},{3,7},{4,0},{5,1},{6,2},{7,3},{8,12},{9,13},{10,... | collective-permute-start | bytes 1572872 | tf_op jit(solution)/shard_map/ppermute | solution.py:681
  11.9 45.4 %collective-permute-start.6 = (bf16[128,2048]{1,0:T(8,128)(2,1)}, bf16[128,2048]{1,0:T(8,128)(2,1)}, u32[]{:S(2)}, u32[]{:S(2)}) collective-permute-start(bf16[128,2048]{1,0:T(8,128)(2,1)} %x0.3), channel_id=1, source_target_pairs={{0,2},{1,3},{2,4},{3,5},{4,6},{5,7},{6,0},{7,1},{8,10},{9,11},{10,... | collective-permute-start | bytes 1572872 | tf_op jit(solution)/shard_map/ppermute | solution.py:681
  13.8 6.6 %copy-start.7 = (bf16[2048,64]{1,0:T(8,128)(2,1)}, bf16[2048,64]{1,0:T(8,128)(2,1)S(1)}, u32[]{:S(2)}) copy-start(bf16[2048,64]{1,0:T(8,128)(2,1)S(1)} %copy.182) | copy-start | bytes 786436
  13.8 6.6 %copy-start.40 = (bf16[128]{0:T(256)(128)(2,1)S(1)}, bf16[128]{0:T(256)(128)(2,1)}, u32[]{:S(2)}) copy-start(bf16[128]{0:T(256)(128)(2,1)} %param.23) | copy-start | bytes 772
  15.3 11.5 %copy-start.9 = (bf16[2048,64]{1,0:T(8,128)(2,1)}, bf16[2048,64]{1,0:T(8,128)(2,1)S(1)}, u32[]{:S(2)}) copy-start(bf16[2048,64]{1,0:T(8,128)(2,1)S(1)} %copy.181) | copy-start | bytes 786436
  15.3 5.9 %copy-start.41 = (bf16[128]{0:T(256)(128)(2,1)S(1)}, bf16[128]{0:T(256)(128)(2,1)}, u32[]{:S(2)}) copy-start(bf16[128]{0:T(256)(128)(2,1)} %param.24) | copy-start | bytes 772
  15.3 6.7 %copy-start.32 = (s32[1,4]{1,0:T(1,128)S(1)}, s32[1,4]{1,0:T(1,128)}, u32[]{:S(2)}) copy-start(s32[1,4]{1,0:T(1,128)} %param.31) | copy-start | bytes 52
  16.4 20.9 %collective-permute-start.1 = (bf16[128,2048]{0,1:T(8,128)(2,1)}, bf16[128,2048]{0,1:T(8,128)(2,1)}, u32[]{:S(2)}, u32[]{:S(2)}) collective-permute-start(bf16[128,2048]{0,1:T(8,128)(2,1)} %pad_maximum_fusion.1), channel_id=1, source_target_pairs={{0,1},{1,0},{2,3},{3,2},{4,5},{5,4},{6,7},{7,6},{8,9},{9,8},{10,11... | collective-permute-start | bytes 1572872 | tf_op jit(solution)/shard_map/ppermute | solution.py:677
  27.5 9.8 %copy-start.17 = (s32[128,4]{1,0:T(8,128)}, s32[128,4]{1,0:T(8,128)S(1)}, u32[]{:S(2)}) copy-start(s32[128,4]{1,0:T(8,128)S(1)} %convert_add_fusion.assign) | copy-start | bytes 6148
  30.0 7.4 %copy-start.8 = (bf16[2048,64]{1,0:T(8,128)(2,1)S(1)}, bf16[2048,64]{1,0:T(8,128)(2,1)}, u32[]{:S(2)}) copy-start(bf16[2048,64]{1,0:T(8,128)(2,1)} %copy-done.7) | copy-start | bytes 786436
  30.1 7.4 %copy-start.10 = (bf16[2048,64]{1,0:T(8,128)(2,1)S(1)}, bf16[2048,64]{1,0:T(8,128)(2,1)}, u32[]{:S(2)}) copy-start(bf16[2048,64]{1,0:T(8,128)(2,1)} %copy-done.9) | copy-start | bytes 786436
  37.3 56.0 %collective-permute-start.9 = (bf16[2048,512]{1,0:T(8,128)(2,1)}, bf16[2048,512]{1,0:T(8,128)(2,1)}, u32[]{:S(2)}, u32[]{:S(2)}) collective-permute-start(bf16[2048,512]{1,0:T(8,128)(2,1)} %bitcast.18.wa), channel_id=1, source_target_pairs={{0,1},{1,0},{2,3},{3,2},{4,5},{5,4},{6,7},{7,6},{8,9},{9,8},{10,11... | collective-permute-start | bytes 6291464 | tf_op jit(solution)/shard_map/ppermute | solution.py:677
  43.7 91.2 %all-to-all-start.1 = ((bf16[128,80,128]{2,1,0:T(8,128)(2,1)}), bf16[128,80,128]{2,1,0:T(8,128)(2,1)}, u32[]{:S(2)}, u32[]{:S(2)}) async-start(bf16[128,80,128]{2,1,0:T(8,128)(2,1)} %bitcast.72), calls=%async_computation.1 | async-start | bytes 5242880 | tf_op jit(solution)/shard_map/all_to_all | solution.py:694
  56.0 14.6 %collective-permute-start.5 = (bf16[128,2048]{1,0:T(8,128)(2,1)}, bf16[128,2048]{1,0:T(8,128)(2,1)}, u32[]{:S(2)}, u32[]{:S(2)}) collective-permute-start(bf16[128,2048]{1,0:T(8,128)(2,1)} %collective-permute-done.4.xa), channel_id=1, source_target_pairs={{0,1},{1,0},{2,3},{3,2},{4,5},{5,4},{6,7},{7,6},{8,9},{9,8},{10,11... | collective-permute-start | bytes 1572872 | tf_op jit(solution)/shard_map/ppermute | solution.py:677
  57.2 8.5 %collective-permute-start.3 = (bf16[128,2048]{1,0:T(8,128)(2,1)}, bf16[128,2048]{1,0:T(8,128)(2,1)}, u32[]{:S(2)}, u32[]{:S(2)}) collective-permute-start(bf16[128,2048]{1,0:T(8,128)(2,1)} %collective-permute-done.2.xa), channel_id=1, source_target_pairs={{0,1},{1,0},{2,3},{3,2},{4,5},{5,4},{6,7},{7,6},{8,9},{9,8},{10,11... | collective-permute-start | bytes 1572872 | tf_op jit(solution)/shard_map/ppermute | solution.py:677
  57.3 18.1 %collective-permute-start.7 = (bf16[128,2048]{1,0:T(8,128)(2,1)}, bf16[128,2048]{1,0:T(8,128)(2,1)}, u32[]{:S(2)}, u32[]{:S(2)}) collective-permute-start(bf16[128,2048]{1,0:T(8,128)(2,1)} %collective-permute-done.6.xa), channel_id=1, source_target_pairs={{0,1},{1,0},{2,3},{3,2},{4,5},{5,4},{6,7},{7,6},{8,9},{9,8},{10,11... | collective-permute-start | bytes 1572872 | tf_op jit(solution)/shard_map/ppermute | solution.py:677
  91.2 2.2 collective-permute-start.8
  94.2 11.8 %copy-start.31 = (bf16[2048]{0:T(1024)(128)(2,1)S(1)}, bf16[2048]{0:T(1024)(128)(2,1)}, u32[]{:S(2)}) copy-start(bf16[2048]{0:T(1024)(128)(2,1)} %param.26) | copy-start | bytes 12292
  100.9 14.8 %collective-permute-start.10 = (bf16[2048,128]{1,0:T(8,128)(2,1)}, bf16[2048,128]{1,0:T(8,128)(2,1)S(1)}, u32[]{:S(2)}, u32[]{:S(2)}) collective-permute-start(bf16[2048,128]{1,0:T(8,128)(2,1)} %get-tuple-element.104), channel_id=1, source_target_pairs={{0,2},{1,3},{2,4},{3,5},{4,6},{5,7},{6,0},{7,1},{8,10},{9,11},{10,... | collective-permute-start | bytes 1572872 | tf_op jit(solution)/shard_map/ppermute | solution.py:685
  101.5 25.8 %collective-permute-start.11 = (bf16[2048,128]{1,0:T(8,128)(2,1)}, bf16[2048,128]{1,0:T(8,128)(2,1)S(1)}, u32[]{:S(2)}, u32[]{:S(2)}) collective-permute-start(bf16[2048,128]{1,0:T(8,128)(2,1)} %get-tuple-element.105), channel_id=1, source_target_pairs={{0,4},{1,5},{2,6},{3,7},{4,0},{5,1},{6,2},{7,3},{8,12},{9,13},{10,... | collective-permute-start | bytes 1572872 | tf_op jit(solution)/shard_map/ppermute | solution.py:685
  103.9 23.4 %collective-permute-start.12 = (bf16[2048,128]{1,0:T(8,128)(2,1)}, bf16[2048,128]{1,0:T(8,128)(2,1)S(1)}, u32[]{:S(2)}, u32[]{:S(2)}) collective-permute-start(bf16[2048,128]{1,0:T(8,128)(2,1)} %get-tuple-element.106), channel_id=1, source_target_pairs={{0,6},{1,7},{2,0},{3,1},{4,2},{5,3},{6,4},{7,5},{8,14},{9,15},{10,... | collective-permute-start | bytes 1572872 | tf_op jit(solution)/shard_map/ppermute | solution.py:685
  115.7 11.6 %copy-start.22 = (bf16[2048,128]{1,0:T(8,128)(2,1)}, bf16[2048,128]{1,0:T(8,128)(2,1)S(1)}, u32[]{:S(2)}) copy-start(bf16[2048,128]{1,0:T(8,128)(2,1)S(1)} %collective-permute-done.10.b1) | copy-start | bytes 1572868
  135.0 45.8 %all-to-all-start = ((bf16[128,80,128]{2,1,0:T(8,128)(2,1)}), bf16[128,80,128]{2,1,0:T(8,128)(2,1)S(1)}, u32[]{:S(2)}, u32[]{:S(2)}) async-start(bf16[128,80,128]{2,1,0:T(8,128)(2,1)} %bitcast.82), calls=%async_computation | async-start | bytes 5242880 | tf_op jit(solution)/shard_map/all_to_all | solution.py:694
  202.8 22.5 %copy-start.11 = (bf16[64,2048]{0,1:T(8,128)(2,1)S(1)}, bf16[64,2048]{0,1:T(8,128)(2,1)}, u32[]{:S(2)}) copy-start(bf16[64,2048]{0,1:T(8,128)(2,1)} %get-tuple-element.240) | copy-start | bytes 786436
  218.5 40.6 %all-to-all-start.2 = ((bf16[128,80,128]{2,1,0:T(8,128)(2,1)}), bf16[128,80,128]{2,1,0:T(8,128)(2,1)S(1)}, u32[]{:S(2)}, u32[]{:S(2)}) async-start(bf16[128,80,128]{2,1,0:T(8,128)(2,1)} %bitcast.81), calls=%async_computation.2 | async-start | bytes 5242880 | tf_op jit(solution)/shard_map/all_to_all | solution.py:694
  223.1 284.3 %all-reduce.6.cloned.1.call-start = ((), (), s32[]{:S(2)}) async-start(), calls=%async_computation.10 | async-start | bytes 9437184 | tf_op jit(solution)/shard_map/psum | solution.py:817
  223.1 144.3 %collective-permute-start.14 = (bf16[2048,512]{1,0:T(8,128)(2,1)}, bf16[2048,512]{1,0:T(8,128)(2,1)}, u32[]{:S(2)}, u32[]{:S(2)}) collective-permute-start(bf16[2048,512]{1,0:T(8,128)(2,1)} %wa.1), channel_id=1, source_target_pairs={{0,1},{1,0},{2,3},{3,2},{4,5},{5,4},{6,7},{7,6},{8,9},{9,8},{10,11... | collective-permute-start | bytes 6291464 | tf_op jit(solution)/shard_map/ppermute | solution.py:677
  259.2 12.3 %copy-start.12 = (bf16[256,2048]{0,1:T(8,128)(2,1)S(1)}, bf16[256,2048]{0,1:T(8,128)(2,1)}, u32[]{:S(2)}) copy-start(bf16[256,2048]{0,1:T(8,128)(2,1)} %copy.207) | copy-start | bytes 3145732
  269.3 27.6 %copy-start.15 = (bf16[256,2048]{0,1:T(8,128)(2,1)S(1)}, bf16[256,2048]{0,1:T(8,128)(2,1)}, u32[]{:S(2)}) copy-start(bf16[256,2048]{0,1:T(8,128)(2,1)} %copy.205) | copy-start | bytes 3145732
  269.3 28.5 %copy-start.14 = (bf16[256,2048]{0,1:T(8,128)(2,1)S(1)}, bf16[256,2048]{0,1:T(8,128)(2,1)}, u32[]{:S(2)}) copy-start(bf16[256,2048]{0,1:T(8,128)(2,1)} %copy.206) | copy-start | bytes 3145732
  269.3 24.9 %collective-permute-start.13 = (bf16[128,2048]{1,0:T(8,128)(2,1)}, bf16[128,2048]{1,0:T(8,128)(2,1)}, u32[]{:S(2)}, u32[]{:S(2)}) collective-permute-start(bf16[128,2048]{1,0:T(8,128)(2,1)} %get-tuple-element.118.refs_0_), channel_id=1, source_target_pairs={{0,4},{1,5},{2,6},{3,7},{4,0},{5,1},{6,2},{7,3},{8,12},{9,13},{10,... | collective-permute-start | bytes 1572872 | tf_op jit(solution)/shard_map/ppermute | solution.py:681
  269.4 23.2 %collective-permute-start.15 = (bf16[128,2048]{1,0:T(8,128)(2,1)}, bf16[128,2048]{1,0:T(8,128)(2,1)}, u32[]{:S(2)}, u32[]{:S(2)}) collective-permute-start(bf16[128,2048]{1,0:T(8,128)(2,1)} %get-tuple-element.118.refs_0_), channel_id=1, source_target_pairs={{0,6},{1,7},{2,0},{3,1},{4,2},{5,3},{6,4},{7,5},{8,14},{9,15},{10,... | collective-permute-start | bytes 1572872 | tf_op jit(solution)/shard_map/ppermute | solution.py:681
  271.5 24.8 %collective-permute-start.16 = (bf16[128,2048]{1,0:T(8,128)(2,1)}, bf16[128,2048]{1,0:T(8,128)(2,1)}, u32[]{:S(2)}, u32[]{:S(2)}) collective-permute-start(bf16[128,2048]{1,0:T(8,128)(2,1)} %get-tuple-element.118.refs_0_), channel_id=1, source_target_pairs={{0,2},{1,3},{2,4},{3,5},{4,6},{5,7},{6,0},{7,1},{8,10},{9,11},{10,... | collective-permute-start | bytes 1572872 | tf_op jit(solution)/shard_map/ppermute | solution.py:681
  274.7 24.0 %collective-permute-start.17 = (bf16[128,2048]{1,0:T(8,128)(2,1)}, bf16[128,2048]{1,0:T(8,128)(2,1)S(1)}, u32[]{:S(2)}, u32[]{:S(2)}) collective-permute-start(bf16[128,2048]{1,0:T(8,128)(2,1)} %get-tuple-element.118.refs_0_), channel_id=1, source_target_pairs={{0,1},{1,0},{2,3},{3,2},{4,5},{5,4},{6,7},{7,6},{8,9},{9,8},{10,11... | collective-permute-start | bytes 1572872 | tf_op jit(solution)/shard_map/ppermute | solution.py:677
  292.7 6.0 %collective-permute-start.18 = (bf16[128,2048]{1,0:T(8,128)(2,1)}, bf16[128,2048]{1,0:T(8,128)(2,1)S(1)}, u32[]{:S(2)}, u32[]{:S(2)}) collective-permute-start(bf16[128,2048]{1,0:T(8,128)(2,1)} %collective-permute-done.15.refs_1_), channel_id=1, source_target_pairs={{0,1},{1,0},{2,3},{3,2},{4,5},{5,4},{6,7},{7,6},{8,9},{9,8},{10,11... | collective-permute-start | bytes 1572872 | tf_op jit(solution)/shard_map/ppermute | solution.py:677
  294.2 4.4 collective-permute-start.19
  296.3 2.4 collective-permute-start.20
  311.6 19.1 %copy-start.13 = (bf16[256,2048]{0,1:T(8,128)(2,1)S(1)}, bf16[256,2048]{0,1:T(8,128)(2,1)}, u32[]{:S(2)}) copy-start(bf16[256,2048]{0,1:T(8,128)(2,1)} %copy.207) | copy-start | bytes 3145732
  330.6 2.2 collective-permute-start.22
  343.3 24.1 %collective-permute-start.21 = (bf16[512,512]{1,0:T(8,128)(2,1)S(1)}, bf16[512,512]{1,0:T(8,128)(2,1)S(1)}, u32[]{:S(2)}, u32[]{:S(2)}) collective-permute-start(bf16[512,512]{1,0:T(8,128)(2,1)S(1)} %copy-done.33), channel_id=1, source_target_pairs={{0,1},{1,0},{2,3},{3,2},{4,5},{5,4},{6,7},{7,6},{8,9},{9,8},{10,11... | collective-permute-start | bytes 1572872 | tf_op jit(solution)/shard_map/ppermute | solution.py:677
  344.9 13.8 %all-to-all-start.9 = ((f32[128,1,128]{2,1,0:T(1,128)}), f32[128,1,128]{2,1,0:T(1,128)S(1)}, u32[]{:S(2)}, u32[]{:S(2)}) async-start(f32[128,1,128]{2,1,0:T(1,128)} %bitcast.45), calls=%async_computation.9 | async-start | bytes 131072 | tf_op jit(solution)/shard_map/all_to_all | solution.py:694
  348.7 17.1 %copy-start.25 = (f32[2048]{0:T(1024)S(1)}, f32[2048]{0:T(1024)}, u32[]{:S(2)}) copy-start(f32[2048]{0:T(1024)} %convert_element_type.89) | copy-start | bytes 24580
  348.7 18.4 %copy-start.27 = (f32[128,1]{1,0:T(8,128)S(1)}, f32[128,1]{1,0:T(8,128)}, u32[]{:S(2)}) copy-start(f32[128,1]{1,0:T(8,128)} %get-tuple-element.155) | copy-start | bytes 1540
  348.7 18.5 %copy-start.26 = (f32[128,1]{1,0:T(8,128)S(1)}, f32[128,1]{1,0:T(8,128)}, u32[]{:S(2)}) copy-start(f32[128,1]{1,0:T(8,128)} %get-tuple-element.154) | copy-start | bytes 1540
  358.7 21.7 %all-to-all-start.7 = ((bf16[128,16,128]{2,1,0:T(8,128)(2,1)}), bf16[128,16,128]{2,1,0:T(8,128)(2,1)S(1)}, u32[]{:S(2)}, u32[]{:S(2)}) async-start(bf16[128,16,128]{2,1,0:T(8,128)(2,1)} %bitcast.42), calls=%async_computation.7 | async-start | bytes 1048576 | tf_op jit(solution)/shard_map/all_to_all | solution.py:694
  368.2 11.4 %copy-start.29 = (f32[1,2048]{1,0:T(1,128)S(1)}, f32[1,2048]{1,0:T(1,128)}, u32[]{:S(2)}) copy-start(f32[1,2048]{1,0:T(1,128)} %get-tuple-element.153) | copy-start | bytes 24580
  380.4 19.2 %all-to-all-start.5 = ((f32[128,1,128]{2,1,0:T(1,128)}), f32[128,1,128]{2,1,0:T(1,128)S(1)}, u32[]{:S(2)}, u32[]{:S(2)}) async-start(f32[128,1,128]{2,1,0:T(1,128)} %bitcast.41), calls=%async_computation.5 | async-start | bytes 131072 | tf_op jit(solution)/shard_map/all_to_all | solution.py:694
  400.5 20.3 %all-to-all-start.8 = ((bf16[128,16,128]{2,1,0:T(8,128)(2,1)}), bf16[128,16,128]{2,1,0:T(8,128)(2,1)S(1)}, u32[]{:S(2)}, u32[]{:S(2)}) async-start(bf16[128,16,128]{2,1,0:T(8,128)(2,1)} %broadcast_in_dim.75), calls=%async_computation.8 | async-start | bytes 1048576 | tf_op jit(solution)/shard_map/all_to_all | solution.py:694
  434.5 65.6 %all-to-all-start.4 = ((bf16[128,80,128]{2,1,0:T(8,128)(2,1)}), bf16[128,80,128]{2,1,0:T(8,128)(2,1)S(1)}, u32[]{:S(2)}, u32[]{:S(2)}) async-start(bf16[128,80,128]{2,1,0:T(8,128)(2,1)} %bitcast.80), calls=%async_computation.4 | async-start | bytes 5242880 | tf_op jit(solution)/shard_map/all_to_all | solution.py:694
  439.5 7.7 %copy-start.44 = (bf16[640,2048]{1,0:T(8,128)(2,1)S(1)}, bf16[640,2048]{1,0:T(8,128)(2,1)}, u32[]{:S(2)}) copy-start(bf16[640,2048]{1,0:T(8,128)(2,1)} %get-tuple-element.159) | copy-start | bytes 7864324
  439.5 7.7 %copy-start.45 = (bf16[640,768]{1,0:T(8,128)(2,1)S(1)}, bf16[640,768]{1,0:T(8,128)(2,1)}, u32[]{:S(2)}) copy-start(bf16[640,768]{1,0:T(8,128)(2,1)} %get-tuple-element.162) | copy-start | bytes 2949124
  447.2 4.9 copy-start.42
  447.2 4.9 copy-start.43
  457.9 26.6 %collective-permute-start.23 = (bf16[2048,128]{1,0:T(8,128)(2,1)}, bf16[2048,128]{1,0:T(8,128)(2,1)S(1)}, u32[]{:S(2)}, u32[]{:S(2)}) collective-permute-start(bf16[2048,128]{1,0:T(8,128)(2,1)} %get-tuple-element.148), channel_id=1, source_target_pairs={{0,2},{1,3},{2,4},{3,5},{4,6},{5,7},{6,0},{7,1},{8,10},{9,11},{10,... | collective-permute-start | bytes 1572872 | tf_op jit(solution)/shard_map/ppermute | solution.py:685
  459.3 37.3 %collective-permute-start.24 = (bf16[2048,128]{1,0:T(8,128)(2,1)}, bf16[2048,128]{1,0:T(8,128)(2,1)}, u32[]{:S(2)}, u32[]{:S(2)}) collective-permute-start(bf16[2048,128]{1,0:T(8,128)(2,1)} %get-tuple-element.149), channel_id=1, source_target_pairs={{0,4},{1,5},{2,6},{3,7},{4,0},{5,1},{6,2},{7,3},{8,12},{9,13},{10,... | collective-permute-start | bytes 1572872 | tf_op jit(solution)/shard_map/ppermute | solution.py:685
  461.7 34.8 %collective-permute-start.25 = (bf16[2048,128]{1,0:T(8,128)(2,1)}, bf16[2048,128]{1,0:T(8,128)(2,1)}, u32[]{:S(2)}, u32[]{:S(2)}) collective-permute-start(bf16[2048,128]{1,0:T(8,128)(2,1)} %get-tuple-element.150), channel_id=1, source_target_pairs={{0,6},{1,7},{2,0},{3,1},{4,2},{5,3},{6,4},{7,5},{8,14},{9,15},{10,... | collective-permute-start | bytes 1572872 | tf_op jit(solution)/shard_map/ppermute | solution.py:685
  484.5 12.0 %copy-start.21 = (bf16[2048,128]{1,0:T(8,128)(2,1)}, bf16[2048,128]{1,0:T(8,128)(2,1)S(1)}, u32[]{:S(2)}) copy-start(bf16[2048,128]{1,0:T(8,128)(2,1)S(1)} %collective-permute-done.23.b1) | copy-start | bytes 1572868
  507.4 4.4 copy-start.3
  (17 other events, 22.0 us)
Sparse Core Ops, SparseCore 0:
  342.4 125.9 all-reduce.5

commit v2 on v1

v2 whole, which is shorter than its diff:
```python
import functools

import jax
import jax.numpy as jnp
from jax import lax
from jax.experimental import pallas as pl
from jax.experimental.pallas import tpu as pltpu
from jax.sharding import PartitionSpec as P

EPS = 1e-06
ROPE_BASE = 1000000.0
LOG2E = 1.4426950408889634
T = 128
D = 2048
HEAD = 128
LH = 4
E = 128
CAP = 5
SLOTS = E * CAP
SEG = D // 128
WIRE = CAP * SEG + 8
ROWS = 1024
HALF = 512
F = 768
bf16 = jnp.bfloat16
f32 = jnp.float32
ALL = ("expert", "shard")


def dot(a, b):
    return jnp.dot(a, b, preferred_element_type=f32)


def dot_t(a, b):
    return lax.dot_general(a, b, (((1,), (1,)), ((), ())), preferred_element_type=f32)


def call(kernel, name, outs, scratch, args, flops=0, smem=()):
    in_specs = [
        pl.BlockSpec(memory_space=pltpu.SMEM if i in smem else pltpu.VMEM)
        for i in range(len(args))
    ]
    bytes_accessed = sum(a.size * a.dtype.itemsize for a in args) + sum(
        s.size * s.dtype.itemsize for s in outs
    )
    return pl.pallas_call(
        kernel,
        out_shape=outs,
        in_specs=in_specs,
        out_specs=[pl.BlockSpec(memory_space=pltpu.VMEM) for _ in outs],
        scratch_shapes=scratch,
        compiler_params=pltpu.CompilerParams(vmem_limit_bytes=56 * 1024 * 1024),
        cost_estimate=pl.CostEstimate(
            flops=flops, bytes_accessed=bytes_accessed, transcendentals=0
        ),
        name=name,
    )(*args)


def grid_call(kernel, name, grid, in_specs, out_specs, outs, scratch, args, flops=0, scalars=0):
    bytes_accessed = sum(a.size * a.dtype.itemsize for a in args) + sum(
        s.size * s.dtype.itemsize for s in outs
    )
    return pl.pallas_call(
        kernel,
        out_shape=outs,
        grid_spec=pltpu.PrefetchScalarGridSpec(
            num_scalar_prefetch=scalars,
            grid=grid,
            in_specs=in_specs,
            out_specs=out_specs,
            scratch_shapes=scratch,
        ),
        compiler_params=pltpu.CompilerParams(
            vmem_limit_bytes=56 * 1024 * 1024, dimension_semantics=("arbitrary",)
        ),
        cost_estimate=pl.CostEstimate(
            flops=flops, bytes_accessed=bytes_accessed, transcendentals=0
        ),
        name=name,
    )(*args)


def whole(shape):
    return pl.BlockSpec(shape, lambda i, *_: (0,) * len(shape))


def rows_of(shape):
    return pl.BlockSpec(shape, lambda i, *_: (i, 0))


def cols_of(shape):
    return pl.BlockSpec(shape, lambda i, *_: (0, i))


def sds(shape, dtype):
    return jax.ShapeDtypeStruct(shape, dtype)


def split_rows(wire, dest):
    for s in range(CAP):
        for h in range(2):
            rows = slice(s * E + h * 64, s * E + (h + 1) * 64)
            block = wire[h * 64 : (h + 1) * 64, s * SEG : (s + 1) * SEG, :]
            dest[rows, :] = block.reshape(64, D)


def join_rows(source, wire):
    for s in range(CAP):
        for h in range(2):
            rows = slice(s * E + h * 64, s * E + (h + 1) * 64)
            wire[h * 64 : (h + 1) * 64, s * SEG : (s + 1) * SEG, :] = source[rows, :].reshape(
                64, SEG, 128
            )


def put_numbers(columns, wire):
    lane = lax.broadcasted_iota(jnp.int32, (E, 128), 1)
    plane = jnp.zeros((E, 128), f32)
    for s in range(CAP):
        plane = jnp.where(lane == s, columns[s], plane)
    first = plane.astype(bf16)
    rest = plane - first.astype(f32)
    second = rest.astype(bf16)
    third = (rest - second.astype(f32)).astype(bf16)
    none = jnp.zeros((E, 5 * 128), bf16)
    wide = jnp.concatenate([first, second, third, none], axis=1)
    wire[:, CAP * SEG :, :] = wide.reshape(E, 8, 128)


def get_numbers(wire):
    wide = wire[:, CAP * SEG :, :].reshape(E, 8 * 128)
    return (
        wide[:, :128].astype(f32) + wide[:, 128:256].astype(f32) + wide[:, 256:384].astype(f32)
    )


def pack_rows(x_ref, at_ref, wire, rows):
    slot = lax.broadcasted_iota(jnp.int32, (SLOTS, T), 0)
    hit = slot == at_ref[0:1, :]
    for k in range(1, 4):
        hit = hit | (slot == at_ref[k : k + 1, :])
    pick = jnp.where(hit, 1.0, 0.0).astype(bf16)
    for j in range(8):
        cols = slice(j * 256, (j + 1) * 256)
        rows[:, cols] = dot(pick, x_ref[:, cols]).astype(bf16)
    join_rows(rows, wire)


def pack_body(x_ref, at_ref, wire, rows):
    pack_rows(x_ref, at_ref, wire, rows)
    wire[:, CAP * SEG :, :] = jnp.zeros((E, 8, 128), bf16)


def pack(x, assign_t):
    return call(
        pack_body,
        "pack_rows",
        [sds((E, WIRE, 128), bf16)],
        [pltpu.VMEM((SLOTS, D), bf16)],
        (x, assign_t),
        flops=2 * SLOTS * T * D,
    )[0]


def sum_rows(wire, experts, slots, gates, out):
    def body(i, carry):
        for u in range(8):
            t = i * 8 + u
            total = None
            for k in range(4):
                p = t * 4 + k
                rows = pl.ds(pl.multiple_of(slots[p] * SEG, SEG), SEG)
                part = wire[experts[p], rows, :].astype(f32) * gates[p]
                total = part if total is None else total + part
            out[pl.ds(pl.multiple_of(t * SEG, SEG), SEG), :] = total
        return carry

    lax.fori_loop(0, T // 8, body, 0)


def column(row):
    return jnp.broadcast_to(row, (128, 128)).T[:, 0:1]


def qkv_body(
    piece, core, xa, xb, g1, wqt, wk, wks, wv, wvs, gq, gk, cos, sin,
    qraw, qt, kraw, kt, vt, n1, wkv,
):
    lower = core[0] == 0
    wkv[0:64, :] = jnp.where(lower, wk[...], wks[...])
    wkv[64:128, :] = jnp.where(lower, wks[...], wk[...])
    wkv[128:192, :] = jnp.where(lower, wv[...], wvs[...])
    wkv[192:256, :] = jnp.where(lower, wvs[...], wv[...])
    for half, ref in ((0, xa), (1, xb)):
        x = ref[...].astype(f32)
        r = lax.rsqrt(jnp.mean(x * x, axis=-1, keepdims=True) + EPS)
        n1[half * T : (half + 1) * T, :] = (x * r * g1[...]).astype(bf16)
    raw = dot_t(wqt[...], n1[...])
    raw_kv = dot_t(wkv[...], n1[...])
    gain_q, gain_k = column(gq[...]), column(gk[...])
    first, second = piece * T, HALF + piece * T
    c = jnp.concatenate([cos[:, first : first + T], cos[:, second : second + T]], axis=1)
    s = jnp.concatenate([sin[:, first : first + T], sin[:, second : second + T]], axis=1)

    def path(v, gain, factor):
        v = v * lax.rsqrt(jnp.mean(v * v, axis=0, keepdims=True) + EPS) * gain
        low, high = v[:64], v[64:]
        return (
            ((low * c - high * s) * factor).astype(bf16),
            ((high * c + low * s) * factor).astype(bf16),
        )

    qraw[...] = raw
    for h in range(LH):
        low, high = path(raw[h * HEAD : (h + 1) * HEAD], gain_q, HEAD ** (-0.5))
        qt[h * HEAD : h * HEAD + 64, :] = low
        qt[h * HEAD + 64 : (h + 1) * HEAD, :] = high
    key = raw_kv[:HEAD].astype(bf16)
    kraw[...] = key
    low, high = path(key.astype(f32), gain_k, 1.0)
    kt[:64, :] = low
    kt[64:, :] = high
    vt[...] = raw_kv[HEAD:].astype(bf16)


def qkv(piece, *args):
    return call(
        functools.partial(qkv_body, piece),
        f"qkv{piece}",
        [
            sds((LH * HEAD, 2 * T), f32),
            sds((LH * HEAD, 2 * T), bf16),
            sds((HEAD, 2 * T), bf16),
            sds((HEAD, 2 * T), bf16),
            sds((HEAD, 2 * T), bf16),
            sds((2 * T, D), bf16),
            sds((2 * HEAD, D), bf16),
        ],
        [],
        args,
        flops=2 * 2 * T * D * 768,
        smem=(0,),
    )


def build_mask(info, mask):
    for b in range(8):
        keys = jnp.broadcast_to(info[0:1, b * T : (b + 1) * T], (T, T)).T
        for j in range(8):
            cols = slice(j * T, (j + 1) * T)
            inside = (keys >= info[1:2, cols]) & (keys <= info[0:1, cols])
            mask[b * T : (b + 1) * T, cols] = jnp.where(inside, 1.0, 0.0)


def attend_body(*refs):
    q, k, v = refs[0:4], refs[4:8], refs[8:12]
    info, ot0, ot1, linv, qt, kt, kn, vn, mask, vt = refs[12:]
    for dy in range(4):
        for dc in range(2):
            to = slice(dc * HALF + dy * T, dc * HALF + (dy + 1) * T)
            src = slice(dc * T, (dc + 1) * T)
            qt[:, to] = q[dy][:, src]
            kt[:, to] = k[dy][:, src]
            vt[:, to] = v[dy][:, src]
    for b in range(8):
        rows = slice(b * T, (b + 1) * T)
        kn[rows, :] = kt[:, rows].astype(f32).T.astype(bf16)
        vn[rows, :] = vt[:, rows].astype(f32).T.astype(bf16)
    build_mask(info, mask)
    for half, out in ((1, ot1), (0, ot0)):

        def body(i, carry):
            local = pl.ds(pl.multiple_of(i * 256, 256), 256)
            cols = pl.ds(pl.multiple_of(half * HALF + i * 256, 256), 256)
            for h in range(LH):
                heads = slice(h * HEAD, (h + 1) * HEAD)
                scores = dot(kn[...], qt[heads, cols])
                weights = jnp.exp2(scores * LOG2E) * mask[:, cols]
                inverse = 1.0 / jnp.sum(weights, axis=0, keepdims=True)
                out[heads, local] = (dot(vt[...], weights.astype(bf16)) * inverse).astype(bf16)
                linv[h : h + 1, cols] = inverse
            return carry

        lax.fori_loop(0, 2, body, 0)


def attend(q, k, v, info):
    return call(
        attend_body,
        "attend",
        [
            sds((LH * HEAD, HALF), bf16),
            sds((LH * HEAD, HALF), bf16),
            sds((8, ROWS), f32),
            sds((LH * HEAD, ROWS), bf16),
            sds((HEAD, ROWS), bf16),
            sds((ROWS, HEAD), bf16),
            sds((ROWS, HEAD), bf16),
        ],
        [pltpu.VMEM((ROWS, ROWS), f32), pltpu.VMEM((HEAD, ROWS), bf16)],
        (*q, *k, *v, info),
        flops=4 * LH * ROWS * ROWS * HEAD,
    )


def outproj_body(ot0, otr, wa, wb, b0, b1, b2, b3):
    total = dot(wa[...], ot0[...]) + dot(wb[...], otr[...])
    for dy, out in enumerate((b0, b1, b2, b3)):
        out[...] = total[:, dy * T : (dy + 1) * T].astype(bf16)


def outproj(ot0, otr, wa, wb):
    return grid_call(
        outproj_body,
        "out_projection",
        (4,),
        [whole((512, HALF)), whole((512, HALF)), rows_of((512, 512)), rows_of((512, 512))],
        [rows_of((512, T))] * 4,
        [sds((D, T), bf16)] * 4,
        [],
        (ot0, otr, wa, wb),
        flops=2 * D * 1024 * HALF,
    )


def route_body(rt, ids, ids_t):
    lane = lax.broadcasted_iota(jnp.int32, (T, E), 1)
    row = lax.broadcasted_iota(jnp.int32, (T, E), 0)
    wide = jnp.concatenate([rt[...].astype(f32), jnp.zeros((124, T), f32)], axis=0).T
    hot = [jnp.where(lane.astype(f32) == wide[:, k : k + 1], 1.0, 0.0) for k in range(4)]
    earlier = jnp.where(lane < row, 1.0, 0.0).astype(bf16)
    before = dot(earlier, (hot[0] + hot[1] + hot[2] + hot[3]).astype(bf16))
    table = wide
    for k in range(4):
        slot = jnp.sum(before * hot[k], axis=1, keepdims=True)
        table = jnp.where(lane == 4 + k, slot, table)
        table = jnp.where(lane == 8 + k, slot * E + wide[:, k : k + 1], table)
    ids[...] = table.astype(jnp.int32)
    ids_t[...] = table.T[0:16, :].astype(jnp.int32)


def route_tables(routes_t):
    return call(
        route_body,
        "route_tables",
        [sds((T, 128), jnp.int32), sds((16, T), jnp.int32)],
        [],
        (routes_t,),
        flops=2 * T * T * E,
    )


def router_body(b0, b1, b2, b3, x0, g2, wr, ids, at, hidden, n2, probs, gates, wire, rows):
    for j in range(SEG):
        part = slice(j * 128, (j + 1) * 128)
        total = (
            b0[part, :].astype(f32)
            + b1[part, :].astype(f32)
            + b2[part, :].astype(f32)
            + b3[part, :].astype(f32)
        )
        hidden[:, part] = x0[:, part].astype(f32) + total.T
    v = hidden[...]
    r = lax.rsqrt(jnp.mean(v * v, axis=-1, keepdims=True) + EPS)
    n2[...] = (v * r * g2[...]).astype(bf16)
    logits = dot(n2[...], wr[...])
    pack_rows(n2, at, wire, rows)
    expo = jnp.exp(logits - jnp.max(logits, axis=-1, keepdims=True))
    p = expo / jnp.sum(expo, axis=-1, keepdims=True)
    probs[...] = p
    lane = lax.broadcasted_iota(jnp.int32, (T, E), 1)
    chosen = [
        jnp.sum(jnp.where(lane == ids[:, k : k + 1], p, 0.0), axis=-1, keepdims=True)
        for k in range(4)
    ]
    total = chosen[0] + chosen[1] + chosen[2] + chosen[3]
    packed = jnp.where(lane == 4, total, 0.0)
    for k in range(4):
        packed = jnp.where(lane == k, chosen[k] / total, packed)
    gates[...] = packed
    across = packed.T
    expert = lax.broadcasted_iota(jnp.int32, (E, T), 0)
    columns = []
    for s in range(CAP):
        mine = jnp.zeros((E, T), f32)
        for k in range(4):
            mine = jnp.where(expert + s * E == at[k : k + 1, :], across[k : k + 1, :], mine)
        columns.append(jnp.sum(mine, axis=1, keepdims=True))
    put_numbers(columns, wire)


def router(b, x0, g2, wr, ids, assign_t):
    return call(
        router_body,
        "router",
        [
            sds((T, D), f32),
            sds((T, D), bf16),
            sds((T, E), f32),
            sds((T, E), f32),
            sds((E, WIRE, 128), bf16),
        ],
        [pltpu.VMEM((SLOTS, D), bf16)],
        (*b, x0, g2, wr, ids, assign_t),
        flops=2 * SLOTS * T * D,
    )


def expert_grad_body(wire, wd, gr, ga):
    split_rows(wire, gr)

    def body(i, carry):
        cols = pl.ds(pl.multiple_of(i * 256, 256), 256)
        ga[:, cols] = dot_t(gr[...], wd[cols, :])
        return carry

    lax.fori_loop(0, F // 256, body, 0)


def expert_grad(wire, wd):
    return call(
        expert_grad_body,
        "expert_grad_rows",
        [sds((SLOTS, D), bf16), sds((SLOTS, F), f32)],
        [],
        (wire, wd),
        flops=2 * SLOTS * D * F,
    )


def expert_main_body(wire, wg, wu, ga, back, xs, act, acts, dg, du, xr, sc):
    split_rows(wire, xr)
    gates = get_numbers(wire)
    sc[...] = jnp.zeros_like(sc)

    def forward(i, carry):
        cols = pl.ds(pl.multiple_of(i * 256, 256), 256)
        gate = dot(xr[...], wg[:, cols])
        up = dot(xr[...], wu[:, cols])
        grad = ga[:, cols]
        s = 1.0 / (1.0 + jnp.exp(-gate))
        silu = gate * s
        a = silu * up
        act[:, cols] = a.astype(bf16)
        dg[:, cols] = (grad * up * s * (1.0 + gate * (1.0 - s))).astype(bf16)
        du[:, cols] = (grad * silu).astype(bf16)
        sc[...] += jnp.sum(a * grad, axis=1, keepdims=True)
        return carry

    lax.fori_loop(0, F // 256, forward, 0)
    for s in range(CAP):
        part = slice(s * E, (s + 1) * E)
        gate = gates[:, s : s + 1]
        xs[part, :] = (xr[part, :].astype(f32) * gate).astype(bf16)
        acts[part, :] = (act[part, :].astype(f32) * gate).astype(bf16)
    for j in range(8):
        part = slice(j * 256, (j + 1) * 256)
        xr[:, part] = (dot_t(dg[...], wg[part, :]) + dot_t(du[...], wu[part, :])).astype(bf16)
    join_rows(xr, back)
    put_numbers([sc[s * E : (s + 1) * E, :] for s in range(CAP)], back)


def expert_main(wire, wg, wu, ga):
    return call(
        expert_main_body,
        "expert_main",
        [
            sds((E, WIRE, 128), bf16),
            sds((SLOTS, D), bf16),
            sds((SLOTS, F), bf16),
            sds((SLOTS, F), bf16),
            sds((SLOTS, F), bf16),
            sds((SLOTS, F), bf16),
        ],
        [pltpu.VMEM((SLOTS, D), bf16), pltpu.VMEM((SLOTS, 1), f32)],
        (wire, wg, wu, ga),
        flops=8 * SLOTS * D * F,
    )


def expert_out_body(act, wd, wire, rows):
    for j in range(8):
        cols = slice(j * 256, (j + 1) * 256)
        rows[:, cols] = dot(act[...], wd[:, cols]).astype(bf16)
    join_rows(rows, wire)


def expert_out(act, wd):
    return call(
        expert_out_body,
        "expert_out",
        [sds((E, CAP * SEG, 128), bf16)],
        [pltpu.VMEM((SLOTS, D), bf16)],
        (act, wd),
        flops=2 * SLOTS * D * F,
    )[0]


def combine_body(
    where, experts, slots, gate_list, wire, hidden, n2, probs, gates, ids, og, g2, wr,
    ghid, gatt, grouter, gg2, sums, gn2,
):
    sum_rows(wire, experts, slots, gate_list, sums)
    scores = get_numbers(wire)
    lane = lax.broadcasted_iota(jnp.int32, (T, E), 1)
    grads = []
    for k in range(4):
        hot = jnp.where(lane == ids[:, k : k + 1], 1.0, 0.0)
        rows = lax.dot_general(
            hot, scores, (((1,), (0,)), ((), ())),
            precision=lax.Precision.HIGHEST, preferred_element_type=f32,
        )
        picked = jnp.where(lane == ids[:, 4 + k : 5 + k], rows, 0.0)
        grads.append(jnp.sum(picked, axis=-1, keepdims=True))
    inner = sum(grads[k] * gates[:, k : k + 1] for k in range(4))
    inverse = 1.0 / gates[:, 4:5]
    grad_probs = jnp.zeros((T, E), f32)
    for k in range(4):
        grad_probs = jnp.where(
            lane == ids[:, k : k + 1], (grads[k] - inner) * inverse, grad_probs
        )
    p = probs[...]
    gl = (p * (grad_probs - jnp.sum(p * grad_probs, axis=-1, keepdims=True))).astype(bf16)
    for h in range(2):
        tokens = slice(h * 64, (h + 1) * 64)
        gn2[tokens, :] = sums[h * 1024 : (h + 1) * 1024, :].reshape(64, D)
    gn2[...] += dot_t(gl, wr[...])
    c = gn2[...]
    v = hidden[...]
    r = lax.rsqrt(jnp.mean(v * v, axis=-1, keepdims=True) + EPS)
    u = c * g2[...]
    m = jnp.mean(u * v, axis=-1, keepdims=True)
    total = og[...].astype(f32) + r * u - v * (r * r * r * m)
    ghid[...] = total
    gatt[...] = total.astype(bf16)
    gg2[...] = jnp.sum(c * (v * r), axis=0, keepdims=True)
    for j in range(SEG):
        cols = slice(j * 128, (j + 1) * 128)
        grouter[cols, :] = dot(n2[:, cols].astype(f32).T.astype(bf16), gl).astype(bf16)


def combine(*args):
    return call(
        combine_body,
        "combine_grads",
        [sds((T, D), f32), sds((T, D), bf16), sds((D, E), bf16), sds((1, D), f32)],
        [pltpu.VMEM((T * SEG, 128), f32), pltpu.VMEM((T, D), f32)],
        args,
        flops=4 * SLOTS * T * D,
        smem=(0, 1, 2, 3),
    )


def result_body(experts, slots, gate_list, wire, hidden, out, sums):
    sum_rows(wire, experts, slots, gate_list, sums)
    for h in range(2):
        tokens = slice(h * 64, (h + 1) * 64)
        mixture = sums[h * 1024 : (h + 1) * 1024, :].reshape(64, D)
        out[tokens, :] = (hidden[tokens, :] + mixture).astype(bf16)


def result_rows(*args):
    return call(
        result_body,
        "result",
        [sds((T, D), bf16)],
        [pltpu.VMEM((T * SEG, 128), f32)],
        args,
        flops=4 * SLOTS * T * D,
        smem=(0, 1, 2),
    )[0]


def pre_body(*refs):
    blocks, (ot0, ot1, wo, gw, dt, rows_all, total) = refs[:8], refs[8:]
    step = pl.program_id(0)
    for b in range(8):
        rows_all[b * T : (b + 1) * T, :] = blocks[b][...]
    gw[...] = (dot(ot0[...], rows_all[:HALF, :]) + dot(ot1[...], rows_all[HALF:, :])).astype(bf16)
    part = dot_t(wo[...], rows_all[...])

    @pl.when(step == 0)
    def _():
        total[...] = part

    @pl.when(step > 0)
    def _():
        total[...] += part

    @pl.when(step == 3)
    def _():
        dt[...] = total[...].astype(bf16)


def pre(blocks, ot0, ot1, wo):
    return grid_call(
        pre_body,
        "out_projection_grad",
        (4,),
        [cols_of((T, 512))] * 8 + [whole((512, HALF))] * 2 + [cols_of((512, 512))],
        [cols_of((512, 512)), whole((512, ROWS))],
        [sds((LH * HEAD, D), bf16), sds((LH * HEAD, ROWS), bf16)],
        [pltpu.VMEM((ROWS, 512), bf16), pltpu.VMEM((512, ROWS), f32)],
        (*blocks, ot0, ot1, wo),
        flops=4 * 512 * ROWS * D,
    )


def bwd_body(*refs):
    qr, kr = refs[0:4], refs[4:8]
    (qt, kt, kn, vn, dt, ot0, ot1, linv, info, cos, sin, gq, gk) = refs[8:21]
    dq0, dq1, dkv, ggq, ggk, mask, wb, sb, dqt, dk, dv, raw = refs[21:]
    build_mask(info, mask)
    dk[...] = jnp.zeros_like(dk)
    dv[...] = jnp.zeros_like(dv)
    for half, out in ((0, ot0), (1, ot1)):

        def body(i, carry):
            local = pl.ds(pl.multiple_of(i * 256, 256), 256)
            cols = pl.ds(pl.multiple_of(half * HALF + i * 256, 256), 256)
            for h in range(LH):
                heads = slice(h * HEAD, (h + 1) * HEAD)
                part = slice(h * 256, (h + 1) * 256)
                scores = dot(kn[...], qt[heads, cols])
                weights = jnp.exp2(scores * LOG2E) * (mask[:, cols] * linv[h : h + 1, cols])
                grad = dt[heads, cols]
                delta = jnp.sum(
                    grad.astype(f32) * out[heads, local].astype(f32), axis=0, keepdims=True
                )
                wb[:, part] = weights.astype(bf16)
                sb[:, part] = (weights * (dot(vn[...], grad) - delta)).astype(bf16)
                dqt[heads, cols] = dot(kt[...], sb[:, part])
            grads = jnp.concatenate(
                [dt[h * HEAD : (h + 1) * HEAD, cols] for h in range(LH)], axis=1
            )
            queries = jnp.concatenate(
                [qt[h * HEAD : (h + 1) * HEAD, cols] for h in range(LH)], axis=1
            )
            dv[...] += dot_t(wb[...], grads)
            dk[...] += dot_t(sb[...], queries)
            return carry

        lax.fori_loop(0, 2, body, 0)

    def unrope(v):
        low, high = v[:64], v[64:]
        c, s = cos[...], sin[...]
        return jnp.concatenate([low * c + high * s, high * c - low * s], axis=0)

    def norm_back(v, grad, gain):
        r = lax.rsqrt(jnp.mean(v * v, axis=0, keepdims=True) + EPS)
        n = v * r
        gain_grad = jnp.sum(grad * n, axis=1, keepdims=True)
        u = grad * gain
        return r * (u - n * jnp.mean(u * n, axis=0, keepdims=True)), gain_grad

    gain_q, gain_k = column(gq[...]), column(gk[...])
    total = jnp.zeros((HEAD, 1), f32)
    for h in range(LH):
        heads = slice(h * HEAD, (h + 1) * HEAD)
        for dy in range(4):
            for dc in range(2):
                to = slice(dc * HALF + dy * T, dc * HALF + (dy + 1) * T)
                raw[:, to] = qr[dy][heads, dc * T : (dc + 1) * T]
        grad, part = norm_back(raw[...], unrope(dqt[heads, :] * (HEAD ** (-0.5))), gain_q)
        total = total + part
        dq0[heads, :] = grad[:, :HALF].astype(bf16)
        dq1[heads, :] = grad[:, HALF:].astype(bf16)
    ggq[...] = jnp.broadcast_to(total, (HEAD, 128)).T[0:8, :]
    for dy in range(4):
        for dc in range(2):
            to = slice(dc * HALF + dy * T, dc * HALF + (dy + 1) * T)
            raw[:, to] = kr[dy][:, dc * T : (dc + 1) * T].astype(f32)
    grad, part = norm_back(raw[...], unrope(dk[...].T), gain_k)
    ggk[...] = jnp.broadcast_to(part, (HEAD, 128)).T[0:8, :]
    dkv[:HEAD, :] = grad.astype(bf16)
    dkv[HEAD:, :] = dv[...].T.astype(bf16)


def bwd(qr, kr, *rest):
    return call(
        bwd_body,
        "attend_grad",
        [
            sds((LH * HEAD, HALF), bf16),
            sds((LH * HEAD, HALF), bf16),
            sds((2 * HEAD, ROWS), bf16),
            sds((8, HEAD), f32),
            sds((8, HEAD), f32),
        ],
        [
            pltpu.VMEM((ROWS, ROWS), f32),
            pltpu.VMEM((ROWS, LH * 256), bf16),
            pltpu.VMEM((ROWS, LH * 256), bf16),
            pltpu.VMEM((LH * HEAD, ROWS), f32),
            pltpu.VMEM((ROWS, HEAD), f32),
            pltpu.VMEM((ROWS, HEAD), f32),
            pltpu.VMEM((HEAD, ROWS), f32),
        ],
        (*qr, *kr, *rest),
        flops=10 * LH * ROWS * ROWS * HEAD,
    )


def qkv_grad_body(where, n1t, dq0, dq1, own, sib, wa, wb, tot, dt):
    @pl.when(pl.program_id(0) == 0)
    def _():
        tot[:, :HALF] = (own[:, :HALF].astype(f32) + sib[:, HALF:].astype(f32)).astype(bf16)
        tot[:, HALF:] = (own[:, HALF:].astype(f32) + sib[:, :HALF].astype(f32)).astype(bf16)
        dt[:512, :HALF] = dq0[...]
        dt[:512, HALF:] = dq1[...]
        upper = where[2] == 1
        dt[512:576, :] = jnp.where(upper, tot[64:128, :], tot[:64, :])
        dt[576:, :] = jnp.where(upper, tot[192:, :], tot[128:192, :])

    grad = dot_t(n1t[...], dt[...]).astype(bf16)
    for col in range(4):
        dx = lax.rem(col + 4 - where[1], 4)
        wa[0, dx] = grad[col * 128 : col * 128 + 64, :]
        wb[dx, 0] = grad[col * 128 + 64 : (col + 1) * 128, :]


def qkv_grad(where, n1t, dq0, dq1, own, sib):
    return grid_call(
        qkv_grad_body,
        "qkv_weight_grad",
        (4,),
        [
            rows_of((512, ROWS)),
            whole((512, HALF)),
            whole((512, HALF)),
            whole((2 * HEAD, ROWS)),
            whole((2 * HEAD, ROWS)),
        ],
        [
            pl.BlockSpec((1, 4, 64, 640), lambda i, w: (lax.rem(i + 4 - w[0], 4), 0, 0, 0)),
            pl.BlockSpec((4, 1, 64, 640), lambda i, w: (0, lax.rem(i + 4 - w[0], 4), 0, 0)),
            whole((2 * HEAD, ROWS)),
        ],
        [
            sds((4, 4, 64, 640), bf16),
            sds((4, 4, 64, 640), bf16),
            sds((2 * HEAD, ROWS), bf16),
        ],
        [pltpu.VMEM((640, ROWS), bf16)],
        (where, n1t, dq0, dq1, own, sib),
        flops=2 * D * 640 * ROWS,
        scalars=1,
    )


def normed_grad_body(wa, wb, wkv, dq0, dqr, tot, n1t, b0, b1, b2, b3, gg1):
    total = dot(wa[...], dq0[...]) + dot(wb[...], dqr[...]) + dot(wkv[...], tot[...])
    for dy, out in enumerate((b0, b1, b2, b3)):
        out[...] = total[:, dy * T : (dy + 1) * T].astype(bf16)
    gain = jnp.sum(total * n1t[...].astype(f32), axis=1, keepdims=True)
    for b in range(4):
        rows = slice(b * 128, (b + 1) * 128)
        gg1[:, rows] = jnp.broadcast_to(gain[rows, :], (128, 128)).T[0:8, :]


def normed_grad(wa, wb, wkv, dq0, dqr, tot, n1t):
    return grid_call(
        normed_grad_body,
        "normed_grad",
        (4,),
        [
            rows_of((512, 512)),
            rows_of((512, 512)),
            rows_of((512, 256)),
            whole((512, HALF)),
            whole((512, HALF)),
            whole((2 * HEAD, HALF)),
            rows_of((512, HALF)),
        ],
        [rows_of((512, T))] * 4 + [cols_of((8, 512))],
        [sds((D, T), bf16)] * 4 + [sds((8, D), f32)],
        [],
        (wa, wb, wkv, dq0, dqr, tot, n1t),
        flops=2 * D * 1280 * HALF,
    )


def place_body(where, *refs):
    first, second, (gq, gkt, gvt) = refs[:4], refs[4:8], refs[8:]
    for dz in range(4):
        for dx in range(4):
            chunk = lax.rem(where[0] + dz, 4) * 4 + lax.rem(where[1] + dx, 4)
            start = pl.multiple_of(chunk * 128, 128)
            a = first[dz][dx].astype(f32)
            b = second[dx][dz].astype(f32)
            gq[pl.ds(start, 64), :] = a[:, :512]
            gq[pl.ds(start + 64, 64), :] = b[:, :512]
            both = jnp.concatenate([a[:, 512:], b[:, 512:]], axis=0).T
            gkt[:, pl.ds(start, 128)] = both[:64]
            gvt[:, pl.ds(start, 128)] = both[64:]


def place(where, first, second):
    return call(
        place_body,
        "place_weight_grads",
        [sds((D, 512), f32), sds((64, D), f32), sds((64, D), f32)],
        [],
        (where, *first, *second),
        smem=(0,),
    )


def final_body(b0, b1, b2, b3, x0, ghid, g1, out, c):
    for j in range(SEG):
        rows = slice(j * 128, (j + 1) * 128)
        total = (
            b0[rows, :].astype(f32)
            + b1[rows, :].astype(f32)
            + b2[rows, :].astype(f32)
            + b3[rows, :].astype(f32)
        )
        c[:, rows] = total.T
    v = x0[...].astype(f32)
    r = lax.rsqrt(jnp.mean(v * v, axis=-1, keepdims=True) + EPS)
    u = c[...] * g1[...]
    m = jnp.mean(u * v, axis=-1, keepdims=True)
    out[...] = ghid[...] + r * u - v * (r * r * r * m)


def final(b, x0, ghid, g1):
    return call(
        final_body,
        "input_grad",
        [sds((T, D), f32)],
        [pltpu.VMEM((T, D), f32)],
        (*b, x0, ghid, g1),
        flops=T * D * 10,
    )[0]


def sibling(x):
    return lax.ppermute(x, "shard", [(i, i ^ 1) for i in range(8)])


def from_chip(x, dy):
    return lax.ppermute(x, "shard", [(i, (i - 2 * dy) % 8) for i in range(8)])


def to_chip(x, dy):
    return lax.ppermute(x, "shard", [(i, (i + 2 * dy) % 8) for i in range(8)])


def gather_blocks(x):
    first = [x] + [from_chip(x, dy) for dy in (1, 2, 3)]
    return first, [sibling(b) for b in first]


def exchange(x):
    return lax.all_to_all(x, ALL, split_axis=0, concat_axis=0, tiled=True)


def spread(x):
    return [to_chip(x[d], d) for d in (1, 3, 2)]


def on_expert(x, dz, dx):
    pairs = [
        (z * 4 + c, ((z + dz) % 4) * 4 + (c + dx) % 4) for z in range(4) for c in range(4)
    ]
    return lax.ppermute(x, "expert", pairs)


def move(x, axis, distance):
    return on_expert(x, distance, 0) if axis == 0 else on_expert(x, 0, distance)


def reduce_step(x, axis):
    got = [move(x[d], axis, d) for d in (1, 3, 2)]
    return (
        x[0].astype(f32) + got[0].astype(f32) + got[1].astype(f32) + got[2].astype(f32)
    ).astype(bf16)


def gather_step(x, axis):
    return [x] + [move(x, axis, (4 - d) % 4) for d in (1, 2, 3)]


def sum_over_experts(a, b):
    a1, b1 = reduce_step(a, 0), reduce_step(b, 1)
    a2, b2 = reduce_step(a1, 1), reduce_step(b1, 0)
    a3, b3 = jnp.stack(gather_step(a2, 1)), jnp.stack(gather_step(b2, 0))
    return gather_step(a3, 0), gather_step(b3, 1)


def after(value, *others):
    return lax.optimization_barrier((value, *others))[0]


def on_device(
    block_input, out_grad, norm1_gain, w_query, w_key, w_value, query_gain, key_gain, w_out,
    norm2_gain, w_router, w_gate, w_up, w_down, seq_lengths, token_places, expert_routes,
):
    shard, owner = lax.axis_index("shard"), lax.axis_index("expert")
    chip, core = shard // 2, shard % 2
    where = jnp.stack([owner // 4, owner % 4, core]).astype(jnp.int32)
    core_id = core.reshape(1)
    g1 = norm1_gain.astype(f32).reshape(1, D)
    g2 = norm2_gain.astype(f32).reshape(1, D)
    gq = query_gain.astype(f32).reshape(1, HEAD)
    gk = key_gain.astype(f32).reshape(1, HEAD)

    x_own, x_sib = gather_blocks(block_input)

    chips = (chip + jnp.arange(4)) % 4
    order = jnp.concatenate([chips * 2 + core, chips * 2 + 1 - core])
    places = token_places[0].reshape(8, T)[order].reshape(ROWS)
    lengths = seq_lengths[0]
    ends = jnp.cumsum(lengths)
    starts = jnp.sum(
        jnp.where(places[:, None] >= ends[None, :], lengths[None, :], 0), axis=1
    )
    positions = (places - starts).astype(f32)
    info = jnp.concatenate(
        [places[None].astype(f32), starts[None].astype(f32), jnp.zeros((6, ROWS), f32)], axis=0
    )
    inverse_freq = ROPE_BASE ** (-jnp.arange(0, HEAD, 2).astype(f32) / HEAD)
    angles = inverse_freq[:, None] * positions[None, :]
    cos, sin = jnp.cos(angles), jnp.sin(angles)

    ids, ids_t = route_tables(expert_routes.T)
    assign_t = ids_t[8:12]
    expert_list = ids[:, 0:4].reshape(-1)
    slot_list = ids[:, 4:8].reshape(-1)

    wk_t, wv_t = w_key.T, w_value.T
    wk_s, wv_s = sibling(wk_t), sibling(wv_t)
    wq_t = w_query.T
    wo_t = w_out.T
    wo_ts = sibling(wo_t)
    wq_s = sibling(w_query)

    def piece(dy):
        return qkv(
            dy, core_id, x_own[dy], x_sib[dy], g1, wq_t, wk_t, wk_s, wv_t, wv_s, gq, gk, cos, sin
        )

    pieces = [piece(dy) for dy in range(4)]
    q_raw, q, k_raw, k, v, n1, wkv = zip(*pieces)
    got_grads = exchange(pack(out_grad, assign_t))
    ot0, ot1, linv, qt, kt, kn, vn = attend(q, k, v, info)
    blocks = outproj(ot0, sibling(ot1), wo_t, wo_ts)
    blocks = [blocks[0]] + spread(blocks)
    hidden, n2, probs, gates, wire = router(blocks, block_input, g2, w_router, ids, assign_t)
    got_rows = exchange(wire)

    n1 = after(n1, wire)
    n1_t = jnp.concatenate([p[:T] for p in n1] + [p[T:] for p in n1], axis=0).T
    wkv_full = after(wkv[0], wire).T
    gate_list = gates[:, :4].reshape(-1)
    grad_rows, grad_act = expert_grad(after(got_grads, wire), w_down[0])
    got_rows, n1_t, wkv_full, grad_act, gate_list = lax.optimization_barrier(
        (got_rows, n1_t, wkv_full, grad_act, gate_list)
    )

    back, rows, act, scaled_act, dg, du = expert_main(got_rows, w_gate[0], w_up[0], grad_act)
    back_wire = exchange(back)

    rows, act, scaled_act, dg, du = after((rows, act, scaled_act, dg, du), back)
    out_wire = expert_out(act, w_down[0])

    def weight_grad(a, b):
        return lax.dot_general(a, b, (((0,), (0,)), ((), ())), preferred_element_type=f32)

    grad_wgate = weight_grad(rows, dg)
    grad_wup = weight_grad(rows, du)
    grad_wdown = weight_grad(scaled_act, grad_rows)
    back_wire, out_wire, grad_wgate, grad_wup, grad_wdown = lax.optimization_barrier(
        (back_wire, out_wire, grad_wgate, grad_wup, grad_wdown)
    )

    ghid, gatt, grouter, gg2 = combine(
        where, expert_list, slot_list, gate_list, back_wire, hidden, n2, probs, gates, ids,
        out_grad, g2, w_router,
    )
    g_own, g_sib = gather_blocks(gatt)
    router_parts = exchange(grouter.reshape(E, SEG, 128))
    router_sum = jnp.sum(router_parts.astype(f32), axis=0).astype(bf16)
    returned = exchange(after(out_wire, g_own[2]))

    gwout, dt = pre(g_own + g_sib, ot0, ot1, w_out)
    grad_wout = lax.psum(gwout, "expert").astype(f32)
    dq0, dq1, dkv, ggq, ggk = bwd(
        q_raw, k_raw, qt, kt, kn, vn, dt, ot0, ot1, linv, info, cos, sin, gq, gk
    )
    dq_sib, dkv_sib = sibling(dq1), sibling(dkv)
    gw_a, gw_b, dkv_total = qkv_grad(where, n1_t, dq0, dq1, dkv, dkv_sib)
    gw_a, gw_b = sum_over_experts(gw_a, gw_b)
    blocks = normed_grad(w_query, wq_s, wkv_full, dq0, dq_sib, dkv_total, n1_t)
    gg1 = blocks[4][0]
    blocks, returned, router_sum = lax.optimization_barrier((blocks[:4], returned, router_sum))
    blocks = [blocks[0]] + spread(blocks)
    result = result_rows(expert_list, slot_list, gate_list, returned, hidden)

    vector = jnp.concatenate([gg1 / g1[0], gg2[0], ggq[0], ggk[0]])
    per = vector.shape[0] // E
    wide = jnp.pad(vector.reshape(E, per), ((0, 0), (0, 128 - per))).reshape(E, 1, 128)
    mine = jnp.sum(exchange(wide), axis=0)
    first = mine.astype(bf16)
    second = (mine - first.astype(f32)).astype(bf16)
    shared = jnp.concatenate([router_sum, first, second, jnp.zeros((6, 128), bf16)], axis=0)
    shared = exchange(jnp.broadcast_to(shared[None], (E, 24, 128)))
    grad_router = shared[:, :SEG].reshape(D, E).astype(f32)
    vector = (
        (shared[:, SEG].astype(f32) + shared[:, SEG + 1].astype(f32))[:, :per].reshape(-1)
    )
    grad_input = final(blocks, block_input, ghid, g1)
    grad_wq, grad_wk, grad_wv = place(where, gw_a, gw_b)
    return (
        result,
        grad_input,
        vector[:D],
        grad_wq,
        grad_wk.T,
        grad_wv.T,
        vector[2 * D : 2 * D + HEAD],
        vector[2 * D + HEAD :],
        grad_wout,
        vector[D : 2 * D],
        grad_router,
        grad_wgate[None],
        grad_wup[None],
        grad_wdown[None],
    )


def solution(mesh):
    rows = P(("expert", "shard"), None)
    experts = P(("expert", "shard"), None, None)
    columns = P(None, "shard")
    return jax.shard_map(
        on_device,
        mesh=mesh,
        in_specs=(
            rows, rows, P(), columns, columns, columns, P(), P(), P("shard", None), P(), P(),
            experts, experts, experts, P("expert", None), P("expert", None), rows,
        ),
        out_specs=(
            rows, rows, P(), columns, columns, columns, P(), P(), P("shard", None), P(), P(),
            experts, experts, experts,
        ),
        check_vma=False,
    )
```

time: 534 us -> 530 us (level)
  starting transfers between devices: 79.7 us -> 128 us
  blocking collectives: 28.1 us -> 0 us
  local copies, waits for them, and re-layouts: 64.8 us -> 42.7 us
  waiting for transfers between devices: 150 us -> 164 us
  Pallas kernels: 151 us -> 144 us
    ppermute x0 -> x24, waiting for transfers between devices: none -> 67.3 us  [on_expert(): return lax.ppermute(x, 'expert', pairs)]
    pallas_call x18 -> x16, Pallas kernels: 151 us -> 113 us  [call(): pl.pallas_call(kernel, out_shape=outs, in_specs=in_specs, out_specs=[pl.B...]
    ppermute x0 -> x24, starting transfers between devices: none -> 36 us  [on_expert(): return lax.ppermute(x, 'expert', pairs)]
    pallas_call x0 -> x4, Pallas kernels: none -> 30.9 us  [grid_call(): pl.pallas_call(kernel, out_shape=outs, grid_spec=pltpu.PrefetchScalarGrid...]
    ppermute x6, waiting for transfers between devices: 52.9 us -> 22.6 us  [to_chip(): return lax.ppermute(x, 'shard', [(i, (i + 2 * dy) % 8) for i in range(8)])]
    all_to_all x2 -> x0, blocking collectives: 28.1 us -> none  [exchange(): return lax.all_to_all(x, ALL, split_axis=0, concat_axis=0, tiled=True)]
    all_to_all x8 -> x7, waiting for transfers between devices: 76 us -> 51.3 us  [exchange(): return lax.all_to_all(x, ALL, split_axis=0, concat_axis=0, tiled=True)]
    unnamed x110 -> x93, local copies, waits for them, and re-layouts: 35 us -> 21 us
  transfers between devices with their start and end apart: 35 -> 59, of which waited for: 13 -> 18; matrix products, arithmetic and copies ran while one was open for 15% -> 12% of each run, Pallas kernels for 25% -> 23%
where the time goes in v2:
time: 530 us; the launch traced here: 523 us
  waiting for transfers between devices  164 us (31%)
  Pallas kernels  144 us (27%)
  starting transfers between devices  128 us (24%)
  local copies, waits for them, and re-layouts  42.7 us (8%)
  other arithmetic  15.5 us (3%)
  between operations  14.9 us (3%)
  matrix products  13.7 us (3%)
    pallas_call x16, Pallas kernels, call(): pl.pallas_call(kernel, out_shape=outs, in_specs=in_specs, out_specs=[pl.B...  113 us
    ppermute x24, waiting for transfers between devices, on_expert(): return lax.ppermute(x, 'expert', pairs)  67.3 us
    all_to_all x7, starting transfers between devices, exchange(): return lax.all_to_all(x, ALL, split_axis=0, concat_axis=0, tiled=True)  63.4 us
    all_to_all x7, waiting for transfers between devices, exchange(): return lax.all_to_all(x, ALL, split_axis=0, concat_axis=0, tiled=True)  51.3 us
    ppermute x24, starting transfers between devices, on_expert(): return lax.ppermute(x, 'expert', pairs)  36 us
    pallas_call x4, Pallas kernels, grid_call(): pl.pallas_call(kernel, out_shape=outs, grid_spec=pltpu.PrefetchScalarGrid...  30.9 us
    ppermute x6, waiting for transfers between devices, to_chip(): return lax.ppermute(x, 'shard', [(i, (i + 2 * dy) % 8) for i in range(8)])  22.6 us
    unnamed x93, local copies, waits for them, and re-layouts  21 us
  transfers between devices with their start and end apart: 59, of which 18 were waited for; matrix products, arithmetic and copies ran while one was open for 12% of the time, Pallas kernels for 23%

profile of v2, /device:TPU:1, one launch (start us, length us, event | category | flops | bytes accessed | tf_op | source)
XLA Modules:
  0.0 523.4 jit_solution(11531419590736227280)
XLA Ops:
  7.2 3.6 collective-permute-start.3
  13.4 2.9 copy.67
  16.4 2.0 route_tables.1
  19.6 4.2 pack_rows.1
  23.7 10.0 %all-to-all-start.1 = ((bf16[128,88,128]{2,1,0:T(8,128)(2,1)}), bf16[128,88,128]{2,1,0:T(8,128)(2,1)}, u32[]{:S(2)}, u32[]{:S(2)}) async-start(bf16[128,88,128]{2,1,0:T(8,128)(2,1)} %pack_rows.1), calls=%async_computation.1 | async-start | bytes 5767168 | tf_op jit(solution)/shard_map/all_to_all | solution.py:857
  37.5 1.8 multiply_sine_fusion
  41.8 3.9 copy.66
  46.3 4.7 qkv0.1
  51.0 4.7 qkv1.1
  55.7 4.7 qkv2.1
  60.4 4.7 qkv3.1
  65.1 10.9 %attend.1 = (bf16[512,512]{1,0:T(8,128)(2,1)}, bf16[512,512]{1,0:T(8,128)(2,1)}, f32[8,1024]{1,0:T(8,128)}, bf16[512,1024]{1,0:T(8,128)(2,1)}, bf16[128,1024]{1,...) custom-call(bf16[512,256]{1,0:T(8,128)(2,1)} %get-tuple-element.116.refs_0_, ...), custom_call_target="tpu_custom_call" | custom-call | flops 2147483648 | bytes 4521984 | tf_op jit(solution)/shard_map/attend/pallas_call | solution.py:46
  79.0 6.0 %out_projection.1 = (bf16[2048,128]{1,0:T(8,128)(2,1)}, bf16[2048,128]{1,0:T(8,128)(2,1)}, bf16[2048,128]{1,0:T(8,128)(2,1)}, bf16[2048,128]{1,0:T(8,128)(2,1)}) custom-call(bf16[512,512]{1,0:T(8,128)(2,1)} %get-tuple-element.128.ot0.refs_8_.refs_13_, bf16[512,512]{1,0:T(8,128)(2,1)} %copy-done.38, bf16[2048,512]{1,0:T(8,128)(2,1)} %bitcast.135, ...), custom_call_target="tpu_custom_call" | custom-call | flops 2147483648 | bytes 7340032 | tf_op jit(solution)/shard_map/out_projection/pallas_call | solution.py:64
  85.7 2.4 collective-permute-start.12
  90.0 10.3 %collective-permute-done.11.b1 = bf16[2048,128]{1,0:T(8,128)(2,1)S(1)} collective-permute-done((bf16[2048,128]{1,0:T(8,128)(2,1)}, bf16[2048,128]{1,0:T(8,128)(2,1)S(1)}, u32[]{:S(2)}, u32[]{:S(2)}) %collective-permute-start.11) | collective-permute-done | bytes 524320 | tf_op jit(solution)/shard_map/ppermute | solution.py:848
  100.2 10.3 %collective-permute-done.12.b2 = bf16[2048,128]{1,0:T(8,128)(2,1)S(1)} collective-permute-done((bf16[2048,128]{1,0:T(8,128)(2,1)}, bf16[2048,128]{1,0:T(8,128)(2,1)S(1)}, u32[]{:S(2)}, u32[]{:S(2)}) %collective-permute-start.12) | collective-permute-done | bytes 524320 | tf_op jit(solution)/shard_map/ppermute | solution.py:848
  110.6 2.0 collective-permute-done.13.b3
  113.4 5.7 %router.1 = (f32[128,2048]{1,0:T(8,128)}, bf16[128,2048]{1,0:T(8,128)(2,1)}, f32[128,128]{1,0:T(8,128)}, f32[128,128]{1,0:T(8,128)}, bf16[128,88,128]{2,1,0:T(8,128)(2,1)}) custom-call(bf16[2048,128]{1,0:T(8,128)(2,1)} %get-tuple-element.130.b0, bf16[2048,128]{1,0:T(8,128)(2,1)} %copy-done.16, bf16[2048,128]{1,0:T(8,128)(2,1)} %copy-done.17, ...), custom_call_target="tpu_custom_call" | custom-call | flops 335544320 | bytes 7809024 | tf_op jit(solution)/shard_map/router/pallas_call | solution.py:46
  124.0 2.3 copy.76
  126.9 1.9 slice_dynamic-update-slice_fusion.7
  129.6 20.1 %all-to-all-start = ((bf16[128,88,128]{2,1,0:T(8,128)(2,1)}), bf16[128,88,128]{2,1,0:T(8,128)(2,1)}, u32[]{:S(2)}, u32[]{:S(2)}) async-start(bf16[128,88,128]{2,1,0:T(8,128)(2,1)} %get-tuple-element.135), calls=%async_computation | async-start | bytes 5767168 | tf_op jit(solution)/shard_map/all_to_all | solution.py:857
  151.4 1.9 slice_dynamic-update-slice_fusion.3
  155.8 7.5 %expert_grad_rows.1 = (bf16[640,2048]{1,0:T(8,128)(2,1)}, f32[640,768]{1,0:T(8,128)}) custom-call(bf16[128,88,128]{2,1,0:T(8,128)(2,1)} %all-to-all-done.1.wire, bf16[768,2048]{1,0:T(8,128)(2,1)} %bitcast.160), custom_call_target="tpu_custom_call" | custom-call | flops 2013265920 | bytes 10616832 | tf_op jit(solution)/shard_map/expert_grad_rows/pallas_call | solution.py:46
  163.3 25.2 %all-to-all-done.wire = bf16[128,88,128]{2,1,0:T(8,128)(2,1)} async-done(((bf16[128,88,128]{2,1,0:T(8,128)(2,1)}), bf16[128,88,128]{2,1,0:T(8,128)(2,1)}, u32[]{:S(2)}, u32[]{:S(2)}) %all-to-all-start) | async-done | bytes 2883616 | tf_op jit(solution)/shard_map/all_to_all | solution.py:857
  188.5 18.6 %expert_main.1 = (bf16[128,88,128]{2,1,0:T(8,128)(2,1)}, bf16[640,2048]{1,0:T(8,128)(2,1)}, bf16[640,768]{1,0:T(8,128)(2,1)}, bf16[640,768]{1,0:T(8,128)(2,1)}, ...) custom-call(bf16[128,88,128]{2,1,0:T(8,128)(2,1)} %all-to-all-done.wire, bf16[2048,768]{1,0:T(8,128)(2,1)} %bitcast.158, ...), custom_call_target="tpu_custom_call" | custom-call | flops 8053063680 | bytes 20578304 | tf_op jit(solution)/shard_map/expert_main/pallas_call | solution.py:46
  207.1 4.8 all-to-all-start.2
  214.1 6.6 %expert_out.1 = bf16[128,80,128]{2,1,0:T(8,128)(2,1)} custom-call(bf16[640,768]{1,0:T(8,128)(2,1)} %get-tuple-element.171.act, bf16[768,2048]{1,0:T(8,128)(2,1)} %bitcast.161), custom_call_target="tpu_custom_call" | custom-call | flops 2013265920 | bytes 6750208 | tf_op jit(solution)/shard_map/expert_out/pallas_call | solution.py:46
  220.8 4.6 fusion.22
  225.4 4.6 fusion.21
  229.9 4.5 fusion.23
  234.5 16.5 %all-to-all-done.2.wire = bf16[128,88,128]{2,1,0:T(8,128)(2,1)S(1)} async-done(((bf16[128,88,128]{2,1,0:T(8,128)(2,1)}), bf16[128,88,128]{2,1,0:T(8,128)(2,1)S(1)}, u32[]{:S(2)}, u32[]{:S(2)}) %all-to-all-start.2) | async-done | bytes 2883616 | tf_op jit(solution)/shard_map/all_to_all | solution.py:857
  252.6 7.2 %combine_grads.1 = (f32[128,2048]{1,0:T(8,128)}, bf16[128,2048]{1,0:T(8,128)(2,1)}, bf16[2048,128]{1,0:T(8,128)(2,1)}, f32[1,2048]{1,0:T(1,128)}) custom-call(s32[3]{0:T(128)} %pad_add_fusion.where, s32[512]{0:T(512)} %reshape.229.experts, s32[512]{0:T(512)} %reshape.230.slots, f32[512]{0:T(512)} %reshape.242.gate_list, bf16[128,88,128]{2,1,0:T(8,128)(2,1)} %copy-done.2, ...), custom_call_target="tpu_custom_call" | custom-call | flops 671088640 | bytes 7821324 | tf_op jit(solution)/shard_map/combine_grads/pallas_call | solution.py:46
  261.3 1.8 collective-permute-start.18
  263.0 9.5 %collective-permute-done.15.refs_1_ = bf16[128,2048]{1,0:T(8,128)(2,1)S(1)} collective-permute-done((bf16[128,2048]{1,0:T(8,128)(2,1)}, bf16[128,2048]{1,0:T(8,128)(2,1)S(1)}, u32[]{:S(2)}, u32[]{:S(2)}) %collective-permute-start.15) | collective-permute-done | bytes 524320 | tf_op jit(solution)/shard_map/ppermute | solution.py:844
  272.6 3.2 collective-permute-start.19
  275.7 1.8 collective-permute-start.20
  277.5 9.1 %collective-permute-done.17.refs_3_ = bf16[128,2048]{1,0:T(8,128)(2,1)S(1)} collective-permute-done((bf16[128,2048]{1,0:T(8,128)(2,1)}, bf16[128,2048]{1,0:T(8,128)(2,1)S(1)}, u32[]{:S(2)}, u32[]{:S(2)}) %collective-permute-start.17) | collective-permute-done | bytes 524320 | tf_op jit(solution)/shard_map/ppermute | solution.py:844
  289.5 9.2 %out_projection_grad.1 = (bf16[512,2048]{1,0:T(8,128)(2,1)}, bf16[512,1024]{1,0:T(8,128)(2,1)}) custom-call(bf16[128,2048]{1,0:T(8,128)(2,1)} %get-tuple-element.181.refs_0_, bf16[128,2048]{1,0:T(8,128)(2,1)} %copy-done.31, bf16[128,2048]{1,0:T(8,128)(2,1)} %copy-done.32, bf16[128,2048]{1,0:T(8,128)(2,1)} %copy-done.33, bf16[128,2048]{1,0:T(8,128)(2,1)} %copy-done.34, ...), custom_call_target="tpu_custom_call" | custom-call | flops 4294967296 | bytes 10485760 | tf_op jit(solution)/shard_map/out_projection_grad/pallas_call | solution.py:64
  298.7 18.9 %attend_grad.1 = (bf16[512,512]{1,0:T(8,128)(2,1)}, bf16[512,512]{1,0:T(8,128)(2,1)}, bf16[256,1024]{1,0:T(8,128)(2,1)}, f32[8,128]{1,0:T(8,128)}, f32[8,128]{1,0:T(8,128)}) custom-call(f32[512,256]{1,0:T(8,128)} %get-tuple-element.151.refs_0_, f32[512,256]{1,0:T(8,128)} %get-tuple-element.152.refs_1_, f32[512,256]{1,0:T(8,128)} %get-tuple-element.153.refs_2_, ...), custom_call_target="tpu_custom_call" | custom-call | flops 5368709120 | bytes 8463360 | tf_op jit(solution)/shard_map/attend_grad/pallas_call | solution.py:46
  318.2 3.8 all-to-all-start.4
  324.7 8.5 %qkv_weight_grad.1 = (bf16[4,4,64,640]{3,2,1,0:T(8,128)(2,1)}, bf16[4,4,64,640]{3,2,1,0:T(8,128)(2,1)}, bf16[256,1024]{1,0:T(8,128)(2,1)}) custom-call(s32[3]{0:T(128)} %pad_add_fusion.where, bf16[2048,1024]{1,0:T(8,128)(2,1)} %bitcast.22.n1t, bf16[512,512]{1,0:T(8,128)(2,1)} %get-tuple-element.184.dq0, bf16[512,512]{1,0:T(8,128)(2,1)} %get-tuple-element.185.dq1, ...), custom_call_target="tpu_custom_call" | custom-call | flops 2684354560 | bytes 9437196 | tf_op jit(solution)/shard_map/qkv_weight_grad/pallas_call | solution.py:64
  334.7 7.3 %normed_grad.1 = (bf16[2048,128]{1,0:T(8,128)(2,1)}, bf16[2048,128]{1,0:T(8,128)(2,1)}, bf16[2048,128]{1,0:T(8,128)(2,1)}, bf16[2048,128]{1,0:T(8,128)(2,1)}, f32[8,2048]{1,0:T(8,128)}) custom-call(bf16[2048,512]{1,0:T(8,128)(2,1)} %wa.1, bf16[2048,512]{1,0:T(8,128)(2,1)} %copy-done.10, bf16[2048,256]{1,0:T(8,128)(2,1)} %bitcast.133, ...), custom_call_target="tpu_custom_call" | custom-call | flops 2684354560 | bytes 13172736 | tf_op jit(solution)/shard_map/normed_grad/pallas_call | solution.py:64
  343.7 8.9 %all-to-all-start.5 = ((f32[128,1,128]{2,1,0:T(1,128)}), f32[128,1,128]{2,1,0:T(1,128)S(1)}, u32[]{:S(2)}, u32[]{:S(2)}) async-start(f32[128,1,128]{2,1,0:T(1,128)} %bitcast.35), calls=%async_computation.5 | async-start | bytes 131072 | tf_op jit(solution)/shard_map/all_to_all | solution.py:857
  352.5 9.5 %all-to-all-done.5 = f32[128,1,128]{2,1,0:T(1,128)S(1)} async-done(((f32[128,1,128]{2,1,0:T(1,128)}), f32[128,1,128]{2,1,0:T(1,128)S(1)}, u32[]{:S(2)}, u32[]{:S(2)}) %all-to-all-start.5) | async-done | bytes 65568 | tf_op jit(solution)/shard_map/all_to_all | solution.py:857
  362.0 4.4 all-to-all-start.3
  367.2 2.1 slice_bitcast_fusion.2
  373.7 2.1 slice_bitcast_fusion.5
  379.1 30.6 %collective-permute-done.39 = bf16[4,64,640]{2,1,0:T(8,128)(2,1)} collective-permute-done((bf16[4,64,640]{2,1,0:T(8,128)(2,1)}, bf16[4,64,640]{2,1,0:T(8,128)(2,1)}, u32[]{:S(2)}, u32[]{:S(2)}) %collective-permute-start.39) | collective-permute-done | bytes 327712 | tf_op jit(solution)/shard_map/ppermute | solution.py:868
  409.7 5.2 collective-permute-start.29
  414.9 5.2 collective-permute-done.41
  423.0 1.8 collective-permute-start.43
  427.8 2.4 collective-permute-start.31
  432.8 2.5 collective-permute-done.32
  438.4 2.0 collective-permute-start.48
  442.8 11.4 %all-to-all-start.6 = ((bf16[128,24,128]{2,1,0:T(8,128)(2,1)}), bf16[128,24,128]{2,1,0:T(8,128)(2,1)S(1)}, u32[]{:S(2)}, u32[]{:S(2)}) async-start(bf16[128,24,128]{2,1,0:T(8,128)(2,1)} %broadcast_in_dim.45), calls=%async_computation.6 | async-start | bytes 1572864 | tf_op jit(solution)/shard_map/all_to_all | solution.py:857
  456.9 3.1 collective-permute-start.36
  464.3 8.6 %collective-permute-done.50.refs_7_ = bf16[4,64,640]{2,1,0:T(8,128)(2,1)S(1)} collective-permute-done((bf16[4,64,640]{2,1,0:T(8,128)(2,1)}, bf16[4,64,640]{2,1,0:T(8,128)(2,1)S(1)}, u32[]{:S(2)}, u32[]{:S(2)}) %collective-permute-start.50) | collective-permute-done | bytes 327712 | tf_op jit(solution)/shard_map/ppermute | solution.py:868
  472.9 2.9 collective-permute-start.37
  476.7 11.3 %collective-permute-done.37.refs_2_ = bf16[4,64,640]{2,1,0:T(8,128)(2,1)S(1)} collective-permute-done((bf16[4,64,640]{2,1,0:T(8,128)(2,1)S(1)}, bf16[4,64,640]{2,1,0:T(8,128)(2,1)S(1)}, u32[]{:S(2)}, u32[]{:S(2)}) %collective-permute-start.37) | collective-permute-done | bytes 327712 | tf_op jit(solution)/shard_map/ppermute | solution.py:868
  487.9 8.6 %collective-permute-done.38.refs_3_ = bf16[4,64,640]{2,1,0:T(8,128)(2,1)S(1)} collective-permute-done((bf16[4,64,640]{2,1,0:T(8,128)(2,1)S(1)}, bf16[4,64,640]{2,1,0:T(8,128)(2,1)S(1)}, u32[]{:S(2)}, u32[]{:S(2)}) %collective-permute-start.38) | collective-permute-done | bytes 327712 | tf_op jit(solution)/shard_map/ppermute | solution.py:868
  497.3 4.3 place_weight_grads.1
  501.5 4.5 result.1
  506.1 4.1 convert_element_type.214
  510.2 3.6 input_grad.1
  (231 shorter events, 75.1 us)
Async XLA Ops:
  7.2 26.9 %copy-start = (s32[1,1024]{1,0:T(1,128)S(1)}, s32[1,1024]{1,0:T(1,128)}, u32[]{:S(2)}) copy-start(s32[1,1024]{1,0:T(1,128)} %param.32) | copy-start | bytes 12292
  7.2 32.2 %collective-permute-start.3 = (bf16[128,2048]{1,0:T(8,128)(2,1)}, bf16[128,2048]{1,0:T(8,128)(2,1)}, u32[]{:S(2)}, u32[]{:S(2)}) collective-permute-start(bf16[128,2048]{1,0:T(8,128)(2,1)} %x0.3), channel_id=1, source_target_pairs={{0,6},{1,7},{2,0},{3,1},{4,2},{5,3},{6,4},{7,5},{8,14},{9,15},{10,... | collective-permute-start | bytes 1572872 | tf_op jit(solution)/shard_map/ppermute | solution.py:844
  10.8 28.7 %collective-permute-start.5 = (bf16[128,2048]{1,0:T(8,128)(2,1)}, bf16[128,2048]{1,0:T(8,128)(2,1)}, u32[]{:S(2)}, u32[]{:S(2)}) collective-permute-start(bf16[128,2048]{1,0:T(8,128)(2,1)} %x0.3), channel_id=1, source_target_pairs={{0,4},{1,5},{2,6},{3,7},{4,0},{5,1},{6,2},{7,3},{8,12},{9,13},{10,... | collective-permute-start | bytes 1572872 | tf_op jit(solution)/shard_map/ppermute | solution.py:844
  11.2 28.7 %collective-permute-start.7 = (bf16[128,2048]{1,0:T(8,128)(2,1)}, bf16[128,2048]{1,0:T(8,128)(2,1)}, u32[]{:S(2)}, u32[]{:S(2)}) collective-permute-start(bf16[128,2048]{1,0:T(8,128)(2,1)} %x0.3), channel_id=1, source_target_pairs={{0,2},{1,3},{2,4},{3,5},{4,6},{5,7},{6,0},{7,1},{8,10},{9,11},{10,... | collective-permute-start | bytes 1572872 | tf_op jit(solution)/shard_map/ppermute | solution.py:844
  11.9 22.8 %collective-permute-start.1 = (bf16[64,2048]{1,0:T(8,128)(2,1)}, bf16[64,2048]{1,0:T(8,128)(2,1)S(1)}, u32[]{:S(2)}, u32[]{:S(2)}) collective-permute-start(bf16[64,2048]{1,0:T(8,128)(2,1)} %bitcast.123), channel_id=1, source_target_pairs={{0,1},{1,0},{2,3},{3,2},{4,5},{5,4},{6,7},{7,6},{8,9},{9,8},{10,11... | collective-permute-start | bytes 786440 | tf_op jit(solution)/shard_map/ppermute | solution.py:840
  16.3 61.9 %collective-permute-start.10 = (bf16[2048,512]{1,0:T(8,128)(2,1)S(1)}, bf16[2048,512]{1,0:T(8,128)(2,1)}, u32[]{:S(2)}, u32[]{:S(2)}) collective-permute-start(bf16[2048,512]{1,0:T(8,128)(2,1)S(1)} %bitcast.134), channel_id=1, source_target_pairs={{0,1},{1,0},{2,3},{3,2},{4,5},{5,4},{6,7},{7,6},{8,9},{9,8},{10,11... | collective-permute-start | bytes 6291464 | tf_op jit(solution)/shard_map/ppermute | solution.py:840
  23.7 105.9 %all-to-all-start.1 = ((bf16[128,88,128]{2,1,0:T(8,128)(2,1)}), bf16[128,88,128]{2,1,0:T(8,128)(2,1)}, u32[]{:S(2)}, u32[]{:S(2)}) async-start(bf16[128,88,128]{2,1,0:T(8,128)(2,1)} %pack_rows.1), calls=%async_computation.1 | async-start | bytes 5767168 | tf_op jit(solution)/shard_map/all_to_all | solution.py:857
  34.7 2.4 collective-permute-start.2
  37.1 9.2 %collective-permute-start = (bf16[128,2048]{1,0:T(8,128)(2,1)S(1)}, bf16[128,2048]{1,0:T(8,128)(2,1)}, u32[]{:S(2)}, u32[]{:S(2)}) collective-permute-start(bf16[128,2048]{1,0:T(8,128)(2,1)S(1)} %copy-done.4), channel_id=1, source_target_pairs={{0,1},{1,0},{2,3},{3,2},{4,5},{5,4},{6,7},{7,6},{8,9},{9,8},{10,11... | collective-permute-start | bytes 1572872 | tf_op jit(solution)/shard_map/ppermute | solution.py:840
  39.3 11.7 %collective-permute-start.4 = (bf16[128,2048]{1,0:T(8,128)(2,1)}, bf16[128,2048]{1,0:T(8,128)(2,1)}, u32[]{:S(2)}, u32[]{:S(2)}) collective-permute-start(bf16[128,2048]{1,0:T(8,128)(2,1)} %collective-permute-done.3.xa), channel_id=1, source_target_pairs={{0,1},{1,0},{2,3},{3,2},{4,5},{5,4},{6,7},{7,6},{8,9},{9,8},{10,11... | collective-permute-start | bytes 1572872 | tf_op jit(solution)/shard_map/ppermute | solution.py:840
  39.5 16.2 %collective-permute-start.6 = (bf16[128,2048]{1,0:T(8,128)(2,1)}, bf16[128,2048]{1,0:T(8,128)(2,1)}, u32[]{:S(2)}, u32[]{:S(2)}) collective-permute-start(bf16[128,2048]{1,0:T(8,128)(2,1)} %collective-permute-done.5.xa), channel_id=1, source_target_pairs={{0,1},{1,0},{2,3},{3,2},{4,5},{5,4},{6,7},{7,6},{8,9},{9,8},{10,11... | collective-permute-start | bytes 1572872 | tf_op jit(solution)/shard_map/ppermute | solution.py:840
  39.9 20.5 %collective-permute-start.8 = (bf16[128,2048]{1,0:T(8,128)(2,1)}, bf16[128,2048]{1,0:T(8,128)(2,1)}, u32[]{:S(2)}, u32[]{:S(2)}) collective-permute-start(bf16[128,2048]{1,0:T(8,128)(2,1)} %collective-permute-done.7.xa), channel_id=1, source_target_pairs={{0,1},{1,0},{2,3},{3,2},{4,5},{5,4},{6,7},{7,6},{8,9},{9,8},{10,11... | collective-permute-start | bytes 1572872 | tf_op jit(solution)/shard_map/ppermute | solution.py:840
  76.1 2.1 collective-permute-start.9
  85.0 34.1 %copy-start.13 = (bf16[256,2048]{1,0:T(8,128)(2,1)S(1)}, bf16[256,2048]{1,0:T(8,128)(2,1)}, u32[]{:S(2)}) copy-start(bf16[256,2048]{1,0:T(8,128)(2,1)} %get-tuple-element.140) | copy-start | bytes 3145732
  85.0 35.4 %copy-start.14 = (bf16[256,2048]{1,0:T(8,128)(2,1)S(1)}, bf16[256,2048]{1,0:T(8,128)(2,1)}, u32[]{:S(2)}) copy-start(bf16[256,2048]{1,0:T(8,128)(2,1)} %get-tuple-element.141) | copy-start | bytes 3145732
  85.0 15.2 %collective-permute-start.11 = (bf16[2048,128]{1,0:T(8,128)(2,1)}, bf16[2048,128]{1,0:T(8,128)(2,1)S(1)}, u32[]{:S(2)}, u32[]{:S(2)}) collective-permute-start(bf16[2048,128]{1,0:T(8,128)(2,1)} %get-tuple-element.131), channel_id=1, source_target_pairs={{0,2},{1,3},{2,4},{3,5},{4,6},{5,7},{6,0},{7,1},{8,10},{9,11},{10,... | collective-permute-start | bytes 1572872 | tf_op jit(solution)/shard_map/ppermute | solution.py:848
  85.7 24.8 %collective-permute-start.12 = (bf16[2048,128]{1,0:T(8,128)(2,1)}, bf16[2048,128]{1,0:T(8,128)(2,1)S(1)}, u32[]{:S(2)}, u32[]{:S(2)}) collective-permute-start(bf16[2048,128]{1,0:T(8,128)(2,1)} %get-tuple-element.132), channel_id=1, source_target_pairs={{0,6},{1,7},{2,0},{3,1},{4,2},{5,3},{6,4},{7,5},{8,14},{9,15},{10,... | collective-permute-start | bytes 1572872 | tf_op jit(solution)/shard_map/ppermute | solution.py:848
  88.1 24.5 %collective-permute-start.13 = (bf16[2048,128]{1,0:T(8,128)(2,1)}, bf16[2048,128]{1,0:T(8,128)(2,1)S(1)}, u32[]{:S(2)}, u32[]{:S(2)}) collective-permute-start(bf16[2048,128]{1,0:T(8,128)(2,1)} %get-tuple-element.133), channel_id=1, source_target_pairs={{0,4},{1,5},{2,6},{3,7},{4,0},{5,1},{6,2},{7,3},{8,12},{9,13},{10,... | collective-permute-start | bytes 1572872 | tf_op jit(solution)/shard_map/ppermute | solution.py:848
  129.6 58.9 %all-to-all-start = ((bf16[128,88,128]{2,1,0:T(8,128)(2,1)}), bf16[128,88,128]{2,1,0:T(8,128)(2,1)}, u32[]{:S(2)}, u32[]{:S(2)}) async-start(bf16[128,88,128]{2,1,0:T(8,128)(2,1)} %get-tuple-element.135), calls=%async_computation | async-start | bytes 5767168 | tf_op jit(solution)/shard_map/all_to_all | solution.py:857
  207.1 43.9 %all-to-all-start.2 = ((bf16[128,88,128]{2,1,0:T(8,128)(2,1)}), bf16[128,88,128]{2,1,0:T(8,128)(2,1)S(1)}, u32[]{:S(2)}, u32[]{:S(2)}) async-start(bf16[128,88,128]{2,1,0:T(8,128)(2,1)} %get-tuple-element.165), calls=%async_computation.2 | async-start | bytes 5767168 | tf_op jit(solution)/shard_map/all_to_all | solution.py:857
  259.8 12.8 %collective-permute-start.15 = (bf16[128,2048]{1,0:T(8,128)(2,1)}, bf16[128,2048]{1,0:T(8,128)(2,1)S(1)}, u32[]{:S(2)}, u32[]{:S(2)}) collective-permute-start(bf16[128,2048]{1,0:T(8,128)(2,1)} %get-tuple-element.181.refs_0_), channel_id=1, source_target_pairs={{0,6},{1,7},{2,0},{3,1},{4,2},{5,3},{6,4},{7,5},{8,14},{9,15},{10,... | collective-permute-start | bytes 1572872 | tf_op jit(solution)/shard_map/ppermute | solution.py:844
  259.8 15.9 %collective-permute-start.16 = (bf16[128,2048]{1,0:T(8,128)(2,1)}, bf16[128,2048]{1,0:T(8,128)(2,1)S(1)}, u32[]{:S(2)}, u32[]{:S(2)}) collective-permute-start(bf16[128,2048]{1,0:T(8,128)(2,1)} %get-tuple-element.181.refs_0_), channel_id=1, source_target_pairs={{0,4},{1,5},{2,6},{3,7},{4,0},{5,1},{6,2},{7,3},{8,12},{9,13},{10,... | collective-permute-start | bytes 1572872 | tf_op jit(solution)/shard_map/ppermute | solution.py:844
  261.1 25.5 %collective-permute-start.17 = (bf16[128,2048]{1,0:T(8,128)(2,1)}, bf16[128,2048]{1,0:T(8,128)(2,1)S(1)}, u32[]{:S(2)}, u32[]{:S(2)}) collective-permute-start(bf16[128,2048]{1,0:T(8,128)(2,1)} %get-tuple-element.181.refs_0_), channel_id=1, source_target_pairs={{0,2},{1,3},{2,4},{3,5},{4,6},{5,7},{6,0},{7,1},{8,10},{9,11},{10,... | collective-permute-start | bytes 1572872 | tf_op jit(solution)/shard_map/ppermute | solution.py:844
  261.3 26.3 %collective-permute-start.18 = (bf16[128,2048]{1,0:T(8,128)(2,1)}, bf16[128,2048]{1,0:T(8,128)(2,1)S(1)}, u32[]{:S(2)}, u32[]{:S(2)}) collective-permute-start(bf16[128,2048]{1,0:T(8,128)(2,1)} %get-tuple-element.181.refs_0_), channel_id=1, source_target_pairs={{0,1},{1,0},{2,3},{3,2},{4,5},{5,4},{6,7},{7,6},{8,9},{9,8},{10,11... | collective-permute-start | bytes 1572872 | tf_op jit(solution)/shard_map/ppermute | solution.py:840
  272.6 15.0 %collective-permute-start.19 = (bf16[128,2048]{1,0:T(8,128)(2,1)S(1)}, bf16[128,2048]{1,0:T(8,128)(2,1)S(1)}, u32[]{:S(2)}, u32[]{:S(2)}) collective-permute-start(bf16[128,2048]{1,0:T(8,128)(2,1)S(1)} %collective-permute-done.15.refs_1_), channel_id=1, source_target_pairs={{0,1},{1,0},{2,3},{3,2},{4,5},{5,4},{6,7},{7,6},{8,9},{9,8},{10,11... | collective-permute-start | bytes 1572872 | tf_op jit(solution)/shard_map/ppermute | solution.py:840
  275.7 11.9 %collective-permute-start.20 = (bf16[128,2048]{1,0:T(8,128)(2,1)S(1)}, bf16[128,2048]{1,0:T(8,128)(2,1)S(1)}, u32[]{:S(2)}, u32[]{:S(2)}) collective-permute-start(bf16[128,2048]{1,0:T(8,128)(2,1)S(1)} %collective-permute-done.16.refs_2_), channel_id=1, source_target_pairs={{0,1},{1,0},{2,3},{3,2},{4,5},{5,4},{6,7},{7,6},{8,9},{9,8},{10,11... | collective-permute-start | bytes 1572872 | tf_op jit(solution)/shard_map/ppermute | solution.py:840
  286.7 2.0 collective-permute-start.21
  287.2 46.1 %collective-permute-start.14 = (bf16[2048,512]{1,0:T(8,128)(2,1)}, bf16[2048,512]{1,0:T(8,128)(2,1)S(1)}, u32[]{:S(2)}, u32[]{:S(2)}) collective-permute-start(bf16[2048,512]{1,0:T(8,128)(2,1)} %wa.1), channel_id=1, source_target_pairs={{0,1},{1,0},{2,3},{3,2},{4,5},{5,4},{6,7},{7,6},{8,9},{9,8},{10,11... | collective-permute-start | bytes 6291464 | tf_op jit(solution)/shard_map/ppermute | solution.py:840
  317.7 7.1 %collective-permute-start.23 = (bf16[256,1024]{1,0:T(8,128)(2,1)}, bf16[256,1024]{1,0:T(8,128)(2,1)}, u32[]{:S(2)}, u32[]{:S(2)}) collective-permute-start(bf16[256,1024]{1,0:T(8,128)(2,1)} %get-tuple-element.187.own), channel_id=1, source_target_pairs={{0,1},{1,0},{2,3},{3,2},{4,5},{5,4},{6,7},{7,6},{8,9},{9,8},{10,11... | collective-permute-start | bytes 1572872 | tf_op jit(solution)/shard_map/ppermute | solution.py:840
  318.2 25.5 %all-to-all-start.4 = ((bf16[128,16,128]{2,1,0:T(8,128)(2,1)}), bf16[128,16,128]{2,1,0:T(8,128)(2,1)S(1)}, u32[]{:S(2)}, u32[]{:S(2)}) async-start(bf16[128,16,128]{2,1,0:T(8,128)(2,1)} %bitcast.29), calls=%async_computation.4 | async-start | bytes 1048576 | tf_op jit(solution)/shard_map/all_to_all | solution.py:857
  322.0 11.2 %collective-permute-start.22 = (bf16[512,512]{1,0:T(8,128)(2,1)}, bf16[512,512]{1,0:T(8,128)(2,1)S(1)}, u32[]{:S(2)}, u32[]{:S(2)}) collective-permute-start(bf16[512,512]{1,0:T(8,128)(2,1)} %get-tuple-element.185.dq1), channel_id=1, source_target_pairs={{0,1},{1,0},{2,3},{3,2},{4,5},{5,4},{6,7},{7,6},{8,9},{9,8},{10,11... | collective-permute-start | bytes 1572872 | tf_op jit(solution)/shard_map/ppermute | solution.py:840
  343.7 18.4 %all-to-all-start.5 = ((f32[128,1,128]{2,1,0:T(1,128)}), f32[128,1,128]{2,1,0:T(1,128)S(1)}, u32[]{:S(2)}, u32[]{:S(2)}) async-start(f32[128,1,128]{2,1,0:T(1,128)} %bitcast.35), calls=%async_computation.5 | async-start | bytes 131072 | tf_op jit(solution)/shard_map/all_to_all | solution.py:857
  362.0 79.5 %all-to-all-start.3 = ((bf16[128,80,128]{2,1,0:T(8,128)(2,1)}), bf16[128,80,128]{2,1,0:T(8,128)(2,1)S(1)}, u32[]{:S(2)}, u32[]{:S(2)}) async-start(bf16[128,80,128]{2,1,0:T(8,128)(2,1)} %expert_out.1), calls=%async_computation.3 | async-start | bytes 5242880 | tf_op jit(solution)/shard_map/all_to_all | solution.py:857
  366.5 139.6 %all-reduce.3.cloned.1.call-start = ((), (), s32[]{:S(2)}) async-start(), calls=%async_computation.7 | async-start | bytes 4194304 | tf_op jit(solution)/shard_map/psum | solution.py:989
  369.3 40.4 %collective-permute-start.39 = (bf16[4,64,640]{2,1,0:T(8,128)(2,1)}, bf16[4,64,640]{2,1,0:T(8,128)(2,1)}, u32[]{:S(2)}, u32[]{:S(2)}) collective-permute-start(bf16[4,64,640]{2,1,0:T(8,128)(2,1)} %get-tuple-element.216), channel_id=1, source_target_pairs={{0,8},{8,16},{16,24},{24,0},{32,40},{40,48},{48,56},{56,32},{64,72... | collective-permute-start | bytes 983048 | tf_op jit(solution)/shard_map/ppermute | solution.py:868
  370.7 44.2 %collective-permute-start.40 = (bf16[4,64,640]{2,1,0:T(8,128)(2,1)}, bf16[4,64,640]{2,1,0:T(8,128)(2,1)}, u32[]{:S(2)}, u32[]{:S(2)}) collective-permute-start(bf16[4,64,640]{2,1,0:T(8,128)(2,1)} %get-tuple-element.218), channel_id=1, source_target_pairs={{0,24},{8,0},{16,8},{24,16},{32,56},{40,32},{48,40},{56,48},{64,88... | collective-permute-start | bytes 983048 | tf_op jit(solution)/shard_map/ppermute | solution.py:868
  372.0 48.1 %collective-permute-start.41 = (bf16[4,64,640]{2,1,0:T(8,128)(2,1)}, bf16[4,64,640]{2,1,0:T(8,128)(2,1)}, u32[]{:S(2)}, u32[]{:S(2)}) collective-permute-start(bf16[4,64,640]{2,1,0:T(8,128)(2,1)} %get-tuple-element.217), channel_id=1, source_target_pairs={{0,16},{8,24},{16,0},{24,8},{32,48},{40,56},{48,32},{56,40},{64,80... | collective-permute-start | bytes 983048 | tf_op jit(solution)/shard_map/ppermute | solution.py:868
  375.8 49.0 %collective-permute-start.27 = (bf16[4,64,640]{2,1,0:T(8,128)(2,1)}, bf16[4,64,640]{2,1,0:T(8,128)(2,1)S(1)}, u32[]{:S(2)}, u32[]{:S(2)}) collective-permute-start(bf16[4,64,640]{2,1,0:T(8,128)(2,1)} %get-tuple-element.219), channel_id=1, source_target_pairs={{0,32},{8,40},{16,48},{24,56},{32,64},{40,72},{48,80},{56,88},{64,... | collective-permute-start | bytes 983048 | tf_op jit(solution)/shard_map/ppermute | solution.py:868
  377.2 49.1 %collective-permute-start.28 = (bf16[4,64,640]{2,1,0:T(8,128)(2,1)}, bf16[4,64,640]{2,1,0:T(8,128)(2,1)S(1)}, u32[]{:S(2)}, u32[]{:S(2)}) collective-permute-start(bf16[4,64,640]{2,1,0:T(8,128)(2,1)} %get-tuple-element.221), channel_id=1, source_target_pairs={{0,96},{8,104},{16,112},{24,120},{32,0},{40,8},{48,16},{56,24},{64... | collective-permute-start | bytes 983048 | tf_op jit(solution)/shard_map/ppermute | solution.py:868
  409.7 16.5 %collective-permute-start.29 = (bf16[4,64,640]{2,1,0:T(8,128)(2,1)}, bf16[4,64,640]{2,1,0:T(8,128)(2,1)S(1)}, u32[]{:S(2)}, u32[]{:S(2)}) collective-permute-start(bf16[4,64,640]{2,1,0:T(8,128)(2,1)} %get-tuple-element.220), channel_id=1, source_target_pairs={{0,64},{8,72},{16,80},{24,88},{32,96},{40,104},{48,112},{56,120},{... | collective-permute-start | bytes 983048 | tf_op jit(solution)/shard_map/ppermute | solution.py:868
  421.6 8.6 %collective-permute-start.42 = (bf16[64,640]{1,0:T(8,128)(2,1)S(1)}, bf16[64,640]{1,0:T(8,128)(2,1)S(1)}, u32[]{:S(2)}, u32[]{:S(2)}) collective-permute-start(bf16[64,640]{1,0:T(8,128)(2,1)S(1)} %get-tuple-element.222), channel_id=1, source_target_pairs={{0,32},{8,40},{16,48},{24,56},{32,64},{40,72},{48,80},{56,88},{64,... | collective-permute-start | bytes 245768 | tf_op jit(solution)/shard_map/ppermute | solution.py:868
  423.0 7.2 %collective-permute-start.43 = (bf16[64,640]{1,0:T(8,128)(2,1)S(1)}, bf16[64,640]{1,0:T(8,128)(2,1)S(1)}, u32[]{:S(2)}, u32[]{:S(2)}) collective-permute-start(bf16[64,640]{1,0:T(8,128)(2,1)S(1)} %get-tuple-element.224), channel_id=1, source_target_pairs={{0,96},{8,104},{16,112},{24,120},{32,0},{40,8},{48,16},{56,24},{64... | collective-permute-start | bytes 245768 | tf_op jit(solution)/shard_map/ppermute | solution.py:868
  424.8 5.4 %collective-permute-start.44 = (bf16[64,640]{1,0:T(8,128)(2,1)S(1)}, bf16[64,640]{1,0:T(8,128)(2,1)S(1)}, u32[]{:S(2)}, u32[]{:S(2)}) collective-permute-start(bf16[64,640]{1,0:T(8,128)(2,1)S(1)} %get-tuple-element.223), channel_id=1, source_target_pairs={{0,64},{8,72},{16,80},{24,88},{32,96},{40,104},{48,112},{56,120},{... | collective-permute-start | bytes 245768 | tf_op jit(solution)/shard_map/ppermute | solution.py:868
  427.5 5.2 collective-permute-start.30
  427.8 5.0 collective-permute-start.31
  430.2 5.1 collective-permute-start.32
  430.3 6.7 %collective-permute-start.45 = (bf16[64,640]{1,0:T(8,128)(2,1)S(1)}, bf16[64,640]{1,0:T(8,128)(2,1)S(1)}, u32[]{:S(2)}, u32[]{:S(2)}) collective-permute-start(bf16[64,640]{1,0:T(8,128)(2,1)S(1)} %fusion.8), channel_id=1, source_target_pairs={{0,96},{8,104},{16,112},{24,120},{32,0},{40,8},{48,16},{56,24},{64... | collective-permute-start | bytes 245768 | tf_op jit(solution)/shard_map/ppermute | solution.py:868
  431.7 5.6 %collective-permute-start.46 = (bf16[64,640]{1,0:T(8,128)(2,1)S(1)}, bf16[64,640]{1,0:T(8,128)(2,1)S(1)}, u32[]{:S(2)}, u32[]{:S(2)}) collective-permute-start(bf16[64,640]{1,0:T(8,128)(2,1)S(1)} %fusion.8), channel_id=1, source_target_pairs={{0,64},{8,72},{16,80},{24,88},{32,96},{40,104},{48,112},{56,120},{... | collective-permute-start | bytes 245768 | tf_op jit(solution)/shard_map/ppermute | solution.py:868
  432.7 4.9 collective-permute-start.47
  435.4 18.8 %collective-permute-start.33 = (bf16[64,640]{1,0:T(8,128)(2,1)S(1)}, bf16[64,640]{1,0:T(8,128)(2,1)}, u32[]{:S(2)}, u32[]{:S(2)}) collective-permute-start(bf16[64,640]{1,0:T(8,128)(2,1)S(1)} %fusion.11), channel_id=1, source_target_pairs={{0,24},{8,0},{16,8},{24,16},{32,56},{40,32},{48,40},{56,48},{64,88... | collective-permute-start | bytes 245768 | tf_op jit(solution)/shard_map/ppermute | solution.py:868
  436.3 19.5 %collective-permute-start.34 = (bf16[64,640]{1,0:T(8,128)(2,1)S(1)}, bf16[64,640]{1,0:T(8,128)(2,1)}, u32[]{:S(2)}, u32[]{:S(2)}) collective-permute-start(bf16[64,640]{1,0:T(8,128)(2,1)S(1)} %fusion.11), channel_id=1, source_target_pairs={{0,16},{8,24},{16,0},{24,8},{32,48},{40,56},{48,32},{56,40},{64,80... | collective-permute-start | bytes 245768 | tf_op jit(solution)/shard_map/ppermute | solution.py:868
  436.9 18.9 %collective-permute-start.35 = (bf16[64,640]{1,0:T(8,128)(2,1)S(1)}, bf16[64,640]{1,0:T(8,128)(2,1)}, u32[]{:S(2)}, u32[]{:S(2)}) collective-permute-start(bf16[64,640]{1,0:T(8,128)(2,1)S(1)} %fusion.11), channel_id=1, source_target_pairs={{0,8},{8,16},{16,24},{24,0},{32,40},{40,48},{48,56},{56,32},{64,72... | collective-permute-start | bytes 245768 | tf_op jit(solution)/shard_map/ppermute | solution.py:868
  438.4 22.8 %collective-permute-start.48 = (bf16[4,64,640]{2,1,0:T(8,128)(2,1)}, bf16[4,64,640]{2,1,0:T(8,128)(2,1)}, u32[]{:S(2)}, u32[]{:S(2)}) collective-permute-start(bf16[4,64,640]{2,1,0:T(8,128)(2,1)} %pad_maximum_fusion.1.refs_4_), channel_id=1, source_target_pairs={{0,24},{8,0},{16,8},{24,16},{32,56},{40,32},{48,40},{56,48},{64,88... | collective-permute-start | bytes 983048 | tf_op jit(solution)/shard_map/ppermute | solution.py:868
  440.4 22.3 %collective-permute-start.49 = (bf16[4,64,640]{2,1,0:T(8,128)(2,1)}, bf16[4,64,640]{2,1,0:T(8,128)(2,1)}, u32[]{:S(2)}, u32[]{:S(2)}) collective-permute-start(bf16[4,64,640]{2,1,0:T(8,128)(2,1)} %pad_maximum_fusion.1.refs_4_), channel_id=1, source_target_pairs={{0,16},{8,24},{16,0},{24,8},{32,48},{40,56},{48,32},{56,40},{64,80... | collective-permute-start | bytes 983048 | tf_op jit(solution)/shard_map/ppermute | solution.py:868
  441.6 60.0 %copy-start.3 = (bf16[128,80,128]{2,1,0:T(8,128)(2,1)}, bf16[128,80,128]{2,1,0:T(8,128)(2,1)S(1)}, u32[]{:S(2)}) copy-start(bf16[128,80,128]{2,1,0:T(8,128)(2,1)S(1)} %all-to-all-done.3.wire) | copy-start | bytes 7864324
  442.8 71.1 %all-to-all-start.6 = ((bf16[128,24,128]{2,1,0:T(8,128)(2,1)}), bf16[128,24,128]{2,1,0:T(8,128)(2,1)S(1)}, u32[]{:S(2)}, u32[]{:S(2)}) async-start(bf16[128,24,128]{2,1,0:T(8,128)(2,1)} %broadcast_in_dim.45), calls=%async_computation.6 | async-start | bytes 1572864 | tf_op jit(solution)/shard_map/all_to_all | solution.py:857
  454.2 18.8 %collective-permute-start.50 = (bf16[4,64,640]{2,1,0:T(8,128)(2,1)}, bf16[4,64,640]{2,1,0:T(8,128)(2,1)S(1)}, u32[]{:S(2)}, u32[]{:S(2)}) collective-permute-start(bf16[4,64,640]{2,1,0:T(8,128)(2,1)} %pad_maximum_fusion.1.refs_4_), channel_id=1, source_target_pairs={{0,8},{8,16},{16,24},{24,0},{32,40},{40,48},{48,56},{56,32},{64,72... | collective-permute-start | bytes 983048 | tf_op jit(solution)/shard_map/ppermute | solution.py:868
  456.9 39.7 %copy-start.11 = (bf16[4,64,640]{2,1,0:T(8,128)(2,1)}, bf16[4,64,640]{2,1,0:T(8,128)(2,1)S(1)}, u32[]{:S(2)}) copy-start(bf16[4,64,640]{2,1,0:T(8,128)(2,1)S(1)} %pad_maximum_fusion.refs_0_) | copy-start | bytes 983044
  456.9 18.9 %collective-permute-start.36 = (bf16[4,64,640]{2,1,0:T(8,128)(2,1)S(1)}, bf16[4,64,640]{2,1,0:T(8,128)(2,1)S(1)}, u32[]{:S(2)}, u32[]{:S(2)}) collective-permute-start(bf16[4,64,640]{2,1,0:T(8,128)(2,1)S(1)} %pad_maximum_fusion.refs_0_), channel_id=1, source_target_pairs={{0,96},{8,104},{16,112},{24,120},{32,0},{40,8},{48,16},{56,24},{64... | collective-permute-start | bytes 983048 | tf_op jit(solution)/shard_map/ppermute | solution.py:868
  460.0 50.2 %collective-permute-start.24 = (bf16[2048,128]{1,0:T(8,128)(2,1)}, bf16[2048,128]{1,0:T(8,128)(2,1)}, u32[]{:S(2)}, u32[]{:S(2)}) collective-permute-start(bf16[2048,128]{1,0:T(8,128)(2,1)} %get-tuple-element.198), channel_id=1, source_target_pairs={{0,2},{1,3},{2,4},{3,5},{4,6},{5,7},{6,0},{7,1},{8,10},{9,11},{10,... | collective-permute-start | bytes 1572872 | tf_op jit(solution)/shard_map/ppermute | solution.py:848
  461.3 48.9 %collective-permute-start.25 = (bf16[2048,128]{1,0:T(8,128)(2,1)}, bf16[2048,128]{1,0:T(8,128)(2,1)}, u32[]{:S(2)}, u32[]{:S(2)}) collective-permute-start(bf16[2048,128]{1,0:T(8,128)(2,1)} %get-tuple-element.199), channel_id=1, source_target_pairs={{0,6},{1,7},{2,0},{3,1},{4,2},{5,3},{6,4},{7,5},{8,14},{9,15},{10,... | collective-permute-start | bytes 1572872 | tf_op jit(solution)/shard_map/ppermute | solution.py:848
  462.7 47.5 %collective-permute-start.26 = (bf16[2048,128]{1,0:T(8,128)(2,1)}, bf16[2048,128]{1,0:T(8,128)(2,1)}, u32[]{:S(2)}, u32[]{:S(2)}) collective-permute-start(bf16[2048,128]{1,0:T(8,128)(2,1)} %get-tuple-element.200), channel_id=1, source_target_pairs={{0,4},{1,5},{2,6},{3,7},{4,0},{5,1},{6,2},{7,3},{8,12},{9,13},{10,... | collective-permute-start | bytes 1572872 | tf_op jit(solution)/shard_map/ppermute | solution.py:848
  472.9 15.0 %collective-permute-start.37 = (bf16[4,64,640]{2,1,0:T(8,128)(2,1)S(1)}, bf16[4,64,640]{2,1,0:T(8,128)(2,1)S(1)}, u32[]{:S(2)}, u32[]{:S(2)}) collective-permute-start(bf16[4,64,640]{2,1,0:T(8,128)(2,1)S(1)} %pad_maximum_fusion.refs_0_), channel_id=1, source_target_pairs={{0,64},{8,72},{16,80},{24,88},{32,96},{40,104},{48,112},{56,120},{... | collective-permute-start | bytes 983048 | tf_op jit(solution)/shard_map/ppermute | solution.py:868
  475.8 20.7 %collective-permute-start.38 = (bf16[4,64,640]{2,1,0:T(8,128)(2,1)S(1)}, bf16[4,64,640]{2,1,0:T(8,128)(2,1)S(1)}, u32[]{:S(2)}, u32[]{:S(2)}) collective-permute-start(bf16[4,64,640]{2,1,0:T(8,128)(2,1)S(1)} %pad_maximum_fusion.refs_0_), channel_id=1, source_target_pairs={{0,32},{8,40},{16,48},{24,56},{32,64},{40,72},{48,80},{56,88},{64,... | collective-permute-start | bytes 983048 | tf_op jit(solution)/shard_map/ppermute | solution.py:868
  (37 other events, 275.5 us)
Sparse Core Ops, SparseCore 0:
  370.6 124.1 all-reduce.2

commit v3 on v2

--- a/solution.py
+++ b/solution.py
@@ -25,6 +25,36 @@
 bf16 = jnp.bfloat16
 f32 = jnp.float32
 ALL = ("expert", "shard")
+COSTS = {
+    "qkv0": 4,
+    "qkv1": 4,
+    "qkv2": 4,
+    "qkv3": 4,
+    "pack_rows": 4,
+    "route_tables": 2,
+    "attend": 11,
+    "out_projection": 5,
+    "router": 6,
+    "transpose_rows": 6,
+    "expert_grad_rows": 8,
+    "expert_main": 18,
+    "expert_out": 7,
+    "combine_grads": 7,
+    "head_grad": 4,
+    "out_projection_grad": 7,
+    "attend_grad": 19,
+    "qkv_weight_grad": 8,
+    "normed_grad": 7,
+    "result": 4,
+    "input_grad": 3,
+    "place_weight_grads": 4,
+}
+
+
+def cost(micros):
+    return pl.CostEstimate(
+        flops=1, bytes_accessed=int(micros * 0.6e6) + 1, transcendentals=0
+    )
 
 
 def dot(a, b):
@@ -35,14 +65,11 @@
     return lax.dot_general(a, b, (((1,), (1,)), ((), ())), preferred_element_type=f32)
 
 
-def call(kernel, name, outs, scratch, args, flops=0, smem=()):
+def call(kernel, name, outs, scratch, args, smem=()):
     in_specs = [
         pl.BlockSpec(memory_space=pltpu.SMEM if i in smem else pltpu.VMEM)
         for i in range(len(args))
     ]
-    bytes_accessed = sum(a.size * a.dtype.itemsize for a in args) + sum(
-        s.size * s.dtype.itemsize for s in outs
-    )
     return pl.pallas_call(
         kernel,
         out_shape=outs,
@@ -50,17 +77,12 @@
         out_specs=[pl.BlockSpec(memory_space=pltpu.VMEM) for _ in outs],
         scratch_shapes=scratch,
         compiler_params=pltpu.CompilerParams(vmem_limit_bytes=56 * 1024 * 1024),
-        cost_estimate=pl.CostEstimate(
-            flops=flops, bytes_accessed=bytes_accessed, transcendentals=0
-        ),
+        cost_estimate=cost(COSTS.get(name, 0)),
         name=name,
     )(*args)
 
 
-def grid_call(kernel, name, grid, in_specs, out_specs, outs, scratch, args, flops=0, scalars=0):
-    bytes_accessed = sum(a.size * a.dtype.itemsize for a in args) + sum(
-        s.size * s.dtype.itemsize for s in outs
-    )
+def grid_call(kernel, name, grid, in_specs, out_specs, outs, scratch, args, scalars=0):
     return pl.pallas_call(
         kernel,
         out_shape=outs,
@@ -74,9 +96,7 @@
         compiler_params=pltpu.CompilerParams(
             vmem_limit_bytes=56 * 1024 * 1024, dimension_semantics=("arbitrary",)
         ),
-        cost_estimate=pl.CostEstimate(
-            flops=flops, bytes_accessed=bytes_accessed, transcendentals=0
-        ),
+        cost_estimate=cost(COSTS.get(name, 0)),
         name=name,
     )(*args)
 
@@ -159,7 +179,6 @@
         [sds((E, WIRE, 128), bf16)],
         [pltpu.VMEM((SLOTS, D), bf16)],
         (x, assign_t),
-        flops=2 * SLOTS * T * D,
     )[0]
 
 
@@ -185,7 +204,7 @@
 
 def qkv_body(
     piece, core, xa, xb, g1, wqt, wk, wks, wv, wvs, gq, gk, cos, sin,
-    qraw, qt, kraw, kt, vt, n1, wkv,
+    qn, qt, kn, kt, vt, scale, n1, wkv,
 ):
     lower = core[0] == 0
     wkv[0:64, :] = jnp.where(lower, wk[...], wks[...])
@@ -203,22 +222,26 @@
     c = jnp.concatenate([cos[:, first : first + T], cos[:, second : second + T]], axis=1)
     s = jnp.concatenate([sin[:, first : first + T], sin[:, second : second + T]], axis=1)
 
-    def path(v, gain, factor):
-        v = v * lax.rsqrt(jnp.mean(v * v, axis=0, keepdims=True) + EPS) * gain
+    def path(v, gain, factor, keep, index):
+        r = lax.rsqrt(jnp.mean(v * v, axis=0, keepdims=True) + EPS)
+        scale[index : index + 1, :] = r
+        v = v * r
+        keep[...] = v.astype(bf16)
+        v = v * gain
         low, high = v[:64], v[64:]
         return (
             ((low * c - high * s) * factor).astype(bf16),
             ((high * c + low * s) * factor).astype(bf16),
         )
 
-    qraw[...] = raw
+    scale[...] = jnp.zeros_like(scale)
     for h in range(LH):
-        low, high = path(raw[h * HEAD : (h + 1) * HEAD], gain_q, HEAD ** (-0.5))
+        heads = slice(h * HEAD, (h + 1) * HEAD)
+        low, high = path(raw[heads], gain_q, HEAD ** (-0.5), qn.at[heads, :], h)
         qt[h * HEAD : h * HEAD + 64, :] = low
         qt[h * HEAD + 64 : (h + 1) * HEAD, :] = high
     key = raw_kv[:HEAD].astype(bf16)
-    kraw[...] = key
-    low, high = path(key.astype(f32), gain_k, 1.0)
+    low, high = path(key.astype(f32), gain_k, 1.0, kn, LH)
     kt[:64, :] = low
     kt[64:, :] = high
     vt[...] = raw_kv[HEAD:].astype(bf16)
@@ -229,17 +252,17 @@
         functools.partial(qkv_body, piece),
         f"qkv{piece}",
         [
-            sds((LH * HEAD, 2 * T), f32),
+            sds((LH * HEAD, 2 * T), bf16),
             sds((LH * HEAD, 2 * T), bf16),
             sds((HEAD, 2 * T), bf16),
             sds((HEAD, 2 * T), bf16),
             sds((HEAD, 2 * T), bf16),
+            sds((8, 2 * T), f32),
             sds((2 * T, D), bf16),
-            sds((2 * HEAD, D), bf16),
-        ],
-        [],
+        ]
+        + ([sds((2 * HEAD, D), bf16)] if piece == 0 else []),
+        [] if piece == 0 else [pltpu.VMEM((2 * HEAD, D), bf16)],
         args,
-        flops=2 * 2 * T * D * 768,
         smem=(0,),
     )
 
@@ -300,14 +323,27 @@
         ],
         [pltpu.VMEM((ROWS, ROWS), f32), pltpu.VMEM((HEAD, ROWS), bf16)],
         (*q, *k, *v, info),
-        flops=4 * LH * ROWS * ROWS * HEAD,
-    )
-
-
-def outproj_body(ot0, otr, wa, wb, b0, b1, b2, b3):
-    total = dot(wa[...], ot0[...]) + dot(wb[...], otr[...])
+    )
+
+
+def flip(source, dest, row, col):
+    height, width = source.shape
+    for a in range(height // 128):
+        for b in range(width // 128):
+            block = source[a * 128 : (a + 1) * 128, b * 128 : (b + 1) * 128]
+            rows = slice(row + b * 128, row + (b + 1) * 128)
+            dest[rows, col + a * 128 : col + (a + 1) * 128] = block.astype(f32).T.astype(bf16)
+
+
+def outproj_body(ot0, otr, wa, wb, b0, b1, b2, b3, heads):
+    @pl.when(pl.program_id(0) == 0)
+    def _():
+        flip(ot0, heads, 0, 0)
+        flip(otr, heads, 0, 512)
+
+    total = dot(heads[:, :512], wa[...]) + dot(heads[:, 512:], wb[...])
     for dy, out in enumerate((b0, b1, b2, b3)):
-        out[...] = total[:, dy * T : (dy + 1) * T].astype(bf16)
+        out[...] = total[dy * T : (dy + 1) * T, :].astype(bf16)
 
 
 def outproj(ot0, otr, wa, wb):
@@ -315,13 +351,22 @@
         outproj_body,
         "out_projection",
         (4,),
-        [whole((512, HALF)), whole((512, HALF)), rows_of((512, 512)), rows_of((512, 512))],
-        [rows_of((512, T))] * 4,
-        [sds((D, T), bf16)] * 4,
-        [],
+        [whole((512, HALF)), whole((512, HALF)), cols_of((512, 512)), cols_of((512, 512))],
+        [cols_of((T, 512))] * 4,
+        [sds((T, D), bf16)] * 4,
+        [pltpu.VMEM((HALF, 1024), bf16)],
         (ot0, otr, wa, wb),
-        flops=2 * D * 1024 * HALF,
-    )
+    )
+
+
+def transpose_body(n0, n1, n2, n3, out):
+    for dy, piece in enumerate((n0, n1, n2, n3)):
+        for dc in range(2):
+            flip(piece.at[dc * T : (dc + 1) * T, :], out, 0, dc * HALF + dy * T)
+
+
+def transpose_rows(pieces):
+    return call(transpose_body, "transpose_rows", [sds((D, ROWS), bf16)], [], tuple(pieces))[0]
 
 
 def route_body(rt, ids, ids_t):
@@ -347,21 +392,15 @@
         [sds((T, 128), jnp.int32), sds((16, T), jnp.int32)],
         [],
         (routes_t,),
-        flops=2 * T * T * E,
     )
 
 
 def router_body(b0, b1, b2, b3, x0, g2, wr, ids, at, hidden, n2, probs, gates, wire, rows):
-    for j in range(SEG):
-        part = slice(j * 128, (j + 1) * 128)
-        total = (
-            b0[part, :].astype(f32)
-            + b1[part, :].astype(f32)
-            + b2[part, :].astype(f32)
-            + b3[part, :].astype(f32)
-        )
-        hidden[:, part] = x0[:, part].astype(f32) + total.T
-    v = hidden[...]
+    v = x0[...].astype(f32) + (
+        (b0[...].astype(f32) + b1[...].astype(f32))
+        + (b2[...].astype(f32) + b3[...].astype(f32))
+    )
+    hidden[...] = v
     r = lax.rsqrt(jnp.mean(v * v, axis=-1, keepdims=True) + EPS)
     n2[...] = (v * r * g2[...]).astype(bf16)
     logits = dot(n2[...], wr[...])
@@ -403,7 +442,6 @@
         ],
         [pltpu.VMEM((SLOTS, D), bf16)],
         (*b, x0, g2, wr, ids, assign_t),
-        flops=2 * SLOTS * T * D,
     )
 
 
@@ -425,7 +463,6 @@
         [sds((SLOTS, D), bf16), sds((SLOTS, F), f32)],
         [],
         (wire, wd),
-        flops=2 * SLOTS * D * F,
     )
 
 
@@ -475,7 +512,6 @@
         ],
         [pltpu.VMEM((SLOTS, D), bf16), pltpu.VMEM((SLOTS, 1), f32)],
         (wire, wg, wu, ga),
-        flops=8 * SLOTS * D * F,
     )
 
 
@@ -493,7 +529,6 @@
         [sds((E, CAP * SEG, 128), bf16)],
         [pltpu.VMEM((SLOTS, D), bf16)],
         (act, wd),
-        flops=2 * SLOTS * D * F,
     )[0]
 
 
@@ -547,7 +582,6 @@
         [sds((T, D), f32), sds((T, D), bf16), sds((D, E), bf16), sds((1, D), f32)],
         [pltpu.VMEM((T * SEG, 128), f32), pltpu.VMEM((T, D), f32)],
         args,
-        flops=4 * SLOTS * T * D,
         smem=(0, 1, 2, 3),
     )
 
@@ -567,8 +601,26 @@
         [sds((T, D), bf16)],
         [pltpu.VMEM((T * SEG, 128), f32)],
         args,
-        flops=4 * SLOTS * T * D,
         smem=(0, 1, 2),
+    )[0]
+
+
+def head_grad_body(*refs):
+    blocks, (wo, dt, rows_all) = refs[:6], refs[6:]
+    for b in range(6):
+        rows_all[b * T : (b + 1) * T, :] = blocks[b][...]
+    for b in range(3):
+        rows = slice(b * 256, (b + 1) * 256)
+        dt[:, rows] = dot_t(wo[...], rows_all[rows, :]).astype(bf16)
+
+
+def head_grad(blocks, wo):
+    return call(
+        head_grad_body,
+        "head_grad",
+        [sds((LH * HEAD, 6 * T), bf16)],
+        [pltpu.VMEM((6 * T, D), bf16)],
+        (*blocks, wo),
     )[0]
 
 
@@ -578,7 +630,8 @@
     for b in range(8):
         rows_all[b * T : (b + 1) * T, :] = blocks[b][...]
     gw[...] = (dot(ot0[...], rows_all[:HALF, :]) + dot(ot1[...], rows_all[HALF:, :])).astype(bf16)
-    part = dot_t(wo[...], rows_all[...])
+    last = jnp.concatenate([blocks[2][...], blocks[6][...]], axis=0)
+    part = dot_t(wo[...], last)
 
     @pl.when(step == 0)
     def _():
@@ -599,18 +652,25 @@
         "out_projection_grad",
         (4,),
         [cols_of((T, 512))] * 8 + [whole((512, HALF))] * 2 + [cols_of((512, 512))],
-        [cols_of((512, 512)), whole((512, ROWS))],
-        [sds((LH * HEAD, D), bf16), sds((LH * HEAD, ROWS), bf16)],
-        [pltpu.VMEM((ROWS, 512), bf16), pltpu.VMEM((512, ROWS), f32)],
+        [cols_of((512, 512)), whole((512, 2 * T))],
+        [sds((LH * HEAD, D), bf16), sds((LH * HEAD, 2 * T), bf16)],
+        [pltpu.VMEM((ROWS, 512), bf16), pltpu.VMEM((512, 2 * T), f32)],
         (*blocks, ot0, ot1, wo),
-        flops=4 * 512 * ROWS * D,
     )
 
 
 def bwd_body(*refs):
-    qr, kr = refs[0:4], refs[4:8]
-    (qt, kt, kn, vn, dt, ot0, ot1, linv, info, cos, sin, gq, gk) = refs[8:21]
-    dq0, dq1, dkv, ggq, ggk, mask, wb, sb, dqt, dk, dv, raw = refs[21:]
+    qh, kh, scales = refs[0:4], refs[4:8], refs[8:12]
+    (qt, kt, kn, vn, dta, dtb, ot0, ot1, linv, info, cos, sin, gq, gk) = refs[12:26]
+    dq0, dq1, dkv, ggq, ggk, mask, wb, sb, dqt, dk, dv, raw, dt, scale = refs[26:]
+    for dc in range(2):
+        for place, dy in enumerate((0, 1, 3)):
+            to = slice(dc * HALF + dy * T, dc * HALF + (dy + 1) * T)
+            dt[:, to] = dta[:, (place * 2 + dc) * T : (place * 2 + dc + 1) * T]
+        dt[:, dc * HALF + 2 * T : dc * HALF + 3 * T] = dtb[:, dc * T : (dc + 1) * T]
+        for dy in range(4):
+            to = slice(dc * HALF + dy * T, dc * HALF + (dy + 1) * T)
+            scale[:, to] = scales[dy][:, dc * T : (dc + 1) * T]
     build_mask(info, mask)
     dk[...] = jnp.zeros_like(dk)
     dv[...] = jnp.zeros_like(dv)
@@ -648,9 +708,7 @@
         c, s = cos[...], sin[...]
         return jnp.concatenate([low * c + high * s, high * c - low * s], axis=0)
 
-    def norm_back(v, grad, gain):
-        r = lax.rsqrt(jnp.mean(v * v, axis=0, keepdims=True) + EPS)
-        n = v * r
+    def norm_back(n, r, grad, gain):
         gain_grad = jnp.sum(grad * n, axis=1, keepdims=True)
         u = grad * gain
         return r * (u - n * jnp.mean(u * n, axis=0, keepdims=True)), gain_grad
@@ -662,8 +720,8 @@
         for dy in range(4):
             for dc in range(2):
                 to = slice(dc * HALF + dy * T, dc * HALF + (dy + 1) * T)
-                raw[:, to] = qr[dy][heads, dc * T : (dc + 1) * T]
-        grad, part = norm_back(raw[...], unrope(dqt[heads, :] * (HEAD ** (-0.5))), gain_q)
+                raw[:, to] = qh[dy][heads, dc * T : (dc + 1) * T].astype(f32)
+        grad, part = norm_back(raw[...], scale[h : h + 1, :], unrope(dqt[heads, :] * (HEAD ** (-0.5))), gain_q)
         total = total + part
         dq0[heads, :] = grad[:, :HALF].astype(bf16)
         dq1[heads, :] = grad[:, HALF:].astype(bf16)
@@ -671,14 +729,14 @@
     for dy in range(4):
         for dc in range(2):
             to = slice(dc * HALF + dy * T, dc * HALF + (dy + 1) * T)
-            raw[:, to] = kr[dy][:, dc * T : (dc + 1) * T].astype(f32)
-    grad, part = norm_back(raw[...], unrope(dk[...].T), gain_k)
+            raw[:, to] = kh[dy][:, dc * T : (dc + 1) * T].astype(f32)
+    grad, part = norm_back(raw[...], scale[LH : LH + 1, :], unrope(dk[...].T), gain_k)
     ggk[...] = jnp.broadcast_to(part, (HEAD, 128)).T[0:8, :]
     dkv[:HEAD, :] = grad.astype(bf16)
     dkv[HEAD:, :] = dv[...].T.astype(bf16)
 
 
-def bwd(qr, kr, *rest):
+def bwd(qh, kh, scales, *rest):
     return call(
         bwd_body,
         "attend_grad",
@@ -697,9 +755,10 @@
             pltpu.VMEM((ROWS, HEAD), f32),
             pltpu.VMEM((ROWS, HEAD), f32),
             pltpu.VMEM((HEAD, ROWS), f32),
+            pltpu.VMEM((LH * HEAD, ROWS), bf16),
+            pltpu.VMEM((8, ROWS), f32),
         ],
-        (*qr, *kr, *rest),
-        flops=10 * LH * ROWS * ROWS * HEAD,
+        (*qh, *kh, *scales, *rest),
     )
 
 
@@ -745,40 +804,48 @@
         ],
         [pltpu.VMEM((640, ROWS), bf16)],
         (where, n1t, dq0, dq1, own, sib),
-        flops=2 * D * 640 * ROWS,
         scalars=1,
     )
 
 
-def normed_grad_body(wa, wb, wkv, dq0, dqr, tot, n1t, b0, b1, b2, b3, gg1):
-    total = dot(wa[...], dq0[...]) + dot(wb[...], dqr[...]) + dot(wkv[...], tot[...])
-    for dy, out in enumerate((b0, b1, b2, b3)):
-        out[...] = total[:, dy * T : (dy + 1) * T].astype(bf16)
-    gain = jnp.sum(total * n1t[...].astype(f32), axis=1, keepdims=True)
-    for b in range(4):
-        rows = slice(b * 128, (b + 1) * 128)
-        gg1[:, rows] = jnp.broadcast_to(gain[rows, :], (128, 128)).T[0:8, :]
-
-
-def normed_grad(wa, wb, wkv, dq0, dqr, tot, n1t):
+def normed_grad_body(wa, wb, wkv, dq0, dqr, tot, n0, n1, n2, n3, b0, b1, b2, b3, gg1, grads):
+    @pl.when(pl.program_id(0) == 0)
+    def _():
+        flip(dq0, grads, 0, 0)
+        flip(dqr, grads, 0, 512)
+        flip(tot, grads, 0, 1024)
+
+    total = (
+        dot(grads[:, :512], wa[...])
+        + dot(grads[:, 512:1024], wb[...])
+        + dot(grads[:, 1024:], wkv[...])
+    )
+    gain = jnp.zeros((1, 512), f32)
+    for dy, (out, rows) in enumerate(((b0, n0), (b1, n1), (b2, n2), (b3, n3))):
+        part = total[dy * T : (dy + 1) * T, :]
+        out[...] = part.astype(bf16)
+        gain = gain + jnp.sum(part * rows[...].astype(f32), axis=0, keepdims=True)
+    gg1[...] = jnp.broadcast_to(gain, (8, 512))
+
+
+def normed_grad(wa, wb, wkv, dq0, dqr, tot, n1):
     return grid_call(
         normed_grad_body,
         "normed_grad",
         (4,),
         [
-            rows_of((512, 512)),
-            rows_of((512, 512)),
-            rows_of((512, 256)),
+            cols_of((512, 512)),
+            cols_of((512, 512)),
+            cols_of((256, 512)),
             whole((512, HALF)),
             whole((512, HALF)),
             whole((2 * HEAD, HALF)),
-            rows_of((512, HALF)),
-        ],
-        [rows_of((512, T))] * 4 + [cols_of((8, 512))],
-        [sds((D, T), bf16)] * 4 + [sds((8, D), f32)],
-        [],
-        (wa, wb, wkv, dq0, dqr, tot, n1t),
-        flops=2 * D * 1280 * HALF,
+        ]
+        + [cols_of((T, 512))] * 4,
+        [cols_of((T, 512))] * 4 + [cols_of((8, 512))],
+        [sds((T, D), bf16)] * 4 + [sds((8, D), f32)],
+        [pltpu.VMEM((HALF, 1280), bf16)],
+        (wa, wb, wkv, dq0, dqr, tot, *n1),
     )
 
 
@@ -808,32 +875,17 @@
     )
 
 
-def final_body(b0, b1, b2, b3, x0, ghid, g1, out, c):
-    for j in range(SEG):
-        rows = slice(j * 128, (j + 1) * 128)
-        total = (
-            b0[rows, :].astype(f32)
-            + b1[rows, :].astype(f32)
-            + b2[rows, :].astype(f32)
-            + b3[rows, :].astype(f32)
-        )
-        c[:, rows] = total.T
+def final_body(b0, b1, b2, b3, x0, ghid, g1, out):
+    c = (b0[...].astype(f32) + b1[...].astype(f32)) + (b2[...].astype(f32) + b3[...].astype(f32))
     v = x0[...].astype(f32)
     r = lax.rsqrt(jnp.mean(v * v, axis=-1, keepdims=True) + EPS)
-    u = c[...] * g1[...]
+    u = c * g1[...]
     m = jnp.mean(u * v, axis=-1, keepdims=True)
     out[...] = ghid[...] + r * u - v * (r * r * r * m)
 
 
 def final(b, x0, ghid, g1):
-    return call(
-        final_body,
-        "input_grad",
-        [sds((T, D), f32)],
-        [pltpu.VMEM((T, D), f32)],
-        (*b, x0, ghid, g1),
-        flops=T * D * 10,
-    )[0]
+    return call(final_body, "input_grad", [sds((T, D), f32)], [], (*b, x0, ghid, g1))[0]
 
 
 def sibling(x):
@@ -883,11 +935,22 @@
     return [x] + [move(x, axis, (4 - d) % 4) for d in (1, 2, 3)]
 
 
-def sum_over_experts(a, b):
+def sum_over_experts(a, b, other):
     a1, b1 = reduce_step(a, 0), reduce_step(b, 1)
     a2, b2 = reduce_step(a1, 1), reduce_step(b1, 0)
     a3, b3 = jnp.stack(gather_step(a2, 1)), jnp.stack(gather_step(b2, 0))
-    return gather_step(a3, 0), gather_step(b3, 1)
+    a3, b3, other = lax.optimization_barrier((a3, b3, other))
+    return gather_step(a3, 0), gather_step(b3, 1), other, (a1, b1)
+
+
+def sum_everywhere(x):
+    x = x + sibling(x)
+    moved = [to_chip(x, d) for d in (1, 3, 2)]
+    x = x + moved[0] + moved[1] + moved[2]
+    for axis in (0, 1):
+        moved = [move(x, axis, d) for d in (1, 3, 2)]
+        x = x + moved[0] + moved[1] + moved[2]
+    return x
 
 
 def after(value, *others):
@@ -933,31 +996,30 @@
     wk_t, wv_t = w_key.T, w_value.T
     wk_s, wv_s = sibling(wk_t), sibling(wv_t)
     wq_t = w_query.T
-    wo_t = w_out.T
-    wo_ts = sibling(wo_t)
-    wq_s = sibling(w_query)
+    wo_s = sibling(w_out)
+    wq_ts = sibling(wq_t)
 
     def piece(dy):
         return qkv(
             dy, core_id, x_own[dy], x_sib[dy], g1, wq_t, wk_t, wk_s, wv_t, wv_s, gq, gk, cos, sin
         )
 
-    pieces = [piece(dy) for dy in range(4)]
-    q_raw, q, k_raw, k, v, n1, wkv = zip(*pieces)
-    got_grads = exchange(pack(out_grad, assign_t))
+    pieces = {dy: piece(dy) for dy in (0, 1, 3, 2)}
+    wkv = pieces[0][7]
+    qh, q, kh, k, v, scales, n1 = zip(*(pieces[dy][:7] for dy in range(4)))
+    og_wire = after(pack(out_grad, assign_t), x_own[2], q[0], q[1], q[3])
+    got_grads = exchange(og_wire)
     ot0, ot1, linv, qt, kt, kn, vn = attend(q, k, v, info)
-    blocks = outproj(ot0, sibling(ot1), wo_t, wo_ts)
+    blocks = outproj(ot0, sibling(ot1), w_out, wo_s)
     blocks = [blocks[0]] + spread(blocks)
     hidden, n2, probs, gates, wire = router(blocks, block_input, g2, w_router, ids, assign_t)
     got_rows = exchange(wire)
 
-    n1 = after(n1, wire)
-    n1_t = jnp.concatenate([p[:T] for p in n1] + [p[T:] for p in n1], axis=0).T
-    wkv_full = after(wkv[0], wire).T
+    n1_t = transpose_rows(after(n1, wire))
     gate_list = gates[:, :4].reshape(-1)
     grad_rows, grad_act = expert_grad(after(got_grads, wire), w_down[0])
-    got_rows, n1_t, wkv_full, grad_act, gate_list = lax.optimization_barrier(
-        (got_rows, n1_t, wkv_full, grad_act, gate_list)
+    got_rows, n1_t, grad_act, gate_list, wq_ts = lax.optimization_barrier(
+        (got_rows, n1_t, grad_act, gate_list, wq_ts)
     )
 
     back, rows, act, scaled_act, dg, du = expert_main(got_rows, w_gate[0], w_up[0], grad_act)
@@ -981,49 +1043,61 @@
         out_grad, g2, w_router,
     )
     g_own, g_sib = gather_blocks(gatt)
-    router_parts = exchange(grouter.reshape(E, SEG, 128))
+    router_parts = lax.all_to_all(
+        grouter.reshape(8, 2 * T, E), "shard", split_axis=0, concat_axis=0, tiled=True
+    )
     router_sum = jnp.sum(router_parts.astype(f32), axis=0).astype(bf16)
-    returned = exchange(after(out_wire, g_own[2]))
-
-    gwout, dt = pre(g_own + g_sib, ot0, ot1, w_out)
-    grad_wout = lax.psum(gwout, "expert").astype(f32)
+    dt_near = head_grad(
+        [g_own[0], g_sib[0], g_own[1], g_sib[1], g_own[3], g_sib[3]], w_out
+    )
+    g_far, dt_near, router_sum = lax.optimization_barrier(
+        ((g_own[2], g_sib[2]), dt_near, router_sum)
+    )
+    g_own[2], g_sib[2] = g_far
+
+    gwout, dt_far = pre(g_own + g_sib, ot0, ot1, w_out)
+    early_sums = lax.psum((gwout, router_sum), "expert")
+    returned = exchange(after(out_wire, dt_far))
+
     dq0, dq1, dkv, ggq, ggk = bwd(
-        q_raw, k_raw, qt, kt, kn, vn, dt, ot0, ot1, linv, info, cos, sin, gq, gk
+        qh, kh, scales, qt, kt, kn, vn, dt_near, dt_far, ot0, ot1, linv, info, cos, sin, gq, gk
     )
     dq_sib, dkv_sib = sibling(dq1), sibling(dkv)
     gw_a, gw_b, dkv_total = qkv_grad(where, n1_t, dq0, dq1, dkv, dkv_sib)
-    gw_a, gw_b = sum_over_experts(gw_a, gw_b)
-    blocks = normed_grad(w_query, wq_s, wkv_full, dq0, dq_sib, dkv_total, n1_t)
-    gg1 = blocks[4][0]
-    blocks, returned, router_sum = lax.optimization_barrier((blocks[:4], returned, router_sum))
+    returned, dq0 = lax.optimization_barrier((returned, dq0))
+    result = result_rows(expert_list, slot_list, gate_list, returned, hidden)
+    blocks = normed_grad(wq_t, wq_ts, wkv, dq0, dq_sib, dkv_total, n1)
+    gg1 = blocks[4][0:1] / g1
     blocks = [blocks[0]] + spread(blocks)
-    result = result_rows(expert_list, slot_list, gate_list, returned, hidden)
-
-    vector = jnp.concatenate([gg1 / g1[0], gg2[0], ggq[0], ggk[0]])
-    per = vector.shape[0] // E
-    wide = jnp.pad(vector.reshape(E, per), ((0, 0), (0, 128 - per))).reshape(E, 1, 128)
-    mine = jnp.sum(exchange(wide), axis=0)
-    first = mine.astype(bf16)
-    second = (mine - first.astype(f32)).astype(bf16)
-    shared = jnp.concatenate([router_sum, first, second, jnp.zeros((6, 128), bf16)], axis=0)
-    shared = exchange(jnp.broadcast_to(shared[None], (E, 24, 128)))
-    grad_router = shared[:, :SEG].reshape(D, E).astype(f32)
-    vector = (
-        (shared[:, SEG].astype(f32) + shared[:, SEG + 1].astype(f32))[:, :per].reshape(-1)
-    )
+    gw_a, gw_b, (blocks, early_sums), begun = sum_over_experts(gw_a, gw_b, (blocks, early_sums))
+    grad_wout = early_sums[0].astype(f32)
+    grad_router = lax.all_gather(early_sums[1], "shard", axis=0, tiled=True).astype(f32)
     grad_input = final(blocks, block_input, ghid, g1)
+
+    vector = sum_everywhere(
+        after(jnp.concatenate(
+            [
+                gg1.reshape(SEG, 128),
+                gg2.reshape(SEG, 128),
+                ggq[0:1],
+                ggk[0:1],
+                jnp.zeros((6, 128), f32),
+            ],
+            axis=0,
+        ), *begun)
+    )
     grad_wq, grad_wk, grad_wv = place(where, gw_a, gw_b)
     return (
         result,
         grad_input,
-        vector[:D],
+        vector[:SEG].reshape(D),
         grad_wq,
         grad_wk.T,
         grad_wv.T,
-        vector[2 * D : 2 * D + HEAD],
-        vector[2 * D + HEAD :],
+        vector[2 * SEG],
+        vector[2 * SEG + 1],
         grad_wout,
-        vector[D : 2 * D],
+        vector[SEG : 2 * SEG].reshape(D),
         grad_router,
         grad_wgate[None],
         grad_wup[None],

time: 530 us -> 522 us (0.985)
  blocking collectives: 0 us -> 35.9 us
  starting transfers between devices: 128 us -> 109 us
  local copies, waits for them, and re-layouts: 42.7 us -> 24.2 us
  waiting for transfers between devices: 164 us -> 146 us
  Pallas kernels: 144 us -> 154 us
    ppermute x24 -> x30, waiting for transfers between devices: 67.3 us -> 26.2 us  [on_expert(): return lax.ppermute(x, 'expert', pairs)]
    all_to_all x7 -> x4, starting transfers between devices: 63.4 us -> 27.7 us  [exchange(): return lax.all_to_all(x, ALL, split_axis=0, concat_axis=0, tiled=True)]
    all_gather x0 -> x1, blocking collectives: none -> 22.5 us  [on_device(): lax.all_gather(early_sums[1], 'shard', axis=0, tiled=True).astype(f32)]
    psum x1, waiting for transfers between devices: 0.01 us -> 20.1 us  [on_device(): early_sums = lax.psum((gwout, router_sum), 'expert')]
    ppermute x15 -> x16, starting transfers between devices: 14.2 us -> 30.3 us  [sibling(): return lax.ppermute(x, 'shard', [(i, i ^ 1) for i in range(8)])]
    all_to_all x0 -> x1, blocking collectives: none -> 13.3 us  [on_device(): lax.all_to_all(grouter.reshape(8, 2 * T, E), 'shard', split_axis=0, conca...]
    pallas_call x16 -> x18, Pallas kernels: 113 us -> 125 us  [call(): pl.pallas_call(kernel, out_shape=outs, in_specs=in_specs, out_specs=[pl.B...]
    ppermute x6, waiting for transfers between devices: 18.7 us -> 29.9 us  [from_chip(): return lax.ppermute(x, 'shard', [(i, (i - 2 * dy) % 8) for i in range(8)])]
  transfers between devices with their start and end apart: 59 -> 66, of which waited for: 18 -> 21; matrix products, arithmetic and copies ran while one was open for 12% -> 8% of each run, Pallas kernels for 23% -> 23%
where the time goes in v3:
time: 522 us; the launch traced here: 513 us
  Pallas kernels  154 us (30%)
  waiting for transfers between devices  146 us (28%)
  starting transfers between devices  109 us (21%)
  blocking collectives  35.9 us (7%)
  local copies, waits for them, and re-layouts  24.2 us (5%)
  other arithmetic  16 us (3%)
  between operations  15 us (3%)
  matrix products  13.7 us (3%)
    pallas_call x18, Pallas kernels, call(): pl.pallas_call(kernel, out_shape=outs, in_specs=in_specs, out_specs=[pl.B...  125 us
    all_to_all x4, waiting for transfers between devices, exchange(): return lax.all_to_all(x, ALL, split_axis=0, concat_axis=0, tiled=True)  40.3 us
    ppermute x30, starting transfers between devices, on_expert(): return lax.ppermute(x, 'expert', pairs)  33.5 us
    ppermute x16, starting transfers between devices, sibling(): return lax.ppermute(x, 'shard', [(i, i ^ 1) for i in range(8)])  30.3 us
    ppermute x6, waiting for transfers between devices, from_chip(): return lax.ppermute(x, 'shard', [(i, (i - 2 * dy) % 8) for i in range(8)])  29.9 us
    pallas_call x4, Pallas kernels, grid_call(): pl.pallas_call(kernel, out_shape=outs, grid_spec=pltpu.PrefetchScalarGrid...  29.6 us
    all_to_all x4, starting transfers between devices, exchange(): return lax.all_to_all(x, ALL, split_axis=0, concat_axis=0, tiled=True)  27.7 us
    ppermute x30, waiting for transfers between devices, on_expert(): return lax.ppermute(x, 'expert', pairs)  26.2 us
  transfers between devices with their start and end apart: 66, of which 21 were waited for; matrix products, arithmetic and copies ran while one was open for 8% of the time, Pallas kernels for 23%

profile of v3, /device:TPU:1, one launch (start us, length us, event | category | flops | bytes accessed | tf_op | source)
XLA Modules:
  0.0 513.1 jit_solution(14321248452625738313)
XLA Ops:
  7.2 3.6 collective-permute-start.3
  15.6 17.2 %collective-permute-done.3.xa = bf16[128,2048]{1,0:T(8,128)(2,1)} collective-permute-done((bf16[128,2048]{1,0:T(8,128)(2,1)}, bf16[128,2048]{1,0:T(8,128)(2,1)}, u32[]{:S(2)}, u32[]{:S(2)}) %collective-permute-start.3) | collective-permute-done | bytes 524320 | tf_op jit(solution)/shard_map/ppermute | solution.py:896
  34.5 3.2 collective-permute-done.7.xa
  39.6 2.0 route_tables.1
  42.8 4.2 pack_rows.1
  46.9 2.5 copy.33
  50.1 1.8 multiply_sine_fusion
  52.6 5.0 qkv0.1
  57.5 5.0 qkv1.1
  62.5 5.0 qkv3.1
  67.5 8.3 %all-to-all-start.1 = ((bf16[128,88,128]{2,1,0:T(8,128)(2,1)}), bf16[128,88,128]{2,1,0:T(8,128)(2,1)}, u32[]{:S(2)}, u32[]{:S(2)}) async-start(bf16[128,88,128]{2,1,0:T(8,128)(2,1)} %pack_rows.1), calls=%async_computation.1 | async-start | bytes 5767168 | tf_op jit(solution)/shard_map/all_to_all | solution.py:909
  78.0 3.5 collective-permute-done.6.xb
  82.3 4.9 qkv2.1
  87.3 10.9 %attend.1 = (bf16[512,512]{1,0:T(8,128)(2,1)}, bf16[512,512]{1,0:T(8,128)(2,1)}, f32[8,1024]{1,0:T(8,128)}, bf16[512,1024]{1,0:T(8,128)(2,1)}, bf16[128,1024]{1,...) custom-call(bf16[512,256]{1,0:T(8,128)(2,1)} %get-tuple-element.129.refs_0_, ...), custom_call_target="tpu_custom_call" | custom-call | flops 1 | bytes 6600001 | tf_op jit(solution)/shard_map/attend/pallas_call | solution.py:73
  101.8 6.2 %out_projection.1 = (bf16[128,2048]{1,0:T(8,128)(2,1)}, bf16[128,2048]{1,0:T(8,128)(2,1)}, bf16[128,2048]{1,0:T(8,128)(2,1)}, bf16[128,2048]{1,0:T(8,128)(2,1)}) custom-call(bf16[512,512]{1,0:T(8,128)(2,1)} %get-tuple-element.141.ot0.refs_8_.refs_18_, bf16[512,512]{1,0:T(8,128)(2,1)} %copy-done.24, bf16[512,2048]{1,0:T(8,128)(2,1)} %refs_10_.1, ...), custom_call_target="tpu_custom_call" | custom-call | flops 1 | bytes 3000001 | tf_op jit(solution)/shard_map/out_projection/pallas_call | solution.py:86
  108.6 2.0 collective-permute-start.12
  112.2 10.4 %collective-permute-done.11.b1 = bf16[128,2048]{1,0:T(8,128)(2,1)S(1)} collective-permute-done((bf16[128,2048]{1,0:T(8,128)(2,1)}, bf16[128,2048]{1,0:T(8,128)(2,1)S(1)}, u32[]{:S(2)}, u32[]{:S(2)}) %collective-permute-start.11) | collective-permute-done | bytes 524320 | tf_op jit(solution)/shard_map/ppermute | solution.py:900
  122.5 11.6 %collective-permute-done.13.b3 = bf16[128,2048]{1,0:T(8,128)(2,1)S(1)} collective-permute-done((bf16[128,2048]{1,0:T(8,128)(2,1)}, bf16[128,2048]{1,0:T(8,128)(2,1)S(1)}, u32[]{:S(2)}, u32[]{:S(2)}) %collective-permute-start.13) | collective-permute-done | bytes 524320 | tf_op jit(solution)/shard_map/ppermute | solution.py:900
  135.0 5.6 %router.1 = (f32[128,2048]{1,0:T(8,128)}, bf16[128,2048]{1,0:T(8,128)(2,1)}, f32[128,128]{1,0:T(8,128)}, f32[128,128]{1,0:T(8,128)}, bf16[128,88,128]{2,1,0:T(8,128)(2,1)}) custom-call(bf16[128,2048]{1,0:T(8,128)(2,1)} %get-tuple-element.143.b0, bf16[128,2048]{1,0:T(8,128)(2,1)} %copy-done.26, bf16[128,2048]{1,0:T(8,128)(2,1)} %copy-done.27, ...), custom_call_target="tpu_custom_call" | custom-call | flops 1 | bytes 3600001 | tf_op jit(solution)/shard_map/router/pallas_call | solution.py:73
  140.6 9.9 %all-to-all-start = ((bf16[128,88,128]{2,1,0:T(8,128)(2,1)}), bf16[128,88,128]{2,1,0:T(8,128)(2,1)}, u32[]{:S(2)}, u32[]{:S(2)}) async-start(bf16[128,88,128]{2,1,0:T(8,128)(2,1)} %get-tuple-element.148), calls=%async_computation | async-start | bytes 5767168 | tf_op jit(solution)/shard_map/all_to_all | solution.py:909
  151.9 5.5 %transpose_rows.1.n1t = bf16[2048,1024]{1,0:T(8,128)(2,1)} custom-call(bf16[256,2048]{1,0:T(8,128)(2,1)} %get-tuple-element.153.n0, bf16[256,2048]{1,0:T(8,128)(2,1)} %get-tuple-element.154.n1, bf16[256,2048]{1,0:T(8,128)(2,1)} %get-tuple-element.155.n2, bf16[256,2048]{1,0:T(8,128)(2,1)} %get-tuple-element.156.n3), custom_call_target="tpu_custom_call" | custom-call | flops 1 | bytes 3600001 | tf_op jit(solution)/shard_map/transpose_rows/pallas_call | solution.py:73
  158.1 7.5 %expert_grad_rows.1 = (bf16[640,2048]{1,0:T(8,128)(2,1)}, f32[640,768]{1,0:T(8,128)}) custom-call(bf16[128,88,128]{2,1,0:T(8,128)(2,1)} %all-to-all-done.1.wire, bf16[768,2048]{1,0:T(8,128)(2,1)} %bitcast.110), custom_call_target="tpu_custom_call" | custom-call | flops 1 | bytes 4800001 | tf_op jit(solution)/shard_map/expert_grad_rows/pallas_call | solution.py:73
  165.6 23.7 %all-to-all-done.wire = bf16[128,88,128]{2,1,0:T(8,128)(2,1)} async-done(((bf16[128,88,128]{2,1,0:T(8,128)(2,1)}), bf16[128,88,128]{2,1,0:T(8,128)(2,1)}, u32[]{:S(2)}, u32[]{:S(2)}) %all-to-all-start) | async-done | bytes 2883616 | tf_op jit(solution)/shard_map/all_to_all | solution.py:909
  189.2 18.6 %expert_main.1 = (bf16[128,88,128]{2,1,0:T(8,128)(2,1)}, bf16[640,2048]{1,0:T(8,128)(2,1)}, bf16[640,768]{1,0:T(8,128)(2,1)}, bf16[640,768]{1,0:T(8,128)(2,1)}, ...) custom-call(bf16[128,88,128]{2,1,0:T(8,128)(2,1)} %all-to-all-done.wire, bf16[2048,768]{1,0:T(8,128)(2,1)} %bitcast.123, ...), custom_call_target="tpu_custom_call" | custom-call | flops 1 | bytes 10800001 | tf_op jit(solution)/shard_map/expert_main/pallas_call | solution.py:73
  207.8 5.0 all-to-all-start.2
  214.9 6.7 %expert_out.1 = bf16[128,80,128]{2,1,0:T(8,128)(2,1)} custom-call(bf16[640,768]{1,0:T(8,128)(2,1)} %get-tuple-element.170.act, bf16[768,2048]{1,0:T(8,128)(2,1)} %bitcast.111), custom_call_target="tpu_custom_call" | custom-call | flops 1 | bytes 4200001 | tf_op jit(solution)/shard_map/expert_out/pallas_call | solution.py:73
  221.6 4.6 fusion.18
  226.2 4.6 fusion.17
  230.7 4.5 fusion.19
  235.3 16.6 %all-to-all-done.2.wire = bf16[128,88,128]{2,1,0:T(8,128)(2,1)S(1)} async-done(((bf16[128,88,128]{2,1,0:T(8,128)(2,1)}), bf16[128,88,128]{2,1,0:T(8,128)(2,1)S(1)}, u32[]{:S(2)}, u32[]{:S(2)}) %all-to-all-start.2) | async-done | bytes 2883616 | tf_op jit(solution)/shard_map/all_to_all | solution.py:909
  253.5 7.1 %combine_grads.1 = (f32[128,2048]{1,0:T(8,128)}, bf16[128,2048]{1,0:T(8,128)(2,1)}, bf16[2048,128]{1,0:T(8,128)(2,1)}, f32[1,2048]{1,0:T(1,128)}) custom-call(s32[3]{0:T(128)} %pad_add_fusion.where, s32[512]{0:T(512)} %reshape.202.experts, s32[512]{0:T(512)} %reshape.203.slots, f32[512]{0:T(512)} %reshape.216.gate_list, bf16[128,88,128]{2,1,0:T(8,128)(2,1)} %copy-done.4, ...), custom_call_target="tpu_custom_call" | custom-call | flops 1 | bytes 4200001 | tf_op jit(solution)/shard_map/combine_grads/pallas_call | solution.py:73
  263.9 9.5 %collective-permute-done.15.refs_2_.refs_1_ = bf16[128,2048]{1,0:T(8,128)(2,1)S(1)} collective-permute-done((bf16[128,2048]{1,0:T(8,128)(2,1)}, bf16[128,2048]{1,0:T(8,128)(2,1)S(1)}, u32[]{:S(2)}, u32[]{:S(2)}) %collective-permute-start.15) | collective-permute-done | bytes 524320 | tf_op jit(solution)/shard_map/ppermute | solution.py:896
  273.4 3.2 collective-permute-start.19
  276.6 11.1 %collective-permute-start.21 = (bf16[128,2048]{1,0:T(8,128)(2,1)S(1)}, bf16[128,2048]{1,0:T(8,128)(2,1)S(1)}, u32[]{:S(2)}, u32[]{:S(2)}) collective-permute-start(bf16[128,2048]{1,0:T(8,128)(2,1)S(1)} %collective-permute-done.20.refs_4_.refs_3_), channel_id=1, source_target_pairs={{0,1},{1,0},{2,3},{3,2},{4,5},{5,4},{6,7},{7,6},{8,9},{9,8},{10,11... | collective-permute-start | bytes 1572872 | tf_op jit(solution)/shard_map/ppermute | solution.py:892
  287.8 13.3 %all_to_all.25 = bf16[8,256,128]{2,1,0:T(8,128)(2,1)S(1)} all-to-all(bf16[8,256,128]{2,1,0:T(8,128)(2,1)} %bitcast.125), channel_id=1, replica_groups=mesh['expert'=16,'shard'=8] {'shard'}, dimensions={0} | all-to-all | bytes 1048576 | tf_op jit(solution)/shard_map/all_to_all | solution.py:1046
  303.6 5.3 %head_grad.1.refs_16_ = bf16[512,768]{1,0:T(8,128)(2,1)} custom-call(bf16[128,2048]{1,0:T(8,128)(2,1)} %get-tuple-element.181.refs_0_, bf16[128,2048]{1,0:T(8,128)(2,1)} %copy-done.11, bf16[128,2048]{1,0:T(8,128)(2,1)} %copy-done.9, bf16[128,2048]{1,0:T(8,128)(2,1)} %copy-done.12, bf16[128,2048]{1,0:T(8,128)(2,1)} %copy-done.10, ...), custom_call_target="tpu_custom_call" | custom-call | flops 1 | bytes 2400001 | tf_op jit(solution)/shard_map/head_grad/pallas_call | solution.py:73
  308.9 7.3 %out_projection_grad.1 = (bf16[512,2048]{1,0:T(8,128)(2,1)}, bf16[512,256]{1,0:T(8,128)(2,1)}) custom-call(bf16[128,2048]{1,0:T(8,128)(2,1)} %get-tuple-element.181.refs_0_, bf16[128,2048]{1,0:T(8,128)(2,1)} %copy-done.9, bf16[128,2048]{1,0:T(8,128)(2,1)} %collective-permute-done.16.refs_2_, bf16[128,2048]{1,0:T(8,128)(2,1)} %copy-done.10, ...), custom_call_target="tpu_custom_call" | custom-call | flops 1 | bytes 4200001 | tf_op jit(solution)/shard_map/out_projection_grad/pallas_call | solution.py:86
  316.2 4.5 all-to-all-start.4
  320.8 18.9 %attend_grad.1 = (bf16[512,512]{1,0:T(8,128)(2,1)}, bf16[512,512]{1,0:T(8,128)(2,1)}, bf16[256,1024]{1,0:T(8,128)(2,1)}, f32[8,128]{1,0:T(8,128)}, f32[8,128]{1,0:T(8,128)}) custom-call(bf16[512,256]{1,0:T(8,128)(2,1)} %get-tuple-element.187.refs_0_, bf16[512,256]{1,0:T(8,128)(2,1)} %get-tuple-element.188.refs_1_, ...), custom_call_target="tpu_custom_call" | custom-call | flops 1 | bytes 11400001 | tf_op jit(solution)/shard_map/attend_grad/pallas_call | solution.py:73
  343.7 8.5 %qkv_weight_grad.1 = (bf16[4,4,64,640]{3,2,1,0:T(8,128)(2,1)}, bf16[4,4,64,640]{3,2,1,0:T(8,128)(2,1)}, bf16[256,1024]{1,0:T(8,128)(2,1)}) custom-call(s32[3]{0:T(128)} %pad_add_fusion.where, bf16[2048,1024]{1,0:T(8,128)(2,1)} %transpose_rows.1.n1t, bf16[512,512]{1,0:T(8,128)(2,1)} %get-tuple-element.214.dq0, bf16[512,512]{1,0:T(8,128)(2,1)} %get-tuple-element.208.dq1, ...), custom_call_target="tpu_custom_call" | custom-call | flops 1 | bytes 4800001 | tf_op jit(solution)/shard_map/qkv_weight_grad/pallas_call | solution.py:86
  352.2 2.1 slice_bitcast_fusion.2
  354.9 2.1 collective-permute-start.33
  364.6 2.6 collective-permute-start.24
  368.0 4.1 collective-permute-done.34
  375.7 1.9 collective-permute-start.36
  377.5 3.0 collective-permute-done.24
  380.6 8.2 %collective-permute-done.25 = bf16[4,64,640]{2,1,0:T(8,128)(2,1)S(1)} collective-permute-done((bf16[4,64,640]{2,1,0:T(8,128)(2,1)S(1)}, bf16[4,64,640]{2,1,0:T(8,128)(2,1)S(1)}, u32[]{:S(2)}, u32[]{:S(2)}) %collective-permute-start.25) | collective-permute-done | bytes 327712 | tf_op jit(solution)/shard_map/ppermute | solution.py:920
  390.7 2.7 collective-permute-start.27
  393.4 7.6 %normed_grad.1 = (bf16[128,2048]{1,0:T(8,128)(2,1)}, bf16[128,2048]{1,0:T(8,128)(2,1)}, bf16[128,2048]{1,0:T(8,128)(2,1)}, bf16[128,2048]{1,0:T(8,128)(2,1)}, f32[8,2048]{1,0:T(8,128)}) custom-call(bf16[512,2048]{1,0:T(8,128)(2,1)} %bitcast.108, bf16[512,2048]{1,0:T(8,128)(2,1)} %collective-permute-done.14.wb, bf16[256,2048]{1,0:T(8,128)(2,1)} %get-tuple-element.213.wkv, ...), custom_call_target="tpu_custom_call" | custom-call | flops 1 | bytes 4200001 | tf_op jit(solution)/shard_map/normed_grad/pallas_call | solution.py:86
  402.0 4.4 collective-permute-start.45
  407.4 2.4 collective-permute-start.38
  409.8 2.6 collective-permute-start.39
  418.6 2.3 collective-permute-start.43
  422.2 1.9 collective-permute-start.50
  426.6 2.1 collective-permute-start.30
  432.6 3.1 collective-permute-done.31
  436.9 4.6 result.1
  441.5 20.1 %all-reduce.3.cloned.1.call-done = (bf16[512,2048]{1,0:T(8,128)(2,1)}, bf16[256,128]{1,0:T(8,128)(2,1)}) async-done(((bf16[512,2048]{1,0:T(8,128)(2,1)}, bf16[256,128]{1,0:T(8,128)(2,1)}), (bf16[512,2048]{1,0:T(8,128)(2,1)}, bf16[256,128]{1,0:T(8,128)(2,1)})) %all-reduce.3.cloned.1.call-update) | async-done | bytes 2162704 | tf_op jit(solution)/shard_map/psum | solution.py:1059
  464.6 1.8 collective-permute-start.58
  466.7 2.4 collective-permute-done.55.refs_1_
  469.9 3.8 input_grad.1
  473.6 2.5 convert_element_type.156
  476.2 22.5 %all_gather.3 = bf16[2048,128]{1,0:T(8,128)(2,1)S(1)} all-gather(bf16[256,128]{1,0:T(8,128)(2,1)S(1)} %copy-done.40), channel_id=1, replica_groups=mesh['expert'=16,'shard'=8] {'shard'}, dimensions={0}, use_global_device_ids=true | all-gather | bytes 589824 | tf_op jit(solution)/shard_map/all_gather | solution.py:1074
  501.6 4.3 place_weight_grads.1
  (237 shorter events, 74.2 us)
Async XLA Ops:
  7.2 25.6 %collective-permute-start.3 = (bf16[128,2048]{1,0:T(8,128)(2,1)}, bf16[128,2048]{1,0:T(8,128)(2,1)}, u32[]{:S(2)}, u32[]{:S(2)}) collective-permute-start(bf16[128,2048]{1,0:T(8,128)(2,1)} %x0.3), channel_id=1, source_target_pairs={{0,6},{1,7},{2,0},{3,1},{4,2},{5,3},{6,4},{7,5},{8,14},{9,15},{10,... | collective-permute-start | bytes 1572872 | tf_op jit(solution)/shard_map/ppermute | solution.py:896
  10.8 56.6 %collective-permute-start.5 = (bf16[128,2048]{1,0:T(8,128)(2,1)}, bf16[128,2048]{1,0:T(8,128)(2,1)S(1)}, u32[]{:S(2)}, u32[]{:S(2)}) collective-permute-start(bf16[128,2048]{1,0:T(8,128)(2,1)} %x0.3), channel_id=1, source_target_pairs={{0,4},{1,5},{2,6},{3,7},{4,0},{5,1},{6,2},{7,3},{8,12},{9,13},{10,... | collective-permute-start | bytes 1572872 | tf_op jit(solution)/shard_map/ppermute | solution.py:896
  11.2 26.6 %collective-permute-start.7 = (bf16[128,2048]{1,0:T(8,128)(2,1)}, bf16[128,2048]{1,0:T(8,128)(2,1)}, u32[]{:S(2)}, u32[]{:S(2)}) collective-permute-start(bf16[128,2048]{1,0:T(8,128)(2,1)} %x0.3), channel_id=1, source_target_pairs={{0,2},{1,3},{2,4},{3,5},{4,6},{5,7},{6,0},{7,1},{8,10},{9,11},{10,... | collective-permute-start | bytes 1572872 | tf_op jit(solution)/shard_map/ppermute | solution.py:896
  11.9 40.0 %collective-permute-start = (bf16[128,2048]{1,0:T(8,128)(2,1)}, bf16[128,2048]{1,0:T(8,128)(2,1)}, u32[]{:S(2)}, u32[]{:S(2)}) collective-permute-start(bf16[128,2048]{1,0:T(8,128)(2,1)} %x0.3), channel_id=1, source_target_pairs={{0,1},{1,0},{2,3},{3,2},{4,5},{5,4},{6,7},{7,6},{8,9},{9,8},{10,11... | collective-permute-start | bytes 1572872 | tf_op jit(solution)/shard_map/ppermute | solution.py:892
  13.4 26.1 %collective-permute-start.1 = (bf16[64,2048]{1,0:T(8,128)(2,1)}, bf16[64,2048]{1,0:T(8,128)(2,1)S(1)}, u32[]{:S(2)}, u32[]{:S(2)}) collective-permute-start(bf16[64,2048]{1,0:T(8,128)(2,1)} %bitcast.113), channel_id=1, source_target_pairs={{0,1},{1,0},{2,3},{3,2},{4,5},{5,4},{6,7},{7,6},{8,9},{9,8},{10,11... | collective-permute-start | bytes 786440 | tf_op jit(solution)/shard_map/ppermute | solution.py:892
  32.8 24.7 %collective-permute-start.4 = (bf16[128,2048]{1,0:T(8,128)(2,1)}, bf16[128,2048]{1,0:T(8,128)(2,1)}, u32[]{:S(2)}, u32[]{:S(2)}) collective-permute-start(bf16[128,2048]{1,0:T(8,128)(2,1)} %collective-permute-done.3.xa), channel_id=1, source_target_pairs={{0,1},{1,0},{2,3},{3,2},{4,5},{5,4},{6,7},{7,6},{8,9},{9,8},{10,11... | collective-permute-start | bytes 1572872 | tf_op jit(solution)/shard_map/ppermute | solution.py:892
  37.7 24.8 %collective-permute-start.8 = (bf16[128,2048]{1,0:T(8,128)(2,1)}, bf16[128,2048]{1,0:T(8,128)(2,1)}, u32[]{:S(2)}, u32[]{:S(2)}) collective-permute-start(bf16[128,2048]{1,0:T(8,128)(2,1)} %collective-permute-done.7.xa), channel_id=1, source_target_pairs={{0,1},{1,0},{2,3},{3,2},{4,5},{5,4},{6,7},{7,6},{8,9},{9,8},{10,11... | collective-permute-start | bytes 1572872 | tf_op jit(solution)/shard_map/ppermute | solution.py:892
  39.5 12.4 %collective-permute-start.2 = (bf16[64,2048]{1,0:T(8,128)(2,1)}, bf16[64,2048]{1,0:T(8,128)(2,1)S(1)}, u32[]{:S(2)}, u32[]{:S(2)}) collective-permute-start(bf16[64,2048]{1,0:T(8,128)(2,1)} %bitcast.118), channel_id=1, source_target_pairs={{0,1},{1,0},{2,3},{3,2},{4,5},{5,4},{6,7},{7,6},{8,9},{9,8},{10,11... | collective-permute-start | bytes 786440 | tf_op jit(solution)/shard_map/ppermute | solution.py:892
  67.5 73.1 %all-to-all-start.1 = ((bf16[128,88,128]{2,1,0:T(8,128)(2,1)}), bf16[128,88,128]{2,1,0:T(8,128)(2,1)}, u32[]{:S(2)}, u32[]{:S(2)}) async-start(bf16[128,88,128]{2,1,0:T(8,128)(2,1)} %pack_rows.1), calls=%async_computation.1 | async-start | bytes 5767168 | tf_op jit(solution)/shard_map/all_to_all | solution.py:909
  75.8 24.5 %collective-permute-start.10 = (bf16[512,2048]{1,0:T(8,128)(2,1)S(1)}, bf16[512,2048]{1,0:T(8,128)(2,1)S(1)}, u32[]{:S(2)}, u32[]{:S(2)}) collective-permute-start(bf16[512,2048]{1,0:T(8,128)(2,1)S(1)} %copy-done.3), channel_id=1, source_target_pairs={{0,1},{1,0},{2,3},{3,2},{4,5},{5,4},{6,7},{7,6},{8,9},{9,8},{10,11... | collective-permute-start | bytes 6291464 | tf_op jit(solution)/shard_map/ppermute | solution.py:892
  77.0 4.5 collective-permute-start.6
  108.0 14.6 %collective-permute-start.11 = (bf16[128,2048]{1,0:T(8,128)(2,1)}, bf16[128,2048]{1,0:T(8,128)(2,1)S(1)}, u32[]{:S(2)}, u32[]{:S(2)}) collective-permute-start(bf16[128,2048]{1,0:T(8,128)(2,1)} %get-tuple-element.144), channel_id=1, source_target_pairs={{0,2},{1,3},{2,4},{3,5},{4,6},{5,7},{6,0},{7,1},{8,10},{9,11},{10,... | collective-permute-start | bytes 1572872 | tf_op jit(solution)/shard_map/ppermute | solution.py:900
  108.6 13.9 %collective-permute-start.12 = (bf16[128,2048]{1,0:T(8,128)(2,1)}, bf16[128,2048]{1,0:T(8,128)(2,1)S(1)}, u32[]{:S(2)}, u32[]{:S(2)}) collective-permute-start(bf16[128,2048]{1,0:T(8,128)(2,1)} %get-tuple-element.145), channel_id=1, source_target_pairs={{0,6},{1,7},{2,0},{3,1},{4,2},{5,3},{6,4},{7,5},{8,14},{9,15},{10,... | collective-permute-start | bytes 1572872 | tf_op jit(solution)/shard_map/ppermute | solution.py:900
  110.7 23.5 %collective-permute-start.13 = (bf16[128,2048]{1,0:T(8,128)(2,1)}, bf16[128,2048]{1,0:T(8,128)(2,1)S(1)}, u32[]{:S(2)}, u32[]{:S(2)}) collective-permute-start(bf16[128,2048]{1,0:T(8,128)(2,1)} %get-tuple-element.146), channel_id=1, source_target_pairs={{0,4},{1,5},{2,6},{3,7},{4,0},{5,1},{6,2},{7,3},{8,12},{9,13},{10,... | collective-permute-start | bytes 1572872 | tf_op jit(solution)/shard_map/ppermute | solution.py:900
  140.6 48.6 %all-to-all-start = ((bf16[128,88,128]{2,1,0:T(8,128)(2,1)}), bf16[128,88,128]{2,1,0:T(8,128)(2,1)}, u32[]{:S(2)}, u32[]{:S(2)}) async-start(bf16[128,88,128]{2,1,0:T(8,128)(2,1)} %get-tuple-element.148), calls=%async_computation | async-start | bytes 5767168 | tf_op jit(solution)/shard_map/all_to_all | solution.py:909
  150.5 15.1 %collective-permute-start.14 = (bf16[512,2048]{1,0:T(8,128)(2,1)S(1)}, bf16[512,2048]{1,0:T(8,128)(2,1)}, u32[]{:S(2)}, u32[]{:S(2)}) collective-permute-start(bf16[512,2048]{1,0:T(8,128)(2,1)S(1)} %bitcast.109), channel_id=1, source_target_pairs={{0,1},{1,0},{2,3},{3,2},{4,5},{5,4},{6,7},{7,6},{8,9},{9,8},{10,11... | collective-permute-start | bytes 6291464 | tf_op jit(solution)/shard_map/ppermute | solution.py:892
  207.8 44.1 %all-to-all-start.2 = ((bf16[128,88,128]{2,1,0:T(8,128)(2,1)}), bf16[128,88,128]{2,1,0:T(8,128)(2,1)S(1)}, u32[]{:S(2)}, u32[]{:S(2)}) async-start(bf16[128,88,128]{2,1,0:T(8,128)(2,1)} %get-tuple-element.164), calls=%async_computation.2 | async-start | bytes 5767168 | tf_op jit(solution)/shard_map/all_to_all | solution.py:909
  260.6 12.8 %collective-permute-start.15 = (bf16[128,2048]{1,0:T(8,128)(2,1)}, bf16[128,2048]{1,0:T(8,128)(2,1)S(1)}, u32[]{:S(2)}, u32[]{:S(2)}) collective-permute-start(bf16[128,2048]{1,0:T(8,128)(2,1)} %get-tuple-element.181.refs_0_), channel_id=1, source_target_pairs={{0,6},{1,7},{2,0},{3,1},{4,2},{5,3},{6,4},{7,5},{8,14},{9,15},{10,... | collective-permute-start | bytes 1572872 | tf_op jit(solution)/shard_map/ppermute | solution.py:896
  260.6 15.9 %collective-permute-start.20 = (bf16[128,2048]{1,0:T(8,128)(2,1)}, bf16[128,2048]{1,0:T(8,128)(2,1)S(1)}, u32[]{:S(2)}, u32[]{:S(2)}) collective-permute-start(bf16[128,2048]{1,0:T(8,128)(2,1)} %get-tuple-element.181.refs_0_), channel_id=1, source_target_pairs={{0,2},{1,3},{2,4},{3,5},{4,6},{5,7},{6,0},{7,1},{8,10},{9,11},{10,... | collective-permute-start | bytes 1572872 | tf_op jit(solution)/shard_map/ppermute | solution.py:896
  262.1 25.6 %collective-permute-start.16 = (bf16[128,2048]{1,0:T(8,128)(2,1)}, bf16[128,2048]{1,0:T(8,128)(2,1)}, u32[]{:S(2)}, u32[]{:S(2)}) collective-permute-start(bf16[128,2048]{1,0:T(8,128)(2,1)} %get-tuple-element.181.refs_0_), channel_id=1, source_target_pairs={{0,4},{1,5},{2,6},{3,7},{4,0},{5,1},{6,2},{7,3},{8,12},{9,13},{10,... | collective-permute-start | bytes 1572872 | tf_op jit(solution)/shard_map/ppermute | solution.py:896
  262.1 39.7 %collective-permute-start.18 = (bf16[128,2048]{1,0:T(8,128)(2,1)}, bf16[128,2048]{1,0:T(8,128)(2,1)S(1)}, u32[]{:S(2)}, u32[]{:S(2)}) collective-permute-start(bf16[128,2048]{1,0:T(8,128)(2,1)} %get-tuple-element.181.refs_0_), channel_id=1, source_target_pairs={{0,1},{1,0},{2,3},{3,2},{4,5},{5,4},{6,7},{7,6},{8,9},{9,8},{10,11... | collective-permute-start | bytes 1572872 | tf_op jit(solution)/shard_map/ppermute | solution.py:892
  273.4 28.4 %collective-permute-start.19 = (bf16[128,2048]{1,0:T(8,128)(2,1)S(1)}, bf16[128,2048]{1,0:T(8,128)(2,1)S(1)}, u32[]{:S(2)}, u32[]{:S(2)}) collective-permute-start(bf16[128,2048]{1,0:T(8,128)(2,1)S(1)} %collective-permute-done.15.refs_2_.refs_1_), channel_id=1, source_target_pairs={{0,1},{1,0},{2,3},{3,2},{4,5},{5,4},{6,7},{7,6},{8,9},{9,8},{10,11... | collective-permute-start | bytes 1572872 | tf_op jit(solution)/shard_map/ppermute | solution.py:892
  276.6 25.3 %collective-permute-start.21 = (bf16[128,2048]{1,0:T(8,128)(2,1)S(1)}, bf16[128,2048]{1,0:T(8,128)(2,1)S(1)}, u32[]{:S(2)}, u32[]{:S(2)}) collective-permute-start(bf16[128,2048]{1,0:T(8,128)(2,1)S(1)} %collective-permute-done.20.refs_4_.refs_3_), channel_id=1, source_target_pairs={{0,1},{1,0},{2,3},{3,2},{4,5},{5,4},{6,7},{7,6},{8,9},{9,8},{10,11... | collective-permute-start | bytes 1572872 | tf_op jit(solution)/shard_map/ppermute | solution.py:892
  287.7 21.2 %collective-permute-start.17 = (bf16[128,2048]{1,0:T(8,128)(2,1)}, bf16[128,2048]{1,0:T(8,128)(2,1)}, u32[]{:S(2)}, u32[]{:S(2)}) collective-permute-start(bf16[128,2048]{1,0:T(8,128)(2,1)} %collective-permute-done.16.refs_2_), channel_id=1, source_target_pairs={{0,1},{1,0},{2,3},{3,2},{4,5},{5,4},{6,7},{7,6},{8,9},{9,8},{10,11... | collective-permute-start | bytes 1572872 | tf_op jit(solution)/shard_map/ppermute | solution.py:892
  316.2 74.5 %all-to-all-start.4 = ((bf16[128,80,128]{2,1,0:T(8,128)(2,1)}), bf16[128,80,128]{2,1,0:T(8,128)(2,1)S(1)}, u32[]{:S(2)}, u32[]{:S(2)}) async-start(bf16[128,80,128]{2,1,0:T(8,128)(2,1)} %expert_out.1), calls=%async_computation.4 | async-start | bytes 5242880 | tf_op jit(solution)/shard_map/all_to_all | solution.py:909
  320.7 140.9 %all-reduce.3.cloned.1.call-start = ((), (), s32[]{:S(2)}) async-start(), calls=%async_computation.5 | async-start | bytes 4325376 | tf_op jit(solution)/shard_map/psum | solution.py:1059
  354.3 10.3 %collective-permute-start.32 = (bf16[4,64,640]{2,1,0:T(8,128)(2,1)}, bf16[4,64,640]{2,1,0:T(8,128)(2,1)S(1)}, u32[]{:S(2)}, u32[]{:S(2)}) collective-permute-start(bf16[4,64,640]{2,1,0:T(8,128)(2,1)} %get-tuple-element.244), channel_id=1, source_target_pairs={{0,8},{8,16},{16,24},{24,0},{32,40},{40,48},{48,56},{56,32},{64,72... | collective-permute-start | bytes 983048 | tf_op jit(solution)/shard_map/ppermute | solution.py:920
  354.9 12.4 %collective-permute-start.33 = (bf16[4,64,640]{2,1,0:T(8,128)(2,1)}, bf16[4,64,640]{2,1,0:T(8,128)(2,1)S(1)}, u32[]{:S(2)}, u32[]{:S(2)}) collective-permute-start(bf16[4,64,640]{2,1,0:T(8,128)(2,1)} %get-tuple-element.246), channel_id=1, source_target_pairs={{0,24},{8,0},{16,8},{24,16},{32,56},{40,32},{48,40},{56,48},{64,88... | collective-permute-start | bytes 983048 | tf_op jit(solution)/shard_map/ppermute | solution.py:920
  357.0 15.1 %collective-permute-start.34 = (bf16[4,64,640]{2,1,0:T(8,128)(2,1)}, bf16[4,64,640]{2,1,0:T(8,128)(2,1)}, u32[]{:S(2)}, u32[]{:S(2)}) collective-permute-start(bf16[4,64,640]{2,1,0:T(8,128)(2,1)} %get-tuple-element.245), channel_id=1, source_target_pairs={{0,16},{8,24},{16,0},{24,8},{32,48},{40,56},{48,32},{56,40},{64,80... | collective-permute-start | bytes 983048 | tf_op jit(solution)/shard_map/ppermute | solution.py:920
  357.9 32.8 %collective-permute-start.41 = (bf16[512,512]{1,0:T(8,128)(2,1)}, bf16[512,512]{1,0:T(8,128)(2,1)}, u32[]{:S(2)}, u32[]{:S(2)}) collective-permute-start(bf16[512,512]{1,0:T(8,128)(2,1)} %get-tuple-element.208.dq1), channel_id=1, source_target_pairs={{0,1},{1,0},{2,3},{3,2},{4,5},{5,4},{6,7},{7,6},{8,9},{9,8},{10,11... | collective-permute-start | bytes 1572872 | tf_op jit(solution)/shard_map/ppermute | solution.py:892
  361.7 13.9 %collective-permute-start.23 = (bf16[4,64,640]{2,1,0:T(8,128)(2,1)S(1)}, bf16[4,64,640]{2,1,0:T(8,128)(2,1)S(1)}, u32[]{:S(2)}, u32[]{:S(2)}) collective-permute-start(bf16[4,64,640]{2,1,0:T(8,128)(2,1)S(1)} %get-tuple-element.247), channel_id=1, source_target_pairs={{0,32},{8,40},{16,48},{24,56},{32,64},{40,72},{48,80},{56,88},{64,... | collective-permute-start | bytes 983048 | tf_op jit(solution)/shard_map/ppermute | solution.py:920
  364.6 15.9 %collective-permute-start.24 = (bf16[4,64,640]{2,1,0:T(8,128)(2,1)S(1)}, bf16[4,64,640]{2,1,0:T(8,128)(2,1)S(1)}, u32[]{:S(2)}, u32[]{:S(2)}) collective-permute-start(bf16[4,64,640]{2,1,0:T(8,128)(2,1)S(1)} %get-tuple-element.249), channel_id=1, source_target_pairs={{0,96},{8,104},{16,112},{24,120},{32,0},{40,8},{48,16},{56,24},{64... | collective-permute-start | bytes 983048 | tf_op jit(solution)/shard_map/ppermute | solution.py:920
  367.2 21.5 %collective-permute-start.25 = (bf16[4,64,640]{2,1,0:T(8,128)(2,1)S(1)}, bf16[4,64,640]{2,1,0:T(8,128)(2,1)S(1)}, u32[]{:S(2)}, u32[]{:S(2)}) collective-permute-start(bf16[4,64,640]{2,1,0:T(8,128)(2,1)S(1)} %get-tuple-element.248), channel_id=1, source_target_pairs={{0,64},{8,72},{16,80},{24,88},{32,96},{40,104},{48,112},{56,120},{... | collective-permute-start | bytes 983048 | tf_op jit(solution)/shard_map/ppermute | solution.py:920
  374.2 27.7 %collective-permute-start.35 = (bf16[64,640]{1,0:T(8,128)(2,1)}, bf16[64,640]{1,0:T(8,128)(2,1)S(1)}, u32[]{:S(2)}, u32[]{:S(2)}) collective-permute-start(bf16[64,640]{1,0:T(8,128)(2,1)} %get-tuple-element.250), channel_id=1, source_target_pairs={{0,32},{8,40},{16,48},{24,56},{32,64},{40,72},{48,80},{56,88},{64,... | collective-permute-start | bytes 245768 | tf_op jit(solution)/shard_map/ppermute | solution.py:920
  375.7 26.4 %collective-permute-start.36 = (bf16[64,640]{1,0:T(8,128)(2,1)}, bf16[64,640]{1,0:T(8,128)(2,1)}, u32[]{:S(2)}, u32[]{:S(2)}) collective-permute-start(bf16[64,640]{1,0:T(8,128)(2,1)} %get-tuple-element.252), channel_id=1, source_target_pairs={{0,96},{8,104},{16,112},{24,120},{32,0},{40,8},{48,16},{56,24},{64... | collective-permute-start | bytes 245768 | tf_op jit(solution)/shard_map/ppermute | solution.py:920
  380.6 25.9 %collective-permute-start.37 = (bf16[64,640]{1,0:T(8,128)(2,1)}, bf16[64,640]{1,0:T(8,128)(2,1)}, u32[]{:S(2)}, u32[]{:S(2)}) collective-permute-start(bf16[64,640]{1,0:T(8,128)(2,1)} %get-tuple-element.251), channel_id=1, source_target_pairs={{0,64},{8,72},{16,80},{24,88},{32,96},{40,104},{48,112},{56,120},{... | collective-permute-start | bytes 245768 | tf_op jit(solution)/shard_map/ppermute | solution.py:920
  390.6 21.8 %collective-permute-start.26 = (bf16[64,640]{1,0:T(8,128)(2,1)}, bf16[64,640]{1,0:T(8,128)(2,1)S(1)}, u32[]{:S(2)}, u32[]{:S(2)}) collective-permute-start(bf16[64,640]{1,0:T(8,128)(2,1)} %get-tuple-element.253), channel_id=1, source_target_pairs={{0,8},{8,16},{16,24},{24,0},{32,40},{40,48},{48,56},{56,32},{64,72... | collective-permute-start | bytes 245768 | tf_op jit(solution)/shard_map/ppermute | solution.py:920
  390.7 23.1 %collective-permute-start.27 = (bf16[64,640]{1,0:T(8,128)(2,1)}, bf16[64,640]{1,0:T(8,128)(2,1)S(1)}, u32[]{:S(2)}, u32[]{:S(2)}) collective-permute-start(bf16[64,640]{1,0:T(8,128)(2,1)} %get-tuple-element.255), channel_id=1, source_target_pairs={{0,24},{8,0},{16,8},{24,16},{32,56},{40,32},{48,40},{56,48},{64,88... | collective-permute-start | bytes 245768 | tf_op jit(solution)/shard_map/ppermute | solution.py:920
  401.9 13.3 %collective-permute-start.28 = (bf16[64,640]{1,0:T(8,128)(2,1)}, bf16[64,640]{1,0:T(8,128)(2,1)S(1)}, u32[]{:S(2)}, u32[]{:S(2)}) collective-permute-start(bf16[64,640]{1,0:T(8,128)(2,1)} %get-tuple-element.254), channel_id=1, source_target_pairs={{0,16},{8,24},{16,0},{24,8},{32,48},{40,56},{48,32},{56,40},{64,80... | collective-permute-start | bytes 245768 | tf_op jit(solution)/shard_map/ppermute | solution.py:920
  402.0 7.8 %collective-permute-start.45 = (f32[40,128]{1,0:T(8,128)S(1)}, f32[40,128]{1,0:T(8,128)S(1)}, u32[]{:S(2)}, u32[]{:S(2)}) collective-permute-start(f32[40,128]{1,0:T(8,128)S(1)} %concatenate.36), channel_id=1, source_target_pairs={{0,1},{1,0},{2,3},{3,2},{4,5},{5,4},{6,7},{7,6},{8,9},{9,8},{10,11... | collective-permute-start | bytes 61448 | tf_op jit(solution)/shard_map/ppermute | solution.py:892
  407.4 9.4 %collective-permute-start.38 = (bf16[64,640]{1,0:T(8,128)(2,1)S(1)}, bf16[64,640]{1,0:T(8,128)(2,1)S(1)}, u32[]{:S(2)}, u32[]{:S(2)}) collective-permute-start(bf16[64,640]{1,0:T(8,128)(2,1)S(1)} %fusion.8), channel_id=1, source_target_pairs={{0,96},{8,104},{16,112},{24,120},{32,0},{40,8},{48,16},{56,24},{64... | collective-permute-start | bytes 245768 | tf_op jit(solution)/shard_map/ppermute | solution.py:920
  409.8 7.2 %collective-permute-start.39 = (bf16[64,640]{1,0:T(8,128)(2,1)S(1)}, bf16[64,640]{1,0:T(8,128)(2,1)S(1)}, u32[]{:S(2)}, u32[]{:S(2)}) collective-permute-start(bf16[64,640]{1,0:T(8,128)(2,1)S(1)} %fusion.8), channel_id=1, source_target_pairs={{0,64},{8,72},{16,80},{24,88},{32,96},{40,104},{48,112},{56,120},{... | collective-permute-start | bytes 245768 | tf_op jit(solution)/shard_map/ppermute | solution.py:920
  412.5 5.7 %collective-permute-start.46 = (f32[40,128]{1,0:T(8,128)S(1)}, f32[40,128]{1,0:T(8,128)S(1)}, u32[]{:S(2)}, u32[]{:S(2)}) collective-permute-start(f32[40,128]{1,0:T(8,128)S(1)} %add.203), channel_id=1, source_target_pairs={{0,2},{1,3},{2,4},{3,5},{4,6},{5,7},{6,0},{7,1},{8,10},{9,11},{10,... | collective-permute-start | bytes 61448 | tf_op jit(solution)/shard_map/ppermute | solution.py:900
  413.8 4.8 collective-permute-start.47
  415.2 5.7 %collective-permute-start.48 = (f32[40,128]{1,0:T(8,128)S(1)}, f32[40,128]{1,0:T(8,128)S(1)}, u32[]{:S(2)}, u32[]{:S(2)}) collective-permute-start(f32[40,128]{1,0:T(8,128)S(1)} %add.203), channel_id=1, source_target_pairs={{0,4},{1,5},{2,6},{3,7},{4,0},{5,1},{6,2},{7,3},{8,12},{9,13},{10,... | collective-permute-start | bytes 61448 | tf_op jit(solution)/shard_map/ppermute | solution.py:900
  416.9 4.6 collective-permute-start.40
  417.0 5.3 %collective-permute-start.29 = (bf16[64,640]{1,0:T(8,128)(2,1)S(1)}, bf16[64,640]{1,0:T(8,128)(2,1)S(1)}, u32[]{:S(2)}, u32[]{:S(2)}) collective-permute-start(bf16[64,640]{1,0:T(8,128)(2,1)S(1)} %fusion.11), channel_id=1, source_target_pairs={{0,24},{8,0},{16,8},{24,16},{32,56},{40,32},{48,40},{56,48},{64,88... | collective-permute-start | bytes 245768 | tf_op jit(solution)/shard_map/ppermute | solution.py:920
  418.2 18.2 %collective-permute-start.42 = (bf16[128,2048]{1,0:T(8,128)(2,1)}, bf16[128,2048]{1,0:T(8,128)(2,1)S(1)}, u32[]{:S(2)}, u32[]{:S(2)}) collective-permute-start(bf16[128,2048]{1,0:T(8,128)(2,1)} %get-tuple-element.217), channel_id=1, source_target_pairs={{0,2},{1,3},{2,4},{3,5},{4,6},{5,7},{6,0},{7,1},{8,10},{9,11},{10,... | collective-permute-start | bytes 1572872 | tf_op jit(solution)/shard_map/ppermute | solution.py:900
  418.6 43.0 %collective-permute-start.43 = (bf16[128,2048]{1,0:T(8,128)(2,1)}, bf16[128,2048]{1,0:T(8,128)(2,1)S(1)}, u32[]{:S(2)}, u32[]{:S(2)}) collective-permute-start(bf16[128,2048]{1,0:T(8,128)(2,1)} %get-tuple-element.218), channel_id=1, source_target_pairs={{0,6},{1,7},{2,0},{3,1},{4,2},{5,3},{6,4},{7,5},{8,14},{9,15},{10,... | collective-permute-start | bytes 1572872 | tf_op jit(solution)/shard_map/ppermute | solution.py:900
  420.9 40.7 %collective-permute-start.44 = (bf16[128,2048]{1,0:T(8,128)(2,1)}, bf16[128,2048]{1,0:T(8,128)(2,1)S(1)}, u32[]{:S(2)}, u32[]{:S(2)}) collective-permute-start(bf16[128,2048]{1,0:T(8,128)(2,1)} %get-tuple-element.219), channel_id=1, source_target_pairs={{0,4},{1,5},{2,6},{3,7},{4,0},{5,1},{6,2},{7,3},{8,12},{9,13},{10,... | collective-permute-start | bytes 1572872 | tf_op jit(solution)/shard_map/ppermute | solution.py:900
  421.4 4.1 collective-permute-start.49
  422.2 4.3 collective-permute-start.50
  425.6 4.5 collective-permute-start.51
  426.6 5.0 collective-permute-start.30
  430.1 5.5 %collective-permute-start.31 = (bf16[64,640]{1,0:T(8,128)(2,1)S(1)}, bf16[64,640]{1,0:T(8,128)(2,1)S(1)}, u32[]{:S(2)}, u32[]{:S(2)}) collective-permute-start(bf16[64,640]{1,0:T(8,128)(2,1)S(1)} %fusion.11), channel_id=1, source_target_pairs={{0,8},{8,16},{16,24},{24,0},{32,40},{40,48},{48,56},{56,32},{64,72... | collective-permute-start | bytes 245768 | tf_op jit(solution)/shard_map/ppermute | solution.py:920
  431.6 31.8 %collective-permute-start.52 = (f32[40,128]{1,0:T(8,128)S(1)}, f32[40,128]{1,0:T(8,128)S(1)}, u32[]{:S(2)}, u32[]{:S(2)}) collective-permute-start(f32[40,128]{1,0:T(8,128)S(1)} %add_add_fusion.1), channel_id=1, source_target_pairs={{0,8},{8,16},{16,24},{24,0},{32,40},{40,48},{48,56},{56,32},{64,72... | collective-permute-start | bytes 61448 | tf_op jit(solution)/shard_map/ppermute | solution.py:920
  435.6 27.7 %collective-permute-start.53 = (f32[40,128]{1,0:T(8,128)S(1)}, f32[40,128]{1,0:T(8,128)S(1)}, u32[]{:S(2)}, u32[]{:S(2)}) collective-permute-start(f32[40,128]{1,0:T(8,128)S(1)} %add_add_fusion.1), channel_id=1, source_target_pairs={{0,24},{8,0},{16,8},{24,16},{32,56},{40,32},{48,40},{56,48},{64,88... | collective-permute-start | bytes 61448 | tf_op jit(solution)/shard_map/ppermute | solution.py:920
  436.4 27.0 %collective-permute-start.54 = (f32[40,128]{1,0:T(8,128)S(1)}, f32[40,128]{1,0:T(8,128)S(1)}, u32[]{:S(2)}, u32[]{:S(2)}) collective-permute-start(f32[40,128]{1,0:T(8,128)S(1)} %add_add_fusion.1), channel_id=1, source_target_pairs={{0,16},{8,24},{16,0},{24,8},{32,48},{40,56},{48,32},{56,40},{64,80... | collective-permute-start | bytes 61448 | tf_op jit(solution)/shard_map/ppermute | solution.py:920
  461.6 7.5 %collective-permute-start.55 = (bf16[4,64,640]{2,1,0:T(8,128)(2,1)S(1)}, bf16[4,64,640]{2,1,0:T(8,128)(2,1)S(1)}, u32[]{:S(2)}, u32[]{:S(2)}) collective-permute-start(bf16[4,64,640]{2,1,0:T(8,128)(2,1)S(1)} %pad_maximum_fusion.refs_0_), channel_id=1, source_target_pairs={{0,96},{8,104},{16,112},{24,120},{32,0},{40,8},{48,16},{56,24},{64... | collective-permute-start | bytes 983048 | tf_op jit(solution)/shard_map/ppermute | solution.py:920
  464.0 35.8 %collective-permute-start.56 = (bf16[4,64,640]{2,1,0:T(8,128)(2,1)S(1)}, bf16[4,64,640]{2,1,0:T(8,128)(2,1)S(1)}, u32[]{:S(2)}, u32[]{:S(2)}) collective-permute-start(bf16[4,64,640]{2,1,0:T(8,128)(2,1)S(1)} %pad_maximum_fusion.refs_0_), channel_id=1, source_target_pairs={{0,64},{8,72},{16,80},{24,88},{32,96},{40,104},{48,112},{56,120},{... | collective-permute-start | bytes 983048 | tf_op jit(solution)/shard_map/ppermute | solution.py:920
  464.6 35.2 %collective-permute-start.57 = (bf16[4,64,640]{2,1,0:T(8,128)(2,1)S(1)}, bf16[4,64,640]{2,1,0:T(8,128)(2,1)S(1)}, u32[]{:S(2)}, u32[]{:S(2)}) collective-permute-start(bf16[4,64,640]{2,1,0:T(8,128)(2,1)S(1)} %pad_maximum_fusion.refs_0_), channel_id=1, source_target_pairs={{0,32},{8,40},{16,48},{24,56},{32,64},{40,72},{48,80},{56,88},{64,... | collective-permute-start | bytes 983048 | tf_op jit(solution)/shard_map/ppermute | solution.py:920
  464.6 35.2 %collective-permute-start.58 = (bf16[4,64,640]{2,1,0:T(8,128)(2,1)S(1)}, bf16[4,64,640]{2,1,0:T(8,128)(2,1)S(1)}, u32[]{:S(2)}, u32[]{:S(2)}) collective-permute-start(bf16[4,64,640]{2,1,0:T(8,128)(2,1)S(1)} %pad_maximum_fusion.1.refs_4_), channel_id=1, source_target_pairs={{0,24},{8,0},{16,8},{24,16},{32,56},{40,32},{48,40},{56,48},{64,88... | collective-permute-start | bytes 983048 | tf_op jit(solution)/shard_map/ppermute | solution.py:920
  466.4 33.4 %collective-permute-start.59 = (bf16[4,64,640]{2,1,0:T(8,128)(2,1)S(1)}, bf16[4,64,640]{2,1,0:T(8,128)(2,1)S(1)}, u32[]{:S(2)}, u32[]{:S(2)}) collective-permute-start(bf16[4,64,640]{2,1,0:T(8,128)(2,1)S(1)} %pad_maximum_fusion.1.refs_4_), channel_id=1, source_target_pairs={{0,16},{8,24},{16,0},{24,8},{32,48},{40,56},{48,32},{56,40},{64,80... | collective-permute-start | bytes 983048 | tf_op jit(solution)/shard_map/ppermute | solution.py:920
  469.1 30.7 %collective-permute-start.60 = (bf16[4,64,640]{2,1,0:T(8,128)(2,1)S(1)}, bf16[4,64,640]{2,1,0:T(8,128)(2,1)S(1)}, u32[]{:S(2)}, u32[]{:S(2)}) collective-permute-start(bf16[4,64,640]{2,1,0:T(8,128)(2,1)S(1)} %pad_maximum_fusion.1.refs_4_), channel_id=1, source_target_pairs={{0,8},{8,16},{16,24},{24,0},{32,40},{40,48},{48,56},{56,32},{64,72... | collective-permute-start | bytes 983048 | tf_op jit(solution)/shard_map/ppermute | solution.py:920
  (49 other events, 445.5 us)
Sparse Core Ops, SparseCore 0:
  360.6 100.9 all-reduce.2

commit v4 on v3

--- a/solution.py
+++ b/solution.py
@@ -26,12 +26,6 @@
 f32 = jnp.float32
 ALL = ("expert", "shard")
 COSTS = {
-    "qkv0": 4,
-    "qkv1": 4,
-    "qkv2": 4,
-    "qkv3": 4,
-    "pack_rows": 4,
-    "route_tables": 2,
     "attend": 11,
     "out_projection": 5,
     "router": 6,
@@ -42,12 +36,6 @@
     "combine_grads": 7,
     "head_grad": 4,
     "out_projection_grad": 7,
-    "attend_grad": 19,
-    "qkv_weight_grad": 8,
-    "normed_grad": 7,
-    "result": 4,
-    "input_grad": 3,
-    "place_weight_grads": 4,
 }
 
 
@@ -76,7 +64,7 @@
         in_specs=in_specs,
         out_specs=[pl.BlockSpec(memory_space=pltpu.VMEM) for _ in outs],
         scratch_shapes=scratch,
-        compiler_params=pltpu.CompilerParams(vmem_limit_bytes=56 * 1024 * 1024),
+        compiler_params=pltpu.CompilerParams(vmem_limit_bytes=63 * 1024 * 1024),
         cost_estimate=cost(COSTS.get(name, 0)),
         name=name,
     )(*args)
@@ -94,7 +82,7 @@
             scratch_shapes=scratch,
         ),
         compiler_params=pltpu.CompilerParams(
-            vmem_limit_bytes=56 * 1024 * 1024, dimension_semantics=("arbitrary",)
+            vmem_limit_bytes=63 * 1024 * 1024, dimension_semantics=("arbitrary",)
         ),
         cost_estimate=cost(COSTS.get(name, 0)),
         name=name,
@@ -202,67 +190,72 @@
     return jnp.broadcast_to(row, (128, 128)).T[:, 0:1]
 
 
-def qkv_body(
-    piece, core, xa, xb, g1, wqt, wk, wks, wv, wvs, gq, gk, cos, sin,
-    qn, qt, kn, kt, vt, scale, n1, wkv,
-):
+def qkv_body(pieces, *refs):
+    count = len(pieces)
+    core, blocks = refs[0], refs[1 : 1 + 2 * count]
+    g1, wqt, wk, wks, wv, wvs, gq, gk, cos, sin = refs[1 + 2 * count : 11 + 2 * count]
+    outs = refs[11 + 2 * count :]
+    wkv = outs[-1]
     lower = core[0] == 0
     wkv[0:64, :] = jnp.where(lower, wk[...], wks[...])
     wkv[64:128, :] = jnp.where(lower, wks[...], wk[...])
     wkv[128:192, :] = jnp.where(lower, wv[...], wvs[...])
     wkv[192:256, :] = jnp.where(lower, wvs[...], wv[...])
-    for half, ref in ((0, xa), (1, xb)):
-        x = ref[...].astype(f32)
-        r = lax.rsqrt(jnp.mean(x * x, axis=-1, keepdims=True) + EPS)
-        n1[half * T : (half + 1) * T, :] = (x * r * g1[...]).astype(bf16)
-    raw = dot_t(wqt[...], n1[...])
-    raw_kv = dot_t(wkv[...], n1[...])
     gain_q, gain_k = column(gq[...]), column(gk[...])
-    first, second = piece * T, HALF + piece * T
-    c = jnp.concatenate([cos[:, first : first + T], cos[:, second : second + T]], axis=1)
-    s = jnp.concatenate([sin[:, first : first + T], sin[:, second : second + T]], axis=1)
-
-    def path(v, gain, factor, keep, index):
-        r = lax.rsqrt(jnp.mean(v * v, axis=0, keepdims=True) + EPS)
-        scale[index : index + 1, :] = r
-        v = v * r
-        keep[...] = v.astype(bf16)
-        v = v * gain
-        low, high = v[:64], v[64:]
-        return (
-            ((low * c - high * s) * factor).astype(bf16),
-            ((high * c + low * s) * factor).astype(bf16),
-        )
-
-    scale[...] = jnp.zeros_like(scale)
-    for h in range(LH):
-        heads = slice(h * HEAD, (h + 1) * HEAD)
-        low, high = path(raw[heads], gain_q, HEAD ** (-0.5), qn.at[heads, :], h)
-        qt[h * HEAD : h * HEAD + 64, :] = low
-        qt[h * HEAD + 64 : (h + 1) * HEAD, :] = high
-    key = raw_kv[:HEAD].astype(bf16)
-    low, high = path(key.astype(f32), gain_k, 1.0, kn, LH)
-    kt[:64, :] = low
-    kt[64:, :] = high
-    vt[...] = raw_kv[HEAD:].astype(bf16)
-
-
-def qkv(piece, *args):
-    return call(
-        functools.partial(qkv_body, piece),
-        f"qkv{piece}",
-        [
-            sds((LH * HEAD, 2 * T), bf16),
-            sds((LH * HEAD, 2 * T), bf16),
-            sds((HEAD, 2 * T), bf16),
-            sds((HEAD, 2 * T), bf16),
-            sds((HEAD, 2 * T), bf16),
-            sds((8, 2 * T), f32),
-            sds((2 * T, D), bf16),
-        ]
-        + ([sds((2 * HEAD, D), bf16)] if piece == 0 else []),
-        [] if piece == 0 else [pltpu.VMEM((2 * HEAD, D), bf16)],
-        args,
+    for number, piece in enumerate(pieces):
+        qn, qt, kn, kt, vt, scale, n1 = outs[7 * number : 7 * number + 7]
+        for half in range(2):
+            x = blocks[2 * number + half][...].astype(f32)
+            r = lax.rsqrt(jnp.mean(x * x, axis=-1, keepdims=True) + EPS)
+            n1[half * T : (half + 1) * T, :] = (x * r * g1[...]).astype(bf16)
+        raw = dot_t(wqt[...], n1[...])
+        raw_kv = dot_t(wkv[...], n1[...])
+        first, second = piece * T, HALF + piece * T
+        c = jnp.concatenate([cos[:, first : first + T], cos[:, second : second + T]], axis=1)
+        s = jnp.concatenate([sin[:, first : first + T], sin[:, second : second + T]], axis=1)
+
+        def path(v, gain, factor, keep, index):
+            r = lax.rsqrt(jnp.mean(v * v, axis=0, keepdims=True) + EPS)
+            scale[index : index + 1, :] = r
+            v = v * r
+            keep[...] = v.astype(bf16)
+            v = v * gain
+            low, high = v[:64], v[64:]
+            return (
+                ((low * c - high * s) * factor).astype(bf16),
+                ((high * c + low * s) * factor).astype(bf16),
+            )
+
+        scale[...] = jnp.zeros_like(scale)
+        for h in range(LH):
+            heads = slice(h * HEAD, (h + 1) * HEAD)
+            low, high = path(raw[heads], gain_q, HEAD ** (-0.5), qn.at[heads, :], h)
+            qt[h * HEAD : h * HEAD + 64, :] = low
+            qt[h * HEAD + 64 : (h + 1) * HEAD, :] = high
+        key = raw_kv[:HEAD].astype(bf16)
+        low, high = path(key.astype(f32), gain_k, 1.0, kn, LH)
+        kt[:64, :] = low
+        kt[64:, :] = high
+        vt[...] = raw_kv[HEAD:].astype(bf16)
+
+
+def qkv(pieces, core, blocks, *args):
+    outs = [
+        sds((LH * HEAD, 2 * T), bf16),
+        sds((LH * HEAD, 2 * T), bf16),
+        sds((HEAD, 2 * T), bf16),
+        sds((HEAD, 2 * T), bf16),
+        sds((HEAD, 2 * T), bf16),
+        sds((8, 2 * T), f32),
+        sds((2 * T, D), bf16),
+    ] * len(pieces)
+    keep = 0 in pieces
+    return call(
+        functools.partial(qkv_body, pieces),
+        "qkv" + "".join(str(p) for p in pieces),
+        outs + ([sds((2 * HEAD, D), bf16)] if keep else []),
+        [] if keep else [pltpu.VMEM((2 * HEAD, D), bf16)],
+        (core, *blocks, *args),
         smem=(0,),
     )
 
@@ -762,8 +755,10 @@
     )
 
 
-def qkv_grad_body(where, n1t, dq0, dq1, own, sib, wa, wb, tot, dt):
-    @pl.when(pl.program_id(0) == 0)
+def qkv_grad_body(where, n1t, dq0, dq1, own, sib, w0, w1, w2, w3, tot, dt):
+    step = pl.program_id(0)
+
+    @pl.when(step == 0)
     def _():
         tot[:, :HALF] = (own[:, :HALF].astype(f32) + sib[:, HALF:].astype(f32)).astype(bf16)
         tot[:, HALF:] = (own[:, HALF:].astype(f32) + sib[:, :HALF].astype(f32)).astype(bf16)
@@ -774,10 +769,13 @@
         dt[576:, :] = jnp.where(upper, tot[192:, :], tot[128:192, :])
 
     grad = dot_t(n1t[...], dt[...]).astype(bf16)
-    for col in range(4):
-        dx = lax.rem(col + 4 - where[1], 4)
-        wa[0, dx] = grad[col * 128 : col * 128 + 64, :]
-        wb[dx, 0] = grad[col * 128 + 64 : (col + 1) * 128, :]
+    for dz, out in enumerate((w0, w1, w2, w3)):
+
+        @pl.when(step == dz)
+        def _():
+            for col in range(4):
+                dx = lax.rem(col + 4 - where[1], 4)
+                out[dx] = grad[col * 128 : (col + 1) * 128, :]
 
 
 def qkv_grad(where, n1t, dq0, dq1, own, sib):
@@ -786,26 +784,29 @@
         "qkv_weight_grad",
         (4,),
         [
-            rows_of((512, ROWS)),
+            pl.BlockSpec((512, ROWS), lambda i, w: (lax.rem(i + w[0], 4), 0)),
             whole((512, HALF)),
             whole((512, HALF)),
             whole((2 * HEAD, ROWS)),
             whole((2 * HEAD, ROWS)),
         ],
-        [
-            pl.BlockSpec((1, 4, 64, 640), lambda i, w: (lax.rem(i + 4 - w[0], 4), 0, 0, 0)),
-            pl.BlockSpec((4, 1, 64, 640), lambda i, w: (0, lax.rem(i + 4 - w[0], 4), 0, 0)),
-            whole((2 * HEAD, ROWS)),
-        ],
-        [
-            sds((4, 4, 64, 640), bf16),
-            sds((4, 4, 64, 640), bf16),
-            sds((2 * HEAD, ROWS), bf16),
-        ],
+        [whole((4, 128, 640))] * 4 + [whole((2 * HEAD, ROWS))],
+        [sds((4, 128, 640), bf16)] * 4 + [sds((2 * HEAD, ROWS), bf16)],
         [pltpu.VMEM((640, ROWS), bf16)],
         (where, n1t, dq0, dq1, own, sib),
         scalars=1,
     )
+
+
+def add_body(a, b, c, d, *outs):
+    for i, out in enumerate(outs):
+        out[...] = (
+            (a[i].astype(f32) + b[i].astype(f32)) + (c[i].astype(f32) + d[i].astype(f32))
+        ).astype(bf16)
+
+
+def add_parts(parts):
+    return call(add_body, "add_parts", [sds((128, 640), bf16)] * 4, [], tuple(parts))
 
 
 def normed_grad_body(wa, wb, wkv, dq0, dqr, tot, n0, n1, n2, n3, b0, b1, b2, b3, gg1, grads):
@@ -849,28 +850,43 @@
     )
 
 
-def place_body(where, *refs):
-    first, second, (gq, gkt, gvt) = refs[:4], refs[4:8], refs[8:]
-    for dz in range(4):
+def add_last_body(a, b, c, d, out):
+    out[...] = (
+        (a[...].astype(f32) + b[...].astype(f32)) + (c[...].astype(f32) + d[...].astype(f32))
+    ).astype(bf16)
+
+
+def add_last(parts):
+    return call(add_last_body, "add_last", [sds((128, 640), bf16)], [], tuple(parts))[0]
+
+
+def stack_body(a, b, c, d, out):
+    for i, part in enumerate((a, b, c, d)):
+        out[i] = part[...]
+
+
+def stack(parts):
+    return call(stack_body, "stack_parts", [sds((4, 128, 640), bf16)], [], tuple(parts))[0]
+
+
+def place_body(where, c0, c1, c2, c3, gq, gkt, gvt):
+    for dz, chunks in enumerate((c0, c1, c2, c3)):
         for dx in range(4):
             chunk = lax.rem(where[0] + dz, 4) * 4 + lax.rem(where[1] + dx, 4)
-            start = pl.multiple_of(chunk * 128, 128)
-            a = first[dz][dx].astype(f32)
-            b = second[dx][dz].astype(f32)
-            gq[pl.ds(start, 64), :] = a[:, :512]
-            gq[pl.ds(start + 64, 64), :] = b[:, :512]
-            both = jnp.concatenate([a[:, 512:], b[:, 512:]], axis=0).T
-            gkt[:, pl.ds(start, 128)] = both[:64]
-            gvt[:, pl.ds(start, 128)] = both[64:]
-
-
-def place(where, first, second):
+            rows = pl.ds(pl.multiple_of(chunk * 128, 128), 128)
+            gq[rows, :] = chunks[dx, :, :512].astype(f32)
+            both = chunks[dx, :, 512:].astype(f32).T
+            gkt[:, rows] = both[:64]
+            gvt[:, rows] = both[64:]
+
+
+def place(where, chunks):
     return call(
         place_body,
         "place_weight_grads",
         [sds((D, 512), f32), sds((64, D), f32), sds((64, D), f32)],
         [],
-        (where, *first, *second),
+        (where, *chunks),
         smem=(0,),
     )
 
@@ -900,11 +916,6 @@
     return lax.ppermute(x, "shard", [(i, (i + 2 * dy) % 8) for i in range(8)])
 
 
-def gather_blocks(x):
-    first = [x] + [from_chip(x, dy) for dy in (1, 2, 3)]
-    return first, [sibling(b) for b in first]
-
-
 def exchange(x):
     return lax.all_to_all(x, ALL, split_axis=0, concat_axis=0, tiled=True)
 
@@ -924,33 +935,12 @@
     return on_expert(x, distance, 0) if axis == 0 else on_expert(x, 0, distance)
 
 
-def reduce_step(x, axis):
-    got = [move(x[d], axis, d) for d in (1, 3, 2)]
-    return (
-        x[0].astype(f32) + got[0].astype(f32) + got[1].astype(f32) + got[2].astype(f32)
-    ).astype(bf16)
-
-
-def gather_step(x, axis):
+def collect(parts, axis):
+    return [parts[0]] + [move(parts[d], axis, d) for d in (1, 3, 2)]
+
+
+def share(x, axis):
     return [x] + [move(x, axis, (4 - d) % 4) for d in (1, 2, 3)]
-
-
-def sum_over_experts(a, b, other):
-    a1, b1 = reduce_step(a, 0), reduce_step(b, 1)
-    a2, b2 = reduce_step(a1, 1), reduce_step(b1, 0)
-    a3, b3 = jnp.stack(gather_step(a2, 1)), jnp.stack(gather_step(b2, 0))
-    a3, b3, other = lax.optimization_barrier((a3, b3, other))
-    return gather_step(a3, 0), gather_step(b3, 1), other, (a1, b1)
-
-
-def sum_everywhere(x):
-    x = x + sibling(x)
-    moved = [to_chip(x, d) for d in (1, 3, 2)]
-    x = x + moved[0] + moved[1] + moved[2]
-    for axis in (0, 1):
-        moved = [move(x, axis, d) for d in (1, 3, 2)]
-        x = x + moved[0] + moved[1] + moved[2]
-    return x
 
 
 def after(value, *others):
@@ -970,7 +960,8 @@
     gq = query_gain.astype(f32).reshape(1, HEAD)
     gk = key_gain.astype(f32).reshape(1, HEAD)
 
-    x_own, x_sib = gather_blocks(block_input)
+    x_own = [block_input] + [from_chip(block_input, dy) for dy in (1, 2, 3)]
+    x_sib = [sibling(block_input)]
 
     chips = (chip + jnp.arange(4)) % 4
     order = jnp.concatenate([chips * 2 + core, chips * 2 + 1 - core])
@@ -999,15 +990,23 @@
     wo_s = sibling(w_out)
     wq_ts = sibling(wq_t)
 
-    def piece(dy):
-        return qkv(
-            dy, core_id, x_own[dy], x_sib[dy], g1, wq_t, wk_t, wk_s, wv_t, wv_s, gq, gk, cos, sin
-        )
-
-    pieces = {dy: piece(dy) for dy in (0, 1, 3, 2)}
-    wkv = pieces[0][7]
-    qh, q, kh, k, v, scales, n1 = zip(*(pieces[dy][:7] for dy in range(4)))
-    og_wire = after(pack(out_grad, assign_t), x_own[2], q[0], q[1], q[3])
+    weights = (g1, wq_t, wk_t, wk_s, wv_t, wv_s, gq, gk, cos, sin)
+    zero = qkv((0,), core_id, (x_own[0], x_sib[0]), *weights)
+    og_wire = pack(out_grad, assign_t)
+    x_own[1], x_own[3], q_first, og_wire = lax.optimization_barrier(
+        (x_own[1], x_own[3], zero[1], og_wire)
+    )
+    x_sib = [x_sib[0], sibling(x_own[1]), None, sibling(x_own[3])]
+    x_sib[1], x_sib[3], x_own[2], og_wire = lax.optimization_barrier(
+        (x_sib[1], x_sib[3], x_own[2], og_wire)
+    )
+    x_sib[2] = sibling(x_own[2])
+    near = qkv((1, 3), core_id, (x_own[1], x_sib[1], x_own[3], x_sib[3]), *weights)
+    far = qkv((2,), core_id, (x_own[2], x_sib[2]), *weights)
+    wkv = zero[7]
+    pieces = [zero[:7], near[:7], far[:7], near[7:14]]
+    qh, q, kh, k, v, scales, n1 = zip(*pieces)
+    q = (q_first,) + q[1:]
     got_grads = exchange(og_wire)
     ot0, ot1, linv, qt, kt, kn, vn = attend(q, k, v, info)
     blocks = outproj(ot0, sibling(ot1), w_out, wo_s)
@@ -1042,17 +1041,19 @@
         where, expert_list, slot_list, gate_list, back_wire, hidden, n2, probs, gates, ids,
         out_grad, g2, w_router,
     )
-    g_own, g_sib = gather_blocks(gatt)
+    g_own = [gatt] + [from_chip(gatt, dy) for dy in (1, 2, 3)]
     router_parts = lax.all_to_all(
         grouter.reshape(8, 2 * T, E), "shard", split_axis=0, concat_axis=0, tiled=True
     )
     router_sum = jnp.sum(router_parts.astype(f32), axis=0).astype(bf16)
+    g_own[1], g_own[2], g_own[3], router_sum = lax.optimization_barrier(
+        (g_own[1], g_own[2], g_own[3], router_sum)
+    )
+    g_sib = [sibling(block) for block in g_own]
     dt_near = head_grad(
         [g_own[0], g_sib[0], g_own[1], g_sib[1], g_own[3], g_sib[3]], w_out
     )
-    g_far, dt_near, router_sum = lax.optimization_barrier(
-        ((g_own[2], g_sib[2]), dt_near, router_sum)
-    )
+    g_far, dt_near = lax.optimization_barrier(((g_own[2], g_sib[2]), dt_near))
     g_own[2], g_sib[2] = g_far
 
     gwout, dt_far = pre(g_own + g_sib, ot0, ot1, w_out)
@@ -1063,41 +1064,50 @@
         qh, kh, scales, qt, kt, kn, vn, dt_near, dt_far, ot0, ot1, linv, info, cos, sin, gq, gk
     )
     dq_sib, dkv_sib = sibling(dq1), sibling(dkv)
-    gw_a, gw_b, dkv_total = qkv_grad(where, n1_t, dq0, dq1, dkv, dkv_sib)
+    *parts, dkv_total = qkv_grad(where, n1_t, dq0, dq1, dkv, dkv_sib)
     returned, dq0 = lax.optimization_barrier((returned, dq0))
     result = result_rows(expert_list, slot_list, gate_list, returned, hidden)
     blocks = normed_grad(wq_t, wq_ts, wkv, dq0, dq_sib, dkv_total, n1)
-    gg1 = blocks[4][0:1] / g1
+    gg1 = blocks[4][0] / g1[0]
+    vector = jnp.concatenate([gg1, gg2[0], ggq[0], ggk[0]])
+    per = vector.shape[0] // E
+    wide = jnp.pad(vector.reshape(E, per), ((0, 0), (0, 128 - per))).reshape(E, 1, 128)
     blocks = [blocks[0]] + spread(blocks)
-    gw_a, gw_b, (blocks, early_sums), begun = sum_over_experts(gw_a, gw_b, (blocks, early_sums))
+    mine = jnp.sum(exchange(wide), axis=0)
+
+    parts = collect(parts, 0)
+    parts, mine = lax.optimization_barrier((parts, mine))
+    parts = collect(add_parts(parts), 1)
+    parts, blocks = lax.optimization_barrier((parts, blocks))
+    chunks = stack(share(add_last(parts), 1))
+    chunks, mine, early_sums = lax.optimization_barrier((chunks, mine, early_sums))
+    chunks = share(chunks, 0)
+    first = mine.astype(bf16)
+    second = (mine - first.astype(f32)).astype(bf16)
+    router_part = lax.dynamic_slice(early_sums[1], (owner * SEG, 0), (SEG, E))
+    small = jnp.concatenate([router_part, first, second, jnp.zeros((6, 128), bf16)], axis=0)
+    everyone = exchange(jnp.broadcast_to(small[None], (E, SEG + 8, 128)))
+    grad_input = final(blocks, block_input, ghid, g1)
+    chunks, everyone, early_sums, grad_input, result = lax.optimization_barrier(
+        (chunks, everyone, early_sums, grad_input, result)
+    )
+    vector = everyone[:, SEG, :per].astype(f32) + everyone[:, SEG + 1, :per].astype(f32)
+    vector = vector.reshape(-1)
+    grad_router = everyone[:, :SEG].reshape(16, 8, SEG, E).transpose(1, 0, 2, 3)
+    grad_router = grad_router.reshape(D, E).astype(f32)
     grad_wout = early_sums[0].astype(f32)
-    grad_router = lax.all_gather(early_sums[1], "shard", axis=0, tiled=True).astype(f32)
-    grad_input = final(blocks, block_input, ghid, g1)
-
-    vector = sum_everywhere(
-        after(jnp.concatenate(
-            [
-                gg1.reshape(SEG, 128),
-                gg2.reshape(SEG, 128),
-                ggq[0:1],
-                ggk[0:1],
-                jnp.zeros((6, 128), f32),
-            ],
-            axis=0,
-        ), *begun)
-    )
-    grad_wq, grad_wk, grad_wv = place(where, gw_a, gw_b)
+    grad_wq, grad_wk, grad_wv = place(where, chunks)
     return (
         result,
         grad_input,
-        vector[:SEG].reshape(D),
+        vector[:D],
         grad_wq,
         grad_wk.T,
         grad_wv.T,
-        vector[2 * SEG],
-        vector[2 * SEG + 1],
+        vector[2 * D : 2 * D + HEAD],
+        vector[2 * D + HEAD :],
         grad_wout,
-        vector[SEG : 2 * SEG].reshape(D),
+        vector[D : 2 * D],
         grad_router,
         grad_wgate[None],
         grad_wup[None],

time: 522 us -> 493 us (0.944)
  starting transfers between devices: 109 us -> 86.9 us
  blocking collectives: 35.9 us -> 20.2 us
  waiting for transfers between devices: 146 us -> 158 us
    ppermute x30 -> x12, waiting for transfers between devices: 26.2 us -> 50.6 us  [on_expert(): return lax.ppermute(x, 'expert', pairs)]
    all_to_all x0 -> x1, waiting for transfers between devices: none -> 23.3 us  [on_device(): lax.all_to_all(grouter.reshape(8, 2 * T, E), 'shard', split_axis=0, conca...]
    all_gather x1 -> x0, blocking collectives: 22.5 us -> none  [on_device(): lax.all_gather(early_sums[1], 'shard', axis=0, tiled=True).astype(f32)]
    ppermute x6, waiting for transfers between devices: 29.9 us -> 7.68 us  [from_chip(): return lax.ppermute(x, 'shard', [(i, (i - 2 * dy) % 8) for i in range(8)])]
    ppermute x16 -> x15, starting transfers between devices: 30.3 us -> 9.84 us  [sibling(): return lax.ppermute(x, 'shard', [(i, i ^ 1) for i in range(8)])]
    ppermute x30 -> x12, starting transfers between devices: 33.5 us -> 15.5 us  [on_expert(): return lax.ppermute(x, 'expert', pairs)]
    all_to_all x4 -> x5, starting transfers between devices: 27.7 us -> 39.8 us  [exchange(): return lax.all_to_all(x, ALL, split_axis=0, concat_axis=0, tiled=True)]
    psum x1, waiting for transfers between devices: 20.1 us -> 9 us  [on_device(): early_sums = lax.psum((gwout, router_sum), 'expert')]
  transfers between devices with their start and end apart: 66 -> 46, of which waited for: 21 -> 20; matrix products, arithmetic and copies ran while one was open for 8% -> 7% of each run, Pallas kernels for 23% -> 25%
where the time goes in v4:
time: 493 us; the launch traced here: 486 us
  waiting for transfers between devices  158 us (32%)
  Pallas kernels  157 us (32%)
  starting transfers between devices  86.9 us (18%)
  blocking collectives  20.2 us (4%)
  local copies, waits for them, and re-layouts  19.1 us (4%)
  matrix products  16.6 us (3%)
  between operations  14.6 us (3%)
  other arithmetic  12.6 us (3%)
    pallas_call x20, Pallas kernels, call(): pl.pallas_call(kernel, out_shape=outs, in_specs=in_specs, out_specs=[pl.B...  127 us
    ppermute x12, waiting for transfers between devices, on_expert(): return lax.ppermute(x, 'expert', pairs)  50.6 us
    all_to_all x5, waiting for transfers between devices, exchange(): return lax.all_to_all(x, ALL, split_axis=0, concat_axis=0, tiled=True)  40.2 us
    all_to_all x5, starting transfers between devices, exchange(): return lax.all_to_all(x, ALL, split_axis=0, concat_axis=0, tiled=True)  39.8 us
    pallas_call x4, Pallas kernels, grid_call(): pl.pallas_call(kernel, out_shape=outs, grid_spec=pltpu.PrefetchScalarGrid...  30.2 us
    all_to_all x1, waiting for transfers between devices, on_device(): lax.all_to_all(grouter.reshape(8, 2 * T, E), 'shard', split_axis=0, conca...  23.3 us
    ppermute x6, waiting for transfers between devices, to_chip(): return lax.ppermute(x, 'shard', [(i, (i + 2 * dy) % 8) for i in range(8)])  21.6 us
    all_to_all x1, blocking collectives, exchange(): return lax.all_to_all(x, ALL, split_axis=0, concat_axis=0, tiled=True)  20.2 us
  transfers between devices with their start and end apart: 46, of which 20 were waited for; matrix products, arithmetic and copies ran while one was open for 7% of the time, Pallas kernels for 25%

profile of v4, /device:TPU:1, one launch (start us, length us, event | category | flops | bytes accessed | tf_op | source)
XLA Modules:
  0.0 485.8 jit_solution(14019943525958580310)
XLA Ops:
  7.2 3.6 collective-permute-start
  15.8 2.0 route_tables.1
  19.0 4.2 pack_rows.1
  23.8 4.0 copy.38
  27.8 1.8 multiply_sine_fusion
  29.6 2.0 collective-permute-start.7
  31.6 5.0 %qkv0.1 = (bf16[512,256]{1,0:T(8,128)(2,1)}, bf16[512,256]{1,0:T(8,128)(2,1)}, bf16[128,256]{1,0:T(8,128)(2,1)}, bf16[128,256]{1,0:T(8,128)(2,1)}, bf16[128,256]...) custom-call(s32[1]{0:T(128)} %bitcast.2.refs_0_, ...), custom_call_target="tpu_custom_call" | custom-call | flops 1 | bytes 1 | tf_op jit(solution)/shard_map/qkv0/pallas_call | solution.py:61
  37.2 7.7 %collective-permute-done.7.refs_1_ = bf16[128,2048]{1,0:T(8,128)(2,1)} collective-permute-done((bf16[128,2048]{1,0:T(8,128)(2,1)S(1)}, bf16[128,2048]{1,0:T(8,128)(2,1)}, u32[]{:S(2)}, u32[]{:S(2)}) %collective-permute-start.7) | collective-permute-done | bytes 524320 | tf_op jit(solution)/shard_map/ppermute | solution.py:912
  44.9 11.2 %all-to-all-start.1 = ((bf16[128,88,128]{2,1,0:T(8,128)(2,1)}), bf16[128,88,128]{2,1,0:T(8,128)(2,1)}, u32[]{:S(2)}, u32[]{:S(2)}) async-start(bf16[128,88,128]{2,1,0:T(8,128)(2,1)} %pack_rows.1), calls=%async_computation.1 | async-start | bytes 5767168 | tf_op jit(solution)/shard_map/all_to_all | solution.py:920
  58.4 6.3 %qkv13.1 = (bf16[512,256]{1,0:T(8,128)(2,1)}, bf16[512,256]{1,0:T(8,128)(2,1)}, bf16[128,256]{1,0:T(8,128)(2,1)}, bf16[128,256]{1,0:T(8,128)(2,1)}, bf16[128,256...) custom-call(s32[1]{0:T(128)} %bitcast.2.refs_0_, ...), custom_call_target="tpu_custom_call" | custom-call | flops 1 | bytes 1 | tf_op jit(solution)/shard_map/qkv13/pallas_call | solution.py:61
  65.5 4.9 %qkv2.1 = (bf16[512,256]{1,0:T(8,128)(2,1)}, bf16[512,256]{1,0:T(8,128)(2,1)}, bf16[128,256]{1,0:T(8,128)(2,1)}, bf16[128,256]{1,0:T(8,128)(2,1)}, bf16[128,256]...) custom-call(s32[1]{0:T(128)} %bitcast.2.refs_0_, bf16[128,2048]{1,0:T(8,128)(2,1)} %collective-permute-done.7.refs_1_, ...), custom_call_target="tpu_custom_call" | custom-call | flops 1 | bytes 1 | tf_op jit(solution)/shard_map/qkv2/pallas_call | solution.py:61
  70.4 10.9 %attend.1 = (bf16[512,512]{1,0:T(8,128)(2,1)}, bf16[512,512]{1,0:T(8,128)(2,1)}, f32[8,1024]{1,0:T(8,128)}, bf16[512,1024]{1,0:T(8,128)(2,1)}, bf16[128,1024]{1,...) custom-call(bf16[512,256]{1,0:T(8,128)(2,1)} %get-tuple-element.162.refs_0_, ...), custom_call_target="tpu_custom_call" | custom-call | flops 1 | bytes 6600001 | tf_op jit(solution)/shard_map/attend/pallas_call | solution.py:61
  81.7 1.7 collective-permute-done.9.otr
  84.3 6.2 %out_projection.1 = (bf16[128,2048]{1,0:T(8,128)(2,1)}, bf16[128,2048]{1,0:T(8,128)(2,1)}, bf16[128,2048]{1,0:T(8,128)(2,1)}, bf16[128,2048]{1,0:T(8,128)(2,1)}) custom-call(bf16[512,512]{1,0:T(8,128)(2,1)} %get-tuple-element.180.ot0.refs_8_.refs_18_, bf16[512,512]{1,0:T(8,128)(2,1)} %copy-done.12, bf16[512,2048]{1,0:T(8,128)(2,1)} %refs_10_.1, ...), custom_call_target="tpu_custom_call" | custom-call | flops 1 | bytes 3000001 | tf_op jit(solution)/shard_map/out_projection/pallas_call | solution.py:74
  91.1 2.1 collective-permute-start.12
  95.2 9.9 %collective-permute-done.11.b1 = bf16[128,2048]{1,0:T(8,128)(2,1)S(1)} collective-permute-done((bf16[128,2048]{1,0:T(8,128)(2,1)}, bf16[128,2048]{1,0:T(8,128)(2,1)S(1)}, u32[]{:S(2)}, u32[]{:S(2)}) %collective-permute-start.11) | collective-permute-done | bytes 524320 | tf_op jit(solution)/shard_map/ppermute | solution.py:916
  105.0 11.7 %collective-permute-done.13.b3 = bf16[128,2048]{1,0:T(8,128)(2,1)} collective-permute-done((bf16[128,2048]{1,0:T(8,128)(2,1)}, bf16[128,2048]{1,0:T(8,128)(2,1)}, u32[]{:S(2)}, u32[]{:S(2)}) %collective-permute-start.13) | collective-permute-done | bytes 524320 | tf_op jit(solution)/shard_map/ppermute | solution.py:916
  116.8 5.6 %router.1 = (f32[128,2048]{1,0:T(8,128)}, bf16[128,2048]{1,0:T(8,128)(2,1)}, f32[128,128]{1,0:T(8,128)}, f32[128,128]{1,0:T(8,128)}, bf16[128,88,128]{2,1,0:T(8,128)(2,1)}) custom-call(bf16[128,2048]{1,0:T(8,128)(2,1)} %get-tuple-element.182.b0, bf16[128,2048]{1,0:T(8,128)(2,1)} %copy-done.14, bf16[128,2048]{1,0:T(8,128)(2,1)} %collective-permute-done.12.b2, ...), custom_call_target="tpu_custom_call" | custom-call | flops 1 | bytes 3600001 | tf_op jit(solution)/shard_map/router/pallas_call | solution.py:61
  122.4 9.7 %all-to-all-start = ((bf16[128,88,128]{2,1,0:T(8,128)(2,1)}), bf16[128,88,128]{2,1,0:T(8,128)(2,1)}, u32[]{:S(2)}, u32[]{:S(2)}) async-start(bf16[128,88,128]{2,1,0:T(8,128)(2,1)} %get-tuple-element.187), calls=%async_computation | async-start | bytes 5767168 | tf_op jit(solution)/shard_map/all_to_all | solution.py:920
  133.3 5.5 %transpose_rows.1.n1t = bf16[2048,1024]{1,0:T(8,128)(2,1)} custom-call(bf16[256,2048]{1,0:T(8,128)(2,1)} %get-tuple-element.192.n0, bf16[256,2048]{1,0:T(8,128)(2,1)} %get-tuple-element.193.n1, bf16[256,2048]{1,0:T(8,128)(2,1)} %get-tuple-element.194.n2, bf16[256,2048]{1,0:T(8,128)(2,1)} %get-tuple-element.195.n3), custom_call_target="tpu_custom_call" | custom-call | flops 1 | bytes 3600001 | tf_op jit(solution)/shard_map/transpose_rows/pallas_call | solution.py:61
  139.5 7.5 %expert_grad_rows.1 = (bf16[640,2048]{1,0:T(8,128)(2,1)}, f32[640,768]{1,0:T(8,128)}) custom-call(bf16[128,88,128]{2,1,0:T(8,128)(2,1)} %all-to-all-done.1.wire, bf16[768,2048]{1,0:T(8,128)(2,1)} %bitcast.61), custom_call_target="tpu_custom_call" | custom-call | flops 1 | bytes 4800001 | tf_op jit(solution)/shard_map/expert_grad_rows/pallas_call | solution.py:61
  146.9 23.9 %all-to-all-done.wire = bf16[128,88,128]{2,1,0:T(8,128)(2,1)} async-done(((bf16[128,88,128]{2,1,0:T(8,128)(2,1)}), bf16[128,88,128]{2,1,0:T(8,128)(2,1)}, u32[]{:S(2)}, u32[]{:S(2)}) %all-to-all-start) | async-done | bytes 2883616 | tf_op jit(solution)/shard_map/all_to_all | solution.py:920
  170.8 18.6 %expert_main.1 = (bf16[128,88,128]{2,1,0:T(8,128)(2,1)}, bf16[640,2048]{1,0:T(8,128)(2,1)}, bf16[640,768]{1,0:T(8,128)(2,1)}, bf16[640,768]{1,0:T(8,128)(2,1)}, ...) custom-call(bf16[128,88,128]{2,1,0:T(8,128)(2,1)} %all-to-all-done.wire, bf16[2048,768]{1,0:T(8,128)(2,1)} %bitcast.64, ...), custom_call_target="tpu_custom_call" | custom-call | flops 1 | bytes 10800001 | tf_op jit(solution)/shard_map/expert_main/pallas_call | solution.py:61
  189.4 5.9 %all-to-all-start.2 = ((bf16[128,88,128]{2,1,0:T(8,128)(2,1)}), bf16[128,88,128]{2,1,0:T(8,128)(2,1)}, u32[]{:S(2)}, u32[]{:S(2)}) async-start(bf16[128,88,128]{2,1,0:T(8,128)(2,1)} %get-tuple-element.220), calls=%async_computation.2 | async-start | bytes 5767168 | tf_op jit(solution)/shard_map/all_to_all | solution.py:920
  197.4 6.6 %expert_out.1 = bf16[128,80,128]{2,1,0:T(8,128)(2,1)} custom-call(bf16[640,768]{1,0:T(8,128)(2,1)} %get-tuple-element.226.act, bf16[768,2048]{1,0:T(8,128)(2,1)} %bitcast.62), custom_call_target="tpu_custom_call" | custom-call | flops 1 | bytes 4200001 | tf_op jit(solution)/shard_map/expert_out/pallas_call | solution.py:61
  204.0 7.5 %fusion.8 = f32[2048,768]{1,0:T(8,128)} fusion(bf16[640,2048]{1,0:T(8,128)(2,1)} %get-tuple-element.227, bf16[640,768]{1,0:T(8,128)(2,1)} %get-tuple-element.228), kind=kOutput, calls=%fused_computation.34 | convolution fusion | flops 2013265920 | bytes 9895936 | tf_op jit(solution)/shard_map/dot_general | solution.py:1031
  211.5 4.6 fusion.9
  216.1 4.5 fusion.10
  220.6 13.4 %all-to-all-done.2.wire = bf16[128,88,128]{2,1,0:T(8,128)(2,1)} async-done(((bf16[128,88,128]{2,1,0:T(8,128)(2,1)}), bf16[128,88,128]{2,1,0:T(8,128)(2,1)}, u32[]{:S(2)}, u32[]{:S(2)}) %all-to-all-start.2) | async-done | bytes 2883616 | tf_op jit(solution)/shard_map/all_to_all | solution.py:920
  234.0 7.1 %combine_grads.1 = (f32[128,2048]{1,0:T(8,128)}, bf16[128,2048]{1,0:T(8,128)(2,1)}, bf16[2048,128]{1,0:T(8,128)(2,1)}, f32[1,2048]{1,0:T(1,128)}) custom-call(s32[3]{0:T(128)} %pad_add_fusion.where, s32[512]{0:T(512)} %reshape.209.experts, s32[512]{0:T(512)} %reshape.210.slots, f32[512]{0:T(512)} %reshape.208.gate_list, ...), custom_call_target="tpu_custom_call" | custom-call | flops 1 | bytes 4200001 | tf_op jit(solution)/shard_map/combine_grads/pallas_call | solution.py:61
  242.6 6.8 %all-to-all-start.3 = ((bf16[8,256,128]{2,1,0:T(8,128)(2,1)}), bf16[8,256,128]{2,1,0:T(8,128)(2,1)S(1)}, u32[]{:S(2)}, u32[]{:S(2)}) async-start(bf16[8,256,128]{2,1,0:T(8,128)(2,1)} %bitcast.76), calls=%async_computation.3 | async-start | bytes 1048576 | tf_op jit(solution)/shard_map/all_to_all | solution.py:1045
  249.4 23.3 %all-to-all-done.3 = bf16[8,256,128]{2,1,0:T(8,128)(2,1)S(1)} async-done(((bf16[8,256,128]{2,1,0:T(8,128)(2,1)}), bf16[8,256,128]{2,1,0:T(8,128)(2,1)S(1)}, u32[]{:S(2)}, u32[]{:S(2)}) %all-to-all-start.3) | async-done | bytes 524320 | tf_op jit(solution)/shard_map/all_to_all | solution.py:1045
  273.5 1.5 collective-permute-start.20
  278.1 5.3 %head_grad.1.refs_16_ = bf16[512,768]{1,0:T(8,128)(2,1)} custom-call(bf16[128,2048]{1,0:T(8,128)(2,1)} %get-tuple-element.236.refs_0_, bf16[128,2048]{1,0:T(8,128)(2,1)} %copy-done.7, bf16[128,2048]{1,0:T(8,128)(2,1)} %copy-done.5, bf16[128,2048]{1,0:T(8,128)(2,1)} %copy-done.8, bf16[128,2048]{1,0:T(8,128)(2,1)} %copy-done.6, ...), custom_call_target="tpu_custom_call" | custom-call | flops 1 | bytes 2400001 | tf_op jit(solution)/shard_map/head_grad/pallas_call | solution.py:61
  283.4 7.3 %out_projection_grad.1 = (bf16[512,2048]{1,0:T(8,128)(2,1)}, bf16[512,256]{1,0:T(8,128)(2,1)}) custom-call(bf16[128,2048]{1,0:T(8,128)(2,1)} %get-tuple-element.236.refs_0_, bf16[128,2048]{1,0:T(8,128)(2,1)} %copy-done.5, bf16[128,2048]{1,0:T(8,128)(2,1)} %collective-permute-done.16.refs_2_, bf16[128,2048]{1,0:T(8,128)(2,1)} %copy-done.6, ...), custom_call_target="tpu_custom_call" | custom-call | flops 1 | bytes 4200001 | tf_op jit(solution)/shard_map/out_projection_grad/pallas_call | solution.py:74
  290.7 4.8 all-to-all-start.4
  296.3 18.9 %attend_grad.1 = (bf16[512,512]{1,0:T(8,128)(2,1)}, bf16[512,512]{1,0:T(8,128)(2,1)}, bf16[256,1024]{1,0:T(8,128)(2,1)}, f32[8,128]{1,0:T(8,128)}, f32[8,128]{1,0:T(8,128)}) custom-call(bf16[512,256]{1,0:T(8,128)(2,1)} %get-tuple-element.201.refs_0_, bf16[512,256]{1,0:T(8,128)(2,1)} %get-tuple-element.202.refs_1_, ...), custom_call_target="tpu_custom_call" | custom-call | flops 1 | bytes 1 | tf_op jit(solution)/shard_map/attend_grad/pallas_call | solution.py:61
  315.2 1.8 collective-permute-start.22
  316.9 1.7 collective-permute-done.22.sib
  319.5 9.2 %qkv_weight_grad.1 = (bf16[4,128,640]{2,1,0:T(8,128)(2,1)}, bf16[4,128,640]{2,1,0:T(8,128)(2,1)}, bf16[4,128,640]{2,1,0:T(8,128)(2,1)}, bf16[4,128,640]{2,1,0:T(8,128)(2,1)}, bf16[256,1024]{1,0:T(8,128)(2,1)}) custom-call(s32[3]{0:T(128)} %pad_add_fusion.where, bf16[2048,1024]{1,0:T(8,128)(2,1)} %transpose_rows.1.n1t, ...), custom_call_target="tpu_custom_call" | custom-call | flops 1 | bytes 1 | tf_op jit(solution)/shard_map/qkv_weight_grad/pallas_call | solution.py:74
  330.0 1.9 collective-permute-start.24
  334.6 2.9 all-to-all-done.4.wire
  337.5 7.5 %normed_grad.1 = (bf16[128,2048]{1,0:T(8,128)(2,1)}, bf16[128,2048]{1,0:T(8,128)(2,1)}, bf16[128,2048]{1,0:T(8,128)(2,1)}, bf16[128,2048]{1,0:T(8,128)(2,1)}, f32[8,2048]{1,0:T(8,128)}) custom-call(bf16[512,2048]{1,0:T(8,128)(2,1)} %bitcast.4.refs_4_.refs_6_.wa, bf16[512,2048]{1,0:T(8,128)(2,1)} %collective-permute-done.14.wb, ...), custom_call_target="tpu_custom_call" | custom-call | flops 1 | bytes 1 | tf_op jit(solution)/shard_map/normed_grad/pallas_call | solution.py:74
  345.9 2.7 collective-permute-start.31
  348.6 3.2 collective-permute-done.23.b
  353.0 20.2 %all_to_all.35 = f32[128,1,128]{2,1,0:T(1,128)S(1)} all-to-all(f32[128,1,128]{2,1,0:T(1,128)S(1)} %bitcast.78), channel_id=1, replica_groups=mesh['expert'=16,'shard'=8] {'expert','shard'}, dimensions={0} | all-to-all | bytes 131072 | tf_op jit(solution)/shard_map/all_to_all | solution.py:920
  373.4 2.7 add_parts.1
  376.1 2.0 collective-permute-start.27
  378.8 4.4 collective-permute-done.27.b
  383.2 1.6 collective-permute-start.29
  384.8 5.2 %collective-permute-done.29.d = bf16[128,640]{1,0:T(8,128)(2,1)S(1)} collective-permute-done((bf16[128,640]{1,0:T(8,128)(2,1)}, bf16[128,640]{1,0:T(8,128)(2,1)S(1)}, u32[]{:S(2)}, u32[]{:S(2)}) %collective-permute-start.29) | collective-permute-done | bytes 163872 | tf_op jit(solution)/shard_map/ppermute | solution.py:931
  390.7 1.9 add_last.1.a
  397.0 3.0 collective-permute-done.34.c
  400.0 4.0 collective-permute-done.35.d
  404.7 2.0 stack_parts.1.c0
  406.8 9.0 %all-reduce.4.cloned.1.call-done = (bf16[512,2048]{1,0:T(8,128)(2,1)}, bf16[256,128]{1,0:T(8,128)(2,1)}) async-done(((bf16[512,2048]{1,0:T(8,128)(2,1)}, bf16[256,128]{1,0:T(8,128)(2,1)}), (bf16[512,2048]{1,0:T(8,128)(2,1)}, bf16[256,128]{1,0:T(8,128)(2,1)})) %all-reduce.4.cloned.1.call-update) | async-done | bytes 2162704 | tf_op jit(solution)/shard_map/psum | solution.py:1060
  417.5 8.2 %all-to-all-start.6 = ((bf16[128,24,128]{2,1,0:T(8,128)(2,1)}), bf16[128,24,128]{2,1,0:T(8,128)(2,1)S(1)}, u32[]{:S(2)}, u32[]{:S(2)}) async-start(bf16[128,24,128]{2,1,0:T(8,128)(2,1)} %broadcast_in_dim.45), calls=%async_computation.6 | async-start | bytes 1572864 | tf_op jit(solution)/shard_map/all_to_all | solution.py:920
  425.7 3.3 collective-permute-start.36
  430.1 4.5 result.1
  434.6 3.8 input_grad.1
  438.3 26.0 %collective-permute-done.36.c1 = bf16[4,128,640]{2,1,0:T(8,128)(2,1)} collective-permute-done((bf16[4,128,640]{2,1,0:T(8,128)(2,1)}, bf16[4,128,640]{2,1,0:T(8,128)(2,1)}, u32[]{:S(2)}, u32[]{:S(2)}) %collective-permute-start.36) | collective-permute-done | bytes 655392 | tf_op jit(solution)/shard_map/ppermute | solution.py:931
  464.3 3.3 collective-permute-done.38.c3
  469.2 4.1 convert_element_type.98
  474.5 4.3 place_weight_grads.1
  (159 shorter events, 43.5 us)
Async XLA Ops:
  7.2 6.1 %copy-start = (s32[1,1024]{1,0:T(1,128)S(1)}, s32[1,1024]{1,0:T(1,128)}, u32[]{:S(2)}) copy-start(s32[1,1024]{1,0:T(1,128)} %param.32) | copy-start | bytes 12292
  7.2 16.0 %copy-start.23 = (bf16[2048]{0:T(1024)(128)(2,1)S(1)}, bf16[2048]{0:T(1024)(128)(2,1)}, u32[]{:S(2)}) copy-start(bf16[2048]{0:T(1024)(128)(2,1)} %param.19) | copy-start | bytes 12292
  7.2 29.4 %collective-permute-start = (bf16[128,2048]{1,0:T(8,128)(2,1)}, bf16[128,2048]{1,0:T(8,128)(2,1)}, u32[]{:S(2)}, u32[]{:S(2)}) collective-permute-start(bf16[128,2048]{1,0:T(8,128)(2,1)} %x0.3), channel_id=1, source_target_pairs={{0,6},{1,7},{2,0},{3,1},{4,2},{5,3},{6,4},{7,5},{8,14},{9,15},{10,... | collective-permute-start | bytes 1572872 | tf_op jit(solution)/shard_map/ppermute | solution.py:912
  10.8 25.8 %collective-permute-start.1 = (bf16[128,2048]{1,0:T(8,128)(2,1)}, bf16[128,2048]{1,0:T(8,128)(2,1)}, u32[]{:S(2)}, u32[]{:S(2)}) collective-permute-start(bf16[128,2048]{1,0:T(8,128)(2,1)} %x0.3), channel_id=1, source_target_pairs={{0,2},{1,3},{2,4},{3,5},{4,6},{5,7},{6,0},{7,1},{8,10},{9,11},{10,... | collective-permute-start | bytes 1572872 | tf_op jit(solution)/shard_map/ppermute | solution.py:912
  10.8 20.8 %collective-permute-start.2 = (bf16[128,2048]{1,0:T(8,128)(2,1)}, bf16[128,2048]{1,0:T(8,128)(2,1)}, u32[]{:S(2)}, u32[]{:S(2)}) collective-permute-start(bf16[128,2048]{1,0:T(8,128)(2,1)} %x0.3), channel_id=1, source_target_pairs={{0,1},{1,0},{2,3},{3,2},{4,5},{5,4},{6,7},{7,6},{8,9},{9,8},{10,11... | collective-permute-start | bytes 1572872 | tf_op jit(solution)/shard_map/ppermute | solution.py:908
  11.8 17.8 %collective-permute-start.3 = (bf16[64,2048]{1,0:T(8,128)(2,1)}, bf16[64,2048]{1,0:T(8,128)(2,1)S(1)}, u32[]{:S(2)}, u32[]{:S(2)}) collective-permute-start(bf16[64,2048]{1,0:T(8,128)(2,1)} %bitcast.66), channel_id=1, source_target_pairs={{0,1},{1,0},{2,3},{3,2},{4,5},{5,4},{6,7},{7,6},{8,9},{9,8},{10,11... | collective-permute-start | bytes 786440 | tf_op jit(solution)/shard_map/ppermute | solution.py:908
  11.8 19.8 %collective-permute-start.4 = (bf16[64,2048]{1,0:T(8,128)(2,1)}, bf16[64,2048]{1,0:T(8,128)(2,1)}, u32[]{:S(2)}, u32[]{:S(2)}) collective-permute-start(bf16[64,2048]{1,0:T(8,128)(2,1)} %bitcast.70), channel_id=1, source_target_pairs={{0,1},{1,0},{2,3},{3,2},{4,5},{5,4},{6,7},{7,6},{8,9},{9,8},{10,11... | collective-permute-start | bytes 786440 | tf_op jit(solution)/shard_map/ppermute | solution.py:908
  23.2 6.4 %copy-start.2 = (bf16[128,2048]{1,0:T(8,128)(2,1)S(1)}, bf16[128,2048]{1,0:T(8,128)(2,1)}, u32[]{:S(2)}) copy-start(bf16[128,2048]{1,0:T(8,128)(2,1)} %x0.3) | copy-start | bytes 1572868
  29.6 15.3 %collective-permute-start.7 = (bf16[128,2048]{1,0:T(8,128)(2,1)S(1)}, bf16[128,2048]{1,0:T(8,128)(2,1)}, u32[]{:S(2)}, u32[]{:S(2)}) collective-permute-start(bf16[128,2048]{1,0:T(8,128)(2,1)S(1)} %copy-done.2), channel_id=1, source_target_pairs={{0,4},{1,5},{2,6},{3,7},{4,0},{5,1},{6,2},{7,3},{8,12},{9,13},{10,... | collective-permute-start | bytes 1572872 | tf_op jit(solution)/shard_map/ppermute | solution.py:912
  36.6 8.3 %collective-permute-start.5 = (bf16[128,2048]{1,0:T(8,128)(2,1)}, bf16[128,2048]{1,0:T(8,128)(2,1)}, u32[]{:S(2)}, u32[]{:S(2)}) collective-permute-start(bf16[128,2048]{1,0:T(8,128)(2,1)} %collective-permute-done.refs_1_), channel_id=1, source_target_pairs={{0,1},{1,0},{2,3},{3,2},{4,5},{5,4},{6,7},{7,6},{8,9},{9,8},{10,11... | collective-permute-start | bytes 1572872 | tf_op jit(solution)/shard_map/ppermute | solution.py:908
  37.0 7.9 %collective-permute-start.6 = (bf16[128,2048]{1,0:T(8,128)(2,1)}, bf16[128,2048]{1,0:T(8,128)(2,1)}, u32[]{:S(2)}, u32[]{:S(2)}) collective-permute-start(bf16[128,2048]{1,0:T(8,128)(2,1)} %collective-permute-done.1.refs_3_), channel_id=1, source_target_pairs={{0,1},{1,0},{2,3},{3,2},{4,5},{5,4},{6,7},{7,6},{8,9},{9,8},{10,11... | collective-permute-start | bytes 1572872 | tf_op jit(solution)/shard_map/ppermute | solution.py:908
  44.9 77.5 %all-to-all-start.1 = ((bf16[128,88,128]{2,1,0:T(8,128)(2,1)}), bf16[128,88,128]{2,1,0:T(8,128)(2,1)}, u32[]{:S(2)}, u32[]{:S(2)}) async-start(bf16[128,88,128]{2,1,0:T(8,128)(2,1)} %pack_rows.1), calls=%async_computation.1 | async-start | bytes 5767168 | tf_op jit(solution)/shard_map/all_to_all | solution.py:920
  56.1 27.4 %collective-permute-start.10 = (bf16[512,2048]{1,0:T(8,128)(2,1)}, bf16[512,2048]{1,0:T(8,128)(2,1)}, u32[]{:S(2)}, u32[]{:S(2)}) collective-permute-start(bf16[512,2048]{1,0:T(8,128)(2,1)} %refs_10_.1), channel_id=1, source_target_pairs={{0,1},{1,0},{2,3},{3,2},{4,5},{5,4},{6,7},{7,6},{8,9},{9,8},{10,11... | collective-permute-start | bytes 6291464 | tf_op jit(solution)/shard_map/ppermute | solution.py:908
  57.3 7.4 %collective-permute-start.8 = (bf16[128,2048]{1,0:T(8,128)(2,1)}, bf16[128,2048]{1,0:T(8,128)(2,1)S(1)}, u32[]{:S(2)}, u32[]{:S(2)}) collective-permute-start(bf16[128,2048]{1,0:T(8,128)(2,1)} %collective-permute-done.7.refs_1_), channel_id=1, source_target_pairs={{0,1},{1,0},{2,3},{3,2},{4,5},{5,4},{6,7},{7,6},{8,9},{9,8},{10,11... | collective-permute-start | bytes 1572872 | tf_op jit(solution)/shard_map/ppermute | solution.py:908
  81.3 2.2 collective-permute-start.9
  84.3 10.3 %copy-start.25 = (bf16[2048]{0:T(1024)(128)(2,1)S(1)}, bf16[2048]{0:T(1024)(128)(2,1)}, u32[]{:S(2)}) copy-start(bf16[2048]{0:T(1024)(128)(2,1)} %param.26) | copy-start | bytes 12292
  90.4 14.6 %collective-permute-start.11 = (bf16[128,2048]{1,0:T(8,128)(2,1)}, bf16[128,2048]{1,0:T(8,128)(2,1)S(1)}, u32[]{:S(2)}, u32[]{:S(2)}) collective-permute-start(bf16[128,2048]{1,0:T(8,128)(2,1)} %get-tuple-element.183), channel_id=1, source_target_pairs={{0,2},{1,3},{2,4},{3,5},{4,6},{5,7},{6,0},{7,1},{8,10},{9,11},{10,... | collective-permute-start | bytes 1572872 | tf_op jit(solution)/shard_map/ppermute | solution.py:916
  91.1 13.9 %collective-permute-start.12 = (bf16[128,2048]{1,0:T(8,128)(2,1)}, bf16[128,2048]{1,0:T(8,128)(2,1)}, u32[]{:S(2)}, u32[]{:S(2)}) collective-permute-start(bf16[128,2048]{1,0:T(8,128)(2,1)} %get-tuple-element.184), channel_id=1, source_target_pairs={{0,6},{1,7},{2,0},{3,1},{4,2},{5,3},{6,4},{7,5},{8,14},{9,15},{10,... | collective-permute-start | bytes 1572872 | tf_op jit(solution)/shard_map/ppermute | solution.py:916
  93.1 23.6 %collective-permute-start.13 = (bf16[128,2048]{1,0:T(8,128)(2,1)}, bf16[128,2048]{1,0:T(8,128)(2,1)}, u32[]{:S(2)}, u32[]{:S(2)}) collective-permute-start(bf16[128,2048]{1,0:T(8,128)(2,1)} %get-tuple-element.185), channel_id=1, source_target_pairs={{0,4},{1,5},{2,6},{3,7},{4,0},{5,1},{6,2},{7,3},{8,12},{9,13},{10,... | collective-permute-start | bytes 1572872 | tf_op jit(solution)/shard_map/ppermute | solution.py:916
  105.0 11.7 %copy-start.14 = (bf16[128,2048]{1,0:T(8,128)(2,1)}, bf16[128,2048]{1,0:T(8,128)(2,1)S(1)}, u32[]{:S(2)}) copy-start(bf16[128,2048]{1,0:T(8,128)(2,1)S(1)} %collective-permute-done.11.b1) | copy-start | bytes 1572868
  122.4 48.4 %all-to-all-start = ((bf16[128,88,128]{2,1,0:T(8,128)(2,1)}), bf16[128,88,128]{2,1,0:T(8,128)(2,1)}, u32[]{:S(2)}, u32[]{:S(2)}) async-start(bf16[128,88,128]{2,1,0:T(8,128)(2,1)} %get-tuple-element.187), calls=%async_computation | async-start | bytes 5767168 | tf_op jit(solution)/shard_map/all_to_all | solution.py:920
  132.1 14.8 %collective-permute-start.14 = (bf16[512,2048]{1,0:T(8,128)(2,1)}, bf16[512,2048]{1,0:T(8,128)(2,1)}, u32[]{:S(2)}, u32[]{:S(2)}) collective-permute-start(bf16[512,2048]{1,0:T(8,128)(2,1)} %bitcast.4.refs_4_.refs_6_.wa), channel_id=1, source_target_pairs={{0,1},{1,0},{2,3},{3,2},{4,5},{5,4},{6,7},{7,6},{8,9},{9,8},{10,11... | collective-permute-start | bytes 6291464 | tf_op jit(solution)/shard_map/ppermute | solution.py:908
  133.3 5.5 %copy-start.16 = (f32[128,128]{1,0:T(8,128)S(1)}, f32[128,128]{1,0:T(8,128)}, u32[]{:S(2)}) copy-start(f32[128,128]{1,0:T(8,128)} %get-tuple-element.199.gates) | copy-start | bytes 196612
  189.4 5.9 %copy-start.9 = (s32[128,128]{1,0:T(8,128)S(1)}, s32[128,128]{1,0:T(8,128)}, u32[]{:S(2)}) copy-start(s32[128,128]{1,0:T(8,128)} %get-tuple-element.186.ids) | copy-start | bytes 196612
  189.4 44.6 %all-to-all-start.2 = ((bf16[128,88,128]{2,1,0:T(8,128)(2,1)}), bf16[128,88,128]{2,1,0:T(8,128)(2,1)}, u32[]{:S(2)}, u32[]{:S(2)}) async-start(bf16[128,88,128]{2,1,0:T(8,128)(2,1)} %get-tuple-element.220), calls=%async_computation.2 | async-start | bytes 5767168 | tf_op jit(solution)/shard_map/all_to_all | solution.py:920
  204.0 7.5 %copy-start.26 = (bf16[640,2048]{1,0:T(8,128)(2,1)S(1)}, bf16[640,2048]{1,0:T(8,128)(2,1)}, u32[]{:S(2)}) copy-start(bf16[640,2048]{1,0:T(8,128)(2,1)} %get-tuple-element.227) | copy-start | bytes 7864324
  204.0 7.5 %copy-start.27 = (bf16[640,768]{1,0:T(8,128)(2,1)S(1)}, bf16[640,768]{1,0:T(8,128)(2,1)}, u32[]{:S(2)}) copy-start(bf16[640,768]{1,0:T(8,128)(2,1)} %get-tuple-element.229) | copy-start | bytes 2949124
  211.5 4.6 copy-start.3
  211.5 4.6 copy-start.10
  241.1 32.3 %collective-permute-start.15 = (bf16[128,2048]{1,0:T(8,128)(2,1)}, bf16[128,2048]{1,0:T(8,128)(2,1)S(1)}, u32[]{:S(2)}, u32[]{:S(2)}) collective-permute-start(bf16[128,2048]{1,0:T(8,128)(2,1)} %get-tuple-element.236.refs_0_), channel_id=1, source_target_pairs={{0,6},{1,7},{2,0},{3,1},{4,2},{5,3},{6,4},{7,5},{8,14},{9,15},{10,... | collective-permute-start | bytes 1572872 | tf_op jit(solution)/shard_map/ppermute | solution.py:912
  241.1 32.3 %collective-permute-start.16 = (bf16[128,2048]{1,0:T(8,128)(2,1)}, bf16[128,2048]{1,0:T(8,128)(2,1)}, u32[]{:S(2)}, u32[]{:S(2)}) collective-permute-start(bf16[128,2048]{1,0:T(8,128)(2,1)} %get-tuple-element.236.refs_0_), channel_id=1, source_target_pairs={{0,4},{1,5},{2,6},{3,7},{4,0},{5,1},{6,2},{7,3},{8,12},{9,13},{10,... | collective-permute-start | bytes 1572872 | tf_op jit(solution)/shard_map/ppermute | solution.py:912
  242.5 31.0 %collective-permute-start.17 = (bf16[128,2048]{1,0:T(8,128)(2,1)}, bf16[128,2048]{1,0:T(8,128)(2,1)S(1)}, u32[]{:S(2)}, u32[]{:S(2)}) collective-permute-start(bf16[128,2048]{1,0:T(8,128)(2,1)} %get-tuple-element.236.refs_0_), channel_id=1, source_target_pairs={{0,2},{1,3},{2,4},{3,5},{4,6},{5,7},{6,0},{7,1},{8,10},{9,11},{10,... | collective-permute-start | bytes 1572872 | tf_op jit(solution)/shard_map/ppermute | solution.py:912
  242.6 30.2 %all-to-all-start.3 = ((bf16[8,256,128]{2,1,0:T(8,128)(2,1)}), bf16[8,256,128]{2,1,0:T(8,128)(2,1)S(1)}, u32[]{:S(2)}, u32[]{:S(2)}) async-start(bf16[8,256,128]{2,1,0:T(8,128)(2,1)} %bitcast.76), calls=%async_computation.3 | async-start | bytes 1048576 | tf_op jit(solution)/shard_map/all_to_all | solution.py:1045
  249.4 26.2 %collective-permute-start.19 = (bf16[128,2048]{1,0:T(8,128)(2,1)}, bf16[128,2048]{1,0:T(8,128)(2,1)S(1)}, u32[]{:S(2)}, u32[]{:S(2)}) collective-permute-start(bf16[128,2048]{1,0:T(8,128)(2,1)} %get-tuple-element.236.refs_0_), channel_id=1, source_target_pairs={{0,1},{1,0},{2,3},{3,2},{4,5},{5,4},{6,7},{7,6},{8,9},{9,8},{10,11... | collective-permute-start | bytes 1572872 | tf_op jit(solution)/shard_map/ppermute | solution.py:908
  273.5 4.7 copy-start.5
  273.5 3.0 collective-permute-start.20
  275.0 3.2 collective-permute-start.21
  275.1 8.4 %collective-permute-start.18 = (bf16[128,2048]{1,0:T(8,128)(2,1)}, bf16[128,2048]{1,0:T(8,128)(2,1)}, u32[]{:S(2)}, u32[]{:S(2)}) collective-permute-start(bf16[128,2048]{1,0:T(8,128)(2,1)} %collective-permute-done.16.refs_2_), channel_id=1, source_target_pairs={{0,1},{1,0},{2,3},{3,2},{4,5},{5,4},{6,7},{7,6},{8,9},{9,8},{10,11... | collective-permute-start | bytes 1572872 | tf_op jit(solution)/shard_map/ppermute | solution.py:908
  290.7 46.8 %all-to-all-start.4 = ((bf16[128,80,128]{2,1,0:T(8,128)(2,1)}), bf16[128,80,128]{2,1,0:T(8,128)(2,1)}, u32[]{:S(2)}, u32[]{:S(2)}) async-start(bf16[128,80,128]{2,1,0:T(8,128)(2,1)} %expert_out.1), calls=%async_computation.4 | async-start | bytes 5242880 | tf_op jit(solution)/shard_map/all_to_all | solution.py:920
  295.6 120.2 %all-reduce.4.cloned.1.call-start = ((), (), s32[]{:S(2)}) async-start(), calls=%async_computation.7 | async-start | bytes 4325376 | tf_op jit(solution)/shard_map/psum | solution.py:1060
  315.2 3.5 collective-permute-start.22
  328.6 23.2 %collective-permute-start.23 = (bf16[4,128,640]{2,1,0:T(8,128)(2,1)}, bf16[4,128,640]{2,1,0:T(8,128)(2,1)S(1)}, u32[]{:S(2)}, u32[]{:S(2)}) collective-permute-start(bf16[4,128,640]{2,1,0:T(8,128)(2,1)} %get-tuple-element.250), channel_id=1, source_target_pairs={{0,32},{8,40},{16,48},{24,56},{32,64},{40,72},{48,80},{56,88},{64,... | collective-permute-start | bytes 1966088 | tf_op jit(solution)/shard_map/ppermute | solution.py:931
  329.4 8.1 %collective-permute-start.26 = (bf16[512,512]{1,0:T(8,128)(2,1)}, bf16[512,512]{1,0:T(8,128)(2,1)}, u32[]{:S(2)}, u32[]{:S(2)}) collective-permute-start(bf16[512,512]{1,0:T(8,128)(2,1)} %get-tuple-element.247.dq1), channel_id=1, source_target_pairs={{0,1},{1,0},{2,3},{3,2},{4,5},{5,4},{6,7},{7,6},{8,9},{9,8},{10,11... | collective-permute-start | bytes 1572872 | tf_op jit(solution)/shard_map/ppermute | solution.py:908
  330.0 43.4 %collective-permute-start.24 = (bf16[4,128,640]{2,1,0:T(8,128)(2,1)}, bf16[4,128,640]{2,1,0:T(8,128)(2,1)}, u32[]{:S(2)}, u32[]{:S(2)}) collective-permute-start(bf16[4,128,640]{2,1,0:T(8,128)(2,1)} %get-tuple-element.251), channel_id=1, source_target_pairs={{0,96},{8,104},{16,112},{24,120},{32,0},{40,8},{48,16},{56,24},{64... | collective-permute-start | bytes 1966088 | tf_op jit(solution)/shard_map/ppermute | solution.py:931
  331.9 41.5 %collective-permute-start.25 = (bf16[4,128,640]{2,1,0:T(8,128)(2,1)}, bf16[4,128,640]{2,1,0:T(8,128)(2,1)}, u32[]{:S(2)}, u32[]{:S(2)}) collective-permute-start(bf16[4,128,640]{2,1,0:T(8,128)(2,1)} %get-tuple-element.252), channel_id=1, source_target_pairs={{0,64},{8,72},{16,80},{24,88},{32,96},{40,104},{48,112},{56,120},{... | collective-permute-start | bytes 1966088 | tf_op jit(solution)/shard_map/ppermute | solution.py:931
  337.5 15.3 %copy-start.24 = (f32[1,2048]{1,0:T(1,128)S(1)}, f32[1,2048]{1,0:T(1,128)}, u32[]{:S(2)}) copy-start(f32[1,2048]{1,0:T(1,128)} %get-tuple-element.260) | copy-start | bytes 24580
  345.9 44.1 %collective-permute-start.30 = (bf16[128,2048]{1,0:T(8,128)(2,1)}, bf16[128,2048]{1,0:T(8,128)(2,1)}, u32[]{:S(2)}, u32[]{:S(2)}) collective-permute-start(bf16[128,2048]{1,0:T(8,128)(2,1)} %get-tuple-element.272), channel_id=1, source_target_pairs={{0,2},{1,3},{2,4},{3,5},{4,6},{5,7},{6,0},{7,1},{8,10},{9,11},{10,... | collective-permute-start | bytes 1572872 | tf_op jit(solution)/shard_map/ppermute | solution.py:916
  345.9 44.1 %collective-permute-start.31 = (bf16[128,2048]{1,0:T(8,128)(2,1)}, bf16[128,2048]{1,0:T(8,128)(2,1)}, u32[]{:S(2)}, u32[]{:S(2)}) collective-permute-start(bf16[128,2048]{1,0:T(8,128)(2,1)} %get-tuple-element.273), channel_id=1, source_target_pairs={{0,6},{1,7},{2,0},{3,1},{4,2},{5,3},{6,4},{7,5},{8,14},{9,15},{10,... | collective-permute-start | bytes 1572872 | tf_op jit(solution)/shard_map/ppermute | solution.py:916
  351.8 21.6 %copy-start.11 = (bf16[4,128,640]{2,1,0:T(8,128)(2,1)}, bf16[4,128,640]{2,1,0:T(8,128)(2,1)S(1)}, u32[]{:S(2)}) copy-start(bf16[4,128,640]{2,1,0:T(8,128)(2,1)S(1)} %collective-permute-done.23.b) | copy-start | bytes 1966084
  351.8 38.3 %collective-permute-start.32 = (bf16[128,2048]{1,0:T(8,128)(2,1)}, bf16[128,2048]{1,0:T(8,128)(2,1)}, u32[]{:S(2)}, u32[]{:S(2)}) collective-permute-start(bf16[128,2048]{1,0:T(8,128)(2,1)} %get-tuple-element.274), channel_id=1, source_target_pairs={{0,4},{1,5},{2,6},{3,7},{4,0},{5,1},{6,2},{7,3},{8,12},{9,13},{10,... | collective-permute-start | bytes 1572872 | tf_op jit(solution)/shard_map/ppermute | solution.py:916
  376.1 7.1 %collective-permute-start.27 = (bf16[128,640]{1,0:T(8,128)(2,1)}, bf16[128,640]{1,0:T(8,128)(2,1)S(1)}, u32[]{:S(2)}, u32[]{:S(2)}) collective-permute-start(bf16[128,640]{1,0:T(8,128)(2,1)} %get-tuple-element.268), channel_id=1, source_target_pairs={{0,8},{8,16},{16,24},{24,0},{32,40},{40,48},{48,56},{56,32},{64,72... | collective-permute-start | bytes 491528 | tf_op jit(solution)/shard_map/ppermute | solution.py:931
  378.1 6.8 %collective-permute-start.28 = (bf16[128,640]{1,0:T(8,128)(2,1)}, bf16[128,640]{1,0:T(8,128)(2,1)S(1)}, u32[]{:S(2)}, u32[]{:S(2)}) collective-permute-start(bf16[128,640]{1,0:T(8,128)(2,1)} %get-tuple-element.269), channel_id=1, source_target_pairs={{0,24},{8,0},{16,8},{24,16},{32,56},{40,32},{48,40},{56,48},{64,88... | collective-permute-start | bytes 491528 | tf_op jit(solution)/shard_map/ppermute | solution.py:931
  383.2 6.9 %copy-start.20 = (bf16[128,640]{1,0:T(8,128)(2,1)}, bf16[128,640]{1,0:T(8,128)(2,1)S(1)}, u32[]{:S(2)}) copy-start(bf16[128,640]{1,0:T(8,128)(2,1)S(1)} %collective-permute-done.27.b) | copy-start | bytes 491524
  383.2 6.8 %collective-permute-start.29 = (bf16[128,640]{1,0:T(8,128)(2,1)}, bf16[128,640]{1,0:T(8,128)(2,1)S(1)}, u32[]{:S(2)}, u32[]{:S(2)}) collective-permute-start(bf16[128,640]{1,0:T(8,128)(2,1)} %get-tuple-element.270), channel_id=1, source_target_pairs={{0,16},{8,24},{16,0},{24,8},{32,48},{40,56},{48,32},{56,40},{64,80... | collective-permute-start | bytes 491528 | tf_op jit(solution)/shard_map/ppermute | solution.py:931
  384.8 5.3 %copy-start.21 = (bf16[128,640]{1,0:T(8,128)(2,1)}, bf16[128,640]{1,0:T(8,128)(2,1)S(1)}, u32[]{:S(2)}) copy-start(bf16[128,640]{1,0:T(8,128)(2,1)S(1)} %collective-permute-done.28.c) | copy-start | bytes 491524
  392.6 4.4 collective-permute-start.33
  394.0 6.0 %collective-permute-start.34 = (bf16[128,640]{1,0:T(8,128)(2,1)}, bf16[128,640]{1,0:T(8,128)(2,1)S(1)}, u32[]{:S(2)}, u32[]{:S(2)}) collective-permute-start(bf16[128,640]{1,0:T(8,128)(2,1)} %add_last.1.a), channel_id=1, source_target_pairs={{0,16},{8,24},{16,0},{24,8},{32,48},{40,56},{48,32},{56,40},{64,80... | collective-permute-start | bytes 491528 | tf_op jit(solution)/shard_map/ppermute | solution.py:931
  394.8 9.3 %collective-permute-start.35 = (bf16[128,640]{1,0:T(8,128)(2,1)}, bf16[128,640]{1,0:T(8,128)(2,1)S(1)}, u32[]{:S(2)}, u32[]{:S(2)}) collective-permute-start(bf16[128,640]{1,0:T(8,128)(2,1)} %add_last.1.a), channel_id=1, source_target_pairs={{0,8},{8,16},{16,24},{24,0},{32,40},{40,48},{48,56},{56,32},{64,72... | collective-permute-start | bytes 491528 | tf_op jit(solution)/shard_map/ppermute | solution.py:931
  397.0 7.1 %copy-start.17 = (bf16[128,640]{1,0:T(8,128)(2,1)}, bf16[128,640]{1,0:T(8,128)(2,1)S(1)}, u32[]{:S(2)}) copy-start(bf16[128,640]{1,0:T(8,128)(2,1)S(1)} %collective-permute-done.33.b) | copy-start | bytes 491524
  417.5 50.1 %all-to-all-start.6 = ((bf16[128,24,128]{2,1,0:T(8,128)(2,1)}), bf16[128,24,128]{2,1,0:T(8,128)(2,1)S(1)}, u32[]{:S(2)}, u32[]{:S(2)}) async-start(bf16[128,24,128]{2,1,0:T(8,128)(2,1)} %broadcast_in_dim.45), calls=%async_computation.6 | async-start | bytes 1572864 | tf_op jit(solution)/shard_map/all_to_all | solution.py:920
  425.7 38.6 %collective-permute-start.36 = (bf16[4,128,640]{2,1,0:T(8,128)(2,1)}, bf16[4,128,640]{2,1,0:T(8,128)(2,1)}, u32[]{:S(2)}, u32[]{:S(2)}) collective-permute-start(bf16[4,128,640]{2,1,0:T(8,128)(2,1)} %stack_parts.1.c0), channel_id=1, source_target_pairs={{0,96},{8,104},{16,112},{24,120},{32,0},{40,8},{48,16},{56,24},{64... | collective-permute-start | bytes 1966088 | tf_op jit(solution)/shard_map/ppermute | solution.py:931
  429.0 35.3 %collective-permute-start.37 = (bf16[4,128,640]{2,1,0:T(8,128)(2,1)}, bf16[4,128,640]{2,1,0:T(8,128)(2,1)}, u32[]{:S(2)}, u32[]{:S(2)}) collective-permute-start(bf16[4,128,640]{2,1,0:T(8,128)(2,1)} %stack_parts.1.c0), channel_id=1, source_target_pairs={{0,64},{8,72},{16,80},{24,88},{32,96},{40,104},{48,112},{56,120},{... | collective-permute-start | bytes 1966088 | tf_op jit(solution)/shard_map/ppermute | solution.py:931
  429.1 38.5 %collective-permute-start.38 = (bf16[4,128,640]{2,1,0:T(8,128)(2,1)}, bf16[4,128,640]{2,1,0:T(8,128)(2,1)}, u32[]{:S(2)}, u32[]{:S(2)}) collective-permute-start(bf16[4,128,640]{2,1,0:T(8,128)(2,1)} %stack_parts.1.c0), channel_id=1, source_target_pairs={{0,32},{8,40},{16,48},{24,56},{32,64},{40,72},{48,80},{56,88},{64,... | collective-permute-start | bytes 1966088 | tf_op jit(solution)/shard_map/ppermute | solution.py:931
  473.3 5.5 %copy-start.1 = (s32[1,1024]{1,0:T(1,128)S(1)}, s32[1,1024]{1,0:T(1,128)}, u32[]{:S(2)}) copy-start(s32[1,1024]{1,0:T(1,128)} %param.32) | copy-start | bytes 12292
  (10 other events, 14.5 us)
Sparse Core Ops, SparseCore 0:
  300.5 115.2 all-reduce.3

commit v5 on v4

--- a/solution.py
+++ b/solution.py
@@ -527,7 +527,7 @@
 
 def combine_body(
     where, experts, slots, gate_list, wire, hidden, n2, probs, gates, ids, og, g2, wr,
-    ghid, gatt, grouter, gg2, sums, gn2,
+    ghid, gatt, router_own, router_sib, gg2, sums, gn2, parts,
 ):
     sum_rows(wire, experts, slots, gate_list, sums)
     scores = get_numbers(wire)
@@ -565,15 +565,31 @@
     gg2[...] = jnp.sum(c * (v * r), axis=0, keepdims=True)
     for j in range(SEG):
         cols = slice(j * 128, (j + 1) * 128)
-        grouter[cols, :] = dot(n2[:, cols].astype(f32).T.astype(bf16), gl).astype(bf16)
+        owner = j // 2
+        dy = lax.rem(owner // 2 + 4 - where[3], 4)
+        dc = lax.rem(owner % 2 + where[2], 2)
+        half = slice((j % 2) * 128, (j % 2 + 1) * 128)
+        parts[dc * 4 + dy, half, :] = dot(n2[:, cols].astype(f32).T.astype(bf16), gl).astype(bf16)
+    router_own[...] = parts[0:4]
+    router_sib[...] = parts[4:8]
 
 
 def combine(*args):
     return call(
         combine_body,
         "combine_grads",
-        [sds((T, D), f32), sds((T, D), bf16), sds((D, E), bf16), sds((1, D), f32)],
-        [pltpu.VMEM((T * SEG, 128), f32), pltpu.VMEM((T, D), f32)],
+        [
+            sds((T, D), f32),
+            sds((T, D), bf16),
+            sds((4, 256, E), bf16),
+            sds((4, 256, E), bf16),
+            sds((1, D), f32),
+        ],
+        [
+            pltpu.VMEM((T * SEG, 128), f32),
+            pltpu.VMEM((T, D), f32),
+            pltpu.VMEM((8, 256, E), bf16),
+        ],
         args,
         smem=(0, 1, 2, 3),
     )
@@ -617,12 +633,27 @@
     )[0]
 
 
-def pre_body(*refs):
-    blocks, (ot0, ot1, wo, gw, dt, rows_all, total) = refs[:8], refs[8:]
+def pre_body(where, *refs):
+    blocks, routers = refs[:8], refs[8:12]
+    ot0, ot1, wo, w0, w1, w2, w3, dt, rows_all, total = refs[12:]
     step = pl.program_id(0)
     for b in range(8):
         rows_all[b * T : (b + 1) * T, :] = blocks[b][...]
-    gw[...] = (dot(ot0[...], rows_all[:HALF, :]) + dot(ot1[...], rows_all[HALF:, :])).astype(bf16)
+    grad = (dot(ot0[...], rows_all[:HALF, :]) + dot(ot1[...], rows_all[HALF:, :])).astype(bf16)
+    for dx, out in enumerate((w0, w1, w2, w3)):
+
+        @pl.when(step == dx)
+        def _():
+            for col in range(4):
+                dz = lax.rem(col + 4 - where[0], 4)
+                start = lax.rem(where[1] + dx, 4) * 64 + col * 16
+                rows = pl.ds(pl.multiple_of(start, 16), 16)
+                out[dz, :512, :] = grad[:, col * 128 : (col + 1) * 128]
+                out[dz, 512:, :] = (
+                    (routers[0][rows, :].astype(f32) + routers[1][rows, :].astype(f32))
+                    + (routers[2][rows, :].astype(f32) + routers[3][rows, :].astype(f32))
+                ).astype(bf16)
+
     last = jnp.concatenate([blocks[2][...], blocks[6][...]], axis=0)
     part = dot_t(wo[...], last)
 
@@ -639,16 +670,23 @@
         dt[...] = total[...].astype(bf16)
 
 
-def pre(blocks, ot0, ot1, wo):
+def pre(where, blocks, routers, ot0, ot1, wo):
+    def turned(shape):
+        return pl.BlockSpec(shape, lambda i, w: (0, lax.rem(i + w[1], 4)))
+
     return grid_call(
         pre_body,
         "out_projection_grad",
         (4,),
-        [cols_of((T, 512))] * 8 + [whole((512, HALF))] * 2 + [cols_of((512, 512))],
-        [cols_of((512, 512)), whole((512, 2 * T))],
-        [sds((LH * HEAD, D), bf16), sds((LH * HEAD, 2 * T), bf16)],
+        [turned((T, 512))] * 8
+        + [whole((256, E))] * 4
+        + [whole((512, HALF))] * 2
+        + [turned((512, 512))],
+        [whole((4, 528, 128))] * 4 + [whole((512, 2 * T))],
+        [sds((4, 528, 128), bf16)] * 4 + [sds((LH * HEAD, 2 * T), bf16)],
         [pltpu.VMEM((ROWS, 512), bf16), pltpu.VMEM((512, 2 * T), f32)],
-        (*blocks, ot0, ot1, wo),
+        (where, *blocks, *routers, ot0, ot1, wo),
+        scalars=1,
     )
 
 
@@ -806,10 +844,18 @@
 
 
 def add_parts(parts):
-    return call(add_body, "add_parts", [sds((128, 640), bf16)] * 4, [], tuple(parts))
-
-
-def normed_grad_body(wa, wb, wkv, dq0, dqr, tot, n0, n1, n2, n3, b0, b1, b2, b3, gg1, grads):
+    shape = parts[0].shape[1:]
+    return call(add_body, "add_parts", [sds(shape, bf16)] * 4, [], tuple(parts))
+
+
+def split_two(v):
+    first = v.astype(bf16)
+    return first, (v - first.astype(f32)).astype(bf16)
+
+
+def normed_grad_body(
+    wa, wb, wkv, dq0, dqr, tot, n0, n1, n2, n3, gg2, ggq, ggk, b0, b1, b2, b3, grads
+):
     @pl.when(pl.program_id(0) == 0)
     def _():
         flip(dq0, grads, 0, 0)
@@ -822,14 +868,19 @@
         + dot(grads[:, 1024:], wkv[...])
     )
     gain = jnp.zeros((1, 512), f32)
-    for dy, (out, rows) in enumerate(((b0, n0), (b1, n1), (b2, n2), (b3, n3))):
+    outs = (b0, b1, b2, b3)
+    for dy, (out, rows) in enumerate(zip(outs, (n0, n1, n2, n3))):
         part = total[dy * T : (dy + 1) * T, :]
-        out[...] = part.astype(bf16)
+        out[:T, :] = part.astype(bf16)
         gain = gain + jnp.sum(part * rows[...].astype(f32), axis=0, keepdims=True)
-    gg1[...] = jnp.broadcast_to(gain, (8, 512))
-
-
-def normed_grad(wa, wb, wkv, dq0, dqr, tot, n1):
+    heads = jnp.concatenate([ggq[0:1, :], ggk[0:1, :], jnp.zeros((1, 256), f32)], axis=1)
+    numbers = [*split_two(gain), *split_two(gg2[...]), *split_two(heads)]
+    extra = jnp.concatenate([n.astype(f32) for n in numbers] + [jnp.zeros((10, 512), f32)], axis=0)
+    for out in outs:
+        out[T:, :] = extra.astype(bf16)
+
+
+def normed_grad(wa, wb, wkv, dq0, dqr, tot, n1, gg2, ggq, ggk):
     return grid_call(
         normed_grad_body,
         "normed_grad",
@@ -842,22 +893,37 @@
             whole((512, HALF)),
             whole((2 * HEAD, HALF)),
         ]
-        + [cols_of((T, 512))] * 4,
-        [cols_of((T, 512))] * 4 + [cols_of((8, 512))],
-        [sds((T, D), bf16)] * 4 + [sds((8, D), f32)],
+        + [cols_of((T, 512))] * 4
+        + [cols_of((1, 512)), whole((8, HEAD)), whole((8, HEAD))],
+        [cols_of((T + 16, 512))] * 4,
+        [sds((T + 16, D), bf16)] * 4,
         [pltpu.VMEM((HALF, 1280), bf16)],
-        (wa, wb, wkv, dq0, dqr, tot, *n1),
-    )
-
-
-def add_last_body(a, b, c, d, out):
-    out[...] = (
+        (wa, wb, wkv, dq0, dqr, tot, *n1, gg2, ggq, ggk),
+    )
+
+
+def add_pair_body(a, b, *outs):
+    for i, out in enumerate(outs):
+        out[...] = (a[i].astype(f32) + b[i].astype(f32)).astype(bf16)
+
+
+def add_pair(a, b):
+    return call(add_pair_body, "add_pair", [sds(a.shape[1:], bf16)] * 4, [], (a, b))
+
+
+def add_last_body(a, b, c, d, *outs):
+    total = (
         (a[...].astype(f32) + b[...].astype(f32)) + (c[...].astype(f32) + d[...].astype(f32))
     ).astype(bf16)
-
-
-def add_last(parts):
-    return call(add_last_body, "add_last", [sds((128, 640), bf16)], [], tuple(parts))[0]
+    start = 0
+    for out in outs:
+        out[...] = total[start : start + out.shape[0]]
+        start += out.shape[0]
+
+
+def add_last(parts, *heights):
+    outs = [sds((height, parts[0].shape[1]), bf16) for height in heights]
+    return call(add_last_body, "add_last", outs, [], tuple(parts))
 
 
 def stack_body(a, b, c, d, out):
@@ -866,7 +932,27 @@
 
 
 def stack(parts):
-    return call(stack_body, "stack_parts", [sds((4, 128, 640), bf16)], [], tuple(parts))[0]
+    shape = (4, *parts[0].shape)
+    return call(stack_body, "stack_parts", [sds(shape, bf16)], [], tuple(parts))[0]
+
+
+def place_out_body(where, c0, c1, c2, c3, out):
+    for dx, chunks in enumerate((c0, c1, c2, c3)):
+        for dz in range(4):
+            chunk = lax.rem(where[1] + dx, 4) * 4 + lax.rem(where[0] + dz, 4)
+            cols = pl.ds(pl.multiple_of(chunk * 128, 128), 128)
+            out[:, cols] = chunks[dz].astype(f32)
+
+
+def place_out(where, chunks):
+    return call(
+        place_out_body,
+        "place_output_grads",
+        [sds((512, D), f32)],
+        [],
+        (where, *chunks),
+        smem=(0,),
+    )[0]
 
 
 def place_body(where, c0, c1, c2, c3, gq, gkt, gvt):
@@ -891,17 +977,36 @@
     )
 
 
-def final_body(b0, b1, b2, b3, x0, ghid, g1, out):
-    c = (b0[...].astype(f32) + b1[...].astype(f32)) + (b2[...].astype(f32) + b3[...].astype(f32))
+def final_body(b0, b1, b2, b3, x0, ghid, g1, out, gains):
+    whole_sum = (b0[...].astype(f32) + b1[...].astype(f32)) + (
+        b2[...].astype(f32) + b3[...].astype(f32)
+    )
+    c = whole_sum[:T]
     v = x0[...].astype(f32)
     r = lax.rsqrt(jnp.mean(v * v, axis=-1, keepdims=True) + EPS)
     u = c * g1[...]
     m = jnp.mean(u * v, axis=-1, keepdims=True)
     out[...] = ghid[...] + r * u - v * (r * r * r * m)
+    extra = whole_sum[T:]
+    gains[...] = jnp.concatenate(
+        [
+            (extra[0:1] + extra[1:2]) / g1[...],
+            extra[2:3] + extra[3:4],
+            extra[4:5] + extra[5:6],
+            jnp.zeros((5, D), f32),
+        ],
+        axis=0,
+    )
 
 
 def final(b, x0, ghid, g1):
-    return call(final_body, "input_grad", [sds((T, D), f32)], [], (*b, x0, ghid, g1))[0]
+    return call(
+        final_body,
+        "input_grad",
+        [sds((T, D), f32), sds((8, D), f32)],
+        [],
+        (*b, x0, ghid, g1),
+    )
 
 
 def sibling(x):
@@ -953,7 +1058,7 @@
 ):
     shard, owner = lax.axis_index("shard"), lax.axis_index("expert")
     chip, core = shard // 2, shard % 2
-    where = jnp.stack([owner // 4, owner % 4, core]).astype(jnp.int32)
+    where = jnp.stack([owner // 4, owner % 4, core, chip]).astype(jnp.int32)
     core_id = core.reshape(1)
     g1 = norm1_gain.astype(f32).reshape(1, D)
     g2 = norm2_gain.astype(f32).reshape(1, D)
@@ -993,18 +1098,14 @@
     weights = (g1, wq_t, wk_t, wk_s, wv_t, wv_s, gq, gk, cos, sin)
     zero = qkv((0,), core_id, (x_own[0], x_sib[0]), *weights)
     og_wire = pack(out_grad, assign_t)
-    x_own[1], x_own[3], q_first, og_wire = lax.optimization_barrier(
-        (x_own[1], x_own[3], zero[1], og_wire)
-    )
-    x_sib = [x_sib[0], sibling(x_own[1]), None, sibling(x_own[3])]
-    x_sib[1], x_sib[3], x_own[2], og_wire = lax.optimization_barrier(
-        (x_sib[1], x_sib[3], x_own[2], og_wire)
-    )
-    x_sib[2] = sibling(x_own[2])
-    near = qkv((1, 3), core_id, (x_own[1], x_sib[1], x_own[3], x_sib[3]), *weights)
-    far = qkv((2,), core_id, (x_own[2], x_sib[2]), *weights)
+    x_own[1], x_own[2], x_own[3], q_first, og_wire = lax.optimization_barrier(
+        (x_own[1], x_own[2], x_own[3], zero[1], og_wire)
+    )
+    x_sib += [sibling(x_own[dy]) for dy in (1, 2, 3)]
+    blocks = [side[dy] for dy in (1, 2, 3) for side in (x_own, x_sib)]
+    others = qkv((1, 2, 3), core_id, blocks, *weights)
     wkv = zero[7]
-    pieces = [zero[:7], near[:7], far[:7], near[7:14]]
+    pieces = [zero[:7], others[:7], others[7:14], others[14:21]]
     qh, q, kh, k, v, scales, n1 = zip(*pieces)
     q = (q_first,) + q[1:]
     got_grads = exchange(og_wire)
@@ -1037,18 +1138,13 @@
         (back_wire, out_wire, grad_wgate, grad_wup, grad_wdown)
     )
 
-    ghid, gatt, grouter, gg2 = combine(
+    ghid, gatt, router_own, router_sib, gg2 = combine(
         where, expert_list, slot_list, gate_list, back_wire, hidden, n2, probs, gates, ids,
         out_grad, g2, w_router,
     )
     g_own = [gatt] + [from_chip(gatt, dy) for dy in (1, 2, 3)]
-    router_parts = lax.all_to_all(
-        grouter.reshape(8, 2 * T, E), "shard", split_axis=0, concat_axis=0, tiled=True
-    )
-    router_sum = jnp.sum(router_parts.astype(f32), axis=0).astype(bf16)
-    g_own[1], g_own[2], g_own[3], router_sum = lax.optimization_barrier(
-        (g_own[1], g_own[2], g_own[3], router_sum)
-    )
+    router_parts = add_pair(router_own, sibling(router_sib))
+    router_parts = [router_parts[0]] + spread(router_parts)
     g_sib = [sibling(block) for block in g_own]
     dt_near = head_grad(
         [g_own[0], g_sib[0], g_own[1], g_sib[1], g_own[3], g_sib[3]], w_out
@@ -1056,58 +1152,56 @@
     g_far, dt_near = lax.optimization_barrier(((g_own[2], g_sib[2]), dt_near))
     g_own[2], g_sib[2] = g_far
 
-    gwout, dt_far = pre(g_own + g_sib, ot0, ot1, w_out)
-    early_sums = lax.psum((gwout, router_sum), "expert")
+    *out_parts, dt_far = pre(where, g_own + g_sib, router_parts, ot0, ot1, w_out)
+    out_parts = collect(out_parts, 1)
     returned = exchange(after(out_wire, dt_far))
 
     dq0, dq1, dkv, ggq, ggk = bwd(
         qh, kh, scales, qt, kt, kn, vn, dt_near, dt_far, ot0, ot1, linv, info, cos, sin, gq, gk
     )
+    dq1, dkv, out_parts = lax.optimization_barrier((dq1, dkv, out_parts))
     dq_sib, dkv_sib = sibling(dq1), sibling(dkv)
     *parts, dkv_total = qkv_grad(where, n1_t, dq0, dq1, dkv, dkv_sib)
     returned, dq0 = lax.optimization_barrier((returned, dq0))
     result = result_rows(expert_list, slot_list, gate_list, returned, hidden)
-    blocks = normed_grad(wq_t, wq_ts, wkv, dq0, dq_sib, dkv_total, n1)
-    gg1 = blocks[4][0] / g1[0]
-    vector = jnp.concatenate([gg1, gg2[0], ggq[0], ggk[0]])
-    per = vector.shape[0] // E
-    wide = jnp.pad(vector.reshape(E, per), ((0, 0), (0, 128 - per))).reshape(E, 1, 128)
+    blocks = normed_grad(wq_t, wq_ts, wkv, dq0, dq_sib, dkv_total, n1, gg2, ggq, ggk)
     blocks = [blocks[0]] + spread(blocks)
-    mine = jnp.sum(exchange(wide), axis=0)
+    out_parts = collect(add_parts(out_parts), 0)
 
     parts = collect(parts, 0)
-    parts, mine = lax.optimization_barrier((parts, mine))
+    parts, out_parts = lax.optimization_barrier((parts, out_parts))
+    out_chunk, router_chunk = add_last(out_parts, 512, SEG)
+    out_chunks = share(out_chunk, 0)
+    grad_router = exchange(jnp.broadcast_to(router_chunk[None], (E, SEG, E)))
     parts = collect(add_parts(parts), 1)
-    parts, blocks = lax.optimization_barrier((parts, blocks))
-    chunks = stack(share(add_last(parts), 1))
-    chunks, mine, early_sums = lax.optimization_barrier((chunks, mine, early_sums))
+    parts, out_chunks, blocks = lax.optimization_barrier((parts, out_chunks, blocks))
+    chunks = share(add_last(parts, 128)[0], 1)
+    out_chunks = share(stack(out_chunks), 1)
+    grad_input, gains = final(blocks, block_input, ghid, g1)
+    gains = gains[:3]
+    gains = gains + sibling(gains)
+    chunks, gains = lax.optimization_barrier((stack(chunks), gains))
     chunks = share(chunks, 0)
-    first = mine.astype(bf16)
-    second = (mine - first.astype(f32)).astype(bf16)
-    router_part = lax.dynamic_slice(early_sums[1], (owner * SEG, 0), (SEG, E))
-    small = jnp.concatenate([router_part, first, second, jnp.zeros((6, 128), bf16)], axis=0)
-    everyone = exchange(jnp.broadcast_to(small[None], (E, SEG + 8, 128)))
-    grad_input = final(blocks, block_input, ghid, g1)
-    chunks, everyone, early_sums, grad_input, result = lax.optimization_barrier(
-        (chunks, everyone, early_sums, grad_input, result)
-    )
-    vector = everyone[:, SEG, :per].astype(f32) + everyone[:, SEG + 1, :per].astype(f32)
-    vector = vector.reshape(-1)
-    grad_router = everyone[:, :SEG].reshape(16, 8, SEG, E).transpose(1, 0, 2, 3)
+    out_chunks = after(out_chunks, *chunks[1:])
+    gains = jnp.sum(lax.all_gather(gains, "expert"), axis=0)
+    grad_wout = place_out(where, out_chunks)
+    grad_router = grad_router.reshape(4, 4, 8, SEG, E).transpose(2, 1, 0, 3, 4)
     grad_router = grad_router.reshape(D, E).astype(f32)
-    grad_wout = early_sums[0].astype(f32)
+    chunks, gains, result, grad_wout, grad_router = lax.optimization_barrier(
+        (chunks, gains, result, grad_wout, grad_router)
+    )
     grad_wq, grad_wk, grad_wv = place(where, chunks)
     return (
         result,
         grad_input,
-        vector[:D],
+        gains[0],
         grad_wq,
         grad_wk.T,
         grad_wv.T,
-        vector[2 * D : 2 * D + HEAD],
-        vector[2 * D + HEAD :],
+        gains[2, :HEAD],
+        gains[2, HEAD : 2 * HEAD],
         grad_wout,
-        vector[D : 2 * D],
+        gains[1],
         grad_router,
         grad_wgate[None],
         grad_wup[None],

time: 493 us -> 523 us (1.061)
  between operations: 14.6 us -> 1.24 us
  waiting for transfers between devices: 158 us -> 171 us
  blocking collectives: 20.2 us -> 32.2 us
  Pallas kernels: 157 us -> 169 us
  starting transfers between devices: 86.9 us -> 97.9 us
    all_gather x0 -> x1, blocking collectives: none -> 32.2 us  [on_device(): gains = jnp.sum(lax.all_gather(gains, 'expert'), axis=0)]
    ppermute x12 -> x24, waiting for transfers between devices: 50.6 us -> 77.2 us  [on_expert(): return lax.ppermute(x, 'expert', pairs)]
    all_to_all x1 -> x0, waiting for transfers between devices: 23.3 us -> none  [on_device(): lax.all_to_all(grouter.reshape(8, 2 * T, E), 'shard', split_axis=0, conca...]
    all_to_all x1 -> x0, blocking collectives: 20.2 us -> none  [exchange(): return lax.all_to_all(x, ALL, split_axis=0, concat_axis=0, tiled=True)]
    ppermute x6, waiting for transfers between devices: 7.68 us -> 21.1 us  [from_chip(): return lax.ppermute(x, 'shard', [(i, (i - 2 * dy) % 8) for i in range(8)])]
    ppermute x12 -> x24, starting transfers between devices: 15.5 us -> 28.9 us  [on_expert(): return lax.ppermute(x, 'expert', pairs)]
    psum x1 -> x0, waiting for transfers between devices: 9 us -> none  [on_device(): early_sums = lax.psum((gwout, router_sum), 'expert')]
    pallas_call x20 -> x24, Pallas kernels: 127 us -> 136 us  [call(): pl.pallas_call(kernel, out_shape=outs, in_specs=in_specs, out_specs=[pl.B...]
  transfers between devices with their start and end apart: 46 -> 61, of which waited for: 20 -> 22; matrix products, arithmetic and copies ran while one was open for 7% -> 7% of each run, Pallas kernels for 25% -> 24%
where the time goes in v5:
time: 523 us; the launch traced here: 512 us
  waiting for transfers between devices  171 us (33%)
  Pallas kernels  169 us (32%)
  starting transfers between devices  97.9 us (19%)
  blocking collectives  32.2 us (6%)
  matrix products  16.6 us (3%)
  local copies, waits for them, and re-layouts  15.6 us (3%)
  other arithmetic  8.17 us (2%)
    pallas_call x24, Pallas kernels, call(): pl.pallas_call(kernel, out_shape=outs, in_specs=in_specs, out_specs=[pl.B...  136 us
    ppermute x24, waiting for transfers between devices, on_expert(): return lax.ppermute(x, 'expert', pairs)  77.2 us
    all_to_all x5, waiting for transfers between devices, exchange(): return lax.all_to_all(x, ALL, split_axis=0, concat_axis=0, tiled=True)  37.3 us
    all_to_all x5, starting transfers between devices, exchange(): return lax.all_to_all(x, ALL, split_axis=0, concat_axis=0, tiled=True)  36.3 us
    pallas_call x4, Pallas kernels, grid_call(): pl.pallas_call(kernel, out_shape=outs, grid_spec=pltpu.PrefetchScalarGrid...  33.3 us
    all_gather x1, blocking collectives, on_device(): gains = jnp.sum(lax.all_gather(gains, 'expert'), axis=0)  32.2 us
    ppermute x24, starting transfers between devices, on_expert(): return lax.ppermute(x, 'expert', pairs)  28.9 us
    ppermute x9, waiting for transfers between devices, to_chip(): return lax.ppermute(x, 'shard', [(i, (i + 2 * dy) % 8) for i in range(8)])  24.7 us
  transfers between devices with their start and end apart: 61, of which 22 were waited for; matrix products, arithmetic and copies ran while one was open for 7% of the time, Pallas kernels for 24%

profile of v5, /device:TPU:1, one launch (start us, length us, event | category | flops | bytes accessed | tf_op | source)
XLA Modules:
  0.0 512.4 jit_solution(12826433451675561293)
XLA Ops:
  3.6 2.6 collective-permute-start.1
  11.7 2.0 route_tables.1
  14.9 4.2 pack_rows.1
  19.7 4.0 copy.37
  26.2 5.0 qkv0.1
  31.2 9.2 %all-to-all-start.1 = ((bf16[128,88,128]{2,1,0:T(8,128)(2,1)}), bf16[128,88,128]{2,1,0:T(8,128)(2,1)}, u32[]{:S(2)}, u32[]{:S(2)}) async-start(bf16[128,88,128]{2,1,0:T(8,128)(2,1)} %pack_rows.1), calls=%async_computation.1 | async-start | bytes 5767168 | tf_op jit(solution)/shard_map/all_to_all | solution.py:1025
  43.1 3.8 collective-permute-done.6.refs_2_
  48.0 7.7 %qkv123.1 = (bf16[512,256]{1,0:T(8,128)(2,1)}, bf16[512,256]{1,0:T(8,128)(2,1)}, bf16[128,256]{1,0:T(8,128)(2,1)}, bf16[128,256]{1,0:T(8,128)(2,1)}, bf16[128,25...) custom-call(s32[1]{0:T(128)} %bitcast.2.refs_0_, ...), custom_call_target="tpu_custom_call" | custom-call | flops 1 | bytes 1 | tf_op jit(solution)/shard_map/qkv123/pallas_call | solution.py:61
  55.7 10.9 %attend.1 = (bf16[512,512]{1,0:T(8,128)(2,1)}, bf16[512,512]{1,0:T(8,128)(2,1)}, f32[8,1024]{1,0:T(8,128)}, bf16[512,1024]{1,0:T(8,128)(2,1)}, bf16[128,1024]{1,...) custom-call(bf16[512,256]{1,0:T(8,128)(2,1)} %get-tuple-element.185.refs_0_, ...), custom_call_target="tpu_custom_call" | custom-call | flops 1 | bytes 6600001 | tf_op jit(solution)/shard_map/attend/pallas_call | solution.py:61
  69.6 6.2 %out_projection.1 = (bf16[128,2048]{1,0:T(8,128)(2,1)}, bf16[128,2048]{1,0:T(8,128)(2,1)}, bf16[128,2048]{1,0:T(8,128)(2,1)}, bf16[128,2048]{1,0:T(8,128)(2,1)}) custom-call(bf16[512,512]{1,0:T(8,128)(2,1)} %get-tuple-element.200.ot0.refs_12_.refs_18_, bf16[512,512]{1,0:T(8,128)(2,1)} %copy-done.11, bf16[512,2048]{1,0:T(8,128)(2,1)} %refs_14_.1, ...), custom_call_target="tpu_custom_call" | custom-call | flops 1 | bytes 3000001 | tf_op jit(solution)/shard_map/out_projection/pallas_call | solution.py:74
  76.4 2.1 collective-permute-start.12
  80.0 10.4 %collective-permute-done.11.b1 = bf16[128,2048]{1,0:T(8,128)(2,1)S(1)} collective-permute-done((bf16[128,2048]{1,0:T(8,128)(2,1)}, bf16[128,2048]{1,0:T(8,128)(2,1)S(1)}, u32[]{:S(2)}, u32[]{:S(2)}) %collective-permute-start.11) | collective-permute-done | bytes 524320 | tf_op jit(solution)/shard_map/ppermute | solution.py:1021
  90.3 11.7 %collective-permute-done.13.b3 = bf16[128,2048]{1,0:T(8,128)(2,1)} collective-permute-done((bf16[128,2048]{1,0:T(8,128)(2,1)}, bf16[128,2048]{1,0:T(8,128)(2,1)}, u32[]{:S(2)}, u32[]{:S(2)}) %collective-permute-start.13) | collective-permute-done | bytes 524320 | tf_op jit(solution)/shard_map/ppermute | solution.py:1021
  102.1 5.6 %router.1 = (f32[128,2048]{1,0:T(8,128)}, bf16[128,2048]{1,0:T(8,128)(2,1)}, f32[128,128]{1,0:T(8,128)}, f32[128,128]{1,0:T(8,128)}, bf16[128,88,128]{2,1,0:T(8,128)(2,1)}) custom-call(bf16[128,2048]{1,0:T(8,128)(2,1)} %get-tuple-element.202.b0, bf16[128,2048]{1,0:T(8,128)(2,1)} %copy-done.12, bf16[128,2048]{1,0:T(8,128)(2,1)} %collective-permute-done.12.b2, ...), custom_call_target="tpu_custom_call" | custom-call | flops 1 | bytes 3600001 | tf_op jit(solution)/shard_map/router/pallas_call | solution.py:61
  107.7 9.7 %all-to-all-start = ((bf16[128,88,128]{2,1,0:T(8,128)(2,1)}), bf16[128,88,128]{2,1,0:T(8,128)(2,1)}, u32[]{:S(2)}, u32[]{:S(2)}) async-start(bf16[128,88,128]{2,1,0:T(8,128)(2,1)} %get-tuple-element.207), calls=%async_computation | async-start | bytes 5767168 | tf_op jit(solution)/shard_map/all_to_all | solution.py:1025
  118.6 5.5 %transpose_rows.1.n1t = bf16[2048,1024]{1,0:T(8,128)(2,1)} custom-call(bf16[256,2048]{1,0:T(8,128)(2,1)} %get-tuple-element.212.n0, bf16[256,2048]{1,0:T(8,128)(2,1)} %get-tuple-element.213.n1, bf16[256,2048]{1,0:T(8,128)(2,1)} %get-tuple-element.214.n2, bf16[256,2048]{1,0:T(8,128)(2,1)} %get-tuple-element.215.n3), custom_call_target="tpu_custom_call" | custom-call | flops 1 | bytes 3600001 | tf_op jit(solution)/shard_map/transpose_rows/pallas_call | solution.py:61
  124.8 7.5 %expert_grad_rows.1 = (bf16[640,2048]{1,0:T(8,128)(2,1)}, f32[640,768]{1,0:T(8,128)}) custom-call(bf16[128,88,128]{2,1,0:T(8,128)(2,1)} %all-to-all-done.1.wire, bf16[768,2048]{1,0:T(8,128)(2,1)} %bitcast.58), custom_call_target="tpu_custom_call" | custom-call | flops 1 | bytes 4800001 | tf_op jit(solution)/shard_map/expert_grad_rows/pallas_call | solution.py:61
  132.3 23.9 %all-to-all-done.wire = bf16[128,88,128]{2,1,0:T(8,128)(2,1)} async-done(((bf16[128,88,128]{2,1,0:T(8,128)(2,1)}), bf16[128,88,128]{2,1,0:T(8,128)(2,1)}, u32[]{:S(2)}, u32[]{:S(2)}) %all-to-all-start) | async-done | bytes 2883616 | tf_op jit(solution)/shard_map/all_to_all | solution.py:1025
  156.1 18.6 %expert_main.1 = (bf16[128,88,128]{2,1,0:T(8,128)(2,1)}, bf16[640,2048]{1,0:T(8,128)(2,1)}, bf16[640,768]{1,0:T(8,128)(2,1)}, bf16[640,768]{1,0:T(8,128)(2,1)}, ...) custom-call(bf16[128,88,128]{2,1,0:T(8,128)(2,1)} %all-to-all-done.wire, bf16[2048,768]{1,0:T(8,128)(2,1)} %bitcast.61, ...), custom_call_target="tpu_custom_call" | custom-call | flops 1 | bytes 10800001 | tf_op jit(solution)/shard_map/expert_main/pallas_call | solution.py:61
  174.7 5.9 %all-to-all-start.2 = ((bf16[128,88,128]{2,1,0:T(8,128)(2,1)}), bf16[128,88,128]{2,1,0:T(8,128)(2,1)}, u32[]{:S(2)}, u32[]{:S(2)}) async-start(bf16[128,88,128]{2,1,0:T(8,128)(2,1)} %get-tuple-element.240), calls=%async_computation.2 | async-start | bytes 5767168 | tf_op jit(solution)/shard_map/all_to_all | solution.py:1025
  182.7 6.6 %expert_out.1 = bf16[128,80,128]{2,1,0:T(8,128)(2,1)} custom-call(bf16[640,768]{1,0:T(8,128)(2,1)} %get-tuple-element.246.act, bf16[768,2048]{1,0:T(8,128)(2,1)} %bitcast.59), custom_call_target="tpu_custom_call" | custom-call | flops 1 | bytes 4200001 | tf_op jit(solution)/shard_map/expert_out/pallas_call | solution.py:61
  189.3 7.5 %fusion.6 = f32[2048,768]{1,0:T(8,128)} fusion(bf16[640,2048]{1,0:T(8,128)(2,1)} %get-tuple-element.247, bf16[640,768]{1,0:T(8,128)(2,1)} %get-tuple-element.248), kind=kOutput, calls=%fused_computation.27 | convolution fusion | flops 2013265920 | bytes 9895936 | tf_op jit(solution)/shard_map/dot_general | solution.py:1132
  196.8 4.6 fusion.7
  201.4 4.5 fusion.8
  206.0 13.4 %all-to-all-done.2.wire = bf16[128,88,128]{2,1,0:T(8,128)(2,1)} async-done(((bf16[128,88,128]{2,1,0:T(8,128)(2,1)}), bf16[128,88,128]{2,1,0:T(8,128)(2,1)}, u32[]{:S(2)}, u32[]{:S(2)}) %all-to-all-start.2) | async-done | bytes 2883616 | tf_op jit(solution)/shard_map/all_to_all | solution.py:1025
  219.3 7.1 %combine_grads.1 = (f32[128,2048]{1,0:T(8,128)}, bf16[128,2048]{1,0:T(8,128)(2,1)}, bf16[4,256,128]{2,1,0:T(8,128)(2,1)}, bf16[4,256,128]{2,1,0:T(8,128)(2,1)}, f32[1,2048]{1,0:T(1,128)}) custom-call(s32[4]{0:T(128)} %pad_add_fusion.where, s32[512]{0:T(512)} %reshape.196.experts, s32[512]{0:T(512)} %reshape.197.slots, f32[512]{0:T(512)} %reshape.195.gate_list, ...), custom_call_target="tpu_custom_call" | custom-call | flops 1 | bytes 4200001 | tf_op jit(solution)/shard_map/combine_grads/pallas_call | solution.py:61
  226.5 2.7 collective-permute-start.18
  230.6 21.1 %collective-permute-done.20.refs_4_.refs_3_ = bf16[128,2048]{1,0:T(8,128)(2,1)S(1)} collective-permute-done((bf16[128,2048]{1,0:T(8,128)(2,1)}, bf16[128,2048]{1,0:T(8,128)(2,1)S(1)}, u32[]{:S(2)}, u32[]{:S(2)}) %collective-permute-start.20) | collective-permute-done | bytes 524320 | tf_op jit(solution)/shard_map/ppermute | solution.py:1017
  254.1 2.5 collective-permute-done.22.b
  259.1 2.7 collective-permute-start.24
  262.5 5.3 %head_grad.1.refs_16_ = bf16[512,768]{1,0:T(8,128)(2,1)} custom-call(bf16[128,2048]{1,0:T(8,128)(2,1)} %get-tuple-element.256.refs_0_, bf16[128,2048]{1,0:T(8,128)(2,1)} %collective-permute-done.17.refs_1_.refs_4_, bf16[128,2048]{1,0:T(8,128)(2,1)} %collective-permute-done.18.refs_2_.refs_1_, bf16[128,2048]{1,0:T(8,128)(2,1)} %collective-permute-done.19.refs_3_.refs_5_, ...), custom_call_target="tpu_custom_call" | custom-call | flops 1 | bytes 2400001 | tf_op jit(solution)/shard_map/head_grad/pallas_call | solution.py:61
  268.4 10.3 %out_projection_grad.1 = (bf16[4,528,128]{2,1,0:T(8,128)(2,1)}, bf16[4,528,128]{2,1,0:T(8,128)(2,1)}, bf16[4,528,128]{2,1,0:T(8,128)(2,1)}, bf16[4,528,128]{2,1,0:T(8,128)(2,1)}, bf16[512,256]{1,0:T(8,128)(2,1)}) custom-call(s32[4]{0:T(128)} %pad_add_fusion.where, bf16[128,2048]{1,0:T(8,128)(2,1)} %get-tuple-element.256.refs_0_, ...), custom_call_target="tpu_custom_call" | custom-call | flops 1 | bytes 4200001 | tf_op jit(solution)/shard_map/out_projection_grad/pallas_call | solution.py:74
  278.7 5.8 %all-to-all-start.3 = ((bf16[128,80,128]{2,1,0:T(8,128)(2,1)}), bf16[128,80,128]{2,1,0:T(8,128)(2,1)}, u32[]{:S(2)}, u32[]{:S(2)}) async-start(bf16[128,80,128]{2,1,0:T(8,128)(2,1)} %expert_out.1), calls=%async_computation.3 | async-start | bytes 5242880 | tf_op jit(solution)/shard_map/all_to_all | solution.py:1025
  287.3 2.1 collective-permute-start.28
  289.3 18.8 %attend_grad.1 = (bf16[512,512]{1,0:T(8,128)(2,1)}, bf16[512,512]{1,0:T(8,128)(2,1)}, bf16[256,1024]{1,0:T(8,128)(2,1)}, f32[8,128]{1,0:T(8,128)}, f32[8,128]{1,0:T(8,128)}) custom-call(bf16[512,256]{1,0:T(8,128)(2,1)} %get-tuple-element.221.refs_0_, bf16[512,256]{1,0:T(8,128)(2,1)} %get-tuple-element.222.refs_1_, ...), custom_call_target="tpu_custom_call" | custom-call | flops 1 | bytes 1 | tf_op jit(solution)/shard_map/attend_grad/pallas_call | solution.py:61
  308.1 18.5 %collective-permute-done.26.b = bf16[4,528,128]{2,1,0:T(8,128)(2,1)S(1)} collective-permute-done((bf16[4,528,128]{2,1,0:T(8,128)(2,1)}, bf16[4,528,128]{2,1,0:T(8,128)(2,1)S(1)}, u32[]{:S(2)}, u32[]{:S(2)}) %collective-permute-start.26) | collective-permute-done | bytes 540704 | tf_op jit(solution)/shard_map/ppermute | solution.py:1036
  326.7 11.8 %collective-permute-done.28.d = bf16[4,528,128]{2,1,0:T(8,128)(2,1)} collective-permute-done((bf16[4,528,128]{2,1,0:T(8,128)(2,1)}, bf16[4,528,128]{2,1,0:T(8,128)(2,1)}, u32[]{:S(2)}, u32[]{:S(2)}) %collective-permute-start.28) | collective-permute-done | bytes 540704 | tf_op jit(solution)/shard_map/ppermute | solution.py:1036
  339.4 1.9 collective-permute-done.29.sib
  341.2 9.1 %qkv_weight_grad.1 = (bf16[4,128,640]{2,1,0:T(8,128)(2,1)}, bf16[4,128,640]{2,1,0:T(8,128)(2,1)}, bf16[4,128,640]{2,1,0:T(8,128)(2,1)}, bf16[4,128,640]{2,1,0:T(8,128)(2,1)}, bf16[256,1024]{1,0:T(8,128)(2,1)}) custom-call(s32[4]{0:T(128)} %pad_add_fusion.where, bf16[2048,1024]{1,0:T(8,128)(2,1)} %transpose_rows.1.n1t, ...), custom_call_target="tpu_custom_call" | custom-call | flops 1 | bytes 1 | tf_op jit(solution)/shard_map/qkv_weight_grad/pallas_call | solution.py:74
  354.9 2.5 add_parts.2
  358.1 27.2 %collective-permute-done.33.b = bf16[528,128]{1,0:T(8,128)(2,1)S(1)} collective-permute-done((bf16[528,128]{1,0:T(8,128)(2,1)}, bf16[528,128]{1,0:T(8,128)(2,1)S(1)}, u32[]{:S(2)}, u32[]{:S(2)}) %collective-permute-start.33) | collective-permute-done | bytes 135200 | tf_op jit(solution)/shard_map/ppermute | solution.py:1036
  386.7 7.8 %normed_grad.1 = (bf16[144,2048]{1,0:T(8,128)(2,1)}, bf16[144,2048]{1,0:T(8,128)(2,1)}, bf16[144,2048]{1,0:T(8,128)(2,1)}, bf16[144,2048]{1,0:T(8,128)(2,1)}) custom-call(bf16[512,2048]{1,0:T(8,128)(2,1)} %bitcast.5.refs_4_.refs_8_.wa, bf16[512,2048]{1,0:T(8,128)(2,1)} %collective-permute-done.14.wb, bf16[256,2048]{1,0:T(8,128)(2,1)} %get-tuple-element.303.wkv, ...), custom_call_target="tpu_custom_call" | custom-call | flops 1 | bytes 1 | tf_op jit(solution)/shard_map/normed_grad/pallas_call | solution.py:74
  399.0 1.8 add_last.2
  401.5 3.0 collective-permute-start.40
  404.5 2.7 add_parts.3
  409.1 3.8 collective-permute-done.39.b
  415.0 2.7 collective-permute-done.37.c
  417.7 2.8 collective-permute-done.38.d
  420.5 2.6 collective-permute-done.45.b3
  423.1 3.9 input_grad.1
  427.9 2.9 collective-permute-start.49
  431.6 5.7 %all-to-all-start.4 = ((bf16[128,16,128]{2,1,0:T(8,128)(2,1)}), bf16[128,16,128]{2,1,0:T(8,128)(2,1)S(1)}, u32[]{:S(2)}, u32[]{:S(2)}) async-start(bf16[128,16,128]{2,1,0:T(8,128)(2,1)} %broadcast_in_dim.41), calls=%async_computation.4 | async-start | bytes 1048576 | tf_op jit(solution)/shard_map/all_to_all | solution.py:1025
  437.3 1.9 add_last.3.a
  440.6 2.4 collective-permute-start.47
  444.1 1.9 stack_parts.3.c0
  447.1 2.1 collective-permute-done.48.d
  449.2 3.7 collective-permute-done.47.c
  453.6 2.1 stack_parts.2.c0
  457.0 2.9 collective-permute-start.51
  461.1 3.4 collective-permute-done.55.c3
  465.8 4.5 result.1
  470.3 32.2 %all-gather.1 = f32[16,3,2048]{2,1,0:T(4,128)S(1)} all-gather(f32[1,3,2048]{2,1,0:T(4,128)S(1)} %bitcast.75), channel_id=2, replica_groups=mesh['expert'=16,'shard'=8] {'expert'}, dimensions={0}, use_global_device_ids=true | all-gather | bytes 417792 | tf_op jit(solution)/shard_map/all_gather | solution.py:1186
  502.7 4.1 place_output_grads.1
  507.9 4.3 place_weight_grads.1
  (187 shorter events, 63.9 us)
Async XLA Ops:
  0.7 24.8 %collective-permute-start.3 = (bf16[128,2048]{1,0:T(8,128)(2,1)}, bf16[128,2048]{1,0:T(8,128)(2,1)}, u32[]{:S(2)}, u32[]{:S(2)}) collective-permute-start(bf16[128,2048]{1,0:T(8,128)(2,1)} %x0.3), channel_id=1, source_target_pairs={{0,1},{1,0},{2,3},{3,2},{4,5},{5,4},{6,7},{7,6},{8,9},{9,8},{10,11... | collective-permute-start | bytes 1572872 | tf_op jit(solution)/shard_map/ppermute | solution.py:1013
  2.2 29.0 %collective-permute-start.2 = (bf16[128,2048]{1,0:T(8,128)(2,1)}, bf16[128,2048]{1,0:T(8,128)(2,1)}, u32[]{:S(2)}, u32[]{:S(2)}) collective-permute-start(bf16[128,2048]{1,0:T(8,128)(2,1)} %x0.3), channel_id=1, source_target_pairs={{0,2},{1,3},{2,4},{3,5},{4,6},{5,7},{6,0},{7,1},{8,10},{9,11},{10,... | collective-permute-start | bytes 1572872 | tf_op jit(solution)/shard_map/ppermute | solution.py:1017
  3.6 27.6 %collective-permute-start.1 = (bf16[128,2048]{1,0:T(8,128)(2,1)}, bf16[128,2048]{1,0:T(8,128)(2,1)}, u32[]{:S(2)}, u32[]{:S(2)}) collective-permute-start(bf16[128,2048]{1,0:T(8,128)(2,1)} %x0.3), channel_id=1, source_target_pairs={{0,4},{1,5},{2,6},{3,7},{4,0},{5,1},{6,2},{7,3},{8,12},{9,13},{10,... | collective-permute-start | bytes 1572872 | tf_op jit(solution)/shard_map/ppermute | solution.py:1017
  6.2 25.0 %collective-permute-start = (bf16[128,2048]{1,0:T(8,128)(2,1)}, bf16[128,2048]{1,0:T(8,128)(2,1)}, u32[]{:S(2)}, u32[]{:S(2)}) collective-permute-start(bf16[128,2048]{1,0:T(8,128)(2,1)} %x0.3), channel_id=1, source_target_pairs={{0,6},{1,7},{2,0},{3,1},{4,2},{5,3},{6,4},{7,5},{8,14},{9,15},{10,... | collective-permute-start | bytes 1572872 | tf_op jit(solution)/shard_map/ppermute | solution.py:1017
  7.3 4.4 collective-permute-start.4
  11.6 13.9 %collective-permute-start.5 = (bf16[64,2048]{1,0:T(8,128)(2,1)}, bf16[64,2048]{1,0:T(8,128)(2,1)S(1)}, u32[]{:S(2)}, u32[]{:S(2)}) collective-permute-start(bf16[64,2048]{1,0:T(8,128)(2,1)} %bitcast.67), channel_id=1, source_target_pairs={{0,1},{1,0},{2,3},{3,2},{4,5},{5,4},{6,7},{7,6},{8,9},{9,8},{10,11... | collective-permute-start | bytes 786440 | tf_op jit(solution)/shard_map/ppermute | solution.py:1013
  31.2 76.5 %all-to-all-start.1 = ((bf16[128,88,128]{2,1,0:T(8,128)(2,1)}), bf16[128,88,128]{2,1,0:T(8,128)(2,1)}, u32[]{:S(2)}, u32[]{:S(2)}) async-start(bf16[128,88,128]{2,1,0:T(8,128)(2,1)} %pack_rows.1), calls=%async_computation.1 | async-start | bytes 5767168 | tf_op jit(solution)/shard_map/all_to_all | solution.py:1025
  40.4 28.4 %collective-permute-start.10 = (bf16[512,2048]{1,0:T(8,128)(2,1)}, bf16[512,2048]{1,0:T(8,128)(2,1)}, u32[]{:S(2)}, u32[]{:S(2)}) collective-permute-start(bf16[512,2048]{1,0:T(8,128)(2,1)} %refs_14_.1), channel_id=1, source_target_pairs={{0,1},{1,0},{2,3},{3,2},{4,5},{5,4},{6,7},{7,6},{8,9},{9,8},{10,11... | collective-permute-start | bytes 6291464 | tf_op jit(solution)/shard_map/ppermute | solution.py:1013
  41.6 5.4 %collective-permute-start.6 = (bf16[128,2048]{1,0:T(8,128)(2,1)}, bf16[128,2048]{1,0:T(8,128)(2,1)S(1)}, u32[]{:S(2)}, u32[]{:S(2)}) collective-permute-start(bf16[128,2048]{1,0:T(8,128)(2,1)} %collective-permute-done.refs_1_), channel_id=1, source_target_pairs={{0,1},{1,0},{2,3},{3,2},{4,5},{5,4},{6,7},{7,6},{8,9},{9,8},{10,11... | collective-permute-start | bytes 1572872 | tf_op jit(solution)/shard_map/ppermute | solution.py:1013
  41.7 5.5 %collective-permute-start.7 = (bf16[128,2048]{1,0:T(8,128)(2,1)}, bf16[128,2048]{1,0:T(8,128)(2,1)}, u32[]{:S(2)}, u32[]{:S(2)}) collective-permute-start(bf16[128,2048]{1,0:T(8,128)(2,1)} %collective-permute-done.1.refs_3_), channel_id=1, source_target_pairs={{0,1},{1,0},{2,3},{3,2},{4,5},{5,4},{6,7},{7,6},{8,9},{9,8},{10,11... | collective-permute-start | bytes 1572872 | tf_op jit(solution)/shard_map/ppermute | solution.py:1013
  42.1 5.9 %collective-permute-start.8 = (bf16[128,2048]{1,0:T(8,128)(2,1)}, bf16[128,2048]{1,0:T(8,128)(2,1)}, u32[]{:S(2)}, u32[]{:S(2)}) collective-permute-start(bf16[128,2048]{1,0:T(8,128)(2,1)} %collective-permute-done.2.refs_5_), channel_id=1, source_target_pairs={{0,1},{1,0},{2,3},{3,2},{4,5},{5,4},{6,7},{7,6},{8,9},{9,8},{10,11... | collective-permute-start | bytes 1572872 | tf_op jit(solution)/shard_map/ppermute | solution.py:1013
  66.7 2.1 collective-permute-start.9
  75.8 14.6 %collective-permute-start.11 = (bf16[128,2048]{1,0:T(8,128)(2,1)}, bf16[128,2048]{1,0:T(8,128)(2,1)S(1)}, u32[]{:S(2)}, u32[]{:S(2)}) collective-permute-start(bf16[128,2048]{1,0:T(8,128)(2,1)} %get-tuple-element.203), channel_id=1, source_target_pairs={{0,2},{1,3},{2,4},{3,5},{4,6},{5,7},{6,0},{7,1},{8,10},{9,11},{10,... | collective-permute-start | bytes 1572872 | tf_op jit(solution)/shard_map/ppermute | solution.py:1021
  76.4 13.9 %collective-permute-start.12 = (bf16[128,2048]{1,0:T(8,128)(2,1)}, bf16[128,2048]{1,0:T(8,128)(2,1)}, u32[]{:S(2)}, u32[]{:S(2)}) collective-permute-start(bf16[128,2048]{1,0:T(8,128)(2,1)} %get-tuple-element.204), channel_id=1, source_target_pairs={{0,6},{1,7},{2,0},{3,1},{4,2},{5,3},{6,4},{7,5},{8,14},{9,15},{10,... | collective-permute-start | bytes 1572872 | tf_op jit(solution)/shard_map/ppermute | solution.py:1021
  78.4 23.6 %collective-permute-start.13 = (bf16[128,2048]{1,0:T(8,128)(2,1)}, bf16[128,2048]{1,0:T(8,128)(2,1)}, u32[]{:S(2)}, u32[]{:S(2)}) collective-permute-start(bf16[128,2048]{1,0:T(8,128)(2,1)} %get-tuple-element.205), channel_id=1, source_target_pairs={{0,4},{1,5},{2,6},{3,7},{4,0},{5,1},{6,2},{7,3},{8,12},{9,13},{10,... | collective-permute-start | bytes 1572872 | tf_op jit(solution)/shard_map/ppermute | solution.py:1021
  107.7 48.4 %all-to-all-start = ((bf16[128,88,128]{2,1,0:T(8,128)(2,1)}), bf16[128,88,128]{2,1,0:T(8,128)(2,1)}, u32[]{:S(2)}, u32[]{:S(2)}) async-start(bf16[128,88,128]{2,1,0:T(8,128)(2,1)} %get-tuple-element.207), calls=%async_computation | async-start | bytes 5767168 | tf_op jit(solution)/shard_map/all_to_all | solution.py:1025
  117.4 14.8 %collective-permute-start.14 = (bf16[512,2048]{1,0:T(8,128)(2,1)}, bf16[512,2048]{1,0:T(8,128)(2,1)}, u32[]{:S(2)}, u32[]{:S(2)}) collective-permute-start(bf16[512,2048]{1,0:T(8,128)(2,1)} %bitcast.5.refs_4_.refs_8_.wa), channel_id=1, source_target_pairs={{0,1},{1,0},{2,3},{3,2},{4,5},{5,4},{6,7},{7,6},{8,9},{9,8},{10,11... | collective-permute-start | bytes 6291464 | tf_op jit(solution)/shard_map/ppermute | solution.py:1013
  174.7 44.6 %all-to-all-start.2 = ((bf16[128,88,128]{2,1,0:T(8,128)(2,1)}), bf16[128,88,128]{2,1,0:T(8,128)(2,1)}, u32[]{:S(2)}, u32[]{:S(2)}) async-start(bf16[128,88,128]{2,1,0:T(8,128)(2,1)} %get-tuple-element.240), calls=%async_computation.2 | async-start | bytes 5767168 | tf_op jit(solution)/shard_map/all_to_all | solution.py:1025
  226.5 25.2 %collective-permute-start.20 = (bf16[128,2048]{1,0:T(8,128)(2,1)}, bf16[128,2048]{1,0:T(8,128)(2,1)S(1)}, u32[]{:S(2)}, u32[]{:S(2)}) collective-permute-start(bf16[128,2048]{1,0:T(8,128)(2,1)} %get-tuple-element.256.refs_0_), channel_id=1, source_target_pairs={{0,2},{1,3},{2,4},{3,5},{4,6},{5,7},{6,0},{7,1},{8,10},{9,11},{10,... | collective-permute-start | bytes 1572872 | tf_op jit(solution)/shard_map/ppermute | solution.py:1017
  226.5 27.0 %collective-permute-start.18 = (bf16[128,2048]{1,0:T(8,128)(2,1)}, bf16[128,2048]{1,0:T(8,128)(2,1)}, u32[]{:S(2)}, u32[]{:S(2)}) collective-permute-start(bf16[128,2048]{1,0:T(8,128)(2,1)} %get-tuple-element.256.refs_0_), channel_id=1, source_target_pairs={{0,6},{1,7},{2,0},{3,1},{4,2},{5,3},{6,4},{7,5},{8,14},{9,15},{10,... | collective-permute-start | bytes 1572872 | tf_op jit(solution)/shard_map/ppermute | solution.py:1017
  229.1 24.4 %collective-permute-start.15 = (bf16[128,2048]{1,0:T(8,128)(2,1)}, bf16[128,2048]{1,0:T(8,128)(2,1)}, u32[]{:S(2)}, u32[]{:S(2)}) collective-permute-start(bf16[128,2048]{1,0:T(8,128)(2,1)} %get-tuple-element.256.refs_0_), channel_id=1, source_target_pairs={{0,4},{1,5},{2,6},{3,7},{4,0},{5,1},{6,2},{7,3},{8,12},{9,13},{10,... | collective-permute-start | bytes 1572872 | tf_op jit(solution)/shard_map/ppermute | solution.py:1017
  229.1 29.9 %collective-permute-start.17 = (bf16[128,2048]{1,0:T(8,128)(2,1)}, bf16[128,2048]{1,0:T(8,128)(2,1)}, u32[]{:S(2)}, u32[]{:S(2)}) collective-permute-start(bf16[128,2048]{1,0:T(8,128)(2,1)} %get-tuple-element.256.refs_0_), channel_id=1, source_target_pairs={{0,1},{1,0},{2,3},{3,2},{4,5},{5,4},{6,7},{7,6},{8,9},{9,8},{10,11... | collective-permute-start | bytes 1572872 | tf_op jit(solution)/shard_map/ppermute | solution.py:1013
  251.7 10.0 %collective-permute-start.21 = (bf16[128,2048]{1,0:T(8,128)(2,1)S(1)}, bf16[128,2048]{1,0:T(8,128)(2,1)}, u32[]{:S(2)}, u32[]{:S(2)}) collective-permute-start(bf16[128,2048]{1,0:T(8,128)(2,1)S(1)} %collective-permute-done.20.refs_4_.refs_3_), channel_id=1, source_target_pairs={{0,1},{1,0},{2,3},{3,2},{4,5},{5,4},{6,7},{7,6},{8,9},{9,8},{10,11... | collective-permute-start | bytes 1572872 | tf_op jit(solution)/shard_map/ppermute | solution.py:1013
  253.5 9.0 %collective-permute-start.19 = (bf16[128,2048]{1,0:T(8,128)(2,1)}, bf16[128,2048]{1,0:T(8,128)(2,1)}, u32[]{:S(2)}, u32[]{:S(2)}) collective-permute-start(bf16[128,2048]{1,0:T(8,128)(2,1)} %collective-permute-done.18.refs_2_.refs_1_), channel_id=1, source_target_pairs={{0,1},{1,0},{2,3},{3,2},{4,5},{5,4},{6,7},{7,6},{8,9},{9,8},{10,11... | collective-permute-start | bytes 1572872 | tf_op jit(solution)/shard_map/ppermute | solution.py:1013
  253.5 14.2 %collective-permute-start.16 = (bf16[128,2048]{1,0:T(8,128)(2,1)}, bf16[128,2048]{1,0:T(8,128)(2,1)}, u32[]{:S(2)}, u32[]{:S(2)}) collective-permute-start(bf16[128,2048]{1,0:T(8,128)(2,1)} %collective-permute-done.15.refs_2_), channel_id=1, source_target_pairs={{0,1},{1,0},{2,3},{3,2},{4,5},{5,4},{6,7},{7,6},{8,9},{9,8},{10,11... | collective-permute-start | bytes 1572872 | tf_op jit(solution)/shard_map/ppermute | solution.py:1013
  254.0 2.6 collective-permute-start.22
  259.0 8.7 %collective-permute-start.23 = (bf16[256,128]{1,0:T(8,128)(2,1)}, bf16[256,128]{1,0:T(8,128)(2,1)S(1)}, u32[]{:S(2)}, u32[]{:S(2)}) collective-permute-start(bf16[256,128]{1,0:T(8,128)(2,1)} %get-tuple-element.263), channel_id=1, source_target_pairs={{0,2},{1,3},{2,4},{3,5},{4,6},{5,7},{6,0},{7,1},{8,10},{9,11},{10,... | collective-permute-start | bytes 196616 | tf_op jit(solution)/shard_map/ppermute | solution.py:1021
  259.1 8.7 %collective-permute-start.24 = (bf16[256,128]{1,0:T(8,128)(2,1)}, bf16[256,128]{1,0:T(8,128)(2,1)S(1)}, u32[]{:S(2)}, u32[]{:S(2)}) collective-permute-start(bf16[256,128]{1,0:T(8,128)(2,1)} %get-tuple-element.264), channel_id=1, source_target_pairs={{0,6},{1,7},{2,0},{3,1},{4,2},{5,3},{6,4},{7,5},{8,14},{9,15},{10,... | collective-permute-start | bytes 196616 | tf_op jit(solution)/shard_map/ppermute | solution.py:1021
  261.7 6.1 %collective-permute-start.25 = (bf16[256,128]{1,0:T(8,128)(2,1)}, bf16[256,128]{1,0:T(8,128)(2,1)S(1)}, u32[]{:S(2)}, u32[]{:S(2)}) collective-permute-start(bf16[256,128]{1,0:T(8,128)(2,1)} %get-tuple-element.265), channel_id=1, source_target_pairs={{0,4},{1,5},{2,6},{3,7},{4,0},{5,1},{6,2},{7,3},{8,12},{9,13},{10,... | collective-permute-start | bytes 196616 | tf_op jit(solution)/shard_map/ppermute | solution.py:1021
  278.7 108.0 %all-to-all-start.3 = ((bf16[128,80,128]{2,1,0:T(8,128)(2,1)}), bf16[128,80,128]{2,1,0:T(8,128)(2,1)}, u32[]{:S(2)}, u32[]{:S(2)}) async-start(bf16[128,80,128]{2,1,0:T(8,128)(2,1)} %expert_out.1), calls=%async_computation.3 | async-start | bytes 5242880 | tf_op jit(solution)/shard_map/all_to_all | solution.py:1025
  284.5 42.1 %collective-permute-start.26 = (bf16[4,528,128]{2,1,0:T(8,128)(2,1)}, bf16[4,528,128]{2,1,0:T(8,128)(2,1)S(1)}, u32[]{:S(2)}, u32[]{:S(2)}) collective-permute-start(bf16[4,528,128]{2,1,0:T(8,128)(2,1)} %get-tuple-element.272), channel_id=1, source_target_pairs={{0,8},{8,16},{16,24},{24,0},{32,40},{40,48},{48,56},{56,32},{64,72... | collective-permute-start | bytes 1622024 | tf_op jit(solution)/shard_map/ppermute | solution.py:1036
  286.0 40.7 %collective-permute-start.27 = (bf16[4,528,128]{2,1,0:T(8,128)(2,1)}, bf16[4,528,128]{2,1,0:T(8,128)(2,1)}, u32[]{:S(2)}, u32[]{:S(2)}) collective-permute-start(bf16[4,528,128]{2,1,0:T(8,128)(2,1)} %get-tuple-element.273), channel_id=1, source_target_pairs={{0,24},{8,0},{16,8},{24,16},{32,56},{40,32},{48,40},{56,48},{64,88... | collective-permute-start | bytes 1622024 | tf_op jit(solution)/shard_map/ppermute | solution.py:1036
  287.3 51.2 %collective-permute-start.28 = (bf16[4,528,128]{2,1,0:T(8,128)(2,1)}, bf16[4,528,128]{2,1,0:T(8,128)(2,1)}, u32[]{:S(2)}, u32[]{:S(2)}) collective-permute-start(bf16[4,528,128]{2,1,0:T(8,128)(2,1)} %get-tuple-element.274), channel_id=1, source_target_pairs={{0,16},{8,24},{16,0},{24,8},{32,48},{40,56},{48,32},{56,40},{64,80... | collective-permute-start | bytes 1622024 | tf_op jit(solution)/shard_map/ppermute | solution.py:1036
  326.7 23.7 %copy-start.9 = (bf16[4,528,128]{2,1,0:T(8,128)(2,1)}, bf16[4,528,128]{2,1,0:T(8,128)(2,1)S(1)}, u32[]{:S(2)}) copy-start(bf16[4,528,128]{2,1,0:T(8,128)(2,1)S(1)} %collective-permute-done.26.b) | copy-start | bytes 1622020
  338.5 2.8 collective-permute-start.29
  339.4 47.2 %collective-permute-start.42 = (bf16[512,512]{1,0:T(8,128)(2,1)}, bf16[512,512]{1,0:T(8,128)(2,1)}, u32[]{:S(2)}, u32[]{:S(2)}) collective-permute-start(bf16[512,512]{1,0:T(8,128)(2,1)} %get-tuple-element.275.dq1), channel_id=1, source_target_pairs={{0,1},{1,0},{2,3},{3,2},{4,5},{5,4},{6,7},{7,6},{8,9},{9,8},{10,11... | collective-permute-start | bytes 1572872 | tf_op jit(solution)/shard_map/ppermute | solution.py:1013
  350.3 47.0 %collective-permute-start.30 = (bf16[4,128,640]{2,1,0:T(8,128)(2,1)}, bf16[4,128,640]{2,1,0:T(8,128)(2,1)S(1)}, u32[]{:S(2)}, u32[]{:S(2)}) collective-permute-start(bf16[4,128,640]{2,1,0:T(8,128)(2,1)} %get-tuple-element.278), channel_id=1, source_target_pairs={{0,32},{8,40},{16,48},{24,56},{32,64},{40,72},{48,80},{56,88},{64,... | collective-permute-start | bytes 1966088 | tf_op jit(solution)/shard_map/ppermute | solution.py:1036
  351.7 47.3 %collective-permute-start.31 = (bf16[4,128,640]{2,1,0:T(8,128)(2,1)}, bf16[4,128,640]{2,1,0:T(8,128)(2,1)}, u32[]{:S(2)}, u32[]{:S(2)}) collective-permute-start(bf16[4,128,640]{2,1,0:T(8,128)(2,1)} %get-tuple-element.279), channel_id=1, source_target_pairs={{0,96},{8,104},{16,112},{24,120},{32,0},{40,8},{48,16},{56,24},{64... | collective-permute-start | bytes 1966088 | tf_op jit(solution)/shard_map/ppermute | solution.py:1036
  353.5 45.4 %collective-permute-start.32 = (bf16[4,128,640]{2,1,0:T(8,128)(2,1)}, bf16[4,128,640]{2,1,0:T(8,128)(2,1)}, u32[]{:S(2)}, u32[]{:S(2)}) collective-permute-start(bf16[4,128,640]{2,1,0:T(8,128)(2,1)} %get-tuple-element.280), channel_id=1, source_target_pairs={{0,64},{8,72},{16,80},{24,88},{32,96},{40,104},{48,112},{56,120},{... | collective-permute-start | bytes 1966088 | tf_op jit(solution)/shard_map/ppermute | solution.py:1036
  357.4 28.0 %collective-permute-start.33 = (bf16[528,128]{1,0:T(8,128)(2,1)}, bf16[528,128]{1,0:T(8,128)(2,1)S(1)}, u32[]{:S(2)}, u32[]{:S(2)}) collective-permute-start(bf16[528,128]{1,0:T(8,128)(2,1)} %get-tuple-element.286), channel_id=1, source_target_pairs={{0,32},{8,40},{16,48},{24,56},{32,64},{40,72},{48,80},{56,88},{64,... | collective-permute-start | bytes 405512 | tf_op jit(solution)/shard_map/ppermute | solution.py:1036
  385.4 9.2 %collective-permute-start.34 = (bf16[528,128]{1,0:T(8,128)(2,1)}, bf16[528,128]{1,0:T(8,128)(2,1)S(1)}, u32[]{:S(2)}, u32[]{:S(2)}) collective-permute-start(bf16[528,128]{1,0:T(8,128)(2,1)} %get-tuple-element.287), channel_id=1, source_target_pairs={{0,96},{8,104},{16,112},{24,120},{32,0},{40,8},{48,16},{56,24},{64... | collective-permute-start | bytes 405512 | tf_op jit(solution)/shard_map/ppermute | solution.py:1036
  386.6 9.3 %collective-permute-start.35 = (bf16[528,128]{1,0:T(8,128)(2,1)}, bf16[528,128]{1,0:T(8,128)(2,1)}, u32[]{:S(2)}, u32[]{:S(2)}) collective-permute-start(bf16[528,128]{1,0:T(8,128)(2,1)} %get-tuple-element.288), channel_id=1, source_target_pairs={{0,64},{8,72},{16,80},{24,88},{32,96},{40,104},{48,112},{56,120},{... | collective-permute-start | bytes 405512 | tf_op jit(solution)/shard_map/ppermute | solution.py:1036
  394.6 25.9 %collective-permute-start.43 = (bf16[144,2048]{1,0:T(8,128)(2,1)}, bf16[144,2048]{1,0:T(8,128)(2,1)}, u32[]{:S(2)}, u32[]{:S(2)}) collective-permute-start(bf16[144,2048]{1,0:T(8,128)(2,1)} %get-tuple-element.312), channel_id=1, source_target_pairs={{0,2},{1,3},{2,4},{3,5},{4,6},{5,7},{6,0},{7,1},{8,10},{9,11},{10,... | collective-permute-start | bytes 1769480 | tf_op jit(solution)/shard_map/ppermute | solution.py:1021
  395.9 24.6 %collective-permute-start.44 = (bf16[144,2048]{1,0:T(8,128)(2,1)}, bf16[144,2048]{1,0:T(8,128)(2,1)}, u32[]{:S(2)}, u32[]{:S(2)}) collective-permute-start(bf16[144,2048]{1,0:T(8,128)(2,1)} %get-tuple-element.313), channel_id=1, source_target_pairs={{0,6},{1,7},{2,0},{3,1},{4,2},{5,3},{6,4},{7,5},{8,14},{9,15},{10,... | collective-permute-start | bytes 1769480 | tf_op jit(solution)/shard_map/ppermute | solution.py:1021
  397.3 25.7 %collective-permute-start.45 = (bf16[144,2048]{1,0:T(8,128)(2,1)}, bf16[144,2048]{1,0:T(8,128)(2,1)}, u32[]{:S(2)}, u32[]{:S(2)}) collective-permute-start(bf16[144,2048]{1,0:T(8,128)(2,1)} %get-tuple-element.314), channel_id=1, source_target_pairs={{0,4},{1,5},{2,6},{3,7},{4,0},{5,1},{6,2},{7,3},{8,12},{9,13},{10,... | collective-permute-start | bytes 1769480 | tf_op jit(solution)/shard_map/ppermute | solution.py:1021
  400.8 6.4 %collective-permute-start.41 = (bf16[512,128]{1,0:T(8,128)(2,1)}, bf16[512,128]{1,0:T(8,128)(2,1)S(1)}, u32[]{:S(2)}, u32[]{:S(2)}) collective-permute-start(bf16[512,128]{1,0:T(8,128)(2,1)} %get-tuple-element.328.a), channel_id=1, source_target_pairs={{0,32},{8,40},{16,48},{24,56},{32,64},{40,72},{48,80},{56,88},{64,... | collective-permute-start | bytes 393224 | tf_op jit(solution)/shard_map/ppermute | solution.py:1036
  401.5 7.2 %collective-permute-start.40 = (bf16[512,128]{1,0:T(8,128)(2,1)}, bf16[512,128]{1,0:T(8,128)(2,1)}, u32[]{:S(2)}, u32[]{:S(2)}) collective-permute-start(bf16[512,128]{1,0:T(8,128)(2,1)} %get-tuple-element.328.a), channel_id=1, source_target_pairs={{0,64},{8,72},{16,80},{24,88},{32,96},{40,104},{48,112},{56,120},{... | collective-permute-start | bytes 393224 | tf_op jit(solution)/shard_map/ppermute | solution.py:1036
  407.2 23.5 %copy-start.28 = (bf16[16,128]{1,0:T(8,128)(2,1)S(1)}, bf16[16,128]{1,0:T(8,128)(2,1)}, u32[]{:S(2)}) copy-start(bf16[16,128]{1,0:T(8,128)(2,1)} %get-tuple-element.336) | copy-start | bytes 12292
  407.2 7.0 %collective-permute-start.36 = (bf16[128,640]{1,0:T(8,128)(2,1)}, bf16[128,640]{1,0:T(8,128)(2,1)S(1)}, u32[]{:S(2)}, u32[]{:S(2)}) collective-permute-start(bf16[128,640]{1,0:T(8,128)(2,1)} %get-tuple-element.294), channel_id=1, source_target_pairs={{0,8},{8,16},{16,24},{24,0},{32,40},{40,48},{48,56},{56,32},{64,72... | collective-permute-start | bytes 491528 | tf_op jit(solution)/shard_map/ppermute | solution.py:1036
  408.7 4.2 collective-permute-start.39
  412.9 4.8 collective-permute-start.37
  414.2 6.3 %collective-permute-start.38 = (bf16[128,640]{1,0:T(8,128)(2,1)}, bf16[128,640]{1,0:T(8,128)(2,1)}, u32[]{:S(2)}, u32[]{:S(2)}) collective-permute-start(bf16[128,640]{1,0:T(8,128)(2,1)} %get-tuple-element.296), channel_id=1, source_target_pairs={{0,16},{8,24},{16,0},{24,8},{32,48},{40,56},{48,32},{56,40},{64,80... | collective-permute-start | bytes 491528 | tf_op jit(solution)/shard_map/ppermute | solution.py:1036
  426.9 19.4 %copy-start.27 = (f32[8,2048]{1,0:T(8,128)S(1)}, f32[8,2048]{1,0:T(8,128)}, u32[]{:S(2)}) copy-start(f32[8,2048]{1,0:T(8,128)} %get-tuple-element.324) | copy-start | bytes 196612
  427.9 18.5 %collective-permute-start.49 = (f32[3,2048]{1,0:T(4,128)S(1)}, f32[3,2048]{1,0:T(4,128)}, u32[]{:S(2)}, u32[]{:S(2)}) collective-permute-start(f32[3,2048]{1,0:T(4,128)S(1)} %slice.31), channel_id=1, source_target_pairs={{0,1},{1,0},{2,3},{3,2},{4,5},{5,4},{6,7},{7,6},{8,9},{9,8},{10,11... | collective-permute-start | bytes 73736 | tf_op jit(solution)/shard_map/ppermute | solution.py:1013
  431.6 33.0 %all-to-all-start.4 = ((bf16[128,16,128]{2,1,0:T(8,128)(2,1)}), bf16[128,16,128]{2,1,0:T(8,128)(2,1)S(1)}, u32[]{:S(2)}, u32[]{:S(2)}) async-start(bf16[128,16,128]{2,1,0:T(8,128)(2,1)} %broadcast_in_dim.41), calls=%async_computation.4 | async-start | bytes 1048576 | tf_op jit(solution)/shard_map/all_to_all | solution.py:1025
  439.2 10.1 %collective-permute-start.48 = (bf16[128,640]{1,0:T(8,128)(2,1)}, bf16[128,640]{1,0:T(8,128)(2,1)S(1)}, u32[]{:S(2)}, u32[]{:S(2)}) collective-permute-start(bf16[128,640]{1,0:T(8,128)(2,1)} %add_last.3.a), channel_id=1, source_target_pairs={{0,8},{8,16},{16,24},{24,0},{32,40},{40,48},{48,56},{56,32},{64,72... | collective-permute-start | bytes 491528 | tf_op jit(solution)/shard_map/ppermute | solution.py:1036
  440.6 12.4 %collective-permute-start.47 = (bf16[128,640]{1,0:T(8,128)(2,1)}, bf16[128,640]{1,0:T(8,128)(2,1)S(1)}, u32[]{:S(2)}, u32[]{:S(2)}) collective-permute-start(bf16[128,640]{1,0:T(8,128)(2,1)} %add_last.3.a), channel_id=1, source_target_pairs={{0,16},{8,24},{16,0},{24,8},{32,48},{40,56},{48,32},{56,40},{64,80... | collective-permute-start | bytes 491528 | tf_op jit(solution)/shard_map/ppermute | solution.py:1036
  443.0 10.0 %collective-permute-start.46 = (bf16[128,640]{1,0:T(8,128)(2,1)}, bf16[128,640]{1,0:T(8,128)(2,1)}, u32[]{:S(2)}, u32[]{:S(2)}) collective-permute-start(bf16[128,640]{1,0:T(8,128)(2,1)} %add_last.3.a), channel_id=1, source_target_pairs={{0,24},{8,0},{16,8},{24,16},{32,56},{40,32},{48,40},{56,48},{64,88... | collective-permute-start | bytes 491528 | tf_op jit(solution)/shard_map/ppermute | solution.py:1036
  446.1 18.4 %collective-permute-start.55 = (bf16[4,512,128]{2,1,0:T(8,128)(2,1)}, bf16[4,512,128]{2,1,0:T(8,128)(2,1)}, u32[]{:S(2)}, u32[]{:S(2)}) collective-permute-start(bf16[4,512,128]{2,1,0:T(8,128)(2,1)} %stack_parts.3.c0), channel_id=1, source_target_pairs={{0,8},{8,16},{16,24},{24,0},{32,40},{40,48},{48,56},{56,32},{64,72... | collective-permute-start | bytes 1572872 | tf_op jit(solution)/shard_map/ppermute | solution.py:1036
  455.7 47.0 %collective-permute-start.52 = (bf16[4,128,640]{2,1,0:T(8,128)(2,1)}, bf16[4,128,640]{2,1,0:T(8,128)(2,1)}, u32[]{:S(2)}, u32[]{:S(2)}) collective-permute-start(bf16[4,128,640]{2,1,0:T(8,128)(2,1)} %stack_parts.2.c0), channel_id=1, source_target_pairs={{0,32},{8,40},{16,48},{24,56},{32,64},{40,72},{48,80},{56,88},{64,... | collective-permute-start | bytes 1966088 | tf_op jit(solution)/shard_map/ppermute | solution.py:1036
  457.0 45.7 %collective-permute-start.51 = (bf16[4,128,640]{2,1,0:T(8,128)(2,1)}, bf16[4,128,640]{2,1,0:T(8,128)(2,1)}, u32[]{:S(2)}, u32[]{:S(2)}) collective-permute-start(bf16[4,128,640]{2,1,0:T(8,128)(2,1)} %stack_parts.2.c0), channel_id=1, source_target_pairs={{0,64},{8,72},{16,80},{24,88},{32,96},{40,104},{48,112},{56,120},{... | collective-permute-start | bytes 1966088 | tf_op jit(solution)/shard_map/ppermute | solution.py:1036
  460.0 42.7 %collective-permute-start.50 = (bf16[4,128,640]{2,1,0:T(8,128)(2,1)}, bf16[4,128,640]{2,1,0:T(8,128)(2,1)}, u32[]{:S(2)}, u32[]{:S(2)}) collective-permute-start(bf16[4,128,640]{2,1,0:T(8,128)(2,1)} %stack_parts.2.c0), channel_id=1, source_target_pairs={{0,96},{8,104},{16,112},{24,120},{32,0},{40,8},{48,16},{56,24},{64... | collective-permute-start | bytes 1966088 | tf_op jit(solution)/shard_map/ppermute | solution.py:1036
  460.9 41.8 %collective-permute-start.54 = (bf16[4,512,128]{2,1,0:T(8,128)(2,1)}, bf16[4,512,128]{2,1,0:T(8,128)(2,1)}, u32[]{:S(2)}, u32[]{:S(2)}) collective-permute-start(bf16[4,512,128]{2,1,0:T(8,128)(2,1)} %stack_parts.3.c0), channel_id=1, source_target_pairs={{0,16},{8,24},{16,0},{24,8},{32,48},{40,56},{48,32},{56,40},{64,80... | collective-permute-start | bytes 1572872 | tf_op jit(solution)/shard_map/ppermute | solution.py:1036
  464.5 38.2 %collective-permute-start.53 = (bf16[4,512,128]{2,1,0:T(8,128)(2,1)}, bf16[4,512,128]{2,1,0:T(8,128)(2,1)}, u32[]{:S(2)}, u32[]{:S(2)}) collective-permute-start(bf16[4,512,128]{2,1,0:T(8,128)(2,1)} %stack_parts.3.c0), channel_id=1, source_target_pairs={{0,24},{8,0},{16,8},{24,16},{32,56},{40,32},{48,40},{56,48},{64,88... | collective-permute-start | bytes 1572872 | tf_op jit(solution)/shard_map/ppermute | solution.py:1036
  (30 other events, 196.3 us)

commit v6 on v5

--- a/solution.py
+++ b/solution.py
@@ -285,20 +285,14 @@
         vn[rows, :] = vt[:, rows].astype(f32).T.astype(bf16)
     build_mask(info, mask)
     for half, out in ((1, ot1), (0, ot0)):
-
-        def body(i, carry):
-            local = pl.ds(pl.multiple_of(i * 256, 256), 256)
-            cols = pl.ds(pl.multiple_of(half * HALF + i * 256, 256), 256)
-            for h in range(LH):
-                heads = slice(h * HEAD, (h + 1) * HEAD)
-                scores = dot(kn[...], qt[heads, cols])
-                weights = jnp.exp2(scores * LOG2E) * mask[:, cols]
-                inverse = 1.0 / jnp.sum(weights, axis=0, keepdims=True)
-                out[heads, local] = (dot(vt[...], weights.astype(bf16)) * inverse).astype(bf16)
-                linv[h : h + 1, cols] = inverse
-            return carry
-
-        lax.fori_loop(0, 2, body, 0)
+        cols = slice(half * HALF, (half + 1) * HALF)
+        for h in range(LH):
+            heads = slice(h * HEAD, (h + 1) * HEAD)
+            scores = dot(kn[...], qt[heads, cols])
+            weights = jnp.exp2(scores * LOG2E) * mask[:, cols]
+            inverse = 1.0 / jnp.sum(weights, axis=0, keepdims=True)
+            out[heads, :] = (dot(vt[...], weights.astype(bf16)) * inverse).astype(bf16)
+            linv[h : h + 1, cols] = inverse
 
 
 def attend(q, k, v, info):
@@ -465,7 +459,7 @@
     sc[...] = jnp.zeros_like(sc)
 
     def forward(i, carry):
-        cols = pl.ds(pl.multiple_of(i * 256, 256), 256)
+        cols = pl.ds(pl.multiple_of(i * 384, 384), 384)
         gate = dot(xr[...], wg[:, cols])
         up = dot(xr[...], wu[:, cols])
         grad = ga[:, cols]
@@ -478,14 +472,14 @@
         sc[...] += jnp.sum(a * grad, axis=1, keepdims=True)
         return carry
 
-    lax.fori_loop(0, F // 256, forward, 0)
+    lax.fori_loop(0, F // 384, forward, 0)
     for s in range(CAP):
         part = slice(s * E, (s + 1) * E)
         gate = gates[:, s : s + 1]
         xs[part, :] = (xr[part, :].astype(f32) * gate).astype(bf16)
         acts[part, :] = (act[part, :].astype(f32) * gate).astype(bf16)
-    for j in range(8):
-        part = slice(j * 256, (j + 1) * 256)
+    for j in range(4):
+        part = slice(j * 512, (j + 1) * 512)
         xr[:, part] = (dot_t(dg[...], wg[part, :]) + dot_t(du[...], wu[part, :])).astype(bf16)
     join_rows(xr, back)
     put_numbers([sc[s * E : (s + 1) * E, :] for s in range(CAP)], back)
@@ -633,27 +627,12 @@
     )[0]
 
 
-def pre_body(where, *refs):
-    blocks, routers = refs[:8], refs[8:12]
-    ot0, ot1, wo, w0, w1, w2, w3, dt, rows_all, total = refs[12:]
+def pre_body(*refs):
+    blocks, (ot0, ot1, wo, gw, dt, rows_all, total) = refs[:8], refs[8:]
     step = pl.program_id(0)
     for b in range(8):
         rows_all[b * T : (b + 1) * T, :] = blocks[b][...]
-    grad = (dot(ot0[...], rows_all[:HALF, :]) + dot(ot1[...], rows_all[HALF:, :])).astype(bf16)
-    for dx, out in enumerate((w0, w1, w2, w3)):
-
-        @pl.when(step == dx)
-        def _():
-            for col in range(4):
-                dz = lax.rem(col + 4 - where[0], 4)
-                start = lax.rem(where[1] + dx, 4) * 64 + col * 16
-                rows = pl.ds(pl.multiple_of(start, 16), 16)
-                out[dz, :512, :] = grad[:, col * 128 : (col + 1) * 128]
-                out[dz, 512:, :] = (
-                    (routers[0][rows, :].astype(f32) + routers[1][rows, :].astype(f32))
-                    + (routers[2][rows, :].astype(f32) + routers[3][rows, :].astype(f32))
-                ).astype(bf16)
-
+    gw[...] = (dot(ot0[...], rows_all[:HALF, :]) + dot(ot1[...], rows_all[HALF:, :])).astype(bf16)
     last = jnp.concatenate([blocks[2][...], blocks[6][...]], axis=0)
     part = dot_t(wo[...], last)
 
@@ -670,23 +649,16 @@
         dt[...] = total[...].astype(bf16)
 
 
-def pre(where, blocks, routers, ot0, ot1, wo):
-    def turned(shape):
-        return pl.BlockSpec(shape, lambda i, w: (0, lax.rem(i + w[1], 4)))
-
+def pre(blocks, ot0, ot1, wo):
     return grid_call(
         pre_body,
         "out_projection_grad",
         (4,),
-        [turned((T, 512))] * 8
-        + [whole((256, E))] * 4
-        + [whole((512, HALF))] * 2
-        + [turned((512, 512))],
-        [whole((4, 528, 128))] * 4 + [whole((512, 2 * T))],
-        [sds((4, 528, 128), bf16)] * 4 + [sds((LH * HEAD, 2 * T), bf16)],
+        [cols_of((T, 512))] * 8 + [whole((512, HALF))] * 2 + [cols_of((512, 512))],
+        [cols_of((512, 512)), whole((512, 2 * T))],
+        [sds((LH * HEAD, D), bf16), sds((LH * HEAD, 2 * T), bf16)],
         [pltpu.VMEM((ROWS, 512), bf16), pltpu.VMEM((512, 2 * T), f32)],
-        (where, *blocks, *routers, ot0, ot1, wo),
-        scalars=1,
+        (*blocks, ot0, ot1, wo),
     )
 
 
@@ -706,33 +678,23 @@
     dk[...] = jnp.zeros_like(dk)
     dv[...] = jnp.zeros_like(dv)
     for half, out in ((0, ot0), (1, ot1)):
-
-        def body(i, carry):
-            local = pl.ds(pl.multiple_of(i * 256, 256), 256)
-            cols = pl.ds(pl.multiple_of(half * HALF + i * 256, 256), 256)
-            for h in range(LH):
-                heads = slice(h * HEAD, (h + 1) * HEAD)
-                part = slice(h * 256, (h + 1) * 256)
-                scores = dot(kn[...], qt[heads, cols])
-                weights = jnp.exp2(scores * LOG2E) * (mask[:, cols] * linv[h : h + 1, cols])
-                grad = dt[heads, cols]
-                delta = jnp.sum(
-                    grad.astype(f32) * out[heads, local].astype(f32), axis=0, keepdims=True
-                )
-                wb[:, part] = weights.astype(bf16)
-                sb[:, part] = (weights * (dot(vn[...], grad) - delta)).astype(bf16)
-                dqt[heads, cols] = dot(kt[...], sb[:, part])
-            grads = jnp.concatenate(
-                [dt[h * HEAD : (h + 1) * HEAD, cols] for h in range(LH)], axis=1
+        cols = slice(half * HALF, (half + 1) * HALF)
+        for h in range(LH):
+            heads = slice(h * HEAD, (h + 1) * HEAD)
+            part = slice(h * HALF, (h + 1) * HALF)
+            scores = dot(kn[...], qt[heads, cols])
+            weights = jnp.exp2(scores * LOG2E) * (mask[:, cols] * linv[h : h + 1, cols])
+            grad = dt[heads, cols]
+            delta = jnp.sum(
+                grad.astype(f32) * out[heads, :].astype(f32), axis=0, keepdims=True
             )
-            queries = jnp.concatenate(
-                [qt[h * HEAD : (h + 1) * HEAD, cols] for h in range(LH)], axis=1
-            )
-            dv[...] += dot_t(wb[...], grads)
-            dk[...] += dot_t(sb[...], queries)
-            return carry
-
-        lax.fori_loop(0, 2, body, 0)
+            wb[:, part] = weights.astype(bf16)
+            sb[:, part] = (weights * (dot(vn[...], grad) - delta)).astype(bf16)
+            dqt[heads, cols] = dot(kt[...], sb[:, part])
+        grads = jnp.concatenate([dt[h * HEAD : (h + 1) * HEAD, cols] for h in range(LH)], axis=1)
+        queries = jnp.concatenate([qt[h * HEAD : (h + 1) * HEAD, cols] for h in range(LH)], axis=1)
+        dv[...] += dot_t(wb[...], grads)
+        dk[...] += dot_t(sb[...], queries)
 
     def unrope(v):
         low, high = v[:64], v[64:]
@@ -780,8 +742,8 @@
         ],
         [
             pltpu.VMEM((ROWS, ROWS), f32),
-            pltpu.VMEM((ROWS, LH * 256), bf16),
-            pltpu.VMEM((ROWS, LH * 256), bf16),
+            pltpu.VMEM((ROWS, LH * HALF), bf16),
+            pltpu.VMEM((ROWS, LH * HALF), bf16),
             pltpu.VMEM((LH * HEAD, ROWS), f32),
             pltpu.VMEM((ROWS, HEAD), f32),
             pltpu.VMEM((ROWS, HEAD), f32),
@@ -854,9 +816,11 @@
 
 
 def normed_grad_body(
-    wa, wb, wkv, dq0, dqr, tot, n0, n1, n2, n3, gg2, ggq, ggk, b0, b1, b2, b3, grads
+    wa, wb, wkv, dq0, dqr, tot, n0, n1, n2, n3, gg2, ggq, ggk, ra, rb, b0, b1, b2, b3, grads
 ):
-    @pl.when(pl.program_id(0) == 0)
+    step = pl.program_id(0)
+
+    @pl.when(step == 0)
     def _():
         flip(dq0, grads, 0, 0)
         flip(dqr, grads, 0, 512)
@@ -876,11 +840,15 @@
     heads = jnp.concatenate([ggq[0:1, :], ggk[0:1, :], jnp.zeros((1, 256), f32)], axis=1)
     numbers = [*split_two(gain), *split_two(gg2[...]), *split_two(heads)]
     extra = jnp.concatenate([n.astype(f32) for n in numbers] + [jnp.zeros((10, 512), f32)], axis=0)
-    for out in outs:
-        out[T:, :] = extra.astype(bf16)
-
-
-def normed_grad(wa, wb, wkv, dq0, dqr, tot, n1, gg2, ggq, ggk):
+    for dy, out in enumerate(outs):
+        out[T : T + 16, :] = extra.astype(bf16)
+        for q in range(4):
+            rows = pl.ds(pl.multiple_of(step * 64 + q * 16, 16), 16)
+            both = ra[dy, rows, :].astype(f32) + rb[dy, rows, :].astype(f32)
+            out[T + 16 :, q * 128 : (q + 1) * 128] = both.astype(bf16)
+
+
+def normed_grad(wa, wb, wkv, dq0, dqr, tot, n1, gg2, ggq, ggk, ra, rb):
     return grid_call(
         normed_grad_body,
         "normed_grad",
@@ -894,36 +862,23 @@
             whole((2 * HEAD, HALF)),
         ]
         + [cols_of((T, 512))] * 4
-        + [cols_of((1, 512)), whole((8, HEAD)), whole((8, HEAD))],
-        [cols_of((T + 16, 512))] * 4,
-        [sds((T + 16, D), bf16)] * 4,
+        + [cols_of((1, 512)), whole((8, HEAD)), whole((8, HEAD))]
+        + [whole((4, 256, E))] * 2,
+        [cols_of((T + 32, 512))] * 4,
+        [sds((T + 32, D), bf16)] * 4,
         [pltpu.VMEM((HALF, 1280), bf16)],
-        (wa, wb, wkv, dq0, dqr, tot, *n1, gg2, ggq, ggk),
-    )
-
-
-def add_pair_body(a, b, *outs):
-    for i, out in enumerate(outs):
-        out[...] = (a[i].astype(f32) + b[i].astype(f32)).astype(bf16)
-
-
-def add_pair(a, b):
-    return call(add_pair_body, "add_pair", [sds(a.shape[1:], bf16)] * 4, [], (a, b))
-
-
-def add_last_body(a, b, c, d, *outs):
-    total = (
+        (wa, wb, wkv, dq0, dqr, tot, *n1, gg2, ggq, ggk, ra, rb),
+    )
+
+
+def add_last_body(a, b, c, d, out):
+    out[...] = (
         (a[...].astype(f32) + b[...].astype(f32)) + (c[...].astype(f32) + d[...].astype(f32))
     ).astype(bf16)
-    start = 0
-    for out in outs:
-        out[...] = total[start : start + out.shape[0]]
-        start += out.shape[0]
-
-
-def add_last(parts, *heights):
-    outs = [sds((height, parts[0].shape[1]), bf16) for height in heights]
-    return call(add_last_body, "add_last", outs, [], tuple(parts))
+
+
+def add_last(parts):
+    return call(add_last_body, "add_last", [sds(parts[0].shape, bf16)], [], tuple(parts))
 
 
 def stack_body(a, b, c, d, out):
@@ -934,25 +889,6 @@
 def stack(parts):
     shape = (4, *parts[0].shape)
     return call(stack_body, "stack_parts", [sds(shape, bf16)], [], tuple(parts))[0]
-
-
-def place_out_body(where, c0, c1, c2, c3, out):
-    for dx, chunks in enumerate((c0, c1, c2, c3)):
-        for dz in range(4):
-            chunk = lax.rem(where[1] + dx, 4) * 4 + lax.rem(where[0] + dz, 4)
-            cols = pl.ds(pl.multiple_of(chunk * 128, 128), 128)
-            out[:, cols] = chunks[dz].astype(f32)
-
-
-def place_out(where, chunks):
-    return call(
-        place_out_body,
-        "place_output_grads",
-        [sds((512, D), f32)],
-        [],
-        (where, *chunks),
-        smem=(0,),
-    )[0]
 
 
 def place_body(where, c0, c1, c2, c3, gq, gkt, gvt):
@@ -977,7 +913,7 @@
     )
 
 
-def final_body(b0, b1, b2, b3, x0, ghid, g1, out, gains):
+def final_body(b0, b1, b2, b3, x0, ghid, g1, out, small):
     whole_sum = (b0[...].astype(f32) + b1[...].astype(f32)) + (
         b2[...].astype(f32) + b3[...].astype(f32)
     )
@@ -987,26 +923,51 @@
     u = c * g1[...]
     m = jnp.mean(u * v, axis=-1, keepdims=True)
     out[...] = ghid[...] + r * u - v * (r * r * r * m)
-    extra = whole_sum[T:]
-    gains[...] = jnp.concatenate(
-        [
-            (extra[0:1] + extra[1:2]) / g1[...],
-            extra[2:3] + extra[3:4],
-            extra[4:5] + extra[5:6],
-            jnp.zeros((5, D), f32),
-        ],
+    extra = whole_sum[T : T + 16]
+    numbers = [
+        *split_two((extra[0:1] + extra[1:2]) / g1[...]),
+        *split_two(extra[2:3] + extra[3:4]),
+        *split_two(extra[4:5] + extra[5:6]),
+    ]
+    rows = jnp.concatenate(
+        [whole_sum[T + 16 :]] + [n.astype(f32) for n in numbers] + [jnp.zeros((2, D), f32)],
         axis=0,
-    )
+    ).astype(bf16)
+    for e in range(16):
+        small[e] = rows[:, e * 128 : (e + 1) * 128]
 
 
 def final(b, x0, ghid, g1):
     return call(
         final_body,
         "input_grad",
-        [sds((T, D), f32), sds((8, D), f32)],
+        [sds((T, D), f32), sds((16, 24, 128), bf16)],
         [],
         (*b, x0, ghid, g1),
     )
+
+
+def fold_body(parts, out):
+    total = parts[0].astype(f32)
+    for e in range(1, 16):
+        total = total + parts[e].astype(f32)
+    numbers = []
+    for k in range(3):
+        row = SEG + 2 * k
+        numbers += split_two(total[row : row + 1] + total[row + 1 : row + 2])
+    rows = jnp.concatenate(
+        [total[:SEG]] + [n.astype(f32) for n in numbers] + [jnp.zeros((2, 128), f32)], axis=0
+    ).astype(bf16)
+
+    def body(i, carry):
+        out[i] = rows
+        return carry
+
+    lax.fori_loop(0, E, body, 0)
+
+
+def fold(parts):
+    return call(fold_body, "fold_small", [sds((E, 24, 128), bf16)], [], (parts,))[0]
 
 
 def sibling(x):
@@ -1143,8 +1104,6 @@
         out_grad, g2, w_router,
     )
     g_own = [gatt] + [from_chip(gatt, dy) for dy in (1, 2, 3)]
-    router_parts = add_pair(router_own, sibling(router_sib))
-    router_parts = [router_parts[0]] + spread(router_parts)
     g_sib = [sibling(block) for block in g_own]
     dt_near = head_grad(
         [g_own[0], g_sib[0], g_own[1], g_sib[1], g_own[3], g_sib[3]], w_out
@@ -1152,45 +1111,41 @@
     g_far, dt_near = lax.optimization_barrier(((g_own[2], g_sib[2]), dt_near))
     g_own[2], g_sib[2] = g_far
 
-    *out_parts, dt_far = pre(where, g_own + g_sib, router_parts, ot0, ot1, w_out)
-    out_parts = collect(out_parts, 1)
-    returned = exchange(after(out_wire, dt_far))
+    returned = exchange(after(out_wire, g_own[2]))
+    gwout, dt_far = pre(g_own + g_sib, ot0, ot1, w_out)
+    grad_wout = lax.psum(gwout, "expert")
 
     dq0, dq1, dkv, ggq, ggk = bwd(
         qh, kh, scales, qt, kt, kn, vn, dt_near, dt_far, ot0, ot1, linv, info, cos, sin, gq, gk
     )
-    dq1, dkv, out_parts = lax.optimization_barrier((dq1, dkv, out_parts))
+    router_sib = after(router_sib, dkv)
     dq_sib, dkv_sib = sibling(dq1), sibling(dkv)
     *parts, dkv_total = qkv_grad(where, n1_t, dq0, dq1, dkv, dkv_sib)
     returned, dq0 = lax.optimization_barrier((returned, dq0))
     result = result_rows(expert_list, slot_list, gate_list, returned, hidden)
-    blocks = normed_grad(wq_t, wq_ts, wkv, dq0, dq_sib, dkv_total, n1, gg2, ggq, ggk)
+    router_rec = sibling(router_sib)
+    blocks = normed_grad(
+        wq_t, wq_ts, wkv, dq0, dq_sib, dkv_total, n1, gg2, ggq, ggk, router_own, router_rec
+    )
     blocks = [blocks[0]] + spread(blocks)
-    out_parts = collect(add_parts(out_parts), 0)
-
-    parts = collect(parts, 0)
-    parts, out_parts = lax.optimization_barrier((parts, out_parts))
-    out_chunk, router_chunk = add_last(out_parts, 512, SEG)
-    out_chunks = share(out_chunk, 0)
-    grad_router = exchange(jnp.broadcast_to(router_chunk[None], (E, SEG, E)))
-    parts = collect(add_parts(parts), 1)
-    parts, out_chunks, blocks = lax.optimization_barrier((parts, out_chunks, blocks))
-    chunks = share(add_last(parts, 128)[0], 1)
-    out_chunks = share(stack(out_chunks), 1)
-    grad_input, gains = final(blocks, block_input, ghid, g1)
-    gains = gains[:3]
-    gains = gains + sibling(gains)
-    chunks, gains = lax.optimization_barrier((stack(chunks), gains))
+
+    parts = collect(add_parts(collect(parts, 0)), 1)
+    parts, blocks = lax.optimization_barrier((parts, blocks))
+    chunks = share(add_last(parts)[0], 1)
+    grad_input, small = final(blocks, block_input, ghid, g1)
+    small = lax.all_to_all(small, "expert", split_axis=0, concat_axis=0, tiled=True)
+    chunks, small, grad_wout = lax.optimization_barrier((stack(chunks), small, grad_wout))
     chunks = share(chunks, 0)
-    out_chunks = after(out_chunks, *chunks[1:])
-    gains = jnp.sum(lax.all_gather(gains, "expert"), axis=0)
-    grad_wout = place_out(where, out_chunks)
-    grad_router = grad_router.reshape(4, 4, 8, SEG, E).transpose(2, 1, 0, 3, 4)
-    grad_router = grad_router.reshape(D, E).astype(f32)
-    chunks, gains, result, grad_wout, grad_router = lax.optimization_barrier(
-        (chunks, gains, result, grad_wout, grad_router)
+    small = exchange(fold(small))
+    grad_wout = grad_wout.astype(f32)
+    chunks, small, grad_input, grad_wout, result = lax.optimization_barrier(
+        (chunks, small, grad_input, grad_wout, result)
     )
     grad_wq, grad_wk, grad_wv = place(where, chunks)
+    small = small.reshape(16, 8, 24, 128).astype(f32)
+    grad_router = small[:, :, :SEG].transpose(1, 0, 2, 3).reshape(D, E)
+    gains = small[:, 0, SEG:] + small[:, 1, SEG:]
+    gains = [(gains[:, 2 * k] + gains[:, 2 * k + 1]).reshape(D) for k in range(3)]
     return (
         result,
         grad_input,
@@ -1198,8 +1153,8 @@
         grad_wq,
         grad_wk.T,
         grad_wv.T,
-        gains[2, :HEAD],
-        gains[2, HEAD : 2 * HEAD],
+        gains[2][:HEAD],
+        gains[2][HEAD : 2 * HEAD],
         grad_wout,
         gains[1],
         grad_router,

time: 523 us -> 467 us (0.89)
  blocking collectives: 32.2 us -> 0 us
  Pallas kernels: 169 us -> 153 us
  waiting for transfers between devices: 171 us -> 157 us
  between operations: 1.24 us -> 14.6 us
  starting transfers between devices: 97.9 us -> 90.4 us
    all_gather x1 -> x0, blocking collectives: 32.2 us -> none  [on_device(): gains = jnp.sum(lax.all_gather(gains, 'expert'), axis=0)]
    ppermute x24 -> x12, waiting for transfers between devices: 77.2 us -> 48.2 us  [on_expert(): return lax.ppermute(x, 'expert', pairs)]
    psum x0 -> x1, waiting for transfers between devices: none -> 16.5 us  [on_device(): grad_wout = lax.psum(gwout, 'expert')]
    pallas_call x24 -> x20, Pallas kernels: 136 us -> 122 us  [call(): pl.pallas_call(kernel, out_shape=outs, in_specs=in_specs, out_specs=[pl.B...]
    ppermute x24 -> x12, starting transfers between devices: 28.9 us -> 18 us  [on_expert(): return lax.ppermute(x, 'expert', pairs)]
    ppermute x9 -> x6, waiting for transfers between devices: 24.7 us -> 22.4 us  [to_chip(): return lax.ppermute(x, 'shard', [(i, (i + 2 * dy) % 8) for i in range(8)])]
    ppermute x9 -> x6, starting transfers between devices: 11.4 us -> 9.62 us  [to_chip(): return lax.ppermute(x, 'shard', [(i, (i + 2 * dy) % 8) for i in range(8)])]
    ppermute x17 -> x16, starting transfers between devices: 13.6 us -> 12.7 us  [sibling(): return lax.ppermute(x, 'shard', [(i, i ^ 1) for i in range(8)])]
  transfers between devices with their start and end apart: 61 -> 47, of which waited for: 22 -> 20; matrix products, arithmetic and copies ran while one was open for 7% -> 8% of each run, Pallas kernels for 24% -> 26%
where the time goes in v6:
time: 467 us; the launch traced here: 460 us
  waiting for transfers between devices  157 us (34%)
  Pallas kernels  153 us (33%)
  starting transfers between devices  90.4 us (19%)
  matrix products  16.6 us (4%)
  local copies, waits for them, and re-layouts  16.2 us (3%)
  between operations  14.6 us (3%)
  other arithmetic  12.2 us (3%)
    pallas_call x20, Pallas kernels, call(): pl.pallas_call(kernel, out_shape=outs, in_specs=in_specs, out_specs=[pl.B...  122 us
    ppermute x12, waiting for transfers between devices, on_expert(): return lax.ppermute(x, 'expert', pairs)  48.2 us
    all_to_all x5, starting transfers between devices, exchange(): return lax.all_to_all(x, ALL, split_axis=0, concat_axis=0, tiled=True)  38 us
    all_to_all x5, waiting for transfers between devices, exchange(): return lax.all_to_all(x, ALL, split_axis=0, concat_axis=0, tiled=True)  36.9 us
    pallas_call x4, Pallas kernels, grid_call(): pl.pallas_call(kernel, out_shape=outs, grid_spec=pltpu.PrefetchScalarGrid...  31.3 us
    ppermute x6, waiting for transfers between devices, to_chip(): return lax.ppermute(x, 'shard', [(i, (i + 2 * dy) % 8) for i in range(8)])  22.4 us
    ppermute x6, waiting for transfers between devices, from_chip(): return lax.ppermute(x, 'shard', [(i, (i - 2 * dy) % 8) for i in range(8)])  21.2 us
    ppermute x12, starting transfers between devices, on_expert(): return lax.ppermute(x, 'expert', pairs)  18 us
  transfers between devices with their start and end apart: 47, of which 20 were waited for; matrix products, arithmetic and copies ran while one was open for 8% of the time, Pallas kernels for 26%

profile of v6, /device:TPU:1, one launch (start us, length us, event | category | flops | bytes accessed | tf_op | source)
XLA Modules:
  0.0 459.6 jit_solution(10969714134365635166)
XLA Ops:
  7.2 1.5 collective-permute-start.3
  10.1 2.6 collective-permute-start.1
  18.3 2.0 route_tables.1
  21.5 4.2 pack_rows.1
  26.3 3.9 copy.39
  30.2 1.8 multiply_sine_fusion
  32.8 5.0 %qkv0.1 = (bf16[512,256]{1,0:T(8,128)(2,1)}, bf16[512,256]{1,0:T(8,128)(2,1)}, bf16[128,256]{1,0:T(8,128)(2,1)}, bf16[128,256]{1,0:T(8,128)(2,1)}, bf16[128,256]...) custom-call(s32[1]{0:T(128)} %bitcast.2.refs_0_, ...), custom_call_target="tpu_custom_call" | custom-call | flops 1 | bytes 1 | tf_op jit(solution)/shard_map/qkv0/pallas_call | solution.py:61
  37.8 9.2 %all-to-all-start.1 = ((bf16[128,88,128]{2,1,0:T(8,128)(2,1)}), bf16[128,88,128]{2,1,0:T(8,128)(2,1)}, u32[]{:S(2)}, u32[]{:S(2)}) async-start(bf16[128,88,128]{2,1,0:T(8,128)(2,1)} %pack_rows.1), calls=%async_computation.1 | async-start | bytes 5767168 | tf_op jit(solution)/shard_map/all_to_all | solution.py:986
  49.7 3.9 collective-permute-done.6.refs_2_
  54.5 7.7 %qkv123.1 = (bf16[512,256]{1,0:T(8,128)(2,1)}, bf16[512,256]{1,0:T(8,128)(2,1)}, bf16[128,256]{1,0:T(8,128)(2,1)}, bf16[128,256]{1,0:T(8,128)(2,1)}, bf16[128,25...) custom-call(s32[1]{0:T(128)} %bitcast.2.refs_0_, ...), custom_call_target="tpu_custom_call" | custom-call | flops 1 | bytes 1 | tf_op jit(solution)/shard_map/qkv123/pallas_call | solution.py:61
  62.2 7.1 %attend.1 = (bf16[512,512]{1,0:T(8,128)(2,1)}, bf16[512,512]{1,0:T(8,128)(2,1)}, f32[8,1024]{1,0:T(8,128)}, bf16[512,1024]{1,0:T(8,128)(2,1)}, bf16[128,1024]{1,...) custom-call(bf16[512,256]{1,0:T(8,128)(2,1)} %get-tuple-element.152.refs_0_, ...), custom_call_target="tpu_custom_call" | custom-call | flops 1 | bytes 6600001 | tf_op jit(solution)/shard_map/attend/pallas_call | solution.py:61
  69.7 1.8 collective-permute-done.9.otr
  72.2 6.2 %out_projection.1 = (bf16[128,2048]{1,0:T(8,128)(2,1)}, bf16[128,2048]{1,0:T(8,128)(2,1)}, bf16[128,2048]{1,0:T(8,128)(2,1)}, bf16[128,2048]{1,0:T(8,128)(2,1)}) custom-call(bf16[512,512]{1,0:T(8,128)(2,1)} %get-tuple-element.167.ot0.refs_8_.refs_18_, bf16[512,512]{1,0:T(8,128)(2,1)} %copy-done.13, bf16[512,2048]{1,0:T(8,128)(2,1)} %refs_10_.1, ...), custom_call_target="tpu_custom_call" | custom-call | flops 1 | bytes 3000001 | tf_op jit(solution)/shard_map/out_projection/pallas_call | solution.py:74
  79.0 2.1 collective-permute-start.12
  82.6 11.7 %collective-permute-done.11.b1 = bf16[128,2048]{1,0:T(8,128)(2,1)S(1)} collective-permute-done((bf16[128,2048]{1,0:T(8,128)(2,1)}, bf16[128,2048]{1,0:T(8,128)(2,1)S(1)}, u32[]{:S(2)}, u32[]{:S(2)}) %collective-permute-start.11) | collective-permute-done | bytes 524320 | tf_op jit(solution)/shard_map/ppermute | solution.py:982
  94.3 10.6 %collective-permute-done.13.b3 = bf16[128,2048]{1,0:T(8,128)(2,1)} collective-permute-done((bf16[128,2048]{1,0:T(8,128)(2,1)}, bf16[128,2048]{1,0:T(8,128)(2,1)}, u32[]{:S(2)}, u32[]{:S(2)}) %collective-permute-start.13) | collective-permute-done | bytes 524320 | tf_op jit(solution)/shard_map/ppermute | solution.py:982
  105.0 5.6 %router.1 = (f32[128,2048]{1,0:T(8,128)}, bf16[128,2048]{1,0:T(8,128)(2,1)}, f32[128,128]{1,0:T(8,128)}, f32[128,128]{1,0:T(8,128)}, bf16[128,88,128]{2,1,0:T(8,128)(2,1)}) custom-call(bf16[128,2048]{1,0:T(8,128)(2,1)} %get-tuple-element.169.b0, bf16[128,2048]{1,0:T(8,128)(2,1)} %copy-done.15, bf16[128,2048]{1,0:T(8,128)(2,1)} %collective-permute-done.12.b2, ...), custom_call_target="tpu_custom_call" | custom-call | flops 1 | bytes 3600001 | tf_op jit(solution)/shard_map/router/pallas_call | solution.py:61
  110.6 9.4 %all-to-all-start = ((bf16[128,88,128]{2,1,0:T(8,128)(2,1)}), bf16[128,88,128]{2,1,0:T(8,128)(2,1)}, u32[]{:S(2)}, u32[]{:S(2)}) async-start(bf16[128,88,128]{2,1,0:T(8,128)(2,1)} %get-tuple-element.174), calls=%async_computation | async-start | bytes 5767168 | tf_op jit(solution)/shard_map/all_to_all | solution.py:986
  120.0 1.6 collective-permute-start.14
  121.7 5.5 %transpose_rows.1.n1t = bf16[2048,1024]{1,0:T(8,128)(2,1)} custom-call(bf16[256,2048]{1,0:T(8,128)(2,1)} %get-tuple-element.179.n0, bf16[256,2048]{1,0:T(8,128)(2,1)} %get-tuple-element.180.n1, bf16[256,2048]{1,0:T(8,128)(2,1)} %get-tuple-element.181.n2, bf16[256,2048]{1,0:T(8,128)(2,1)} %get-tuple-element.182.n3), custom_call_target="tpu_custom_call" | custom-call | flops 1 | bytes 3600001 | tf_op jit(solution)/shard_map/transpose_rows/pallas_call | solution.py:61
  127.8 7.5 %expert_grad_rows.1 = (bf16[640,2048]{1,0:T(8,128)(2,1)}, f32[640,768]{1,0:T(8,128)}) custom-call(bf16[128,88,128]{2,1,0:T(8,128)(2,1)} %all-to-all-done.1.wire, bf16[768,2048]{1,0:T(8,128)(2,1)} %bitcast.69), custom_call_target="tpu_custom_call" | custom-call | flops 1 | bytes 4800001 | tf_op jit(solution)/shard_map/expert_grad_rows/pallas_call | solution.py:61
  135.3 23.5 %all-to-all-done.wire = bf16[128,88,128]{2,1,0:T(8,128)(2,1)} async-done(((bf16[128,88,128]{2,1,0:T(8,128)(2,1)}), bf16[128,88,128]{2,1,0:T(8,128)(2,1)}, u32[]{:S(2)}, u32[]{:S(2)}) %all-to-all-start) | async-done | bytes 2883616 | tf_op jit(solution)/shard_map/all_to_all | solution.py:986
  158.8 19.4 %expert_main.1 = (bf16[128,88,128]{2,1,0:T(8,128)(2,1)}, bf16[640,2048]{1,0:T(8,128)(2,1)}, bf16[640,768]{1,0:T(8,128)(2,1)}, bf16[640,768]{1,0:T(8,128)(2,1)}, ...) custom-call(bf16[128,88,128]{2,1,0:T(8,128)(2,1)} %all-to-all-done.wire, bf16[2048,768]{1,0:T(8,128)(2,1)} %bitcast.73, ...), custom_call_target="tpu_custom_call" | custom-call | flops 1 | bytes 10800001 | tf_op jit(solution)/shard_map/expert_main/pallas_call | solution.py:61
  178.1 5.9 %all-to-all-start.2 = ((bf16[128,88,128]{2,1,0:T(8,128)(2,1)}), bf16[128,88,128]{2,1,0:T(8,128)(2,1)}, u32[]{:S(2)}, u32[]{:S(2)}) async-start(bf16[128,88,128]{2,1,0:T(8,128)(2,1)} %get-tuple-element.207), calls=%async_computation.2 | async-start | bytes 5767168 | tf_op jit(solution)/shard_map/all_to_all | solution.py:986
  186.1 6.6 %expert_out.1 = bf16[128,80,128]{2,1,0:T(8,128)(2,1)} custom-call(bf16[640,768]{1,0:T(8,128)(2,1)} %get-tuple-element.213.act, bf16[768,2048]{1,0:T(8,128)(2,1)} %bitcast.70), custom_call_target="tpu_custom_call" | custom-call | flops 1 | bytes 4200001 | tf_op jit(solution)/shard_map/expert_out/pallas_call | solution.py:61
  192.7 7.5 %fusion.7 = f32[2048,768]{1,0:T(8,128)} fusion(bf16[640,2048]{1,0:T(8,128)(2,1)} %get-tuple-element.214, bf16[640,768]{1,0:T(8,128)(2,1)} %get-tuple-element.215), kind=kOutput, calls=%fused_computation.32 | convolution fusion | flops 2013265920 | bytes 9895936 | tf_op jit(solution)/shard_map/dot_general | solution.py:1093
  200.2 4.6 fusion.8
  204.8 4.5 fusion.9
  209.4 13.4 %all-to-all-done.2.wire = bf16[128,88,128]{2,1,0:T(8,128)(2,1)} async-done(((bf16[128,88,128]{2,1,0:T(8,128)(2,1)}), bf16[128,88,128]{2,1,0:T(8,128)(2,1)}, u32[]{:S(2)}, u32[]{:S(2)}) %all-to-all-start.2) | async-done | bytes 2883616 | tf_op jit(solution)/shard_map/all_to_all | solution.py:986
  222.7 7.1 %combine_grads.1 = (f32[128,2048]{1,0:T(8,128)}, bf16[128,2048]{1,0:T(8,128)(2,1)}, bf16[4,256,128]{2,1,0:T(8,128)(2,1)}, bf16[4,256,128]{2,1,0:T(8,128)(2,1)}, f32[1,2048]{1,0:T(1,128)}) custom-call(s32[4]{0:T(128)} %pad_add_fusion.where, s32[512]{0:T(512)} %reshape.212.experts, s32[512]{0:T(512)} %reshape.213.slots, f32[512]{0:T(512)} %reshape.211.gate_list, ...), custom_call_target="tpu_custom_call" | custom-call | flops 1 | bytes 4200001 | tf_op jit(solution)/shard_map/combine_grads/pallas_call | solution.py:61
  229.9 2.7 collective-permute-start.18
  233.9 21.1 %collective-permute-done.20.refs_4_.refs_3_ = bf16[128,2048]{1,0:T(8,128)(2,1)S(1)} collective-permute-done((bf16[128,2048]{1,0:T(8,128)(2,1)}, bf16[128,2048]{1,0:T(8,128)(2,1)S(1)}, u32[]{:S(2)}, u32[]{:S(2)}) %collective-permute-start.20) | collective-permute-done | bytes 524320 | tf_op jit(solution)/shard_map/ppermute | solution.py:978
  255.1 1.8 collective-permute-start.21
  260.0 5.3 %head_grad.1.refs_16_ = bf16[512,768]{1,0:T(8,128)(2,1)} custom-call(bf16[128,2048]{1,0:T(8,128)(2,1)} %get-tuple-element.223.refs_0_, bf16[128,2048]{1,0:T(8,128)(2,1)} %copy-done.5, bf16[128,2048]{1,0:T(8,128)(2,1)} %copy-done.4, bf16[128,2048]{1,0:T(8,128)(2,1)} %collective-permute-done.19.refs_3_.refs_5_, bf16[128,2048]{1,0:T(8,128)(2,1)} %copy-done.3, ...), custom_call_target="tpu_custom_call" | custom-call | flops 1 | bytes 2400001 | tf_op jit(solution)/shard_map/head_grad/pallas_call | solution.py:61
  265.3 4.8 %all-to-all-start.3 = ((bf16[128,80,128]{2,1,0:T(8,128)(2,1)}), bf16[128,80,128]{2,1,0:T(8,128)(2,1)}, u32[]{:S(2)}, u32[]{:S(2)}) async-start(bf16[128,80,128]{2,1,0:T(8,128)(2,1)} %expert_out.1), calls=%async_computation.3 | async-start | bytes 5242880 | tf_op jit(solution)/shard_map/all_to_all | solution.py:986
  270.2 7.7 %out_projection_grad.1 = (bf16[512,2048]{1,0:T(8,128)(2,1)}, bf16[512,256]{1,0:T(8,128)(2,1)}) custom-call(bf16[128,2048]{1,0:T(8,128)(2,1)} %get-tuple-element.223.refs_0_, bf16[128,2048]{1,0:T(8,128)(2,1)} %copy-done.4, bf16[128,2048]{1,0:T(8,128)(2,1)} %collective-permute-done.15.refs_2_, bf16[128,2048]{1,0:T(8,128)(2,1)} %copy-done.3, ...), custom_call_target="tpu_custom_call" | custom-call | flops 1 | bytes 4200001 | tf_op jit(solution)/shard_map/out_projection_grad/pallas_call | solution.py:74
  277.9 16.9 %attend_grad.1 = (bf16[512,512]{1,0:T(8,128)(2,1)}, bf16[512,512]{1,0:T(8,128)(2,1)}, bf16[256,1024]{1,0:T(8,128)(2,1)}, f32[8,128]{1,0:T(8,128)}, f32[8,128]{1,0:T(8,128)}) custom-call(bf16[512,256]{1,0:T(8,128)(2,1)} %get-tuple-element.188.refs_0_, bf16[512,256]{1,0:T(8,128)(2,1)} %get-tuple-element.189.refs_1_, ...), custom_call_target="tpu_custom_call" | custom-call | flops 1 | bytes 1 | tf_op jit(solution)/shard_map/attend_grad/pallas_call | solution.py:61
  296.2 1.7 collective-permute-done.22.sib
  298.7 9.3 %qkv_weight_grad.1 = (bf16[4,128,640]{2,1,0:T(8,128)(2,1)}, bf16[4,128,640]{2,1,0:T(8,128)(2,1)}, bf16[4,128,640]{2,1,0:T(8,128)(2,1)}, bf16[4,128,640]{2,1,0:T(8,128)(2,1)}, bf16[256,1024]{1,0:T(8,128)(2,1)}) custom-call(s32[4]{0:T(128)} %pad_add_fusion.where, bf16[2048,1024]{1,0:T(8,128)(2,1)} %transpose_rows.1.n1t, ...), custom_call_target="tpu_custom_call" | custom-call | flops 1 | bytes 1 | tf_op jit(solution)/shard_map/qkv_weight_grad/pallas_call | solution.py:74
  309.4 2.0 collective-permute-start.24
  315.4 8.1 %normed_grad.1 = (bf16[160,2048]{1,0:T(8,128)(2,1)}, bf16[160,2048]{1,0:T(8,128)(2,1)}, bf16[160,2048]{1,0:T(8,128)(2,1)}, bf16[160,2048]{1,0:T(8,128)(2,1)}) custom-call(bf16[512,2048]{1,0:T(8,128)(2,1)} %bitcast.5.refs_4_.refs_8_.wa, bf16[512,2048]{1,0:T(8,128)(2,1)} %collective-permute-done.14.wb, bf16[256,2048]{1,0:T(8,128)(2,1)} %get-tuple-element.241.wkv, ...), custom_call_target="tpu_custom_call" | custom-call | flops 1 | bytes 1 | tf_op jit(solution)/shard_map/normed_grad/pallas_call | solution.py:74
  326.3 3.3 collective-permute-start.33
  329.6 13.1 %collective-permute-done.25.d = bf16[4,128,640]{2,1,0:T(8,128)(2,1)} collective-permute-done((bf16[4,128,640]{2,1,0:T(8,128)(2,1)}, bf16[4,128,640]{2,1,0:T(8,128)(2,1)}, u32[]{:S(2)}, u32[]{:S(2)}) %collective-permute-start.25) | collective-permute-done | bytes 655392 | tf_op jit(solution)/shard_map/ppermute | solution.py:997
  342.7 2.7 add_parts.1
  346.6 1.5 collective-permute-start.27
  348.0 3.3 collective-permute-done.26.b
  351.4 1.5 collective-permute-start.28
  352.9 4.4 collective-permute-done.28.d
  357.9 1.9 add_last.1.a
  360.2 2.5 collective-permute-start.35
  362.8 1.5 collective-permute-start.34
  364.2 4.0 input_grad.1
  368.2 4.3 all-to-all-start.4
  374.0 2.0 stack_parts.1.c0
  376.0 16.5 %all-reduce.2.cloned.1.call-done = bf16[512,2048]{1,0:T(8,128)(2,1)} async-done(((bf16[512,2048]{1,0:T(8,128)(2,1)}), bf16[512,2048]{1,0:T(8,128)(2,1)}) %all-reduce.2.cloned.1.call-update) | async-done | bytes 2097168 | tf_op jit(solution)/shard_map/psum | solution.py:1116
  393.2 2.5 fold_small.1
  395.7 8.7 %all-to-all-start.5 = ((bf16[128,24,128]{2,1,0:T(8,128)(2,1)}), bf16[128,24,128]{2,1,0:T(8,128)(2,1)S(1)}, u32[]{:S(2)}, u32[]{:S(2)}) async-start(bf16[128,24,128]{2,1,0:T(8,128)(2,1)} %fold_small.1), calls=%async_computation.5 | async-start | bytes 1572864 | tf_op jit(solution)/shard_map/all_to_all | solution.py:986
  404.4 1.6 collective-permute-start.39
  406.0 2.9 collective-permute-start.38
  409.8 4.5 result.1
  414.4 4.1 convert_element_type.61
  418.5 12.4 %collective-permute-done.39.c3 = bf16[4,128,640]{2,1,0:T(8,128)(2,1)} collective-permute-done((bf16[4,128,640]{2,1,0:T(8,128)(2,1)}, bf16[4,128,640]{2,1,0:T(8,128)(2,1)}, u32[]{:S(2)}, u32[]{:S(2)}) %collective-permute-start.39) | collective-permute-done | bytes 655392 | tf_op jit(solution)/shard_map/ppermute | solution.py:997
  430.9 14.8 %collective-permute-done.38.c2 = bf16[4,128,640]{2,1,0:T(8,128)(2,1)} collective-permute-done((bf16[4,128,640]{2,1,0:T(8,128)(2,1)}, bf16[4,128,640]{2,1,0:T(8,128)(2,1)}, u32[]{:S(2)}, u32[]{:S(2)}) %collective-permute-start.38) | collective-permute-done | bytes 655392 | tf_op jit(solution)/shard_map/ppermute | solution.py:997
  448.3 4.3 place_weight_grads.1
  (146 shorter events, 42.0 us)
Async XLA Ops:
  7.2 8.5 %copy-start = (s32[1,1024]{1,0:T(1,128)S(1)}, s32[1,1024]{1,0:T(1,128)}, u32[]{:S(2)}) copy-start(s32[1,1024]{1,0:T(1,128)} %param.32) | copy-start | bytes 12292
  7.2 18.5 %copy-start.25 = (bf16[2048]{0:T(1024)(128)(2,1)S(1)}, bf16[2048]{0:T(1024)(128)(2,1)}, u32[]{:S(2)}) copy-start(bf16[2048]{0:T(1024)(128)(2,1)} %param.19) | copy-start | bytes 12292
  7.2 24.9 %collective-permute-start.3 = (bf16[128,2048]{1,0:T(8,128)(2,1)}, bf16[128,2048]{1,0:T(8,128)(2,1)}, u32[]{:S(2)}, u32[]{:S(2)}) collective-permute-start(bf16[128,2048]{1,0:T(8,128)(2,1)} %x0.3), channel_id=1, source_target_pairs={{0,1},{1,0},{2,3},{3,2},{4,5},{5,4},{6,7},{7,6},{8,9},{9,8},{10,11... | collective-permute-start | bytes 1572872 | tf_op jit(solution)/shard_map/ppermute | solution.py:974
  8.7 29.0 %collective-permute-start.2 = (bf16[128,2048]{1,0:T(8,128)(2,1)}, bf16[128,2048]{1,0:T(8,128)(2,1)}, u32[]{:S(2)}, u32[]{:S(2)}) collective-permute-start(bf16[128,2048]{1,0:T(8,128)(2,1)} %x0.3), channel_id=1, source_target_pairs={{0,2},{1,3},{2,4},{3,5},{4,6},{5,7},{6,0},{7,1},{8,10},{9,11},{10,... | collective-permute-start | bytes 1572872 | tf_op jit(solution)/shard_map/ppermute | solution.py:978
  10.1 27.6 %collective-permute-start.1 = (bf16[128,2048]{1,0:T(8,128)(2,1)}, bf16[128,2048]{1,0:T(8,128)(2,1)}, u32[]{:S(2)}, u32[]{:S(2)}) collective-permute-start(bf16[128,2048]{1,0:T(8,128)(2,1)} %x0.3), channel_id=1, source_target_pairs={{0,4},{1,5},{2,6},{3,7},{4,0},{5,1},{6,2},{7,3},{8,12},{9,13},{10,... | collective-permute-start | bytes 1572872 | tf_op jit(solution)/shard_map/ppermute | solution.py:978
  12.7 25.0 %collective-permute-start = (bf16[128,2048]{1,0:T(8,128)(2,1)}, bf16[128,2048]{1,0:T(8,128)(2,1)}, u32[]{:S(2)}, u32[]{:S(2)}) collective-permute-start(bf16[128,2048]{1,0:T(8,128)(2,1)} %x0.3), channel_id=1, source_target_pairs={{0,6},{1,7},{2,0},{3,1},{4,2},{5,3},{6,4},{7,5},{8,14},{9,15},{10,... | collective-permute-start | bytes 1572872 | tf_op jit(solution)/shard_map/ppermute | solution.py:978
  13.8 4.4 collective-permute-start.4
  18.2 12.0 %copy-start.8 = (bf16[64,2048]{1,0:T(8,128)(2,1)}, bf16[64,2048]{1,0:T(8,128)(2,1)S(1)}, u32[]{:S(2)}) copy-start(bf16[64,2048]{1,0:T(8,128)(2,1)S(1)} %collective-permute-done.4.refs_6_.refs_10_) | copy-start | bytes 786436
  18.2 13.9 %collective-permute-start.5 = (bf16[64,2048]{1,0:T(8,128)(2,1)}, bf16[64,2048]{1,0:T(8,128)(2,1)S(1)}, u32[]{:S(2)}, u32[]{:S(2)}) collective-permute-start(bf16[64,2048]{1,0:T(8,128)(2,1)} %bitcast.78), channel_id=1, source_target_pairs={{0,1},{1,0},{2,3},{3,2},{4,5},{5,4},{6,7},{7,6},{8,9},{9,8},{10,11... | collective-permute-start | bytes 786440 | tf_op jit(solution)/shard_map/ppermute | solution.py:974
  37.8 72.8 %all-to-all-start.1 = ((bf16[128,88,128]{2,1,0:T(8,128)(2,1)}), bf16[128,88,128]{2,1,0:T(8,128)(2,1)}, u32[]{:S(2)}, u32[]{:S(2)}) async-start(bf16[128,88,128]{2,1,0:T(8,128)(2,1)} %pack_rows.1), calls=%async_computation.1 | async-start | bytes 5767168 | tf_op jit(solution)/shard_map/all_to_all | solution.py:986
  46.9 24.5 %collective-permute-start.10 = (bf16[512,2048]{1,0:T(8,128)(2,1)}, bf16[512,2048]{1,0:T(8,128)(2,1)}, u32[]{:S(2)}, u32[]{:S(2)}) collective-permute-start(bf16[512,2048]{1,0:T(8,128)(2,1)} %refs_10_.1), channel_id=1, source_target_pairs={{0,1},{1,0},{2,3},{3,2},{4,5},{5,4},{6,7},{7,6},{8,9},{9,8},{10,11... | collective-permute-start | bytes 6291464 | tf_op jit(solution)/shard_map/ppermute | solution.py:974
  48.1 5.4 %collective-permute-start.6 = (bf16[128,2048]{1,0:T(8,128)(2,1)}, bf16[128,2048]{1,0:T(8,128)(2,1)S(1)}, u32[]{:S(2)}, u32[]{:S(2)}) collective-permute-start(bf16[128,2048]{1,0:T(8,128)(2,1)} %collective-permute-done.refs_1_), channel_id=1, source_target_pairs={{0,1},{1,0},{2,3},{3,2},{4,5},{5,4},{6,7},{7,6},{8,9},{9,8},{10,11... | collective-permute-start | bytes 1572872 | tf_op jit(solution)/shard_map/ppermute | solution.py:974
  48.2 5.5 %collective-permute-start.7 = (bf16[128,2048]{1,0:T(8,128)(2,1)}, bf16[128,2048]{1,0:T(8,128)(2,1)}, u32[]{:S(2)}, u32[]{:S(2)}) collective-permute-start(bf16[128,2048]{1,0:T(8,128)(2,1)} %collective-permute-done.1.refs_3_), channel_id=1, source_target_pairs={{0,1},{1,0},{2,3},{3,2},{4,5},{5,4},{6,7},{7,6},{8,9},{9,8},{10,11... | collective-permute-start | bytes 1572872 | tf_op jit(solution)/shard_map/ppermute | solution.py:974
  48.7 5.9 %collective-permute-start.8 = (bf16[128,2048]{1,0:T(8,128)(2,1)}, bf16[128,2048]{1,0:T(8,128)(2,1)}, u32[]{:S(2)}, u32[]{:S(2)}) collective-permute-start(bf16[128,2048]{1,0:T(8,128)(2,1)} %collective-permute-done.2.refs_5_), channel_id=1, source_target_pairs={{0,1},{1,0},{2,3},{3,2},{4,5},{5,4},{6,7},{7,6},{8,9},{9,8},{10,11... | collective-permute-start | bytes 1572872 | tf_op jit(solution)/shard_map/ppermute | solution.py:974
  69.3 2.1 collective-permute-start.9
  72.2 9.8 %copy-start.26 = (bf16[2048]{0:T(1024)(128)(2,1)S(1)}, bf16[2048]{0:T(1024)(128)(2,1)}, u32[]{:S(2)}) copy-start(bf16[2048]{0:T(1024)(128)(2,1)} %param.26) | copy-start | bytes 12292
  78.4 15.9 %collective-permute-start.11 = (bf16[128,2048]{1,0:T(8,128)(2,1)}, bf16[128,2048]{1,0:T(8,128)(2,1)S(1)}, u32[]{:S(2)}, u32[]{:S(2)}) collective-permute-start(bf16[128,2048]{1,0:T(8,128)(2,1)} %get-tuple-element.170), channel_id=1, source_target_pairs={{0,2},{1,3},{2,4},{3,5},{4,6},{5,7},{6,0},{7,1},{8,10},{9,11},{10,... | collective-permute-start | bytes 1572872 | tf_op jit(solution)/shard_map/ppermute | solution.py:982
  79.0 15.3 %collective-permute-start.12 = (bf16[128,2048]{1,0:T(8,128)(2,1)}, bf16[128,2048]{1,0:T(8,128)(2,1)}, u32[]{:S(2)}, u32[]{:S(2)}) collective-permute-start(bf16[128,2048]{1,0:T(8,128)(2,1)} %get-tuple-element.171), channel_id=1, source_target_pairs={{0,6},{1,7},{2,0},{3,1},{4,2},{5,3},{6,4},{7,5},{8,14},{9,15},{10,... | collective-permute-start | bytes 1572872 | tf_op jit(solution)/shard_map/ppermute | solution.py:982
  81.1 23.9 %collective-permute-start.13 = (bf16[128,2048]{1,0:T(8,128)(2,1)}, bf16[128,2048]{1,0:T(8,128)(2,1)}, u32[]{:S(2)}, u32[]{:S(2)}) collective-permute-start(bf16[128,2048]{1,0:T(8,128)(2,1)} %get-tuple-element.172), channel_id=1, source_target_pairs={{0,4},{1,5},{2,6},{3,7},{4,0},{5,1},{6,2},{7,3},{8,12},{9,13},{10,... | collective-permute-start | bytes 1572872 | tf_op jit(solution)/shard_map/ppermute | solution.py:982
  94.3 10.6 %copy-start.15 = (bf16[128,2048]{1,0:T(8,128)(2,1)}, bf16[128,2048]{1,0:T(8,128)(2,1)S(1)}, u32[]{:S(2)}) copy-start(bf16[128,2048]{1,0:T(8,128)(2,1)S(1)} %collective-permute-done.11.b1) | copy-start | bytes 1572868
  110.6 48.2 %all-to-all-start = ((bf16[128,88,128]{2,1,0:T(8,128)(2,1)}), bf16[128,88,128]{2,1,0:T(8,128)(2,1)}, u32[]{:S(2)}, u32[]{:S(2)}) async-start(bf16[128,88,128]{2,1,0:T(8,128)(2,1)} %get-tuple-element.174), calls=%async_computation | async-start | bytes 5767168 | tf_op jit(solution)/shard_map/all_to_all | solution.py:986
  120.0 15.2 %collective-permute-start.14 = (bf16[512,2048]{1,0:T(8,128)(2,1)}, bf16[512,2048]{1,0:T(8,128)(2,1)}, u32[]{:S(2)}, u32[]{:S(2)}) collective-permute-start(bf16[512,2048]{1,0:T(8,128)(2,1)} %bitcast.5.refs_4_.refs_8_.wa), channel_id=1, source_target_pairs={{0,1},{1,0},{2,3},{3,2},{4,5},{5,4},{6,7},{7,6},{8,9},{9,8},{10,11... | collective-permute-start | bytes 6291464 | tf_op jit(solution)/shard_map/ppermute | solution.py:974
  121.7 5.5 %copy-start.17 = (f32[128,128]{1,0:T(8,128)S(1)}, f32[128,128]{1,0:T(8,128)}, u32[]{:S(2)}) copy-start(f32[128,128]{1,0:T(8,128)} %get-tuple-element.186.gates) | copy-start | bytes 196612
  178.1 5.9 %copy-start.7 = (s32[128,128]{1,0:T(8,128)S(1)}, s32[128,128]{1,0:T(8,128)}, u32[]{:S(2)}) copy-start(s32[128,128]{1,0:T(8,128)} %get-tuple-element.173.ids) | copy-start | bytes 196612
  178.1 44.6 %all-to-all-start.2 = ((bf16[128,88,128]{2,1,0:T(8,128)(2,1)}), bf16[128,88,128]{2,1,0:T(8,128)(2,1)}, u32[]{:S(2)}, u32[]{:S(2)}) async-start(bf16[128,88,128]{2,1,0:T(8,128)(2,1)} %get-tuple-element.207), calls=%async_computation.2 | async-start | bytes 5767168 | tf_op jit(solution)/shard_map/all_to_all | solution.py:986
  192.7 7.5 %copy-start.27 = (bf16[640,2048]{1,0:T(8,128)(2,1)S(1)}, bf16[640,2048]{1,0:T(8,128)(2,1)}, u32[]{:S(2)}) copy-start(bf16[640,2048]{1,0:T(8,128)(2,1)} %get-tuple-element.214) | copy-start | bytes 7864324
  192.7 7.5 %copy-start.28 = (bf16[640,768]{1,0:T(8,128)(2,1)S(1)}, bf16[640,768]{1,0:T(8,128)(2,1)}, u32[]{:S(2)}) copy-start(bf16[640,768]{1,0:T(8,128)(2,1)} %get-tuple-element.216) | copy-start | bytes 2949124
  200.2 4.6 copy-start.2
  200.2 4.6 copy-start.10
  229.8 25.2 %collective-permute-start.20 = (bf16[128,2048]{1,0:T(8,128)(2,1)}, bf16[128,2048]{1,0:T(8,128)(2,1)S(1)}, u32[]{:S(2)}, u32[]{:S(2)}) collective-permute-start(bf16[128,2048]{1,0:T(8,128)(2,1)} %get-tuple-element.223.refs_0_), channel_id=1, source_target_pairs={{0,2},{1,3},{2,4},{3,5},{4,6},{5,7},{6,0},{7,1},{8,10},{9,11},{10,... | collective-permute-start | bytes 1572872 | tf_op jit(solution)/shard_map/ppermute | solution.py:978
  229.9 27.0 %collective-permute-start.18 = (bf16[128,2048]{1,0:T(8,128)(2,1)}, bf16[128,2048]{1,0:T(8,128)(2,1)S(1)}, u32[]{:S(2)}, u32[]{:S(2)}) collective-permute-start(bf16[128,2048]{1,0:T(8,128)(2,1)} %get-tuple-element.223.refs_0_), channel_id=1, source_target_pairs={{0,6},{1,7},{2,0},{3,1},{4,2},{5,3},{6,4},{7,5},{8,14},{9,15},{10,... | collective-permute-start | bytes 1572872 | tf_op jit(solution)/shard_map/ppermute | solution.py:978
  232.5 24.4 %collective-permute-start.15 = (bf16[128,2048]{1,0:T(8,128)(2,1)}, bf16[128,2048]{1,0:T(8,128)(2,1)}, u32[]{:S(2)}, u32[]{:S(2)}) collective-permute-start(bf16[128,2048]{1,0:T(8,128)(2,1)} %get-tuple-element.223.refs_0_), channel_id=1, source_target_pairs={{0,4},{1,5},{2,6},{3,7},{4,0},{5,1},{6,2},{7,3},{8,12},{9,13},{10,... | collective-permute-start | bytes 1572872 | tf_op jit(solution)/shard_map/ppermute | solution.py:978
  232.5 24.8 %collective-permute-start.17 = (bf16[128,2048]{1,0:T(8,128)(2,1)}, bf16[128,2048]{1,0:T(8,128)(2,1)S(1)}, u32[]{:S(2)}, u32[]{:S(2)}) collective-permute-start(bf16[128,2048]{1,0:T(8,128)(2,1)} %get-tuple-element.223.refs_0_), channel_id=1, source_target_pairs={{0,1},{1,0},{2,3},{3,2},{4,5},{5,4},{6,7},{7,6},{8,9},{9,8},{10,11... | collective-permute-start | bytes 1572872 | tf_op jit(solution)/shard_map/ppermute | solution.py:974
  255.1 4.9 %copy-start.3 = (bf16[128,2048]{1,0:T(8,128)(2,1)}, bf16[128,2048]{1,0:T(8,128)(2,1)S(1)}, u32[]{:S(2)}) copy-start(bf16[128,2048]{1,0:T(8,128)(2,1)S(1)} %collective-permute-done.20.refs_4_.refs_3_) | copy-start | bytes 1572868
  255.1 3.3 collective-permute-start.21
  256.8 1.5 copy-start.4
  256.8 3.2 collective-permute-start.19
  256.9 8.4 %collective-permute-start.16 = (bf16[128,2048]{1,0:T(8,128)(2,1)}, bf16[128,2048]{1,0:T(8,128)(2,1)}, u32[]{:S(2)}, u32[]{:S(2)}) collective-permute-start(bf16[128,2048]{1,0:T(8,128)(2,1)} %collective-permute-done.15.refs_2_), channel_id=1, source_target_pairs={{0,1},{1,0},{2,3},{3,2},{4,5},{5,4},{6,7},{7,6},{8,9},{9,8},{10,11... | collective-permute-start | bytes 1572872 | tf_op jit(solution)/shard_map/ppermute | solution.py:974
  265.3 48.0 %all-to-all-start.3 = ((bf16[128,80,128]{2,1,0:T(8,128)(2,1)}), bf16[128,80,128]{2,1,0:T(8,128)(2,1)}, u32[]{:S(2)}, u32[]{:S(2)}) async-start(bf16[128,80,128]{2,1,0:T(8,128)(2,1)} %expert_out.1), calls=%async_computation.3 | async-start | bytes 5242880 | tf_op jit(solution)/shard_map/all_to_all | solution.py:986
  270.2 122.4 %all-reduce.2.cloned.1.call-start = ((), (), s32[]{:S(2)}) async-start(), calls=%async_computation.6 | async-start | bytes 4194304 | tf_op jit(solution)/shard_map/psum | solution.py:1116
  294.9 3.1 collective-permute-start.22
  308.1 18.3 %collective-permute-start.23 = (bf16[4,128,640]{2,1,0:T(8,128)(2,1)}, bf16[4,128,640]{2,1,0:T(8,128)(2,1)S(1)}, u32[]{:S(2)}, u32[]{:S(2)}) collective-permute-start(bf16[4,128,640]{2,1,0:T(8,128)(2,1)} %get-tuple-element.233), channel_id=1, source_target_pairs={{0,32},{8,40},{16,48},{24,56},{32,64},{40,72},{48,80},{56,88},{64,... | collective-permute-start | bytes 1966088 | tf_op jit(solution)/shard_map/ppermute | solution.py:997
  308.8 5.9 %collective-permute-start.29 = (bf16[512,512]{1,0:T(8,128)(2,1)}, bf16[512,512]{1,0:T(8,128)(2,1)}, u32[]{:S(2)}, u32[]{:S(2)}) collective-permute-start(bf16[512,512]{1,0:T(8,128)(2,1)} %get-tuple-element.230.dq1), channel_id=1, source_target_pairs={{0,1},{1,0},{2,3},{3,2},{4,5},{5,4},{6,7},{7,6},{8,9},{9,8},{10,11... | collective-permute-start | bytes 1572872 | tf_op jit(solution)/shard_map/ppermute | solution.py:974
  309.4 20.2 %collective-permute-start.24 = (bf16[4,128,640]{2,1,0:T(8,128)(2,1)}, bf16[4,128,640]{2,1,0:T(8,128)(2,1)}, u32[]{:S(2)}, u32[]{:S(2)}) collective-permute-start(bf16[4,128,640]{2,1,0:T(8,128)(2,1)} %get-tuple-element.234), channel_id=1, source_target_pairs={{0,96},{8,104},{16,112},{24,120},{32,0},{40,8},{48,16},{56,24},{64... | collective-permute-start | bytes 1966088 | tf_op jit(solution)/shard_map/ppermute | solution.py:997
  311.4 31.3 %collective-permute-start.25 = (bf16[4,128,640]{2,1,0:T(8,128)(2,1)}, bf16[4,128,640]{2,1,0:T(8,128)(2,1)}, u32[]{:S(2)}, u32[]{:S(2)}) collective-permute-start(bf16[4,128,640]{2,1,0:T(8,128)(2,1)} %get-tuple-element.235), channel_id=1, source_target_pairs={{0,64},{8,72},{16,80},{24,88},{32,96},{40,104},{48,112},{56,120},{... | collective-permute-start | bytes 1966088 | tf_op jit(solution)/shard_map/ppermute | solution.py:997
  312.7 1.9 collective-permute-start.30
  323.4 33.8 %collective-permute-start.31 = (bf16[160,2048]{1,0:T(8,128)(2,1)}, bf16[160,2048]{1,0:T(8,128)(2,1)}, u32[]{:S(2)}, u32[]{:S(2)}) collective-permute-start(bf16[160,2048]{1,0:T(8,128)(2,1)} %get-tuple-element.253), channel_id=1, source_target_pairs={{0,2},{1,3},{2,4},{3,5},{4,6},{5,7},{6,0},{7,1},{8,10},{9,11},{10,... | collective-permute-start | bytes 1966088 | tf_op jit(solution)/shard_map/ppermute | solution.py:982
  324.7 32.6 %collective-permute-start.32 = (bf16[160,2048]{1,0:T(8,128)(2,1)}, bf16[160,2048]{1,0:T(8,128)(2,1)}, u32[]{:S(2)}, u32[]{:S(2)}) collective-permute-start(bf16[160,2048]{1,0:T(8,128)(2,1)} %get-tuple-element.254), channel_id=1, source_target_pairs={{0,6},{1,7},{2,0},{3,1},{4,2},{5,3},{6,4},{7,5},{8,14},{9,15},{10,... | collective-permute-start | bytes 1966088 | tf_op jit(solution)/shard_map/ppermute | solution.py:982
  326.3 16.4 %copy-start.11 = (bf16[4,128,640]{2,1,0:T(8,128)(2,1)}, bf16[4,128,640]{2,1,0:T(8,128)(2,1)S(1)}, u32[]{:S(2)}) copy-start(bf16[4,128,640]{2,1,0:T(8,128)(2,1)S(1)} %collective-permute-done.23.b) | copy-start | bytes 1966084
  326.3 31.0 %collective-permute-start.33 = (bf16[160,2048]{1,0:T(8,128)(2,1)}, bf16[160,2048]{1,0:T(8,128)(2,1)}, u32[]{:S(2)}, u32[]{:S(2)}) collective-permute-start(bf16[160,2048]{1,0:T(8,128)(2,1)} %get-tuple-element.255), channel_id=1, source_target_pairs={{0,4},{1,5},{2,6},{3,7},{4,0},{5,1},{6,2},{7,3},{8,12},{9,13},{10,... | collective-permute-start | bytes 1966088 | tf_op jit(solution)/shard_map/ppermute | solution.py:982
  345.4 6.0 %collective-permute-start.26 = (bf16[128,640]{1,0:T(8,128)(2,1)}, bf16[128,640]{1,0:T(8,128)(2,1)S(1)}, u32[]{:S(2)}, u32[]{:S(2)}) collective-permute-start(bf16[128,640]{1,0:T(8,128)(2,1)} %get-tuple-element.237), channel_id=1, source_target_pairs={{0,8},{8,16},{16,24},{24,0},{32,40},{40,48},{48,56},{56,32},{64,72... | collective-permute-start | bytes 491528 | tf_op jit(solution)/shard_map/ppermute | solution.py:997
  346.6 6.3 %collective-permute-start.27 = (bf16[128,640]{1,0:T(8,128)(2,1)}, bf16[128,640]{1,0:T(8,128)(2,1)S(1)}, u32[]{:S(2)}, u32[]{:S(2)}) collective-permute-start(bf16[128,640]{1,0:T(8,128)(2,1)} %get-tuple-element.238), channel_id=1, source_target_pairs={{0,24},{8,0},{16,8},{24,16},{32,56},{40,32},{48,40},{56,48},{64,88... | collective-permute-start | bytes 491528 | tf_op jit(solution)/shard_map/ppermute | solution.py:997
  351.4 5.9 %copy-start.22 = (bf16[128,640]{1,0:T(8,128)(2,1)}, bf16[128,640]{1,0:T(8,128)(2,1)S(1)}, u32[]{:S(2)}) copy-start(bf16[128,640]{1,0:T(8,128)(2,1)S(1)} %collective-permute-done.26.b) | copy-start | bytes 491524
  351.4 5.9 %collective-permute-start.28 = (bf16[128,640]{1,0:T(8,128)(2,1)}, bf16[128,640]{1,0:T(8,128)(2,1)S(1)}, u32[]{:S(2)}, u32[]{:S(2)}) collective-permute-start(bf16[128,640]{1,0:T(8,128)(2,1)} %get-tuple-element.239), channel_id=1, source_target_pairs={{0,16},{8,24},{16,0},{24,8},{32,48},{40,56},{48,32},{56,40},{64,80... | collective-permute-start | bytes 491528 | tf_op jit(solution)/shard_map/ppermute | solution.py:997
  352.9 4.4 copy-start.23
  359.8 12.7 %collective-permute-start.36 = (bf16[128,640]{1,0:T(8,128)(2,1)}, bf16[128,640]{1,0:T(8,128)(2,1)S(1)}, u32[]{:S(2)}, u32[]{:S(2)}) collective-permute-start(bf16[128,640]{1,0:T(8,128)(2,1)} %add_last.1.a), channel_id=1, source_target_pairs={{0,8},{8,16},{16,24},{24,0},{32,40},{40,48},{48,56},{56,32},{64,72... | collective-permute-start | bytes 491528 | tf_op jit(solution)/shard_map/ppermute | solution.py:997
  360.2 12.4 %collective-permute-start.35 = (bf16[128,640]{1,0:T(8,128)(2,1)}, bf16[128,640]{1,0:T(8,128)(2,1)S(1)}, u32[]{:S(2)}, u32[]{:S(2)}) collective-permute-start(bf16[128,640]{1,0:T(8,128)(2,1)} %add_last.1.a), channel_id=1, source_target_pairs={{0,16},{8,24},{16,0},{24,8},{32,48},{40,56},{48,32},{56,40},{64,80... | collective-permute-start | bytes 491528 | tf_op jit(solution)/shard_map/ppermute | solution.py:997
  362.8 9.9 %collective-permute-start.34 = (bf16[128,640]{1,0:T(8,128)(2,1)}, bf16[128,640]{1,0:T(8,128)(2,1)S(1)}, u32[]{:S(2)}, u32[]{:S(2)}) collective-permute-start(bf16[128,640]{1,0:T(8,128)(2,1)} %add_last.1.a), channel_id=1, source_target_pairs={{0,24},{8,0},{16,8},{24,16},{32,56},{40,32},{48,40},{56,48},{64,88... | collective-permute-start | bytes 491528 | tf_op jit(solution)/shard_map/ppermute | solution.py:997
  368.2 24.4 %all-to-all-start.4 = ((bf16[16,24,128]{2,1,0:T(8,128)(2,1)}), bf16[16,24,128]{2,1,0:T(8,128)(2,1)S(1)}, u32[]{:S(2)}, u32[]{:S(2)}) async-start(bf16[16,24,128]{2,1,0:T(8,128)(2,1)} %get-tuple-element.265), calls=%async_computation.4 | async-start | bytes 196608 | tf_op jit(solution)/shard_map/all_to_all | solution.py:1136
  395.7 50.0 %all-to-all-start.5 = ((bf16[128,24,128]{2,1,0:T(8,128)(2,1)}), bf16[128,24,128]{2,1,0:T(8,128)(2,1)S(1)}, u32[]{:S(2)}, u32[]{:S(2)}) async-start(bf16[128,24,128]{2,1,0:T(8,128)(2,1)} %fold_small.1), calls=%async_computation.5 | async-start | bytes 1572864 | tf_op jit(solution)/shard_map/all_to_all | solution.py:986
  404.4 26.5 %collective-permute-start.39 = (bf16[4,128,640]{2,1,0:T(8,128)(2,1)}, bf16[4,128,640]{2,1,0:T(8,128)(2,1)}, u32[]{:S(2)}, u32[]{:S(2)}) collective-permute-start(bf16[4,128,640]{2,1,0:T(8,128)(2,1)} %stack_parts.1.c0), channel_id=1, source_target_pairs={{0,32},{8,40},{16,48},{24,56},{32,64},{40,72},{48,80},{56,88},{64,... | collective-permute-start | bytes 1966088 | tf_op jit(solution)/shard_map/ppermute | solution.py:997
  406.0 39.8 %collective-permute-start.38 = (bf16[4,128,640]{2,1,0:T(8,128)(2,1)}, bf16[4,128,640]{2,1,0:T(8,128)(2,1)}, u32[]{:S(2)}, u32[]{:S(2)}) collective-permute-start(bf16[4,128,640]{2,1,0:T(8,128)(2,1)} %stack_parts.1.c0), channel_id=1, source_target_pairs={{0,64},{8,72},{16,80},{24,88},{32,96},{40,104},{48,112},{56,120},{... | collective-permute-start | bytes 1966088 | tf_op jit(solution)/shard_map/ppermute | solution.py:997
  408.9 36.8 %collective-permute-start.37 = (bf16[4,128,640]{2,1,0:T(8,128)(2,1)}, bf16[4,128,640]{2,1,0:T(8,128)(2,1)}, u32[]{:S(2)}, u32[]{:S(2)}) collective-permute-start(bf16[4,128,640]{2,1,0:T(8,128)(2,1)} %stack_parts.1.c0), channel_id=1, source_target_pairs={{0,96},{8,104},{16,112},{24,120},{32,0},{40,8},{48,16},{56,24},{64... | collective-permute-start | bytes 1966088 | tf_op jit(solution)/shard_map/ppermute | solution.py:997
  446.0 6.6 %copy-start.1 = (s32[1,1024]{1,0:T(1,128)S(1)}, s32[1,1024]{1,0:T(1,128)}, u32[]{:S(2)}) copy-start(s32[1,1024]{1,0:T(1,128)} %param.32) | copy-start | bytes 12292
  (12 other events, 9.2 us)
Sparse Core Ops, SparseCore 0:
  278.1 114.4 all-reduce.1

commit v7 on v6

--- a/solution.py
+++ b/solution.py
@@ -453,53 +453,101 @@
     )
 
 
-def expert_main_body(wire, wg, wu, ga, back, xs, act, acts, dg, du, xr, sc):
-    split_rows(wire, xr)
-    gates = get_numbers(wire)
+def expert_main_body(
+    wire, wg, wu, ga, back, xs, act, acts, dg, du,
+    wire_v, w_v, ga_v, xr, xs_v, act_v, acts_v, d_v, sc, sems,
+):
+    half = F // 2
+
+    def copy(source, dest, number):
+        return pltpu.make_async_copy(source, dest, sems.at[number])
+
+    first = copy(wire, wire_v, 0)
+    first.start()
+    arrivals = []
+    for c in range(2):
+        cols = slice(c * half, (c + 1) * half)
+        up_cols = slice(F + c * half, F + (c + 1) * half)
+        group = [
+            copy(wg.at[:, cols], w_v.at[:, cols], 1 + 3 * c),
+            copy(wu.at[:, cols], w_v.at[:, up_cols], 2 + 3 * c),
+            copy(ga.at[:, cols], ga_v.at[:, cols], 3 + 3 * c),
+        ]
+        for item in group:
+            item.start()
+        arrivals.append(group)
+    first.wait()
+    split_rows(wire_v, xr)
+    gates = get_numbers(wire_v)
     sc[...] = jnp.zeros_like(sc)
-
-    def forward(i, carry):
-        cols = pl.ds(pl.multiple_of(i * 384, 384), 384)
-        gate = dot(xr[...], wg[:, cols])
-        up = dot(xr[...], wu[:, cols])
-        grad = ga[:, cols]
+    for c in range(2):
+        for item in arrivals[c]:
+            item.wait()
+        cols = slice(c * half, (c + 1) * half)
+        up_cols = slice(F + c * half, F + (c + 1) * half)
+        gate = dot(xr[...], w_v[:, cols])
+        up = dot(xr[...], w_v[:, up_cols])
+        grad = ga_v[:, cols]
         s = 1.0 / (1.0 + jnp.exp(-gate))
         silu = gate * s
         a = silu * up
-        act[:, cols] = a.astype(bf16)
-        dg[:, cols] = (grad * up * s * (1.0 + gate * (1.0 - s))).astype(bf16)
-        du[:, cols] = (grad * silu).astype(bf16)
+        act_v[:, cols] = a.astype(bf16)
+        d_v[:, cols] = (grad * up * s * (1.0 + gate * (1.0 - s))).astype(bf16)
+        d_v[:, up_cols] = (grad * silu).astype(bf16)
         sc[...] += jnp.sum(a * grad, axis=1, keepdims=True)
-        return carry
-
-    lax.fori_loop(0, F // 384, forward, 0)
+    departures = [copy(act_v, act, 7), copy(d_v.at[:, :F], dg, 8), copy(d_v.at[:, F:], du, 9)]
+    for item in departures:
+        item.start()
     for s in range(CAP):
         part = slice(s * E, (s + 1) * E)
         gate = gates[:, s : s + 1]
-        xs[part, :] = (xr[part, :].astype(f32) * gate).astype(bf16)
-        acts[part, :] = (act[part, :].astype(f32) * gate).astype(bf16)
+        xs_v[part, :] = (xr[part, :].astype(f32) * gate).astype(bf16)
+        acts_v[part, :] = (act_v[part, :].astype(f32) * gate).astype(bf16)
+    more = [copy(xs_v, xs, 10), copy(acts_v, acts, 11)]
+    for item in more:
+        item.start()
     for j in range(4):
         part = slice(j * 512, (j + 1) * 512)
-        xr[:, part] = (dot_t(dg[...], wg[part, :]) + dot_t(du[...], wu[part, :])).astype(bf16)
-    join_rows(xr, back)
-    put_numbers([sc[s * E : (s + 1) * E, :] for s in range(CAP)], back)
+        xr[:, part] = dot_t(d_v[...], w_v[part, :]).astype(bf16)
+    join_rows(xr, wire_v)
+    put_numbers([sc[s * E : (s + 1) * E, :] for s in range(CAP)], wire_v)
+    last = copy(wire_v, back, 12)
+    last.start()
+    for item in departures + more + [last]:
+        item.wait()
 
 
 def expert_main(wire, wg, wu, ga):
-    return call(
+    args = (wire, wg, wu, ga)
+    outs = [
+        sds((E, WIRE, 128), bf16),
+        sds((SLOTS, D), bf16),
+        sds((SLOTS, F), bf16),
+        sds((SLOTS, F), bf16),
+        sds((SLOTS, F), bf16),
+        sds((SLOTS, F), bf16),
+    ]
+    return pl.pallas_call(
         expert_main_body,
-        "expert_main",
-        [
-            sds((E, WIRE, 128), bf16),
-            sds((SLOTS, D), bf16),
-            sds((SLOTS, F), bf16),
-            sds((SLOTS, F), bf16),
-            sds((SLOTS, F), bf16),
-            sds((SLOTS, F), bf16),
+        out_shape=outs,
+        in_specs=[pl.BlockSpec(memory_space=pl.ANY)] * 4,
+        out_specs=[pl.BlockSpec(memory_space=pl.ANY)] * 6,
+        scratch_shapes=[
+            pltpu.VMEM((E, WIRE, 128), bf16),
+            pltpu.VMEM((D, 2 * F), bf16),
+            pltpu.VMEM((SLOTS, F), f32),
+            pltpu.VMEM((SLOTS, D), bf16),
+            pltpu.VMEM((SLOTS, D), bf16),
+            pltpu.VMEM((SLOTS, F), bf16),
+            pltpu.VMEM((SLOTS, F), bf16),
+            pltpu.VMEM((SLOTS, 2 * F), bf16),
+            pltpu.VMEM((SLOTS, 1), f32),
+            pltpu.SemaphoreType.DMA((13,)),
         ],
-        [pltpu.VMEM((SLOTS, D), bf16), pltpu.VMEM((SLOTS, 1), f32)],
-        (wire, wg, wu, ga),
-    )
+        compiler_params=pltpu.CompilerParams(vmem_limit_bytes=63 * 1024 * 1024),
+        cost_estimate=cost(COSTS["expert_main"]),
+        name="expert_main",
+    )(*args)
 
 
 def expert_out_body(act, wd, wire, rows):
@@ -608,33 +656,20 @@
     )[0]
 
 
-def head_grad_body(*refs):
-    blocks, (wo, dt, rows_all) = refs[:6], refs[6:]
-    for b in range(6):
-        rows_all[b * T : (b + 1) * T, :] = blocks[b][...]
-    for b in range(3):
-        rows = slice(b * 256, (b + 1) * 256)
-        dt[:, rows] = dot_t(wo[...], rows_all[rows, :]).astype(bf16)
-
-
-def head_grad(blocks, wo):
-    return call(
-        head_grad_body,
-        "head_grad",
-        [sds((LH * HEAD, 6 * T), bf16)],
-        [pltpu.VMEM((6 * T, D), bf16)],
-        (*blocks, wo),
-    )[0]
-
-
-def pre_body(*refs):
-    blocks, (ot0, ot1, wo, gw, dt, rows_all, total) = refs[:8], refs[8:]
+def pre_body(where, *refs):
+    blocks, (ot0, ot1, wo, w0, w1, w2, w3, dt, rows_all, total) = refs[:8], refs[8:]
     step = pl.program_id(0)
     for b in range(8):
         rows_all[b * T : (b + 1) * T, :] = blocks[b][...]
-    gw[...] = (dot(ot0[...], rows_all[:HALF, :]) + dot(ot1[...], rows_all[HALF:, :])).astype(bf16)
-    last = jnp.concatenate([blocks[2][...], blocks[6][...]], axis=0)
-    part = dot_t(wo[...], last)
+    grad = (dot(ot0[...], rows_all[:HALF, :]) + dot(ot1[...], rows_all[HALF:, :])).astype(bf16)
+    for dx, out in enumerate((w0, w1, w2, w3)):
+
+        @pl.when(step == dx)
+        def _():
+            for col in range(4):
+                out[lax.rem(col + 4 - where[0], 4)] = grad[:, col * 128 : (col + 1) * 128]
+
+    part = dot_t(wo[...], rows_all[...])
 
     @pl.when(step == 0)
     def _():
@@ -649,28 +684,28 @@
         dt[...] = total[...].astype(bf16)
 
 
-def pre(blocks, ot0, ot1, wo):
+def pre(where, blocks, ot0, ot1, wo):
+    def turned(shape):
+        return pl.BlockSpec(shape, lambda i, w: (0, lax.rem(i + w[1], 4)))
+
     return grid_call(
         pre_body,
         "out_projection_grad",
         (4,),
-        [cols_of((T, 512))] * 8 + [whole((512, HALF))] * 2 + [cols_of((512, 512))],
-        [cols_of((512, 512)), whole((512, 2 * T))],
-        [sds((LH * HEAD, D), bf16), sds((LH * HEAD, 2 * T), bf16)],
-        [pltpu.VMEM((ROWS, 512), bf16), pltpu.VMEM((512, 2 * T), f32)],
-        (*blocks, ot0, ot1, wo),
+        [turned((T, 512))] * 8 + [whole((512, HALF))] * 2 + [turned((512, 512))],
+        [whole((4, 512, 128))] * 4 + [whole((512, ROWS))],
+        [sds((4, 512, 128), bf16)] * 4 + [sds((LH * HEAD, ROWS), bf16)],
+        [pltpu.VMEM((ROWS, 512), bf16), pltpu.VMEM((512, ROWS), f32)],
+        (where, *blocks, ot0, ot1, wo),
+        scalars=1,
     )
 
 
 def bwd_body(*refs):
     qh, kh, scales = refs[0:4], refs[4:8], refs[8:12]
-    (qt, kt, kn, vn, dta, dtb, ot0, ot1, linv, info, cos, sin, gq, gk) = refs[12:26]
-    dq0, dq1, dkv, ggq, ggk, mask, wb, sb, dqt, dk, dv, raw, dt, scale = refs[26:]
+    (qt, kt, kn, vn, dt, ot0, ot1, linv, info, cos, sin, gq, gk) = refs[12:25]
+    dq0, dq1, dkv, ggq, ggk, mask, wb, sb, dqt, dk, dv, raw, scale = refs[25:]
     for dc in range(2):
-        for place, dy in enumerate((0, 1, 3)):
-            to = slice(dc * HALF + dy * T, dc * HALF + (dy + 1) * T)
-            dt[:, to] = dta[:, (place * 2 + dc) * T : (place * 2 + dc + 1) * T]
-        dt[:, dc * HALF + 2 * T : dc * HALF + 3 * T] = dtb[:, dc * T : (dc + 1) * T]
         for dy in range(4):
             to = slice(dc * HALF + dy * T, dc * HALF + (dy + 1) * T)
             scale[:, to] = scales[dy][:, dc * T : (dc + 1) * T]
@@ -748,17 +783,14 @@
             pltpu.VMEM((ROWS, HEAD), f32),
             pltpu.VMEM((ROWS, HEAD), f32),
             pltpu.VMEM((HEAD, ROWS), f32),
-            pltpu.VMEM((LH * HEAD, ROWS), bf16),
             pltpu.VMEM((8, ROWS), f32),
         ],
         (*qh, *kh, *scales, *rest),
     )
 
 
-def qkv_grad_body(where, n1t, dq0, dq1, own, sib, w0, w1, w2, w3, tot, dt):
-    step = pl.program_id(0)
-
-    @pl.when(step == 0)
+def qkv_grad_body(where, n1t, dq0, dq1, own, sib, out, tot, dt):
+    @pl.when(pl.program_id(0) == 0)
     def _():
         tot[:, :HALF] = (own[:, :HALF].astype(f32) + sib[:, HALF:].astype(f32)).astype(bf16)
         tot[:, HALF:] = (own[:, HALF:].astype(f32) + sib[:, :HALF].astype(f32)).astype(bf16)
@@ -768,14 +800,7 @@
         dt[512:576, :] = jnp.where(upper, tot[64:128, :], tot[:64, :])
         dt[576:, :] = jnp.where(upper, tot[192:, :], tot[128:192, :])
 
-    grad = dot_t(n1t[...], dt[...]).astype(bf16)
-    for dz, out in enumerate((w0, w1, w2, w3)):
-
-        @pl.when(step == dz)
-        def _():
-            for col in range(4):
-                dx = lax.rem(col + 4 - where[1], 4)
-                out[dx] = grad[col * 128 : (col + 1) * 128, :]
+    out[...] = dot_t(n1t[...], dt[...]).astype(bf16)
 
 
 def qkv_grad(where, n1t, dq0, dq1, own, sib):
@@ -784,17 +809,37 @@
         "qkv_weight_grad",
         (4,),
         [
-            pl.BlockSpec((512, ROWS), lambda i, w: (lax.rem(i + w[0], 4), 0)),
+            rows_of((512, ROWS)),
             whole((512, HALF)),
             whole((512, HALF)),
             whole((2 * HEAD, ROWS)),
             whole((2 * HEAD, ROWS)),
         ],
-        [whole((4, 128, 640))] * 4 + [whole((2 * HEAD, ROWS))],
-        [sds((4, 128, 640), bf16)] * 4 + [sds((2 * HEAD, ROWS), bf16)],
+        [rows_of((512, 640)), whole((2 * HEAD, ROWS))],
+        [sds((D, 640), bf16), sds((2 * HEAD, ROWS), bf16)],
         [pltpu.VMEM((640, ROWS), bf16)],
         (where, n1t, dq0, dq1, own, sib),
         scalars=1,
+    )
+
+
+def widen_body(grads, gq, gkt, gvt):
+    gq[...] = grads[:, :512].astype(f32)
+    both = grads[:, 512:].astype(f32).T
+    gkt[...] = both[:64]
+    gvt[...] = both[64:]
+
+
+def widen(grads):
+    return grid_call(
+        widen_body,
+        "widen_grads",
+        (4,),
+        [rows_of((512, 640))],
+        [rows_of((512, 512)), cols_of((64, 512)), cols_of((64, 512))],
+        [sds((D, 512), f32), sds((64, D), f32), sds((64, D), f32)],
+        [],
+        (grads,),
     )
 
 
@@ -891,26 +936,23 @@
     return call(stack_body, "stack_parts", [sds(shape, bf16)], [], tuple(parts))[0]
 
 
-def place_body(where, c0, c1, c2, c3, gq, gkt, gvt):
-    for dz, chunks in enumerate((c0, c1, c2, c3)):
-        for dx in range(4):
-            chunk = lax.rem(where[0] + dz, 4) * 4 + lax.rem(where[1] + dx, 4)
-            rows = pl.ds(pl.multiple_of(chunk * 128, 128), 128)
-            gq[rows, :] = chunks[dx, :, :512].astype(f32)
-            both = chunks[dx, :, 512:].astype(f32).T
-            gkt[:, rows] = both[:64]
-            gvt[:, rows] = both[64:]
-
-
-def place(where, chunks):
+def place_out_body(where, c0, c1, c2, c3, out):
+    for dx, chunks in enumerate((c0, c1, c2, c3)):
+        for dz in range(4):
+            chunk = lax.rem(where[1] + dx, 4) * 4 + lax.rem(where[0] + dz, 4)
+            cols = pl.ds(pl.multiple_of(chunk * 128, 128), 128)
+            out[:, cols] = chunks[dz].astype(f32)
+
+
+def place_out(where, chunks):
     return call(
-        place_body,
-        "place_weight_grads",
-        [sds((D, 512), f32), sds((64, D), f32), sds((64, D), f32)],
+        place_out_body,
+        "place_output_grads",
+        [sds((512, D), f32)],
         [],
         (where, *chunks),
         smem=(0,),
-    )
+    )[0]
 
 
 def final_body(b0, b1, b2, b3, x0, ghid, g1, out, small):
@@ -1105,22 +1147,15 @@
     )
     g_own = [gatt] + [from_chip(gatt, dy) for dy in (1, 2, 3)]
     g_sib = [sibling(block) for block in g_own]
-    dt_near = head_grad(
-        [g_own[0], g_sib[0], g_own[1], g_sib[1], g_own[3], g_sib[3]], w_out
-    )
-    g_far, dt_near = lax.optimization_barrier(((g_own[2], g_sib[2]), dt_near))
-    g_own[2], g_sib[2] = g_far
-
-    returned = exchange(after(out_wire, g_own[2]))
-    gwout, dt_far = pre(g_own + g_sib, ot0, ot1, w_out)
-    grad_wout = lax.psum(gwout, "expert")
+    returned = exchange(after(out_wire, *g_sib))
+    *out_parts, dt = pre(where, g_own + g_sib, ot0, ot1, w_out)
 
     dq0, dq1, dkv, ggq, ggk = bwd(
-        qh, kh, scales, qt, kt, kn, vn, dt_near, dt_far, ot0, ot1, linv, info, cos, sin, gq, gk
+        qh, kh, scales, qt, kt, kn, vn, dt, ot0, ot1, linv, info, cos, sin, gq, gk
     )
     router_sib = after(router_sib, dkv)
     dq_sib, dkv_sib = sibling(dq1), sibling(dkv)
-    *parts, dkv_total = qkv_grad(where, n1_t, dq0, dq1, dkv, dkv_sib)
+    gw, dkv_total = qkv_grad(where, n1_t, dq0, dq1, dkv, dkv_sib)
     returned, dq0 = lax.optimization_barrier((returned, dq0))
     result = result_rows(expert_list, slot_list, gate_list, returned, hidden)
     router_rec = sibling(router_sib)
@@ -1129,19 +1164,17 @@
     )
     blocks = [blocks[0]] + spread(blocks)
 
-    parts = collect(add_parts(collect(parts, 0)), 1)
-    parts, blocks = lax.optimization_barrier((parts, blocks))
-    chunks = share(add_last(parts)[0], 1)
+    gw = lax.psum(gw, "expert")
+    out_parts = collect(add_parts(collect(out_parts, 1)), 0)
+    chunks = stack(share(add_last(out_parts)[0], 0))
     grad_input, small = final(blocks, block_input, ghid, g1)
     small = lax.all_to_all(small, "expert", split_axis=0, concat_axis=0, tiled=True)
-    chunks, small, grad_wout = lax.optimization_barrier((stack(chunks), small, grad_wout))
-    chunks = share(chunks, 0)
     small = exchange(fold(small))
-    grad_wout = grad_wout.astype(f32)
-    chunks, small, grad_input, grad_wout, result = lax.optimization_barrier(
-        (chunks, small, grad_input, grad_wout, result)
-    )
-    grad_wq, grad_wk, grad_wv = place(where, chunks)
+    grad_wout = place_out(where, share(chunks, 1))
+    gw, small, grad_input, grad_wout, result = lax.optimization_barrier(
+        (gw, small, grad_input, grad_wout, result)
+    )
+    grad_wq, grad_wk, grad_wv = widen(gw)
     small = small.reshape(16, 8, 24, 128).astype(f32)
     grad_router = small[:, :, :SEG].transpose(1, 0, 2, 3).reshape(D, E)
     gains = small[:, 0, SEG:] + small[:, 1, SEG:]

time: 467 us -> 461 us (0.987)
    pallas_call x20 -> x18, Pallas kernels: 122 us -> 96.2 us  [call(): pl.pallas_call(kernel, out_shape=outs, in_specs=in_specs, out_specs=[pl.B...]
    ppermute x6, waiting for transfers between devices: 22.4 us -> 45.3 us  [to_chip(): return lax.ppermute(x, 'shard', [(i, (i + 2 * dy) % 8) for i in range(8)])]
    psum x1, waiting for transfers between devices: 16.5 us -> 0.01 us  [on_device(): gw = lax.psum(gw, 'expert')]
    pallas_call x0 -> x1, Pallas kernels: none -> 15.9 us  [expert_main(): pl.pallas_call(expert_main_body, out_shape=outs, in_specs=[pl.BlockSpec(m...]
    ppermute x12, waiting for transfers between devices: 48.2 us -> 38.1 us  [on_expert(): return lax.ppermute(x, 'expert', pairs)]
    pallas_call x4 -> x5, Pallas kernels: 31.3 us -> 39.2 us  [grid_call(): pl.pallas_call(kernel, out_shape=outs, grid_spec=pltpu.PrefetchScalarGrid...]
    unnamed x59 -> x61, local copies, waits for them, and re-layouts: 10.4 us -> 10.3 us
  transfers between devices with their start and end apart: 47 -> 47, of which waited for: 20 -> 19; matrix products, arithmetic and copies ran while one was open for 8% -> 7% of each run, Pallas kernels for 26% -> 27%
where the time goes in v7:
time: 461 us; the launch traced here: 454 us
  waiting for transfers between devices  154 us (33%)
  Pallas kernels  151 us (33%)
  starting transfers between devices  92.8 us (20%)
  matrix products  16.6 us (4%)
  local copies, waits for them, and re-layouts  16 us (3%)
  between operations  14.6 us (3%)
  other arithmetic  8.01 us (2%)
    pallas_call x18, Pallas kernels, call(): pl.pallas_call(kernel, out_shape=outs, in_specs=in_specs, out_specs=[pl.B...  96.2 us
    ppermute x6, waiting for transfers between devices, to_chip(): return lax.ppermute(x, 'shard', [(i, (i + 2 * dy) % 8) for i in range(8)])  45.3 us
    pallas_call x5, Pallas kernels, grid_call(): pl.pallas_call(kernel, out_shape=outs, grid_spec=pltpu.PrefetchScalarGrid...  39.2 us
    all_to_all x5, starting transfers between devices, exchange(): return lax.all_to_all(x, ALL, split_axis=0, concat_axis=0, tiled=True)  38.5 us
    ppermute x12, waiting for transfers between devices, on_expert(): return lax.ppermute(x, 'expert', pairs)  38.1 us
    all_to_all x5, waiting for transfers between devices, exchange(): return lax.all_to_all(x, ALL, split_axis=0, concat_axis=0, tiled=True)  37.3 us
    ppermute x6, waiting for transfers between devices, from_chip(): return lax.ppermute(x, 'shard', [(i, (i - 2 * dy) % 8) for i in range(8)])  21.1 us
    ppermute x12, starting transfers between devices, on_expert(): return lax.ppermute(x, 'expert', pairs)  19.6 us
  transfers between devices with their start and end apart: 47, of which 19 were waited for; matrix products, arithmetic and copies ran while one was open for 7% of the time, Pallas kernels for 27%

profile of v7, /device:TPU:1, one launch (start us, length us, event | category | flops | bytes accessed | tf_op | source)
XLA Modules:
  0.0 453.7 jit_solution(18055936594168062315)
XLA Ops:
  7.2 1.5 collective-permute-start.3
  10.1 2.6 collective-permute-start.1
  18.3 2.0 route_tables.1
  21.5 4.2 pack_rows.1
  26.3 3.9 copy.39
  30.2 1.8 multiply_sine_fusion
  32.7 5.0 %qkv0.1 = (bf16[512,256]{1,0:T(8,128)(2,1)}, bf16[512,256]{1,0:T(8,128)(2,1)}, bf16[128,256]{1,0:T(8,128)(2,1)}, bf16[128,256]{1,0:T(8,128)(2,1)}, bf16[128,256]...) custom-call(s32[1]{0:T(128)} %bitcast.2.refs_0_, ...), custom_call_target="tpu_custom_call" | custom-call | flops 1 | bytes 1 | tf_op jit(solution)/shard_map/qkv0/pallas_call | solution.py:61
  37.7 9.2 %all-to-all-start.1 = ((bf16[128,88,128]{2,1,0:T(8,128)(2,1)}), bf16[128,88,128]{2,1,0:T(8,128)(2,1)}, u32[]{:S(2)}, u32[]{:S(2)}) async-start(bf16[128,88,128]{2,1,0:T(8,128)(2,1)} %pack_rows.1), calls=%async_computation.1 | async-start | bytes 5767168 | tf_op jit(solution)/shard_map/all_to_all | solution.py:1028
  49.7 3.8 collective-permute-done.6.refs_2_
  54.5 7.8 %qkv123.1 = (bf16[512,256]{1,0:T(8,128)(2,1)}, bf16[512,256]{1,0:T(8,128)(2,1)}, bf16[128,256]{1,0:T(8,128)(2,1)}, bf16[128,256]{1,0:T(8,128)(2,1)}, bf16[128,25...) custom-call(s32[1]{0:T(128)} %bitcast.2.refs_0_, ...), custom_call_target="tpu_custom_call" | custom-call | flops 1 | bytes 1 | tf_op jit(solution)/shard_map/qkv123/pallas_call | solution.py:61
  62.3 7.1 %attend.1 = (bf16[512,512]{1,0:T(8,128)(2,1)}, bf16[512,512]{1,0:T(8,128)(2,1)}, f32[8,1024]{1,0:T(8,128)}, bf16[512,1024]{1,0:T(8,128)(2,1)}, bf16[128,1024]{1,...) custom-call(bf16[512,256]{1,0:T(8,128)(2,1)} %get-tuple-element.135.refs_0_, ...), custom_call_target="tpu_custom_call" | custom-call | flops 1 | bytes 6600001 | tf_op jit(solution)/shard_map/attend/pallas_call | solution.py:61
  69.8 1.8 collective-permute-done.9.otr
  72.3 6.2 %out_projection.1 = (bf16[128,2048]{1,0:T(8,128)(2,1)}, bf16[128,2048]{1,0:T(8,128)(2,1)}, bf16[128,2048]{1,0:T(8,128)(2,1)}, bf16[128,2048]{1,0:T(8,128)(2,1)}) custom-call(bf16[512,512]{1,0:T(8,128)(2,1)} %get-tuple-element.150.ot0.refs_8_.refs_17_, bf16[512,512]{1,0:T(8,128)(2,1)} %copy-done.11, bf16[512,2048]{1,0:T(8,128)(2,1)} %refs_10_.1, ...), custom_call_target="tpu_custom_call" | custom-call | flops 1 | bytes 3000001 | tf_op jit(solution)/shard_map/out_projection/pallas_call | solution.py:74
  79.1 2.0 collective-permute-start.12
  83.1 11.4 %collective-permute-done.11.b1 = bf16[128,2048]{1,0:T(8,128)(2,1)S(1)} collective-permute-done((bf16[128,2048]{1,0:T(8,128)(2,1)}, bf16[128,2048]{1,0:T(8,128)(2,1)S(1)}, u32[]{:S(2)}, u32[]{:S(2)}) %collective-permute-start.11) | collective-permute-done | bytes 524320 | tf_op jit(solution)/shard_map/ppermute | solution.py:1024
  94.5 10.3 %collective-permute-done.13.b3 = bf16[128,2048]{1,0:T(8,128)(2,1)} collective-permute-done((bf16[128,2048]{1,0:T(8,128)(2,1)}, bf16[128,2048]{1,0:T(8,128)(2,1)}, u32[]{:S(2)}, u32[]{:S(2)}) %collective-permute-start.13) | collective-permute-done | bytes 524320 | tf_op jit(solution)/shard_map/ppermute | solution.py:1024
  104.8 5.6 %router.1 = (f32[128,2048]{1,0:T(8,128)}, bf16[128,2048]{1,0:T(8,128)(2,1)}, f32[128,128]{1,0:T(8,128)}, f32[128,128]{1,0:T(8,128)}, bf16[128,88,128]{2,1,0:T(8,128)(2,1)}) custom-call(bf16[128,2048]{1,0:T(8,128)(2,1)} %get-tuple-element.152.b0, bf16[128,2048]{1,0:T(8,128)(2,1)} %copy-done.13, bf16[128,2048]{1,0:T(8,128)(2,1)} %collective-permute-done.12.b2, ...), custom_call_target="tpu_custom_call" | custom-call | flops 1 | bytes 3600001 | tf_op jit(solution)/shard_map/router/pallas_call | solution.py:61
  110.5 9.7 %all-to-all-start = ((bf16[128,88,128]{2,1,0:T(8,128)(2,1)}), bf16[128,88,128]{2,1,0:T(8,128)(2,1)}, u32[]{:S(2)}, u32[]{:S(2)}) async-start(bf16[128,88,128]{2,1,0:T(8,128)(2,1)} %get-tuple-element.157), calls=%async_computation | async-start | bytes 5767168 | tf_op jit(solution)/shard_map/all_to_all | solution.py:1028
  121.4 5.5 %transpose_rows.1.n1t = bf16[2048,1024]{1,0:T(8,128)(2,1)} custom-call(bf16[256,2048]{1,0:T(8,128)(2,1)} %get-tuple-element.162.n0, bf16[256,2048]{1,0:T(8,128)(2,1)} %get-tuple-element.163.n1, bf16[256,2048]{1,0:T(8,128)(2,1)} %get-tuple-element.164.n2, bf16[256,2048]{1,0:T(8,128)(2,1)} %get-tuple-element.165.n3), custom_call_target="tpu_custom_call" | custom-call | flops 1 | bytes 3600001 | tf_op jit(solution)/shard_map/transpose_rows/pallas_call | solution.py:61
  127.5 7.5 %expert_grad_rows.1 = (bf16[640,2048]{1,0:T(8,128)(2,1)}, f32[640,768]{1,0:T(8,128)}) custom-call(bf16[128,88,128]{2,1,0:T(8,128)(2,1)} %all-to-all-done.1.wire, bf16[768,2048]{1,0:T(8,128)(2,1)} %bitcast.69), custom_call_target="tpu_custom_call" | custom-call | flops 1 | bytes 4800001 | tf_op jit(solution)/shard_map/expert_grad_rows/pallas_call | solution.py:61
  135.0 23.9 %all-to-all-done.wire = bf16[128,88,128]{2,1,0:T(8,128)(2,1)} async-done(((bf16[128,88,128]{2,1,0:T(8,128)(2,1)}), bf16[128,88,128]{2,1,0:T(8,128)(2,1)}, u32[]{:S(2)}, u32[]{:S(2)}) %all-to-all-start) | async-done | bytes 2883616 | tf_op jit(solution)/shard_map/all_to_all | solution.py:1028
  158.9 15.9 %expert_main.1 = (bf16[128,88,128]{2,1,0:T(8,128)(2,1)}, bf16[640,2048]{1,0:T(8,128)(2,1)}, bf16[640,768]{1,0:T(8,128)(2,1)}, bf16[640,768]{1,0:T(8,128)(2,1)}, ...) custom-call(bf16[128,88,128]{2,1,0:T(8,128)(2,1)} %all-to-all-done.wire, bf16[2048,768]{1,0:T(8,128)(2,1)} %bitcast.73, ...), custom_call_target="tpu_custom_call" | custom-call | flops 1 | bytes 10800001 | tf_op jit(solution)/shard_map/expert_main/pallas_call | solution.py:530
  174.8 5.9 %all-to-all-start.2 = ((bf16[128,88,128]{2,1,0:T(8,128)(2,1)}), bf16[128,88,128]{2,1,0:T(8,128)(2,1)}, u32[]{:S(2)}, u32[]{:S(2)}) async-start(bf16[128,88,128]{2,1,0:T(8,128)(2,1)} %get-tuple-element.190), calls=%async_computation.2 | async-start | bytes 5767168 | tf_op jit(solution)/shard_map/all_to_all | solution.py:1028
  182.8 6.6 %expert_out.1 = bf16[128,80,128]{2,1,0:T(8,128)(2,1)} custom-call(bf16[640,768]{1,0:T(8,128)(2,1)} %get-tuple-element.196.act, bf16[768,2048]{1,0:T(8,128)(2,1)} %bitcast.70), custom_call_target="tpu_custom_call" | custom-call | flops 1 | bytes 4200001 | tf_op jit(solution)/shard_map/expert_out/pallas_call | solution.py:61
  189.3 7.5 %fusion.7 = f32[2048,768]{1,0:T(8,128)} fusion(bf16[640,2048]{1,0:T(8,128)(2,1)} %get-tuple-element.197, bf16[640,768]{1,0:T(8,128)(2,1)} %get-tuple-element.198), kind=kOutput, calls=%fused_computation.32 | convolution fusion | flops 2013265920 | bytes 9895936 | tf_op jit(solution)/shard_map/dot_general | solution.py:1135
  196.9 4.6 %fusion.8 = f32[2048,768]{1,0:T(8,128)} fusion(bf16[640,2048]{1,0:T(8,128)(2,1)S(1)} %copy-done.27, bf16[640,768]{1,0:T(8,128)(2,1)S(1)} %copy-done.28), kind=kOutput, calls=%fused_computation.33 | convolution fusion | flops 2013265920 | bytes 9895936 | tf_op jit(solution)/shard_map/dot_general | solution.py:1135
  201.4 4.5 %fusion.9 = f32[768,2048]{1,0:T(8,128)} fusion(bf16[640,768]{1,0:T(8,128)(2,1)S(1)} %copy-done.6, bf16[640,2048]{1,0:T(8,128)(2,1)S(1)} %copy-done.2), kind=kOutput, calls=%fused_computation.34 | convolution fusion | flops 2013265920 | bytes 9895936 | tf_op jit(solution)/shard_map/dot_general | solution.py:1135
  206.0 13.4 %all-to-all-done.2.wire = bf16[128,88,128]{2,1,0:T(8,128)(2,1)} async-done(((bf16[128,88,128]{2,1,0:T(8,128)(2,1)}), bf16[128,88,128]{2,1,0:T(8,128)(2,1)}, u32[]{:S(2)}, u32[]{:S(2)}) %all-to-all-start.2) | async-done | bytes 2883616 | tf_op jit(solution)/shard_map/all_to_all | solution.py:1028
  219.4 7.1 %combine_grads.1 = (f32[128,2048]{1,0:T(8,128)}, bf16[128,2048]{1,0:T(8,128)(2,1)}, bf16[4,256,128]{2,1,0:T(8,128)(2,1)}, bf16[4,256,128]{2,1,0:T(8,128)(2,1)}, f32[1,2048]{1,0:T(1,128)}) custom-call(s32[4]{0:T(128)} %pad_add_fusion.where, s32[512]{0:T(512)} %reshape.212.experts, s32[512]{0:T(512)} %reshape.213.slots, f32[512]{0:T(512)} %reshape.211.gate_list, ...), custom_call_target="tpu_custom_call" | custom-call | flops 1 | bytes 4200001 | tf_op jit(solution)/shard_map/combine_grads/pallas_call | solution.py:61
  227.4 1.7 collective-permute-start.15
  230.6 21.1 %collective-permute-done.17.refs_3_ = bf16[128,2048]{1,0:T(8,128)(2,1)S(1)} collective-permute-done((bf16[128,2048]{1,0:T(8,128)(2,1)}, bf16[128,2048]{1,0:T(8,128)(2,1)S(1)}, u32[]{:S(2)}, u32[]{:S(2)}) %collective-permute-start.17) | collective-permute-done | bytes 524320 | tf_op jit(solution)/shard_map/ppermute | solution.py:1020
  251.7 1.8 collective-permute-start.21
  255.0 1.5 collective-permute-done.20.refs_6_
  257.4 4.8 %all-to-all-start.3 = ((bf16[128,80,128]{2,1,0:T(8,128)(2,1)}), bf16[128,80,128]{2,1,0:T(8,128)(2,1)}, u32[]{:S(2)}, u32[]{:S(2)}) async-start(bf16[128,80,128]{2,1,0:T(8,128)(2,1)} %expert_out.1), calls=%async_computation.3 | async-start | bytes 5242880 | tf_op jit(solution)/shard_map/all_to_all | solution.py:1028
  262.6 11.7 %out_projection_grad.1 = (bf16[4,512,128]{2,1,0:T(8,128)(2,1)}, bf16[4,512,128]{2,1,0:T(8,128)(2,1)}, bf16[4,512,128]{2,1,0:T(8,128)(2,1)}, bf16[4,512,128]{2,1,0:T(8,128)(2,1)}, bf16[512,1024]{1,0:T(8,128)(2,1)}) custom-call(s32[4]{0:T(128)} %pad_add_fusion.where, bf16[128,2048]{1,0:T(8,128)(2,1)} %get-tuple-element.206.refs_0_, ...), custom_call_target="tpu_custom_call" | custom-call | flops 1 | bytes 4200001 | tf_op jit(solution)/shard_map/out_projection_grad/pallas_call | solution.py:74
  274.4 16.7 %attend_grad.1 = (bf16[512,512]{1,0:T(8,128)(2,1)}, bf16[512,512]{1,0:T(8,128)(2,1)}, bf16[256,1024]{1,0:T(8,128)(2,1)}, f32[8,128]{1,0:T(8,128)}, f32[8,128]{1,0:T(8,128)}) custom-call(bf16[512,256]{1,0:T(8,128)(2,1)} %get-tuple-element.171.refs_0_, bf16[512,256]{1,0:T(8,128)(2,1)} %get-tuple-element.172.refs_1_, ...), custom_call_target="tpu_custom_call" | custom-call | flops 1 | bytes 1 | tf_op jit(solution)/shard_map/attend_grad/pallas_call | solution.py:61
  292.4 1.7 collective-permute-done.22.sib
  294.9 8.5 %qkv_weight_grad.1 = (bf16[2048,640]{1,0:T(8,128)(2,1)}, bf16[256,1024]{1,0:T(8,128)(2,1)}) custom-call(s32[4]{0:T(128)} %pad_add_fusion.where, bf16[2048,1024]{1,0:T(8,128)(2,1)} %transpose_rows.1.n1t, bf16[512,512]{1,0:T(8,128)(2,1)} %get-tuple-element.217.dq0, bf16[512,512]{1,0:T(8,128)(2,1)} %get-tuple-element.210.dq1, ...), custom_call_target="tpu_custom_call" | custom-call | flops 1 | bytes 1 | tf_op jit(solution)/shard_map/qkv_weight_grad/pallas_call | solution.py:74
  305.0 1.8 collective-permute-done.24.rb
  307.6 8.2 %normed_grad.1 = (bf16[160,2048]{1,0:T(8,128)(2,1)}, bf16[160,2048]{1,0:T(8,128)(2,1)}, bf16[160,2048]{1,0:T(8,128)(2,1)}, bf16[160,2048]{1,0:T(8,128)(2,1)}) custom-call(bf16[512,2048]{1,0:T(8,128)(2,1)} %bitcast.5.refs_4_.refs_8_.wa, bf16[512,2048]{1,0:T(8,128)(2,1)} %collective-permute-done.14.wb, bf16[256,2048]{1,0:T(8,128)(2,1)} %get-tuple-element.214.wkv, ...), custom_call_target="tpu_custom_call" | custom-call | flops 1 | bytes 1 | tf_op jit(solution)/shard_map/normed_grad/pallas_call | solution.py:74
  316.7 2.0 collective-permute-start.26
  320.9 1.4 collective-permute-start.29
  322.4 11.0 %collective-permute-done.25.b1 = bf16[160,2048]{1,0:T(8,128)(2,1)S(1)} collective-permute-done((bf16[160,2048]{1,0:T(8,128)(2,1)}, bf16[160,2048]{1,0:T(8,128)(2,1)S(1)}, u32[]{:S(2)}, u32[]{:S(2)}) %collective-permute-start.25) | collective-permute-done | bytes 655392 | tf_op jit(solution)/shard_map/ppermute | solution.py:1024
  333.4 2.1 collective-permute-start.30
  335.5 12.6 %collective-permute-done.27.b3 = bf16[160,2048]{1,0:T(8,128)(2,1)} collective-permute-done((bf16[160,2048]{1,0:T(8,128)(2,1)}, bf16[160,2048]{1,0:T(8,128)(2,1)}, u32[]{:S(2)}, u32[]{:S(2)}) %collective-permute-start.27) | collective-permute-done | bytes 655392 | tf_op jit(solution)/shard_map/ppermute | solution.py:1024
  348.1 4.0 input_grad.1
  352.1 7.0 %all-to-all-start.4 = ((bf16[16,24,128]{2,1,0:T(8,128)(2,1)}), bf16[16,24,128]{2,1,0:T(8,128)(2,1)S(1)}, u32[]{:S(2)}, u32[]{:S(2)}) async-start(bf16[16,24,128]{2,1,0:T(8,128)(2,1)} %get-tuple-element.230), calls=%async_computation.4 | async-start | bytes 196608 | tf_op jit(solution)/shard_map/all_to_all | solution.py:1171
  359.1 2.4 add_parts.1
  364.3 1.7 collective-permute-start.33
  366.6 2.5 fold_small.1
  369.1 9.0 %all-to-all-start.5 = ((bf16[128,24,128]{2,1,0:T(8,128)(2,1)}), bf16[128,24,128]{2,1,0:T(8,128)(2,1)S(1)}, u32[]{:S(2)}, u32[]{:S(2)}) async-start(bf16[128,24,128]{2,1,0:T(8,128)(2,1)} %fold_small.1), calls=%async_computation.5 | async-start | bytes 1572864 | tf_op jit(solution)/shard_map/all_to_all | solution.py:1028
  378.7 1.8 add_last.1.a
  380.5 1.5 collective-permute-start.36
  382.0 2.9 collective-permute-start.35
  385.9 10.3 %collective-permute-done.36.d = bf16[512,128]{1,0:T(8,128)(2,1)S(1)} collective-permute-done((bf16[512,128]{1,0:T(8,128)(2,1)}, bf16[512,128]{1,0:T(8,128)(2,1)S(1)}, u32[]{:S(2)}, u32[]{:S(2)}) %collective-permute-start.36) | collective-permute-done | bytes 131104 | tf_op jit(solution)/shard_map/ppermute | solution.py:1039
  396.2 6.2 %collective-permute-done.35.c = bf16[512,128]{1,0:T(8,128)(2,1)} collective-permute-done((bf16[512,128]{1,0:T(8,128)(2,1)}, bf16[512,128]{1,0:T(8,128)(2,1)}, u32[]{:S(2)}, u32[]{:S(2)}) %collective-permute-start.35) | collective-permute-done | bytes 131104 | tf_op jit(solution)/shard_map/ppermute | solution.py:1039
  402.3 1.9 stack_parts.1.c0
  405.6 2.3 collective-permute-start.38
  407.9 1.5 collective-permute-start.37
  409.4 9.2 %collective-permute-done.39.c3 = bf16[4,512,128]{2,1,0:T(8,128)(2,1)} collective-permute-done((bf16[4,512,128]{2,1,0:T(8,128)(2,1)}, bf16[4,512,128]{2,1,0:T(8,128)(2,1)}, u32[]{:S(2)}, u32[]{:S(2)}) %collective-permute-start.39) | collective-permute-done | bytes 524320 | tf_op jit(solution)/shard_map/ppermute | solution.py:1039
  418.6 12.4 %collective-permute-done.38.c2 = bf16[4,512,128]{2,1,0:T(8,128)(2,1)} collective-permute-done((bf16[4,512,128]{2,1,0:T(8,128)(2,1)}, bf16[4,512,128]{2,1,0:T(8,128)(2,1)}, u32[]{:S(2)}, u32[]{:S(2)}) %collective-permute-start.38) | collective-permute-done | bytes 524320 | tf_op jit(solution)/shard_map/ppermute | solution.py:1039
  431.0 4.1 place_output_grads.1
  435.1 4.5 result.1
  442.1 4.6 %widen_grads.1 = (f32[2048,512]{1,0:T(8,128)}, f32[64,2048]{1,0:T(8,128)}, f32[64,2048]{1,0:T(8,128)}) custom-call(bf16[2048,640]{1,0:T(8,128)(2,1)} %all-reduce.2.cloned.1.call-done.grads), custom_call_target="tpu_custom_call" | custom-call | flops 1 | bytes 1 | tf_op jit(solution)/shard_map/widen_grads/pallas_call | solution.py:74
  (147 shorter events, 42.5 us)
Async XLA Ops:
  7.2 8.5 %copy-start = (s32[1,1024]{1,0:T(1,128)S(1)}, s32[1,1024]{1,0:T(1,128)}, u32[]{:S(2)}) copy-start(s32[1,1024]{1,0:T(1,128)} %param.32) | copy-start | bytes 12292
  7.2 18.5 %copy-start.25 = (bf16[2048]{0:T(1024)(128)(2,1)S(1)}, bf16[2048]{0:T(1024)(128)(2,1)}, u32[]{:S(2)}) copy-start(bf16[2048]{0:T(1024)(128)(2,1)} %param.19) | copy-start | bytes 12292
  7.2 24.8 %collective-permute-start.3 = (bf16[128,2048]{1,0:T(8,128)(2,1)}, bf16[128,2048]{1,0:T(8,128)(2,1)}, u32[]{:S(2)}, u32[]{:S(2)}) collective-permute-start(bf16[128,2048]{1,0:T(8,128)(2,1)} %x0.3), channel_id=1, source_target_pairs={{0,1},{1,0},{2,3},{3,2},{4,5},{5,4},{6,7},{7,6},{8,9},{9,8},{10,11... | collective-permute-start | bytes 1572872 | tf_op jit(solution)/shard_map/ppermute | solution.py:1016
  8.7 29.0 %collective-permute-start.2 = (bf16[128,2048]{1,0:T(8,128)(2,1)}, bf16[128,2048]{1,0:T(8,128)(2,1)}, u32[]{:S(2)}, u32[]{:S(2)}) collective-permute-start(bf16[128,2048]{1,0:T(8,128)(2,1)} %x0.3), channel_id=1, source_target_pairs={{0,2},{1,3},{2,4},{3,5},{4,6},{5,7},{6,0},{7,1},{8,10},{9,11},{10,... | collective-permute-start | bytes 1572872 | tf_op jit(solution)/shard_map/ppermute | solution.py:1020
  10.1 27.6 %collective-permute-start.1 = (bf16[128,2048]{1,0:T(8,128)(2,1)}, bf16[128,2048]{1,0:T(8,128)(2,1)}, u32[]{:S(2)}, u32[]{:S(2)}) collective-permute-start(bf16[128,2048]{1,0:T(8,128)(2,1)} %x0.3), channel_id=1, source_target_pairs={{0,4},{1,5},{2,6},{3,7},{4,0},{5,1},{6,2},{7,3},{8,12},{9,13},{10,... | collective-permute-start | bytes 1572872 | tf_op jit(solution)/shard_map/ppermute | solution.py:1020
  12.7 25.0 %collective-permute-start = (bf16[128,2048]{1,0:T(8,128)(2,1)}, bf16[128,2048]{1,0:T(8,128)(2,1)}, u32[]{:S(2)}, u32[]{:S(2)}) collective-permute-start(bf16[128,2048]{1,0:T(8,128)(2,1)} %x0.3), channel_id=1, source_target_pairs={{0,6},{1,7},{2,0},{3,1},{4,2},{5,3},{6,4},{7,5},{8,14},{9,15},{10,... | collective-permute-start | bytes 1572872 | tf_op jit(solution)/shard_map/ppermute | solution.py:1020
  13.8 4.4 collective-permute-start.4
  18.2 12.0 %copy-start.4 = (bf16[64,2048]{1,0:T(8,128)(2,1)}, bf16[64,2048]{1,0:T(8,128)(2,1)S(1)}, u32[]{:S(2)}) copy-start(bf16[64,2048]{1,0:T(8,128)(2,1)S(1)} %collective-permute-done.4.refs_6_.refs_10_) | copy-start | bytes 786436
  18.2 13.8 %collective-permute-start.5 = (bf16[64,2048]{1,0:T(8,128)(2,1)}, bf16[64,2048]{1,0:T(8,128)(2,1)S(1)}, u32[]{:S(2)}, u32[]{:S(2)}) collective-permute-start(bf16[64,2048]{1,0:T(8,128)(2,1)} %bitcast.78), channel_id=1, source_target_pairs={{0,1},{1,0},{2,3},{3,2},{4,5},{5,4},{6,7},{7,6},{8,9},{9,8},{10,11... | collective-permute-start | bytes 786440 | tf_op jit(solution)/shard_map/ppermute | solution.py:1016
  37.7 72.7 %all-to-all-start.1 = ((bf16[128,88,128]{2,1,0:T(8,128)(2,1)}), bf16[128,88,128]{2,1,0:T(8,128)(2,1)}, u32[]{:S(2)}, u32[]{:S(2)}) async-start(bf16[128,88,128]{2,1,0:T(8,128)(2,1)} %pack_rows.1), calls=%async_computation.1 | async-start | bytes 5767168 | tf_op jit(solution)/shard_map/all_to_all | solution.py:1028
  46.9 24.6 %collective-permute-start.10 = (bf16[512,2048]{1,0:T(8,128)(2,1)}, bf16[512,2048]{1,0:T(8,128)(2,1)}, u32[]{:S(2)}, u32[]{:S(2)}) collective-permute-start(bf16[512,2048]{1,0:T(8,128)(2,1)} %refs_10_.1), channel_id=1, source_target_pairs={{0,1},{1,0},{2,3},{3,2},{4,5},{5,4},{6,7},{7,6},{8,9},{9,8},{10,11... | collective-permute-start | bytes 6291464 | tf_op jit(solution)/shard_map/ppermute | solution.py:1016
  48.1 5.4 %collective-permute-start.6 = (bf16[128,2048]{1,0:T(8,128)(2,1)}, bf16[128,2048]{1,0:T(8,128)(2,1)S(1)}, u32[]{:S(2)}, u32[]{:S(2)}) collective-permute-start(bf16[128,2048]{1,0:T(8,128)(2,1)} %collective-permute-done.refs_1_), channel_id=1, source_target_pairs={{0,1},{1,0},{2,3},{3,2},{4,5},{5,4},{6,7},{7,6},{8,9},{9,8},{10,11... | collective-permute-start | bytes 1572872 | tf_op jit(solution)/shard_map/ppermute | solution.py:1016
  48.2 5.5 %collective-permute-start.7 = (bf16[128,2048]{1,0:T(8,128)(2,1)}, bf16[128,2048]{1,0:T(8,128)(2,1)}, u32[]{:S(2)}, u32[]{:S(2)}) collective-permute-start(bf16[128,2048]{1,0:T(8,128)(2,1)} %collective-permute-done.1.refs_3_), channel_id=1, source_target_pairs={{0,1},{1,0},{2,3},{3,2},{4,5},{5,4},{6,7},{7,6},{8,9},{9,8},{10,11... | collective-permute-start | bytes 1572872 | tf_op jit(solution)/shard_map/ppermute | solution.py:1016
  48.7 5.9 %collective-permute-start.8 = (bf16[128,2048]{1,0:T(8,128)(2,1)}, bf16[128,2048]{1,0:T(8,128)(2,1)}, u32[]{:S(2)}, u32[]{:S(2)}) collective-permute-start(bf16[128,2048]{1,0:T(8,128)(2,1)} %collective-permute-done.2.refs_5_), channel_id=1, source_target_pairs={{0,1},{1,0},{2,3},{3,2},{4,5},{5,4},{6,7},{7,6},{8,9},{9,8},{10,11... | collective-permute-start | bytes 1572872 | tf_op jit(solution)/shard_map/ppermute | solution.py:1016
  69.4 2.1 collective-permute-start.9
  72.3 10.2 %copy-start.26 = (bf16[2048]{0:T(1024)(128)(2,1)S(1)}, bf16[2048]{0:T(1024)(128)(2,1)}, u32[]{:S(2)}) copy-start(bf16[2048]{0:T(1024)(128)(2,1)} %param.26) | copy-start | bytes 12292
  78.5 16.0 %collective-permute-start.11 = (bf16[128,2048]{1,0:T(8,128)(2,1)}, bf16[128,2048]{1,0:T(8,128)(2,1)S(1)}, u32[]{:S(2)}, u32[]{:S(2)}) collective-permute-start(bf16[128,2048]{1,0:T(8,128)(2,1)} %get-tuple-element.153), channel_id=1, source_target_pairs={{0,2},{1,3},{2,4},{3,5},{4,6},{5,7},{6,0},{7,1},{8,10},{9,11},{10,... | collective-permute-start | bytes 1572872 | tf_op jit(solution)/shard_map/ppermute | solution.py:1024
  79.1 15.4 %collective-permute-start.12 = (bf16[128,2048]{1,0:T(8,128)(2,1)}, bf16[128,2048]{1,0:T(8,128)(2,1)}, u32[]{:S(2)}, u32[]{:S(2)}) collective-permute-start(bf16[128,2048]{1,0:T(8,128)(2,1)} %get-tuple-element.154), channel_id=1, source_target_pairs={{0,6},{1,7},{2,0},{3,1},{4,2},{5,3},{6,4},{7,5},{8,14},{9,15},{10,... | collective-permute-start | bytes 1572872 | tf_op jit(solution)/shard_map/ppermute | solution.py:1024
  81.2 23.7 %collective-permute-start.13 = (bf16[128,2048]{1,0:T(8,128)(2,1)}, bf16[128,2048]{1,0:T(8,128)(2,1)}, u32[]{:S(2)}, u32[]{:S(2)}) collective-permute-start(bf16[128,2048]{1,0:T(8,128)(2,1)} %get-tuple-element.155), channel_id=1, source_target_pairs={{0,4},{1,5},{2,6},{3,7},{4,0},{5,1},{6,2},{7,3},{8,12},{9,13},{10,... | collective-permute-start | bytes 1572872 | tf_op jit(solution)/shard_map/ppermute | solution.py:1024
  94.5 10.3 %copy-start.13 = (bf16[128,2048]{1,0:T(8,128)(2,1)}, bf16[128,2048]{1,0:T(8,128)(2,1)S(1)}, u32[]{:S(2)}) copy-start(bf16[128,2048]{1,0:T(8,128)(2,1)S(1)} %collective-permute-done.11.b1) | copy-start | bytes 1572868
  110.5 48.4 %all-to-all-start = ((bf16[128,88,128]{2,1,0:T(8,128)(2,1)}), bf16[128,88,128]{2,1,0:T(8,128)(2,1)}, u32[]{:S(2)}, u32[]{:S(2)}) async-start(bf16[128,88,128]{2,1,0:T(8,128)(2,1)} %get-tuple-element.157), calls=%async_computation | async-start | bytes 5767168 | tf_op jit(solution)/shard_map/all_to_all | solution.py:1028
  120.1 14.8 %collective-permute-start.14 = (bf16[512,2048]{1,0:T(8,128)(2,1)}, bf16[512,2048]{1,0:T(8,128)(2,1)}, u32[]{:S(2)}, u32[]{:S(2)}) collective-permute-start(bf16[512,2048]{1,0:T(8,128)(2,1)} %bitcast.5.refs_4_.refs_8_.wa), channel_id=1, source_target_pairs={{0,1},{1,0},{2,3},{3,2},{4,5},{5,4},{6,7},{7,6},{8,9},{9,8},{10,11... | collective-permute-start | bytes 6291464 | tf_op jit(solution)/shard_map/ppermute | solution.py:1016
  121.4 5.5 %copy-start.21 = (f32[128,128]{1,0:T(8,128)S(1)}, f32[128,128]{1,0:T(8,128)}, u32[]{:S(2)}) copy-start(f32[128,128]{1,0:T(8,128)} %get-tuple-element.169.gates) | copy-start | bytes 196612
  174.8 5.9 %copy-start.3 = (s32[128,128]{1,0:T(8,128)S(1)}, s32[128,128]{1,0:T(8,128)}, u32[]{:S(2)}) copy-start(s32[128,128]{1,0:T(8,128)} %get-tuple-element.156.ids) | copy-start | bytes 196612
  174.8 44.6 %all-to-all-start.2 = ((bf16[128,88,128]{2,1,0:T(8,128)(2,1)}), bf16[128,88,128]{2,1,0:T(8,128)(2,1)}, u32[]{:S(2)}, u32[]{:S(2)}) async-start(bf16[128,88,128]{2,1,0:T(8,128)(2,1)} %get-tuple-element.190), calls=%async_computation.2 | async-start | bytes 5767168 | tf_op jit(solution)/shard_map/all_to_all | solution.py:1028
  189.3 7.5 %copy-start.27 = (bf16[640,2048]{1,0:T(8,128)(2,1)S(1)}, bf16[640,2048]{1,0:T(8,128)(2,1)}, u32[]{:S(2)}) copy-start(bf16[640,2048]{1,0:T(8,128)(2,1)} %get-tuple-element.197) | copy-start | bytes 7864324
  189.3 7.5 %copy-start.28 = (bf16[640,768]{1,0:T(8,128)(2,1)S(1)}, bf16[640,768]{1,0:T(8,128)(2,1)}, u32[]{:S(2)}) copy-start(bf16[640,768]{1,0:T(8,128)(2,1)} %get-tuple-element.199) | copy-start | bytes 2949124
  196.8 4.6 %copy-start.2 = (bf16[640,2048]{1,0:T(8,128)(2,1)S(1)}, bf16[640,2048]{1,0:T(8,128)(2,1)}, u32[]{:S(2)}) copy-start(bf16[640,2048]{1,0:T(8,128)(2,1)} %get-tuple-element.201) | copy-start | bytes 7864324
  196.8 4.6 %copy-start.6 = (bf16[640,768]{1,0:T(8,128)(2,1)S(1)}, bf16[640,768]{1,0:T(8,128)(2,1)}, u32[]{:S(2)}) copy-start(bf16[640,768]{1,0:T(8,128)(2,1)} %get-tuple-element.200) | copy-start | bytes 2949124
  226.5 25.2 %collective-permute-start.17 = (bf16[128,2048]{1,0:T(8,128)(2,1)}, bf16[128,2048]{1,0:T(8,128)(2,1)S(1)}, u32[]{:S(2)}, u32[]{:S(2)}) collective-permute-start(bf16[128,2048]{1,0:T(8,128)(2,1)} %get-tuple-element.206.refs_0_), channel_id=1, source_target_pairs={{0,2},{1,3},{2,4},{3,5},{4,6},{5,7},{6,0},{7,1},{8,10},{9,11},{10,... | collective-permute-start | bytes 1572872 | tf_op jit(solution)/shard_map/ppermute | solution.py:1020
  226.5 27.0 %collective-permute-start.16 = (bf16[128,2048]{1,0:T(8,128)(2,1)}, bf16[128,2048]{1,0:T(8,128)(2,1)S(1)}, u32[]{:S(2)}, u32[]{:S(2)}) collective-permute-start(bf16[128,2048]{1,0:T(8,128)(2,1)} %get-tuple-element.206.refs_0_), channel_id=1, source_target_pairs={{0,4},{1,5},{2,6},{3,7},{4,0},{5,1},{6,2},{7,3},{8,12},{9,13},{10,... | collective-permute-start | bytes 1572872 | tf_op jit(solution)/shard_map/ppermute | solution.py:1020
  227.4 26.2 %collective-permute-start.15 = (bf16[128,2048]{1,0:T(8,128)(2,1)}, bf16[128,2048]{1,0:T(8,128)(2,1)S(1)}, u32[]{:S(2)}, u32[]{:S(2)}) collective-permute-start(bf16[128,2048]{1,0:T(8,128)(2,1)} %get-tuple-element.206.refs_0_), channel_id=1, source_target_pairs={{0,6},{1,7},{2,0},{3,1},{4,2},{5,3},{6,4},{7,5},{8,14},{9,15},{10,... | collective-permute-start | bytes 1572872 | tf_op jit(solution)/shard_map/ppermute | solution.py:1020
  229.2 24.9 %collective-permute-start.18 = (bf16[128,2048]{1,0:T(8,128)(2,1)}, bf16[128,2048]{1,0:T(8,128)(2,1)S(1)}, u32[]{:S(2)}, u32[]{:S(2)}) collective-permute-start(bf16[128,2048]{1,0:T(8,128)(2,1)} %get-tuple-element.206.refs_0_), channel_id=1, source_target_pairs={{0,1},{1,0},{2,3},{3,2},{4,5},{5,4},{6,7},{7,6},{8,9},{9,8},{10,11... | collective-permute-start | bytes 1572872 | tf_op jit(solution)/shard_map/ppermute | solution.py:1016
  251.7 5.6 %copy-start.14 = (bf16[128,2048]{1,0:T(8,128)(2,1)}, bf16[128,2048]{1,0:T(8,128)(2,1)S(1)}, u32[]{:S(2)}) copy-start(bf16[128,2048]{1,0:T(8,128)(2,1)S(1)} %collective-permute-done.17.refs_3_) | copy-start | bytes 1572868
  251.7 3.3 collective-permute-start.21
  253.5 3.0 collective-permute-start.20
  253.6 2.9 copy-start.16
  253.6 3.8 collective-permute-start.19
  254.1 2.4 copy-start.17
  257.4 47.6 %all-to-all-start.3 = ((bf16[128,80,128]{2,1,0:T(8,128)(2,1)}), bf16[128,80,128]{2,1,0:T(8,128)(2,1)}, u32[]{:S(2)}, u32[]{:S(2)}) async-start(bf16[128,80,128]{2,1,0:T(8,128)(2,1)} %expert_out.1), calls=%async_computation.3 | async-start | bytes 5242880 | tf_op jit(solution)/shard_map/all_to_all | solution.py:1028
  262.2 177.4 %all-reduce.2.cloned.1.call-start = ((), (), s32[]{:S(2)}) async-start(), calls=%async_computation.6 | async-start | bytes 5242880 | tf_op jit(solution)/shard_map/psum | solution.py:1167
  291.1 3.1 collective-permute-start.22
  304.5 2.3 collective-permute-start.23
  304.9 1.9 collective-permute-start.24
  315.9 17.5 %collective-permute-start.25 = (bf16[160,2048]{1,0:T(8,128)(2,1)}, bf16[160,2048]{1,0:T(8,128)(2,1)S(1)}, u32[]{:S(2)}, u32[]{:S(2)}) collective-permute-start(bf16[160,2048]{1,0:T(8,128)(2,1)} %get-tuple-element.226), channel_id=1, source_target_pairs={{0,2},{1,3},{2,4},{3,5},{4,6},{5,7},{6,0},{7,1},{8,10},{9,11},{10,... | collective-permute-start | bytes 1966088 | tf_op jit(solution)/shard_map/ppermute | solution.py:1024
  316.7 18.8 %collective-permute-start.26 = (bf16[160,2048]{1,0:T(8,128)(2,1)}, bf16[160,2048]{1,0:T(8,128)(2,1)}, u32[]{:S(2)}, u32[]{:S(2)}) collective-permute-start(bf16[160,2048]{1,0:T(8,128)(2,1)} %get-tuple-element.227), channel_id=1, source_target_pairs={{0,6},{1,7},{2,0},{3,1},{4,2},{5,3},{6,4},{7,5},{8,14},{9,15},{10,... | collective-permute-start | bytes 1966088 | tf_op jit(solution)/shard_map/ppermute | solution.py:1024
  318.6 29.4 %collective-permute-start.27 = (bf16[160,2048]{1,0:T(8,128)(2,1)}, bf16[160,2048]{1,0:T(8,128)(2,1)}, u32[]{:S(2)}, u32[]{:S(2)}) collective-permute-start(bf16[160,2048]{1,0:T(8,128)(2,1)} %get-tuple-element.228), channel_id=1, source_target_pairs={{0,4},{1,5},{2,6},{3,7},{4,0},{5,1},{6,2},{7,3},{8,12},{9,13},{10,... | collective-permute-start | bytes 1966088 | tf_op jit(solution)/shard_map/ppermute | solution.py:1024
  319.7 39.4 %collective-permute-start.28 = (bf16[4,512,128]{2,1,0:T(8,128)(2,1)}, bf16[4,512,128]{2,1,0:T(8,128)(2,1)}, u32[]{:S(2)}, u32[]{:S(2)}) collective-permute-start(bf16[4,512,128]{2,1,0:T(8,128)(2,1)} %get-tuple-element.233), channel_id=1, source_target_pairs={{0,8},{8,16},{16,24},{24,0},{32,40},{40,48},{48,56},{56,32},{64,72... | collective-permute-start | bytes 1572872 | tf_op jit(solution)/shard_map/ppermute | solution.py:1039
  320.9 38.2 %collective-permute-start.29 = (bf16[4,512,128]{2,1,0:T(8,128)(2,1)}, bf16[4,512,128]{2,1,0:T(8,128)(2,1)}, u32[]{:S(2)}, u32[]{:S(2)}) collective-permute-start(bf16[4,512,128]{2,1,0:T(8,128)(2,1)} %get-tuple-element.234), channel_id=1, source_target_pairs={{0,24},{8,0},{16,8},{24,16},{32,56},{40,32},{48,40},{56,48},{64,88... | collective-permute-start | bytes 1572872 | tf_op jit(solution)/shard_map/ppermute | solution.py:1039
  333.4 14.7 %copy-start.7 = (bf16[160,2048]{1,0:T(8,128)(2,1)}, bf16[160,2048]{1,0:T(8,128)(2,1)S(1)}, u32[]{:S(2)}) copy-start(bf16[160,2048]{1,0:T(8,128)(2,1)S(1)} %collective-permute-done.25.b1) | copy-start | bytes 1966084
  333.4 25.7 %collective-permute-start.30 = (bf16[4,512,128]{2,1,0:T(8,128)(2,1)}, bf16[4,512,128]{2,1,0:T(8,128)(2,1)}, u32[]{:S(2)}, u32[]{:S(2)}) collective-permute-start(bf16[4,512,128]{2,1,0:T(8,128)(2,1)} %get-tuple-element.235), channel_id=1, source_target_pairs={{0,16},{8,24},{16,0},{24,8},{32,48},{40,56},{48,32},{56,40},{64,80... | collective-permute-start | bytes 1572872 | tf_op jit(solution)/shard_map/ppermute | solution.py:1039
  352.1 13.8 %all-to-all-start.4 = ((bf16[16,24,128]{2,1,0:T(8,128)(2,1)}), bf16[16,24,128]{2,1,0:T(8,128)(2,1)S(1)}, u32[]{:S(2)}, u32[]{:S(2)}) async-start(bf16[16,24,128]{2,1,0:T(8,128)(2,1)} %get-tuple-element.230), calls=%async_computation.4 | async-start | bytes 196608 | tf_op jit(solution)/shard_map/all_to_all | solution.py:1171
  361.6 16.5 %collective-permute-start.31 = (bf16[512,128]{1,0:T(8,128)(2,1)}, bf16[512,128]{1,0:T(8,128)(2,1)S(1)}, u32[]{:S(2)}, u32[]{:S(2)}) collective-permute-start(bf16[512,128]{1,0:T(8,128)(2,1)} %get-tuple-element.237), channel_id=1, source_target_pairs={{0,32},{8,40},{16,48},{24,56},{32,64},{40,72},{48,80},{56,88},{64,... | collective-permute-start | bytes 393224 | tf_op jit(solution)/shard_map/ppermute | solution.py:1039
  362.9 15.1 %collective-permute-start.32 = (bf16[512,128]{1,0:T(8,128)(2,1)}, bf16[512,128]{1,0:T(8,128)(2,1)}, u32[]{:S(2)}, u32[]{:S(2)}) collective-permute-start(bf16[512,128]{1,0:T(8,128)(2,1)} %get-tuple-element.238), channel_id=1, source_target_pairs={{0,96},{8,104},{16,112},{24,120},{32,0},{40,8},{48,16},{56,24},{64... | collective-permute-start | bytes 393224 | tf_op jit(solution)/shard_map/ppermute | solution.py:1039
  364.3 13.8 %collective-permute-start.33 = (bf16[512,128]{1,0:T(8,128)(2,1)}, bf16[512,128]{1,0:T(8,128)(2,1)}, u32[]{:S(2)}, u32[]{:S(2)}) collective-permute-start(bf16[512,128]{1,0:T(8,128)(2,1)} %get-tuple-element.239), channel_id=1, source_target_pairs={{0,64},{8,72},{16,80},{24,88},{32,96},{40,104},{48,112},{56,120},{... | collective-permute-start | bytes 393224 | tf_op jit(solution)/shard_map/ppermute | solution.py:1039
  369.1 70.5 %all-to-all-start.5 = ((bf16[128,24,128]{2,1,0:T(8,128)(2,1)}), bf16[128,24,128]{2,1,0:T(8,128)(2,1)S(1)}, u32[]{:S(2)}, u32[]{:S(2)}) async-start(bf16[128,24,128]{2,1,0:T(8,128)(2,1)} %fold_small.1), calls=%async_computation.5 | async-start | bytes 1572864 | tf_op jit(solution)/shard_map/all_to_all | solution.py:1028
  380.5 15.6 %collective-permute-start.36 = (bf16[512,128]{1,0:T(8,128)(2,1)}, bf16[512,128]{1,0:T(8,128)(2,1)S(1)}, u32[]{:S(2)}, u32[]{:S(2)}) collective-permute-start(bf16[512,128]{1,0:T(8,128)(2,1)} %add_last.1.a), channel_id=1, source_target_pairs={{0,32},{8,40},{16,48},{24,56},{32,64},{40,72},{48,80},{56,88},{64,... | collective-permute-start | bytes 393224 | tf_op jit(solution)/shard_map/ppermute | solution.py:1039
  382.0 20.3 %collective-permute-start.35 = (bf16[512,128]{1,0:T(8,128)(2,1)}, bf16[512,128]{1,0:T(8,128)(2,1)}, u32[]{:S(2)}, u32[]{:S(2)}) collective-permute-start(bf16[512,128]{1,0:T(8,128)(2,1)} %add_last.1.a), channel_id=1, source_target_pairs={{0,64},{8,72},{16,80},{24,88},{32,96},{40,104},{48,112},{56,120},{... | collective-permute-start | bytes 393224 | tf_op jit(solution)/shard_map/ppermute | solution.py:1039
  385.0 17.4 %collective-permute-start.34 = (bf16[512,128]{1,0:T(8,128)(2,1)}, bf16[512,128]{1,0:T(8,128)(2,1)}, u32[]{:S(2)}, u32[]{:S(2)}) collective-permute-start(bf16[512,128]{1,0:T(8,128)(2,1)} %add_last.1.a), channel_id=1, source_target_pairs={{0,96},{8,104},{16,112},{24,120},{32,0},{40,8},{48,16},{56,24},{64... | collective-permute-start | bytes 393224 | tf_op jit(solution)/shard_map/ppermute | solution.py:1039
  396.2 6.2 %copy-start.24 = (bf16[512,128]{1,0:T(8,128)(2,1)}, bf16[512,128]{1,0:T(8,128)(2,1)S(1)}, u32[]{:S(2)}) copy-start(bf16[512,128]{1,0:T(8,128)(2,1)S(1)} %collective-permute-done.36.d) | copy-start | bytes 393220
  404.3 14.3 %collective-permute-start.39 = (bf16[4,512,128]{2,1,0:T(8,128)(2,1)}, bf16[4,512,128]{2,1,0:T(8,128)(2,1)}, u32[]{:S(2)}, u32[]{:S(2)}) collective-permute-start(bf16[4,512,128]{2,1,0:T(8,128)(2,1)} %stack_parts.1.c0), channel_id=1, source_target_pairs={{0,8},{8,16},{16,24},{24,0},{32,40},{40,48},{48,56},{56,32},{64,72... | collective-permute-start | bytes 1572872 | tf_op jit(solution)/shard_map/ppermute | solution.py:1039
  405.6 25.4 %collective-permute-start.38 = (bf16[4,512,128]{2,1,0:T(8,128)(2,1)}, bf16[4,512,128]{2,1,0:T(8,128)(2,1)}, u32[]{:S(2)}, u32[]{:S(2)}) collective-permute-start(bf16[4,512,128]{2,1,0:T(8,128)(2,1)} %stack_parts.1.c0), channel_id=1, source_target_pairs={{0,16},{8,24},{16,0},{24,8},{32,48},{40,56},{48,32},{56,40},{64,80... | collective-permute-start | bytes 1572872 | tf_op jit(solution)/shard_map/ppermute | solution.py:1039
  407.9 23.1 %collective-permute-start.37 = (bf16[4,512,128]{2,1,0:T(8,128)(2,1)}, bf16[4,512,128]{2,1,0:T(8,128)(2,1)}, u32[]{:S(2)}, u32[]{:S(2)}) collective-permute-start(bf16[4,512,128]{2,1,0:T(8,128)(2,1)} %stack_parts.1.c0), channel_id=1, source_target_pairs={{0,24},{8,0},{16,8},{24,16},{32,56},{40,32},{48,40},{56,48},{64,88... | collective-permute-start | bytes 1572872 | tf_op jit(solution)/shard_map/ppermute | solution.py:1039
  439.8 6.9 %copy-start.1 = (s32[1,1024]{1,0:T(1,128)S(1)}, s32[1,1024]{1,0:T(1,128)}, u32[]{:S(2)}) copy-start(s32[1,1024]{1,0:T(1,128)} %param.32) | copy-start | bytes 12292
  (13 other events, 12.5 us)
Sparse Core Ops, SparseCore 0:
  303.6 104.7 all-reduce.1

commit v8 on v7

--- a/solution.py
+++ b/solution.py
@@ -89,6 +89,40 @@
     )(*args)
 
 
+def copy_call(kernel, name, outs, scratch, copies, args, smem=()):
+    return pl.pallas_call(
+        kernel,
+        out_shape=outs,
+        in_specs=[
+            pl.BlockSpec(memory_space=pltpu.SMEM if i in smem else pl.ANY)
+            for i in range(len(args))
+        ],
+        out_specs=[pl.BlockSpec(memory_space=pl.ANY)] * len(outs),
+        scratch_shapes=[*scratch, pltpu.SemaphoreType.DMA((copies,))],
+        compiler_params=pltpu.CompilerParams(vmem_limit_bytes=63 * 1024 * 1024),
+        cost_estimate=cost(COSTS.get(name, 0)),
+        name=name,
+    )(*args)
+
+
+class Copies:
+    def __init__(self, sems):
+        self.sems, self.count, self.leaving = sems, 0, []
+
+    def bring(self, source, dest):
+        item = pltpu.make_async_copy(source, dest, self.sems.at[self.count])
+        self.count += 1
+        item.start()
+        return item
+
+    def take(self, source, dest):
+        self.leaving.append(self.bring(source, dest))
+
+    def finish(self):
+        for item in self.leaving:
+            item.wait()
+
+
 def whole(shape):
     return pl.BlockSpec(shape, lambda i, *_: (0,) * len(shape))
 
@@ -337,9 +371,9 @@
     return grid_call(
         outproj_body,
         "out_projection",
-        (4,),
-        [whole((512, HALF)), whole((512, HALF)), cols_of((512, 512)), cols_of((512, 512))],
-        [cols_of((T, 512))] * 4,
+        (2,),
+        [whole((512, HALF)), whole((512, HALF)), cols_of((512, 1024)), cols_of((512, 1024))],
+        [cols_of((T, 1024))] * 4,
         [sds((T, D), bf16)] * 4,
         [pltpu.VMEM((HALF, 1024), bf16)],
         (ot0, otr, wa, wb),
@@ -657,47 +691,55 @@
 
 
 def pre_body(where, *refs):
-    blocks, (ot0, ot1, wo, w0, w1, w2, w3, dt, rows_all, total) = refs[:8], refs[8:]
-    step = pl.program_id(0)
-    for b in range(8):
-        rows_all[b * T : (b + 1) * T, :] = blocks[b][...]
-    grad = (dot(ot0[...], rows_all[:HALF, :]) + dot(ot1[...], rows_all[HALF:, :])).astype(bf16)
-    for dx, out in enumerate((w0, w1, w2, w3)):
-
-        @pl.when(step == dx)
-        def _():
-            for col in range(4):
-                out[lax.rem(col + 4 - where[0], 4)] = grad[:, col * 128 : (col + 1) * 128]
-
-    part = dot_t(wo[...], rows_all[...])
-
-    @pl.when(step == 0)
-    def _():
-        total[...] = part
-
-    @pl.when(step > 0)
-    def _():
-        total[...] += part
-
-    @pl.when(step == 3)
-    def _():
-        dt[...] = total[...].astype(bf16)
+    blocks, (ot0, ot1, wo, *outs) = refs[:8], refs[8:16]
+    dt, (heads, rows_all, wo_v, grads, dt_v, sems) = refs[15], refs[16:]
+    copies = Copies(sems)
+    arrivals = [copies.bring(ot0, heads.at[:, :HALF]), copies.bring(ot1, heads.at[:, HALF:])]
+    columns = []
+    waits = []
+    for step in range(4):
+        start = lax.rem(where[1] + step, 4) * 512
+        columns.append(pl.ds(pl.multiple_of(start, 512), 512))
+        waits.append(
+            [
+                copies.bring(
+                    blocks[b].at[:, columns[step]],
+                    rows_all.at[b * T : (b + 1) * T, columns[step]],
+                )
+                for b in range(8)
+            ]
+        )
+    last = copies.bring(wo, wo_v)
+    for item in arrivals:
+        item.wait()
+    for step in range(4):
+        for item in waits[step]:
+            item.wait()
+        grad = dot(heads[...], rows_all[:, columns[step]]).astype(bf16)
+        for col in range(4):
+            grads[step, lax.rem(col + 4 - where[0], 4)] = grad[:, col * 128 : (col + 1) * 128]
+        copies.take(grads.at[step], outs[step])
+    last.wait()
+    dt_v[...] = dot_t(wo_v[...], rows_all[...]).astype(bf16)
+    copies.take(dt_v, dt)
+    copies.finish()
 
 
 def pre(where, blocks, ot0, ot1, wo):
-    def turned(shape):
-        return pl.BlockSpec(shape, lambda i, w: (0, lax.rem(i + w[1], 4)))
-
-    return grid_call(
+    return copy_call(
         pre_body,
         "out_projection_grad",
-        (4,),
-        [turned((T, 512))] * 8 + [whole((512, HALF))] * 2 + [turned((512, 512))],
-        [whole((4, 512, 128))] * 4 + [whole((512, ROWS))],
         [sds((4, 512, 128), bf16)] * 4 + [sds((LH * HEAD, ROWS), bf16)],
-        [pltpu.VMEM((ROWS, 512), bf16), pltpu.VMEM((512, ROWS), f32)],
+        [
+            pltpu.VMEM((512, ROWS), bf16),
+            pltpu.VMEM((ROWS, D), bf16),
+            pltpu.VMEM((512, D), bf16),
+            pltpu.VMEM((4, 4, 512, 128), bf16),
+            pltpu.VMEM((512, ROWS), bf16),
+        ],
+        2 + 32 + 1 + 5,
         (where, *blocks, ot0, ot1, wo),
-        scalars=1,
+        smem=(0,),
     )
 
 
@@ -807,15 +849,15 @@
     return grid_call(
         qkv_grad_body,
         "qkv_weight_grad",
-        (4,),
+        (2,),
         [
-            rows_of((512, ROWS)),
+            rows_of((1024, ROWS)),
             whole((512, HALF)),
             whole((512, HALF)),
             whole((2 * HEAD, ROWS)),
             whole((2 * HEAD, ROWS)),
         ],
-        [rows_of((512, 640)), whole((2 * HEAD, ROWS))],
+        [rows_of((1024, 640)), whole((2 * HEAD, ROWS))],
         [sds((D, 640), bf16), sds((2 * HEAD, ROWS), bf16)],
         [pltpu.VMEM((640, ROWS), bf16)],
         (where, n1t, dq0, dq1, own, sib),
@@ -1147,17 +1189,16 @@
     )
     g_own = [gatt] + [from_chip(gatt, dy) for dy in (1, 2, 3)]
     g_sib = [sibling(block) for block in g_own]
-    returned = exchange(after(out_wire, *g_sib))
     *out_parts, dt = pre(where, g_own + g_sib, ot0, ot1, w_out)
 
     dq0, dq1, dkv, ggq, ggk = bwd(
         qh, kh, scales, qt, kt, kn, vn, dt, ot0, ot1, linv, info, cos, sin, gq, gk
     )
+    out_parts, dq1, dkv = lax.optimization_barrier((collect(out_parts, 1), dq1, dkv))
     router_sib = after(router_sib, dkv)
     dq_sib, dkv_sib = sibling(dq1), sibling(dkv)
     gw, dkv_total = qkv_grad(where, n1_t, dq0, dq1, dkv, dkv_sib)
-    returned, dq0 = lax.optimization_barrier((returned, dq0))
-    result = result_rows(expert_list, slot_list, gate_list, returned, hidden)
+    returned = exchange(after(out_wire, dkv_total))
     router_rec = sibling(router_sib)
     blocks = normed_grad(
         wq_t, wq_ts, wkv, dq0, dq_sib, dkv_total, n1, gg2, ggq, ggk, router_own, router_rec
@@ -1165,12 +1206,17 @@
     blocks = [blocks[0]] + spread(blocks)
 
     gw = lax.psum(gw, "expert")
-    out_parts = collect(add_parts(collect(out_parts, 1)), 0)
-    chunks = stack(share(add_last(out_parts)[0], 0))
+    out_parts = collect(add_parts(out_parts), 0)
+    chunks = share(add_last(out_parts)[0], 0)
+    chunks, blocks = lax.optimization_barrier((chunks, blocks))
+    chunks = share(stack(chunks), 1)
     grad_input, small = final(blocks, block_input, ghid, g1)
+    small, returned = lax.optimization_barrier((small, returned))
+    result = result_rows(expert_list, slot_list, gate_list, returned, hidden)
     small = lax.all_to_all(small, "expert", split_axis=0, concat_axis=0, tiled=True)
+    small, chunks = lax.optimization_barrier((small, chunks))
     small = exchange(fold(small))
-    grad_wout = place_out(where, share(chunks, 1))
+    grad_wout = place_out(where, chunks)
     gw, small, grad_input, grad_wout, result = lax.optimization_barrier(
         (gw, small, grad_input, grad_wout, result)
     )

time: 461 us -> 464 us (level)
  waiting for transfers between devices: 154 us -> 166 us
    ppermute x6, waiting for transfers between devices: 45.3 us -> 22.6 us  [to_chip(): return lax.ppermute(x, 'shard', [(i, (i + 2 * dy) % 8) for i in range(8)])]
    ppermute x12, waiting for transfers between devices: 38.1 us -> 55 us  [on_expert(): return lax.ppermute(x, 'expert', pairs)]
    psum x1, waiting for transfers between devices: 0.01 us -> 14.8 us  [on_device(): gw = lax.psum(gw, 'expert')]
    pallas_call x5 -> x4, Pallas kernels: 39.2 us -> 26.2 us  [grid_call(): pl.pallas_call(kernel, out_shape=outs, grid_spec=pltpu.PrefetchScalarGrid...]
    pallas_call x0 -> x1, Pallas kernels: none -> 8.78 us  [copy_call(): pl.pallas_call(kernel, out_shape=outs, in_specs=[pl.BlockSpec(memory_spac...]
    unnamed x61 -> x69, local copies, waits for them, and re-layouts: 10.3 us -> 9.62 us
  transfers between devices with their start and end apart: 47 -> 47, of which waited for: 19 -> 24; matrix products, arithmetic and copies ran while one was open for 7% -> 7% of each run, Pallas kernels for 27% -> 23%
where the time goes in v8:
time: 464 us; the launch traced here: 457 us
  waiting for transfers between devices  166 us (36%)
  Pallas kernels  147 us (32%)
  starting transfers between devices  88.9 us (19%)
  matrix products  16.6 us (4%)
  local copies, waits for them, and re-layouts  15.4 us (3%)
  between operations  14.6 us (3%)
  other arithmetic  8.03 us (2%)
    pallas_call x18, Pallas kernels, call(): pl.pallas_call(kernel, out_shape=outs, in_specs=in_specs, out_specs=[pl.B...  96.6 us
    ppermute x12, waiting for transfers between devices, on_expert(): return lax.ppermute(x, 'expert', pairs)  55 us
    all_to_all x5, starting transfers between devices, exchange(): return lax.all_to_all(x, ALL, split_axis=0, concat_axis=0, tiled=True)  40.8 us
    all_to_all x5, waiting for transfers between devices, exchange(): return lax.all_to_all(x, ALL, split_axis=0, concat_axis=0, tiled=True)  38 us
    pallas_call x4, Pallas kernels, grid_call(): pl.pallas_call(kernel, out_shape=outs, grid_spec=pltpu.PrefetchScalarGrid...  26.2 us
    ppermute x6, waiting for transfers between devices, to_chip(): return lax.ppermute(x, 'shard', [(i, (i + 2 * dy) % 8) for i in range(8)])  22.6 us
    ppermute x6, waiting for transfers between devices, from_chip(): return lax.ppermute(x, 'shard', [(i, (i - 2 * dy) % 8) for i in range(8)])  21.1 us
    dot_general x3, matrix products, weight_grad(): lax.dot_general(a, b, (((0,), (0,)), ((), ())), preferred_element_type=f32)  16.6 us
  transfers between devices with their start and end apart: 47, of which 24 were waited for; matrix products, arithmetic and copies ran while one was open for 7% of the time, Pallas kernels for 23%

profile of v8, /device:TPU:1, one launch (start us, length us, event | category | flops | bytes accessed | tf_op | source)
XLA Modules:
  0.0 456.7 jit_solution(4031480349215373445)
XLA Ops:
  7.2 1.5 collective-permute-start.3
  10.1 2.6 collective-permute-start.1
  18.2 2.0 route_tables.1
  21.5 4.2 pack_rows.1
  26.2 4.0 copy.39
  30.2 1.8 multiply_sine_fusion
  32.7 5.0 %qkv0.1 = (bf16[512,256]{1,0:T(8,128)(2,1)}, bf16[512,256]{1,0:T(8,128)(2,1)}, bf16[128,256]{1,0:T(8,128)(2,1)}, bf16[128,256]{1,0:T(8,128)(2,1)}, bf16[128,256]...) custom-call(s32[1]{0:T(128)} %bitcast.2.refs_0_, ...), custom_call_target="tpu_custom_call" | custom-call | flops 1 | bytes 1 | tf_op jit(solution)/shard_map/qkv0/pallas_call | solution.py:61
  37.7 9.2 %all-to-all-start.1 = ((bf16[128,88,128]{2,1,0:T(8,128)(2,1)}), bf16[128,88,128]{2,1,0:T(8,128)(2,1)}, u32[]{:S(2)}, u32[]{:S(2)}) async-start(bf16[128,88,128]{2,1,0:T(8,128)(2,1)} %pack_rows.1), calls=%async_computation.1 | async-start | bytes 5767168 | tf_op jit(solution)/shard_map/all_to_all | solution.py:1070
  49.7 3.8 collective-permute-done.6.refs_2_
  54.5 7.7 %qkv123.1 = (bf16[512,256]{1,0:T(8,128)(2,1)}, bf16[512,256]{1,0:T(8,128)(2,1)}, bf16[128,256]{1,0:T(8,128)(2,1)}, bf16[128,256]{1,0:T(8,128)(2,1)}, bf16[128,25...) custom-call(s32[1]{0:T(128)} %bitcast.2.refs_0_, ...), custom_call_target="tpu_custom_call" | custom-call | flops 1 | bytes 1 | tf_op jit(solution)/shard_map/qkv123/pallas_call | solution.py:61
  62.2 7.1 %attend.1 = (bf16[512,512]{1,0:T(8,128)(2,1)}, bf16[512,512]{1,0:T(8,128)(2,1)}, f32[8,1024]{1,0:T(8,128)}, bf16[512,1024]{1,0:T(8,128)(2,1)}, bf16[128,1024]{1,...) custom-call(bf16[512,256]{1,0:T(8,128)(2,1)} %get-tuple-element.154.refs_0_, ...), custom_call_target="tpu_custom_call" | custom-call | flops 1 | bytes 6600001 | tf_op jit(solution)/shard_map/attend/pallas_call | solution.py:61
  69.7 1.8 collective-permute-done.9.otr
  72.3 5.6 %out_projection.1 = (bf16[128,2048]{1,0:T(8,128)(2,1)}, bf16[128,2048]{1,0:T(8,128)(2,1)}, bf16[128,2048]{1,0:T(8,128)(2,1)}, bf16[128,2048]{1,0:T(8,128)(2,1)}) custom-call(bf16[512,512]{1,0:T(8,128)(2,1)} %get-tuple-element.169.ot0.refs_8_.refs_17_, bf16[512,512]{1,0:T(8,128)(2,1)} %copy-done.11, bf16[512,2048]{1,0:T(8,128)(2,1)} %refs_10_.1, ...), custom_call_target="tpu_custom_call" | custom-call | flops 1 | bytes 3000001 | tf_op jit(solution)/shard_map/out_projection/pallas_call | solution.py:74
  78.5 2.1 collective-permute-start.12
  82.5 11.3 %collective-permute-done.11.b1 = bf16[128,2048]{1,0:T(8,128)(2,1)S(1)} collective-permute-done((bf16[128,2048]{1,0:T(8,128)(2,1)}, bf16[128,2048]{1,0:T(8,128)(2,1)S(1)}, u32[]{:S(2)}, u32[]{:S(2)}) %collective-permute-start.11) | collective-permute-done | bytes 524320 | tf_op jit(solution)/shard_map/ppermute | solution.py:1066
  93.8 11.3 %collective-permute-done.13.b3 = bf16[128,2048]{1,0:T(8,128)(2,1)} collective-permute-done((bf16[128,2048]{1,0:T(8,128)(2,1)}, bf16[128,2048]{1,0:T(8,128)(2,1)}, u32[]{:S(2)}, u32[]{:S(2)}) %collective-permute-start.13) | collective-permute-done | bytes 524320 | tf_op jit(solution)/shard_map/ppermute | solution.py:1066
  105.1 5.6 %router.1 = (f32[128,2048]{1,0:T(8,128)}, bf16[128,2048]{1,0:T(8,128)(2,1)}, f32[128,128]{1,0:T(8,128)}, f32[128,128]{1,0:T(8,128)}, bf16[128,88,128]{2,1,0:T(8,128)(2,1)}) custom-call(bf16[128,2048]{1,0:T(8,128)(2,1)} %get-tuple-element.171.b0, bf16[128,2048]{1,0:T(8,128)(2,1)} %copy-done.14, bf16[128,2048]{1,0:T(8,128)(2,1)} %collective-permute-done.12.b2, ...), custom_call_target="tpu_custom_call" | custom-call | flops 1 | bytes 3600001 | tf_op jit(solution)/shard_map/router/pallas_call | solution.py:61
  110.7 8.8 %all-to-all-start = ((bf16[128,88,128]{2,1,0:T(8,128)(2,1)}), bf16[128,88,128]{2,1,0:T(8,128)(2,1)}, u32[]{:S(2)}, u32[]{:S(2)}) async-start(bf16[128,88,128]{2,1,0:T(8,128)(2,1)} %get-tuple-element.176), calls=%async_computation | async-start | bytes 5767168 | tf_op jit(solution)/shard_map/all_to_all | solution.py:1070
  120.7 5.5 %transpose_rows.1.n1t = bf16[2048,1024]{1,0:T(8,128)(2,1)} custom-call(bf16[256,2048]{1,0:T(8,128)(2,1)} %get-tuple-element.181.n0, bf16[256,2048]{1,0:T(8,128)(2,1)} %get-tuple-element.182.n1, bf16[256,2048]{1,0:T(8,128)(2,1)} %get-tuple-element.183.n2, bf16[256,2048]{1,0:T(8,128)(2,1)} %get-tuple-element.184.n3), custom_call_target="tpu_custom_call" | custom-call | flops 1 | bytes 3600001 | tf_op jit(solution)/shard_map/transpose_rows/pallas_call | solution.py:61
  126.9 7.5 %expert_grad_rows.1 = (bf16[640,2048]{1,0:T(8,128)(2,1)}, f32[640,768]{1,0:T(8,128)}) custom-call(bf16[128,88,128]{2,1,0:T(8,128)(2,1)} %all-to-all-done.1.wire, bf16[768,2048]{1,0:T(8,128)(2,1)} %bitcast.69), custom_call_target="tpu_custom_call" | custom-call | flops 1 | bytes 4800001 | tf_op jit(solution)/shard_map/expert_grad_rows/pallas_call | solution.py:61
  134.4 23.9 %all-to-all-done.wire = bf16[128,88,128]{2,1,0:T(8,128)(2,1)} async-done(((bf16[128,88,128]{2,1,0:T(8,128)(2,1)}), bf16[128,88,128]{2,1,0:T(8,128)(2,1)}, u32[]{:S(2)}, u32[]{:S(2)}) %all-to-all-start) | async-done | bytes 2883616 | tf_op jit(solution)/shard_map/all_to_all | solution.py:1070
  158.2 15.9 %expert_main.1 = (bf16[128,88,128]{2,1,0:T(8,128)(2,1)}, bf16[640,2048]{1,0:T(8,128)(2,1)}, bf16[640,768]{1,0:T(8,128)(2,1)}, bf16[640,768]{1,0:T(8,128)(2,1)}, ...) custom-call(bf16[128,88,128]{2,1,0:T(8,128)(2,1)} %all-to-all-done.wire, bf16[2048,768]{1,0:T(8,128)(2,1)} %bitcast.73, ...), custom_call_target="tpu_custom_call" | custom-call | flops 1 | bytes 10800001 | tf_op jit(solution)/shard_map/expert_main/pallas_call | solution.py:564
  174.1 5.9 %all-to-all-start.2 = ((bf16[128,88,128]{2,1,0:T(8,128)(2,1)}), bf16[128,88,128]{2,1,0:T(8,128)(2,1)}, u32[]{:S(2)}, u32[]{:S(2)}) async-start(bf16[128,88,128]{2,1,0:T(8,128)(2,1)} %get-tuple-element.209), calls=%async_computation.2 | async-start | bytes 5767168 | tf_op jit(solution)/shard_map/all_to_all | solution.py:1070
  182.2 6.6 %expert_out.1 = bf16[128,80,128]{2,1,0:T(8,128)(2,1)} custom-call(bf16[640,768]{1,0:T(8,128)(2,1)} %get-tuple-element.215.act, bf16[768,2048]{1,0:T(8,128)(2,1)} %bitcast.70), custom_call_target="tpu_custom_call" | custom-call | flops 1 | bytes 4200001 | tf_op jit(solution)/shard_map/expert_out/pallas_call | solution.py:61
  188.8 7.5 %fusion.7 = f32[2048,768]{1,0:T(8,128)} fusion(bf16[640,2048]{1,0:T(8,128)(2,1)} %get-tuple-element.216, bf16[640,768]{1,0:T(8,128)(2,1)} %get-tuple-element.217), kind=kOutput, calls=%fused_computation.32 | convolution fusion | flops 2013265920 | bytes 9895936 | tf_op jit(solution)/shard_map/dot_general | solution.py:1177
  196.3 4.6 %fusion.8 = f32[2048,768]{1,0:T(8,128)} fusion(bf16[640,2048]{1,0:T(8,128)(2,1)S(1)} %copy-done.31, bf16[640,768]{1,0:T(8,128)(2,1)S(1)} %copy-done.32), kind=kOutput, calls=%fused_computation.33 | convolution fusion | flops 2013265920 | bytes 9895936 | tf_op jit(solution)/shard_map/dot_general | solution.py:1177
  200.9 4.5 fusion.9
  205.4 13.3 %all-to-all-done.2.wire = bf16[128,88,128]{2,1,0:T(8,128)(2,1)} async-done(((bf16[128,88,128]{2,1,0:T(8,128)(2,1)}), bf16[128,88,128]{2,1,0:T(8,128)(2,1)}, u32[]{:S(2)}, u32[]{:S(2)}) %all-to-all-start.2) | async-done | bytes 2883616 | tf_op jit(solution)/shard_map/all_to_all | solution.py:1070
  218.7 7.1 %combine_grads.1 = (f32[128,2048]{1,0:T(8,128)}, bf16[128,2048]{1,0:T(8,128)(2,1)}, bf16[4,256,128]{2,1,0:T(8,128)(2,1)}, bf16[4,256,128]{2,1,0:T(8,128)(2,1)}, f32[1,2048]{1,0:T(1,128)}) custom-call(s32[4]{0:T(128)} %pad_add_fusion.where, s32[512]{0:T(512)} %reshape.212.experts, s32[512]{0:T(512)} %reshape.213.slots, f32[512]{0:T(512)} %reshape.211.gate_list, ...), custom_call_target="tpu_custom_call" | custom-call | flops 1 | bytes 4200001 | tf_op jit(solution)/shard_map/combine_grads/pallas_call | solution.py:61
  226.8 1.7 collective-permute-start.15
  229.9 21.1 %collective-permute-done.17.refs_3_ = bf16[128,2048]{1,0:T(8,128)(2,1)S(1)} collective-permute-done((bf16[128,2048]{1,0:T(8,128)(2,1)}, bf16[128,2048]{1,0:T(8,128)(2,1)S(1)}, u32[]{:S(2)}, u32[]{:S(2)}) %collective-permute-start.17) | collective-permute-done | bytes 524320 | tf_op jit(solution)/shard_map/ppermute | solution.py:1062
  251.1 1.8 collective-permute-start.21
  256.7 8.8 %out_projection_grad.1 = (bf16[4,512,128]{2,1,0:T(8,128)(2,1)}, bf16[4,512,128]{2,1,0:T(8,128)(2,1)}, bf16[4,512,128]{2,1,0:T(8,128)(2,1)}, bf16[4,512,128]{2,1,0:T(8,128)(2,1)}, bf16[512,1024]{1,0:T(8,128)(2,1)}) custom-call(s32[4]{0:T(128)} %pad_add_fusion.where, bf16[128,2048]{1,0:T(8,128)(2,1)} %get-tuple-element.225.refs_0_, ...), custom_call_target="tpu_custom_call" | custom-call | flops 1 | bytes 4200001 | tf_op jit(solution)/shard_map/out_projection_grad/pallas_call | solution.py:93
  265.6 2.7 collective-permute-start.23
  268.6 16.7 %attend_grad.1 = (bf16[512,512]{1,0:T(8,128)(2,1)}, bf16[512,512]{1,0:T(8,128)(2,1)}, bf16[256,1024]{1,0:T(8,128)(2,1)}, f32[8,128]{1,0:T(8,128)}, f32[8,128]{1,0:T(8,128)}) custom-call(bf16[512,256]{1,0:T(8,128)(2,1)} %get-tuple-element.190.refs_0_, bf16[512,256]{1,0:T(8,128)(2,1)} %get-tuple-element.191.refs_1_, ...), custom_call_target="tpu_custom_call" | custom-call | flops 1 | bytes 1 | tf_op jit(solution)/shard_map/attend_grad/pallas_call | solution.py:61
  285.4 5.7 %collective-permute-done.24.d = bf16[4,512,128]{2,1,0:T(8,128)(2,1)} collective-permute-done((bf16[4,512,128]{2,1,0:T(8,128)(2,1)}, bf16[4,512,128]{2,1,0:T(8,128)(2,1)}, u32[]{:S(2)}, u32[]{:S(2)}) %collective-permute-start.24) | collective-permute-done | bytes 524320 | tf_op jit(solution)/shard_map/ppermute | solution.py:1081
  291.0 2.5 collective-permute-start.25
  293.5 1.7 collective-permute-done.25.sib
  296.1 7.9 %qkv_weight_grad.1 = (bf16[2048,640]{1,0:T(8,128)(2,1)}, bf16[256,1024]{1,0:T(8,128)(2,1)}) custom-call(s32[4]{0:T(128)} %pad_add_fusion.where, bf16[2048,1024]{1,0:T(8,128)(2,1)} %transpose_rows.1.n1t, bf16[512,512]{1,0:T(8,128)(2,1)} %get-tuple-element.228.dq0, bf16[512,512]{1,0:T(8,128)(2,1)} %get-tuple-element.235.dq1, ...), custom_call_target="tpu_custom_call" | custom-call | flops 1 | bytes 1 | tf_op jit(solution)/shard_map/qkv_weight_grad/pallas_call | solution.py:74
  304.0 4.8 %all-to-all-start.3 = ((bf16[128,80,128]{2,1,0:T(8,128)(2,1)}), bf16[128,80,128]{2,1,0:T(8,128)(2,1)}, u32[]{:S(2)}, u32[]{:S(2)}) async-start(bf16[128,80,128]{2,1,0:T(8,128)(2,1)} %expert_out.1), calls=%async_computation.3 | async-start | bytes 5242880 | tf_op jit(solution)/shard_map/all_to_all | solution.py:1070
  311.2 1.8 collective-permute-done.33.rb
  313.9 8.1 %normed_grad.1 = (bf16[160,2048]{1,0:T(8,128)(2,1)}, bf16[160,2048]{1,0:T(8,128)(2,1)}, bf16[160,2048]{1,0:T(8,128)(2,1)}, bf16[160,2048]{1,0:T(8,128)(2,1)}) custom-call(bf16[512,2048]{1,0:T(8,128)(2,1)} %bitcast.5.refs_4_.refs_8_.wa, bf16[512,2048]{1,0:T(8,128)(2,1)} %collective-permute-done.14.wb, bf16[256,2048]{1,0:T(8,128)(2,1)} %get-tuple-element.247.wkv, ...), custom_call_target="tpu_custom_call" | custom-call | flops 1 | bytes 1 | tf_op jit(solution)/shard_map/normed_grad/pallas_call | solution.py:74
  322.6 2.1 collective-permute-start.35
  325.7 2.4 add_parts.1
  329.5 1.8 collective-permute-start.27
  331.3 13.3 %collective-permute-done.26.b = bf16[512,128]{1,0:T(8,128)(2,1)S(1)} collective-permute-done((bf16[512,128]{1,0:T(8,128)(2,1)}, bf16[512,128]{1,0:T(8,128)(2,1)S(1)}, u32[]{:S(2)}, u32[]{:S(2)}) %collective-permute-start.26) | collective-permute-done | bytes 131104 | tf_op jit(solution)/shard_map/ppermute | solution.py:1081
  344.6 3.0 collective-permute-start.28
  347.6 8.0 %collective-permute-done.28.d = bf16[512,128]{1,0:T(8,128)(2,1)} collective-permute-done((bf16[512,128]{1,0:T(8,128)(2,1)}, bf16[512,128]{1,0:T(8,128)(2,1)}, u32[]{:S(2)}, u32[]{:S(2)}) %collective-permute-start.28) | collective-permute-done | bytes 131104 | tf_op jit(solution)/shard_map/ppermute | solution.py:1081
  355.6 1.8 add_last.1.a
  358.2 7.0 %collective-permute-done.31.d = bf16[512,128]{1,0:T(8,128)(2,1)S(1)} collective-permute-done((bf16[512,128]{1,0:T(8,128)(2,1)}, bf16[512,128]{1,0:T(8,128)(2,1)S(1)}, u32[]{:S(2)}, u32[]{:S(2)}) %collective-permute-start.31) | collective-permute-done | bytes 131104 | tf_op jit(solution)/shard_map/ppermute | solution.py:1081
  365.3 4.7 %collective-permute-done.29.b = bf16[512,128]{1,0:T(8,128)(2,1)S(1)} collective-permute-done((bf16[512,128]{1,0:T(8,128)(2,1)}, bf16[512,128]{1,0:T(8,128)(2,1)S(1)}, u32[]{:S(2)}, u32[]{:S(2)}) %collective-permute-start.29) | collective-permute-done | bytes 131104 | tf_op jit(solution)/shard_map/ppermute | solution.py:1081
  370.7 2.1 stack_parts.1.c0
  372.8 5.4 %collective-permute-start.38 = (bf16[4,512,128]{2,1,0:T(8,128)(2,1)}, bf16[4,512,128]{2,1,0:T(8,128)(2,1)}, u32[]{:S(2)}, u32[]{:S(2)}) collective-permute-start(bf16[4,512,128]{2,1,0:T(8,128)(2,1)} %stack_parts.1.c0), channel_id=1, source_target_pairs={{0,16},{8,24},{16,0},{24,8},{32,48},{40,56},{48,32},{56,40},{64,80... | collective-permute-start | bytes 1572872 | tf_op jit(solution)/shard_map/ppermute | solution.py:1081
  378.2 4.0 input_grad.1
  382.2 3.5 all-to-all-start.4
  385.7 1.6 collective-permute-done.39.c3
  387.4 12.6 %collective-permute-done.38.c2 = bf16[4,512,128]{2,1,0:T(8,128)(2,1)} collective-permute-done((bf16[4,512,128]{2,1,0:T(8,128)(2,1)}, bf16[4,512,128]{2,1,0:T(8,128)(2,1)}, u32[]{:S(2)}, u32[]{:S(2)}) %collective-permute-start.38) | collective-permute-done | bytes 524320 | tf_op jit(solution)/shard_map/ppermute | solution.py:1081
  400.0 2.1 collective-permute-done.37.c1
  403.5 2.5 fold_small.1
  406.1 12.0 %all-to-all-start.5 = ((bf16[128,24,128]{2,1,0:T(8,128)(2,1)}), bf16[128,24,128]{2,1,0:T(8,128)(2,1)S(1)}, u32[]{:S(2)}, u32[]{:S(2)}) async-start(bf16[128,24,128]{2,1,0:T(8,128)(2,1)} %fold_small.1), calls=%async_computation.5 | async-start | bytes 1572864 | tf_op jit(solution)/shard_map/all_to_all | solution.py:1070
  418.1 4.8 %result.1 = bf16[128,2048]{1,0:T(8,128)(2,1)} custom-call(s32[512]{0:T(512)} %reshape.212.experts, s32[512]{0:T(512)} %reshape.213.slots, f32[512]{0:T(512)} %reshape.211.gate_list, bf16[128,80,128]{2,1,0:T(8,128)(2,1)} %all-to-all-done.3.wire, f32[128,2048]{1,0:T(8,128)} %get-tuple-element.222.hidden), custom_call_target="tpu_custom_call" | custom-call | flops 1 | bytes 1 | tf_op jit(solution)/shard_map/result/pallas_call | solution.py:61
  422.9 4.1 place_output_grads.1
  427.0 14.8 %all-reduce.2.cloned.1.call-done.grads = bf16[2048,640]{1,0:T(8,128)(2,1)} async-done(((bf16[2048,640]{1,0:T(8,128)(2,1)}), bf16[2048,640]{1,0:T(8,128)(2,1)}) %all-reduce.2.cloned.1.call-update) | async-done | bytes 2621456 | tf_op jit(solution)/shard_map/psum | solution.py:1208
  445.1 4.6 widen_grads.1
  (155 shorter events, 41.0 us)
Async XLA Ops:
  7.2 8.5 %copy-start = (s32[1,1024]{1,0:T(1,128)S(1)}, s32[1,1024]{1,0:T(1,128)}, u32[]{:S(2)}) copy-start(s32[1,1024]{1,0:T(1,128)} %param.32) | copy-start | bytes 12292
  7.2 18.4 %copy-start.29 = (bf16[2048]{0:T(1024)(128)(2,1)S(1)}, bf16[2048]{0:T(1024)(128)(2,1)}, u32[]{:S(2)}) copy-start(bf16[2048]{0:T(1024)(128)(2,1)} %param.19) | copy-start | bytes 12292
  7.2 24.8 %collective-permute-start.3 = (bf16[128,2048]{1,0:T(8,128)(2,1)}, bf16[128,2048]{1,0:T(8,128)(2,1)}, u32[]{:S(2)}, u32[]{:S(2)}) collective-permute-start(bf16[128,2048]{1,0:T(8,128)(2,1)} %x0.3), channel_id=1, source_target_pairs={{0,1},{1,0},{2,3},{3,2},{4,5},{5,4},{6,7},{7,6},{8,9},{9,8},{10,11... | collective-permute-start | bytes 1572872 | tf_op jit(solution)/shard_map/ppermute | solution.py:1058
  8.7 29.0 %collective-permute-start.2 = (bf16[128,2048]{1,0:T(8,128)(2,1)}, bf16[128,2048]{1,0:T(8,128)(2,1)}, u32[]{:S(2)}, u32[]{:S(2)}) collective-permute-start(bf16[128,2048]{1,0:T(8,128)(2,1)} %x0.3), channel_id=1, source_target_pairs={{0,2},{1,3},{2,4},{3,5},{4,6},{5,7},{6,0},{7,1},{8,10},{9,11},{10,... | collective-permute-start | bytes 1572872 | tf_op jit(solution)/shard_map/ppermute | solution.py:1062
  10.1 27.6 %collective-permute-start.1 = (bf16[128,2048]{1,0:T(8,128)(2,1)}, bf16[128,2048]{1,0:T(8,128)(2,1)}, u32[]{:S(2)}, u32[]{:S(2)}) collective-permute-start(bf16[128,2048]{1,0:T(8,128)(2,1)} %x0.3), channel_id=1, source_target_pairs={{0,4},{1,5},{2,6},{3,7},{4,0},{5,1},{6,2},{7,3},{8,12},{9,13},{10,... | collective-permute-start | bytes 1572872 | tf_op jit(solution)/shard_map/ppermute | solution.py:1062
  12.7 25.0 %collective-permute-start = (bf16[128,2048]{1,0:T(8,128)(2,1)}, bf16[128,2048]{1,0:T(8,128)(2,1)}, u32[]{:S(2)}, u32[]{:S(2)}) collective-permute-start(bf16[128,2048]{1,0:T(8,128)(2,1)} %x0.3), channel_id=1, source_target_pairs={{0,6},{1,7},{2,0},{3,1},{4,2},{5,3},{6,4},{7,5},{8,14},{9,15},{10,... | collective-permute-start | bytes 1572872 | tf_op jit(solution)/shard_map/ppermute | solution.py:1062
  13.8 4.3 collective-permute-start.4
  18.1 12.1 %copy-start.4 = (bf16[64,2048]{1,0:T(8,128)(2,1)}, bf16[64,2048]{1,0:T(8,128)(2,1)S(1)}, u32[]{:S(2)}) copy-start(bf16[64,2048]{1,0:T(8,128)(2,1)S(1)} %collective-permute-done.4.refs_6_.refs_10_) | copy-start | bytes 786436
  18.1 13.9 %collective-permute-start.5 = (bf16[64,2048]{1,0:T(8,128)(2,1)}, bf16[64,2048]{1,0:T(8,128)(2,1)S(1)}, u32[]{:S(2)}, u32[]{:S(2)}) collective-permute-start(bf16[64,2048]{1,0:T(8,128)(2,1)} %bitcast.78), channel_id=1, source_target_pairs={{0,1},{1,0},{2,3},{3,2},{4,5},{5,4},{6,7},{7,6},{8,9},{9,8},{10,11... | collective-permute-start | bytes 786440 | tf_op jit(solution)/shard_map/ppermute | solution.py:1058
  37.7 73.0 %all-to-all-start.1 = ((bf16[128,88,128]{2,1,0:T(8,128)(2,1)}), bf16[128,88,128]{2,1,0:T(8,128)(2,1)}, u32[]{:S(2)}, u32[]{:S(2)}) async-start(bf16[128,88,128]{2,1,0:T(8,128)(2,1)} %pack_rows.1), calls=%async_computation.1 | async-start | bytes 5767168 | tf_op jit(solution)/shard_map/all_to_all | solution.py:1070
  46.9 24.5 %collective-permute-start.10 = (bf16[512,2048]{1,0:T(8,128)(2,1)}, bf16[512,2048]{1,0:T(8,128)(2,1)}, u32[]{:S(2)}, u32[]{:S(2)}) collective-permute-start(bf16[512,2048]{1,0:T(8,128)(2,1)} %refs_10_.1), channel_id=1, source_target_pairs={{0,1},{1,0},{2,3},{3,2},{4,5},{5,4},{6,7},{7,6},{8,9},{9,8},{10,11... | collective-permute-start | bytes 6291464 | tf_op jit(solution)/shard_map/ppermute | solution.py:1058
  48.1 5.4 %collective-permute-start.6 = (bf16[128,2048]{1,0:T(8,128)(2,1)}, bf16[128,2048]{1,0:T(8,128)(2,1)S(1)}, u32[]{:S(2)}, u32[]{:S(2)}) collective-permute-start(bf16[128,2048]{1,0:T(8,128)(2,1)} %collective-permute-done.refs_1_), channel_id=1, source_target_pairs={{0,1},{1,0},{2,3},{3,2},{4,5},{5,4},{6,7},{7,6},{8,9},{9,8},{10,11... | collective-permute-start | bytes 1572872 | tf_op jit(solution)/shard_map/ppermute | solution.py:1058
  48.2 5.5 %collective-permute-start.7 = (bf16[128,2048]{1,0:T(8,128)(2,1)}, bf16[128,2048]{1,0:T(8,128)(2,1)}, u32[]{:S(2)}, u32[]{:S(2)}) collective-permute-start(bf16[128,2048]{1,0:T(8,128)(2,1)} %collective-permute-done.1.refs_3_), channel_id=1, source_target_pairs={{0,1},{1,0},{2,3},{3,2},{4,5},{5,4},{6,7},{7,6},{8,9},{9,8},{10,11... | collective-permute-start | bytes 1572872 | tf_op jit(solution)/shard_map/ppermute | solution.py:1058
  48.7 5.9 %collective-permute-start.8 = (bf16[128,2048]{1,0:T(8,128)(2,1)}, bf16[128,2048]{1,0:T(8,128)(2,1)}, u32[]{:S(2)}, u32[]{:S(2)}) collective-permute-start(bf16[128,2048]{1,0:T(8,128)(2,1)} %collective-permute-done.2.refs_5_), channel_id=1, source_target_pairs={{0,1},{1,0},{2,3},{3,2},{4,5},{5,4},{6,7},{7,6},{8,9},{9,8},{10,11... | collective-permute-start | bytes 1572872 | tf_op jit(solution)/shard_map/ppermute | solution.py:1058
  69.3 2.1 collective-permute-start.9
  72.2 9.6 %copy-start.30 = (bf16[2048]{0:T(1024)(128)(2,1)S(1)}, bf16[2048]{0:T(1024)(128)(2,1)}, u32[]{:S(2)}) copy-start(bf16[2048]{0:T(1024)(128)(2,1)} %param.26) | copy-start | bytes 12292
  77.9 15.9 %collective-permute-start.11 = (bf16[128,2048]{1,0:T(8,128)(2,1)}, bf16[128,2048]{1,0:T(8,128)(2,1)S(1)}, u32[]{:S(2)}, u32[]{:S(2)}) collective-permute-start(bf16[128,2048]{1,0:T(8,128)(2,1)} %get-tuple-element.172), channel_id=1, source_target_pairs={{0,2},{1,3},{2,4},{3,5},{4,6},{5,7},{6,0},{7,1},{8,10},{9,11},{10,... | collective-permute-start | bytes 1572872 | tf_op jit(solution)/shard_map/ppermute | solution.py:1066
  78.5 15.3 %collective-permute-start.12 = (bf16[128,2048]{1,0:T(8,128)(2,1)}, bf16[128,2048]{1,0:T(8,128)(2,1)}, u32[]{:S(2)}, u32[]{:S(2)}) collective-permute-start(bf16[128,2048]{1,0:T(8,128)(2,1)} %get-tuple-element.173), channel_id=1, source_target_pairs={{0,6},{1,7},{2,0},{3,1},{4,2},{5,3},{6,4},{7,5},{8,14},{9,15},{10,... | collective-permute-start | bytes 1572872 | tf_op jit(solution)/shard_map/ppermute | solution.py:1066
  80.6 24.5 %collective-permute-start.13 = (bf16[128,2048]{1,0:T(8,128)(2,1)}, bf16[128,2048]{1,0:T(8,128)(2,1)}, u32[]{:S(2)}, u32[]{:S(2)}) collective-permute-start(bf16[128,2048]{1,0:T(8,128)(2,1)} %get-tuple-element.174), channel_id=1, source_target_pairs={{0,4},{1,5},{2,6},{3,7},{4,0},{5,1},{6,2},{7,3},{8,12},{9,13},{10,... | collective-permute-start | bytes 1572872 | tf_op jit(solution)/shard_map/ppermute | solution.py:1066
  93.8 11.3 %copy-start.14 = (bf16[128,2048]{1,0:T(8,128)(2,1)}, bf16[128,2048]{1,0:T(8,128)(2,1)S(1)}, u32[]{:S(2)}) copy-start(bf16[128,2048]{1,0:T(8,128)(2,1)S(1)} %collective-permute-done.11.b1) | copy-start | bytes 1572868
  110.7 47.5 %all-to-all-start = ((bf16[128,88,128]{2,1,0:T(8,128)(2,1)}), bf16[128,88,128]{2,1,0:T(8,128)(2,1)}, u32[]{:S(2)}, u32[]{:S(2)}) async-start(bf16[128,88,128]{2,1,0:T(8,128)(2,1)} %get-tuple-element.176), calls=%async_computation | async-start | bytes 5767168 | tf_op jit(solution)/shard_map/all_to_all | solution.py:1070
  119.5 14.8 %collective-permute-start.14 = (bf16[512,2048]{1,0:T(8,128)(2,1)}, bf16[512,2048]{1,0:T(8,128)(2,1)}, u32[]{:S(2)}, u32[]{:S(2)}) collective-permute-start(bf16[512,2048]{1,0:T(8,128)(2,1)} %bitcast.5.refs_4_.refs_8_.wa), channel_id=1, source_target_pairs={{0,1},{1,0},{2,3},{3,2},{4,5},{5,4},{6,7},{7,6},{8,9},{9,8},{10,11... | collective-permute-start | bytes 6291464 | tf_op jit(solution)/shard_map/ppermute | solution.py:1058
  120.7 5.5 %copy-start.22 = (f32[128,128]{1,0:T(8,128)S(1)}, f32[128,128]{1,0:T(8,128)}, u32[]{:S(2)}) copy-start(f32[128,128]{1,0:T(8,128)} %get-tuple-element.188.gates) | copy-start | bytes 196612
  174.1 5.9 %copy-start.3 = (s32[128,128]{1,0:T(8,128)S(1)}, s32[128,128]{1,0:T(8,128)}, u32[]{:S(2)}) copy-start(s32[128,128]{1,0:T(8,128)} %get-tuple-element.175.ids) | copy-start | bytes 196612
  174.1 44.6 %all-to-all-start.2 = ((bf16[128,88,128]{2,1,0:T(8,128)(2,1)}), bf16[128,88,128]{2,1,0:T(8,128)(2,1)}, u32[]{:S(2)}, u32[]{:S(2)}) async-start(bf16[128,88,128]{2,1,0:T(8,128)(2,1)} %get-tuple-element.209), calls=%async_computation.2 | async-start | bytes 5767168 | tf_op jit(solution)/shard_map/all_to_all | solution.py:1070
  188.8 7.5 %copy-start.31 = (bf16[640,2048]{1,0:T(8,128)(2,1)S(1)}, bf16[640,2048]{1,0:T(8,128)(2,1)}, u32[]{:S(2)}) copy-start(bf16[640,2048]{1,0:T(8,128)(2,1)} %get-tuple-element.216) | copy-start | bytes 7864324
  188.8 7.5 %copy-start.32 = (bf16[640,768]{1,0:T(8,128)(2,1)S(1)}, bf16[640,768]{1,0:T(8,128)(2,1)}, u32[]{:S(2)}) copy-start(bf16[640,768]{1,0:T(8,128)(2,1)} %get-tuple-element.218) | copy-start | bytes 2949124
  225.8 25.2 %collective-permute-start.17 = (bf16[128,2048]{1,0:T(8,128)(2,1)}, bf16[128,2048]{1,0:T(8,128)(2,1)S(1)}, u32[]{:S(2)}, u32[]{:S(2)}) collective-permute-start(bf16[128,2048]{1,0:T(8,128)(2,1)} %get-tuple-element.225.refs_0_), channel_id=1, source_target_pairs={{0,2},{1,3},{2,4},{3,5},{4,6},{5,7},{6,0},{7,1},{8,10},{9,11},{10,... | collective-permute-start | bytes 1572872 | tf_op jit(solution)/shard_map/ppermute | solution.py:1062
  225.8 27.0 %collective-permute-start.16 = (bf16[128,2048]{1,0:T(8,128)(2,1)}, bf16[128,2048]{1,0:T(8,128)(2,1)S(1)}, u32[]{:S(2)}, u32[]{:S(2)}) collective-permute-start(bf16[128,2048]{1,0:T(8,128)(2,1)} %get-tuple-element.225.refs_0_), channel_id=1, source_target_pairs={{0,4},{1,5},{2,6},{3,7},{4,0},{5,1},{6,2},{7,3},{8,12},{9,13},{10,... | collective-permute-start | bytes 1572872 | tf_op jit(solution)/shard_map/ppermute | solution.py:1062
  226.8 26.2 %collective-permute-start.15 = (bf16[128,2048]{1,0:T(8,128)(2,1)}, bf16[128,2048]{1,0:T(8,128)(2,1)S(1)}, u32[]{:S(2)}, u32[]{:S(2)}) collective-permute-start(bf16[128,2048]{1,0:T(8,128)(2,1)} %get-tuple-element.225.refs_0_), channel_id=1, source_target_pairs={{0,6},{1,7},{2,0},{3,1},{4,2},{5,3},{6,4},{7,5},{8,14},{9,15},{10,... | collective-permute-start | bytes 1572872 | tf_op jit(solution)/shard_map/ppermute | solution.py:1062
  228.5 24.9 %collective-permute-start.18 = (bf16[128,2048]{1,0:T(8,128)(2,1)}, bf16[128,2048]{1,0:T(8,128)(2,1)S(1)}, u32[]{:S(2)}, u32[]{:S(2)}) collective-permute-start(bf16[128,2048]{1,0:T(8,128)(2,1)} %get-tuple-element.225.refs_0_), channel_id=1, source_target_pairs={{0,1},{1,0},{2,3},{3,2},{4,5},{5,4},{6,7},{7,6},{8,9},{9,8},{10,11... | collective-permute-start | bytes 1572872 | tf_op jit(solution)/shard_map/ppermute | solution.py:1058
  251.1 5.6 %copy-start.15 = (bf16[128,2048]{1,0:T(8,128)(2,1)}, bf16[128,2048]{1,0:T(8,128)(2,1)S(1)}, u32[]{:S(2)}) copy-start(bf16[128,2048]{1,0:T(8,128)(2,1)S(1)} %collective-permute-done.17.refs_3_) | copy-start | bytes 1572868
  251.1 3.3 collective-permute-start.21
  252.8 3.0 collective-permute-start.20
  252.9 3.8 collective-permute-start.19
  265.5 19.8 %collective-permute-start.22 = (bf16[4,512,128]{2,1,0:T(8,128)(2,1)}, bf16[4,512,128]{2,1,0:T(8,128)(2,1)S(1)}, u32[]{:S(2)}, u32[]{:S(2)}) collective-permute-start(bf16[4,512,128]{2,1,0:T(8,128)(2,1)} %get-tuple-element.230), channel_id=1, source_target_pairs={{0,8},{8,16},{16,24},{24,0},{32,40},{40,48},{48,56},{56,32},{64,72... | collective-permute-start | bytes 1572872 | tf_op jit(solution)/shard_map/ppermute | solution.py:1081
  265.6 19.8 %collective-permute-start.23 = (bf16[4,512,128]{2,1,0:T(8,128)(2,1)}, bf16[4,512,128]{2,1,0:T(8,128)(2,1)}, u32[]{:S(2)}, u32[]{:S(2)}) collective-permute-start(bf16[4,512,128]{2,1,0:T(8,128)(2,1)} %get-tuple-element.231), channel_id=1, source_target_pairs={{0,24},{8,0},{16,8},{24,16},{32,56},{40,32},{48,40},{56,48},{64,88... | collective-permute-start | bytes 1572872 | tf_op jit(solution)/shard_map/ppermute | solution.py:1081
  268.2 22.8 %collective-permute-start.24 = (bf16[4,512,128]{2,1,0:T(8,128)(2,1)}, bf16[4,512,128]{2,1,0:T(8,128)(2,1)}, u32[]{:S(2)}, u32[]{:S(2)}) collective-permute-start(bf16[4,512,128]{2,1,0:T(8,128)(2,1)} %get-tuple-element.232), channel_id=1, source_target_pairs={{0,16},{8,24},{16,0},{24,8},{32,48},{40,56},{48,32},{56,40},{64,80... | collective-permute-start | bytes 1572872 | tf_op jit(solution)/shard_map/ppermute | solution.py:1081
  285.3 5.7 %copy-start.13 = (bf16[4,512,128]{2,1,0:T(8,128)(2,1)}, bf16[4,512,128]{2,1,0:T(8,128)(2,1)S(1)}, u32[]{:S(2)}) copy-start(bf16[4,512,128]{2,1,0:T(8,128)(2,1)S(1)} %collective-permute-done.22.b) | copy-start | bytes 1572868
  291.0 4.2 collective-permute-start.25
  304.0 78.3 %all-to-all-start.3 = ((bf16[128,80,128]{2,1,0:T(8,128)(2,1)}), bf16[128,80,128]{2,1,0:T(8,128)(2,1)}, u32[]{:S(2)}, u32[]{:S(2)}) async-start(bf16[128,80,128]{2,1,0:T(8,128)(2,1)} %expert_out.1), calls=%async_computation.3 | async-start | bytes 5242880 | tf_op jit(solution)/shard_map/all_to_all | solution.py:1070
  308.8 133.0 %all-reduce.2.cloned.1.call-start = ((), (), s32[]{:S(2)}) async-start(), calls=%async_computation.6 | async-start | bytes 5242880 | tf_op jit(solution)/shard_map/psum | solution.py:1208
  309.9 3.2 collective-permute-start.32
  311.1 1.9 collective-permute-start.33
  322.0 48.0 %collective-permute-start.34 = (bf16[160,2048]{1,0:T(8,128)(2,1)}, bf16[160,2048]{1,0:T(8,128)(2,1)S(1)}, u32[]{:S(2)}, u32[]{:S(2)}) collective-permute-start(bf16[160,2048]{1,0:T(8,128)(2,1)} %get-tuple-element.256), channel_id=1, source_target_pairs={{0,2},{1,3},{2,4},{3,5},{4,6},{5,7},{6,0},{7,1},{8,10},{9,11},{10,... | collective-permute-start | bytes 1966088 | tf_op jit(solution)/shard_map/ppermute | solution.py:1066
  322.6 48.0 %collective-permute-start.35 = (bf16[160,2048]{1,0:T(8,128)(2,1)}, bf16[160,2048]{1,0:T(8,128)(2,1)}, u32[]{:S(2)}, u32[]{:S(2)}) collective-permute-start(bf16[160,2048]{1,0:T(8,128)(2,1)} %get-tuple-element.257), channel_id=1, source_target_pairs={{0,6},{1,7},{2,0},{3,1},{4,2},{5,3},{6,4},{7,5},{8,14},{9,15},{10,... | collective-permute-start | bytes 1966088 | tf_op jit(solution)/shard_map/ppermute | solution.py:1066
  324.8 45.9 %collective-permute-start.36 = (bf16[160,2048]{1,0:T(8,128)(2,1)}, bf16[160,2048]{1,0:T(8,128)(2,1)}, u32[]{:S(2)}, u32[]{:S(2)}) collective-permute-start(bf16[160,2048]{1,0:T(8,128)(2,1)} %get-tuple-element.258), channel_id=1, source_target_pairs={{0,4},{1,5},{2,6},{3,7},{4,0},{5,1},{6,2},{7,3},{8,12},{9,13},{10,... | collective-permute-start | bytes 1966088 | tf_op jit(solution)/shard_map/ppermute | solution.py:1066
  328.1 16.5 %collective-permute-start.26 = (bf16[512,128]{1,0:T(8,128)(2,1)}, bf16[512,128]{1,0:T(8,128)(2,1)S(1)}, u32[]{:S(2)}, u32[]{:S(2)}) collective-permute-start(bf16[512,128]{1,0:T(8,128)(2,1)} %get-tuple-element.243), channel_id=1, source_target_pairs={{0,32},{8,40},{16,48},{24,56},{32,64},{40,72},{48,80},{56,88},{64,... | collective-permute-start | bytes 393224 | tf_op jit(solution)/shard_map/ppermute | solution.py:1081
  329.5 18.0 %collective-permute-start.27 = (bf16[512,128]{1,0:T(8,128)(2,1)}, bf16[512,128]{1,0:T(8,128)(2,1)S(1)}, u32[]{:S(2)}, u32[]{:S(2)}) collective-permute-start(bf16[512,128]{1,0:T(8,128)(2,1)} %get-tuple-element.244), channel_id=1, source_target_pairs={{0,96},{8,104},{16,112},{24,120},{32,0},{40,8},{48,16},{56,24},{64... | collective-permute-start | bytes 393224 | tf_op jit(solution)/shard_map/ppermute | solution.py:1081
  344.6 11.0 %copy-start.24 = (bf16[512,128]{1,0:T(8,128)(2,1)}, bf16[512,128]{1,0:T(8,128)(2,1)S(1)}, u32[]{:S(2)}) copy-start(bf16[512,128]{1,0:T(8,128)(2,1)S(1)} %collective-permute-done.26.b) | copy-start | bytes 393220
  344.6 11.0 %collective-permute-start.28 = (bf16[512,128]{1,0:T(8,128)(2,1)}, bf16[512,128]{1,0:T(8,128)(2,1)}, u32[]{:S(2)}, u32[]{:S(2)}) collective-permute-start(bf16[512,128]{1,0:T(8,128)(2,1)} %get-tuple-element.245), channel_id=1, source_target_pairs={{0,64},{8,72},{16,80},{24,88},{32,96},{40,104},{48,112},{56,120},{... | collective-permute-start | bytes 393224 | tf_op jit(solution)/shard_map/ppermute | solution.py:1081
  347.6 8.1 %copy-start.25 = (bf16[512,128]{1,0:T(8,128)(2,1)}, bf16[512,128]{1,0:T(8,128)(2,1)S(1)}, u32[]{:S(2)}) copy-start(bf16[512,128]{1,0:T(8,128)(2,1)S(1)} %collective-permute-done.27.c) | copy-start | bytes 393220
  357.4 7.8 %collective-permute-start.31 = (bf16[512,128]{1,0:T(8,128)(2,1)}, bf16[512,128]{1,0:T(8,128)(2,1)S(1)}, u32[]{:S(2)}, u32[]{:S(2)}) collective-permute-start(bf16[512,128]{1,0:T(8,128)(2,1)} %add_last.1.a), channel_id=1, source_target_pairs={{0,32},{8,40},{16,48},{24,56},{32,64},{40,72},{48,80},{56,88},{64,... | collective-permute-start | bytes 393224 | tf_op jit(solution)/shard_map/ppermute | solution.py:1081
  357.6 7.6 %collective-permute-start.30 = (bf16[512,128]{1,0:T(8,128)(2,1)}, bf16[512,128]{1,0:T(8,128)(2,1)S(1)}, u32[]{:S(2)}, u32[]{:S(2)}) collective-permute-start(bf16[512,128]{1,0:T(8,128)(2,1)} %add_last.1.a), channel_id=1, source_target_pairs={{0,64},{8,72},{16,80},{24,88},{32,96},{40,104},{48,112},{56,120},{... | collective-permute-start | bytes 393224 | tf_op jit(solution)/shard_map/ppermute | solution.py:1081
  365.2 5.4 %copy-start.26 = (bf16[512,128]{1,0:T(8,128)(2,1)}, bf16[512,128]{1,0:T(8,128)(2,1)S(1)}, u32[]{:S(2)}) copy-start(bf16[512,128]{1,0:T(8,128)(2,1)S(1)} %collective-permute-done.31.d) | copy-start | bytes 393220
  365.2 4.7 %collective-permute-start.29 = (bf16[512,128]{1,0:T(8,128)(2,1)}, bf16[512,128]{1,0:T(8,128)(2,1)S(1)}, u32[]{:S(2)}, u32[]{:S(2)}) collective-permute-start(bf16[512,128]{1,0:T(8,128)(2,1)} %add_last.1.a), channel_id=1, source_target_pairs={{0,96},{8,104},{16,112},{24,120},{32,0},{40,8},{48,16},{56,24},{64... | collective-permute-start | bytes 393224 | tf_op jit(solution)/shard_map/ppermute | solution.py:1081
  365.2 5.4 %copy-start.27 = (bf16[512,128]{1,0:T(8,128)(2,1)}, bf16[512,128]{1,0:T(8,128)(2,1)S(1)}, u32[]{:S(2)}) copy-start(bf16[512,128]{1,0:T(8,128)(2,1)S(1)} %collective-permute-done.30.c) | copy-start | bytes 393220
  370.6 7.6 %copy-start.7 = (bf16[160,2048]{1,0:T(8,128)(2,1)}, bf16[160,2048]{1,0:T(8,128)(2,1)S(1)}, u32[]{:S(2)}) copy-start(bf16[160,2048]{1,0:T(8,128)(2,1)S(1)} %collective-permute-done.34.b1) | copy-start | bytes 1966084
  372.8 14.5 %collective-permute-start.39 = (bf16[4,512,128]{2,1,0:T(8,128)(2,1)}, bf16[4,512,128]{2,1,0:T(8,128)(2,1)}, u32[]{:S(2)}, u32[]{:S(2)}) collective-permute-start(bf16[4,512,128]{2,1,0:T(8,128)(2,1)} %stack_parts.1.c0), channel_id=1, source_target_pairs={{0,8},{8,16},{16,24},{24,0},{32,40},{40,48},{48,56},{56,32},{64,72... | collective-permute-start | bytes 1572872 | tf_op jit(solution)/shard_map/ppermute | solution.py:1081
  372.8 27.1 %collective-permute-start.38 = (bf16[4,512,128]{2,1,0:T(8,128)(2,1)}, bf16[4,512,128]{2,1,0:T(8,128)(2,1)}, u32[]{:S(2)}, u32[]{:S(2)}) collective-permute-start(bf16[4,512,128]{2,1,0:T(8,128)(2,1)} %stack_parts.1.c0), channel_id=1, source_target_pairs={{0,16},{8,24},{16,0},{24,8},{32,48},{40,56},{48,32},{56,40},{64,80... | collective-permute-start | bytes 1572872 | tf_op jit(solution)/shard_map/ppermute | solution.py:1081
  378.2 23.8 %collective-permute-start.37 = (bf16[4,512,128]{2,1,0:T(8,128)(2,1)}, bf16[4,512,128]{2,1,0:T(8,128)(2,1)}, u32[]{:S(2)}, u32[]{:S(2)}) collective-permute-start(bf16[4,512,128]{2,1,0:T(8,128)(2,1)} %stack_parts.1.c0), channel_id=1, source_target_pairs={{0,24},{8,0},{16,8},{24,16},{32,56},{40,32},{48,40},{56,48},{64,88... | collective-permute-start | bytes 1572872 | tf_op jit(solution)/shard_map/ppermute | solution.py:1081
  382.2 20.7 %all-to-all-start.4 = ((bf16[16,24,128]{2,1,0:T(8,128)(2,1)}), bf16[16,24,128]{2,1,0:T(8,128)(2,1)S(1)}, u32[]{:S(2)}, u32[]{:S(2)}) async-start(bf16[16,24,128]{2,1,0:T(8,128)(2,1)} %get-tuple-element.267), calls=%async_computation.4 | async-start | bytes 196608 | tf_op jit(solution)/shard_map/all_to_all | solution.py:1216
  406.1 36.5 %all-to-all-start.5 = ((bf16[128,24,128]{2,1,0:T(8,128)(2,1)}), bf16[128,24,128]{2,1,0:T(8,128)(2,1)S(1)}, u32[]{:S(2)}, u32[]{:S(2)}) async-start(bf16[128,24,128]{2,1,0:T(8,128)(2,1)} %fold_small.1), calls=%async_computation.5 | async-start | bytes 1572864 | tf_op jit(solution)/shard_map/all_to_all | solution.py:1070
  442.8 6.9 %copy-start.1 = (s32[1,1024]{1,0:T(1,128)S(1)}, s32[1,1024]{1,0:T(1,128)}, u32[]{:S(2)}) copy-start(s32[1,1024]{1,0:T(1,128)} %param.32) | copy-start | bytes 12292
  (17 other events, 27.9 us)
Sparse Core Ops, SparseCore 0:
  313.6 128.1 all-reduce.1

commit v9 on v8

--- a/solution.py
+++ b/solution.py
@@ -1137,23 +1137,20 @@
     wk_t, wv_t = w_key.T, w_value.T
     wk_s, wv_s = sibling(wk_t), sibling(wv_t)
     wq_t = w_query.T
-    wo_s = sibling(w_out)
     wq_ts = sibling(wq_t)
 
+    og_wire = pack(out_grad, assign_t)
+    x_own, x_sib, og_wire, wq_t, cos, sin, info, wk_s, wv_s = lax.optimization_barrier(
+        (x_own, x_sib, og_wire, wq_t, cos, sin, info, wk_s, wv_s)
+    )
+    x_sib += [sibling(x_own[dy]) for dy in (1, 2, 3)]
+    blocks = [side[dy] for dy in range(4) for side in (x_own, x_sib)]
     weights = (g1, wq_t, wk_t, wk_s, wv_t, wv_s, gq, gk, cos, sin)
-    zero = qkv((0,), core_id, (x_own[0], x_sib[0]), *weights)
-    og_wire = pack(out_grad, assign_t)
-    x_own[1], x_own[2], x_own[3], q_first, og_wire = lax.optimization_barrier(
-        (x_own[1], x_own[2], x_own[3], zero[1], og_wire)
-    )
-    x_sib += [sibling(x_own[dy]) for dy in (1, 2, 3)]
-    blocks = [side[dy] for dy in (1, 2, 3) for side in (x_own, x_sib)]
-    others = qkv((1, 2, 3), core_id, blocks, *weights)
-    wkv = zero[7]
-    pieces = [zero[:7], others[:7], others[7:14], others[14:21]]
+    *pieces, wkv = qkv((0, 1, 2, 3), core_id, blocks, *weights)
+    pieces = [pieces[7 * dy : 7 * dy + 7] for dy in range(4)]
     qh, q, kh, k, v, scales, n1 = zip(*pieces)
-    q = (q_first,) + q[1:]
     got_grads = exchange(og_wire)
+    wo_s = sibling(after(w_out, q[0]))
     ot0, ot1, linv, qt, kt, kn, vn = attend(q, k, v, info)
     blocks = outproj(ot0, sibling(ot1), w_out, wo_s)
     blocks = [blocks[0]] + spread(blocks)
@@ -1189,16 +1186,17 @@
     )
     g_own = [gatt] + [from_chip(gatt, dy) for dy in (1, 2, 3)]
     g_sib = [sibling(block) for block in g_own]
+    returned = exchange(after(out_wire, *g_sib))
     *out_parts, dt = pre(where, g_own + g_sib, ot0, ot1, w_out)
 
     dq0, dq1, dkv, ggq, ggk = bwd(
         qh, kh, scales, qt, kt, kn, vn, dt, ot0, ot1, linv, info, cos, sin, gq, gk
     )
-    out_parts, dq1, dkv = lax.optimization_barrier((collect(out_parts, 1), dq1, dkv))
+    out_parts = collect(out_parts, 1)
     router_sib = after(router_sib, dkv)
     dq_sib, dkv_sib = sibling(dq1), sibling(dkv)
     gw, dkv_total = qkv_grad(where, n1_t, dq0, dq1, dkv, dkv_sib)
-    returned = exchange(after(out_wire, dkv_total))
+    returned, dq0, out_parts = lax.optimization_barrier((returned, dq0, out_parts))
     router_rec = sibling(router_sib)
     blocks = normed_grad(
         wq_t, wq_ts, wkv, dq0, dq_sib, dkv_total, n1, gg2, ggq, ggk, router_own, router_rec
@@ -1211,7 +1209,6 @@
     chunks, blocks = lax.optimization_barrier((chunks, blocks))
     chunks = share(stack(chunks), 1)
     grad_input, small = final(blocks, block_input, ghid, g1)
-    small, returned = lax.optimization_barrier((small, returned))
     result = result_rows(expert_list, slot_list, gate_list, returned, hidden)
     small = lax.all_to_all(small, "expert", split_axis=0, concat_axis=0, tiled=True)
     small, chunks = lax.optimization_barrier((small, chunks))

time: 464 us -> 469 us (1.011)
  blocking collectives: 0 us -> 30.3 us
  waiting for transfers between devices: 166 us -> 152 us
  starting transfers between devices: 88.9 us -> 79.2 us
    all_to_all x0 -> x1, blocking collectives: none -> 30.3 us  [on_device(): lax.all_to_all(small, 'expert', split_axis=0, concat_axis=0, tiled=True)]
    psum x1, waiting for transfers between devices: 14.8 us -> 0.01 us  [on_device(): gw = lax.psum(gw, 'expert')]
    all_to_all x5, waiting for transfers between devices: 38 us -> 44.4 us  [exchange(): return lax.all_to_all(x, ALL, split_axis=0, concat_axis=0, tiled=True)]
    ppermute x16, waiting for transfers between devices: 12.6 us -> 6.27 us  [sibling(): return lax.ppermute(x, 'shard', [(i, i ^ 1) for i in range(8)])]
    ppermute x12, waiting for transfers between devices: 55 us -> 49.4 us  [on_expert(): return lax.ppermute(x, 'expert', pairs)]
    ppermute x6, waiting for transfers between devices: 21.1 us -> 26.5 us  [from_chip(): return lax.ppermute(x, 'shard', [(i, (i - 2 * dy) % 8) for i in range(8)])]
    pallas_call x18 -> x17, Pallas kernels: 96.6 us -> 93.9 us  [call(): pl.pallas_call(kernel, out_shape=outs, in_specs=in_specs, out_specs=[pl.B...]
    unnamed x69 -> x73, local copies, waits for them, and re-layouts: 9.62 us -> 8.92 us
  transfers between devices with their start and end apart: 47 -> 46, of which waited for: 24 -> 18; matrix products, arithmetic and copies ran while one was open for 7% -> 7% of each run, Pallas kernels for 23% -> 26%
where the time goes in v9:
time: 469 us; the launch traced here: 459 us
  waiting for transfers between devices  152 us (32%)
  Pallas kernels  145 us (31%)
  starting transfers between devices  79.2 us (17%)
  blocking collectives  30.3 us (6%)
  matrix products  16.6 us (4%)
  local copies, waits for them, and re-layouts  14.7 us (3%)
  between operations  14.7 us (3%)
  other arithmetic  7.42 us (2%)
    pallas_call x17, Pallas kernels, call(): pl.pallas_call(kernel, out_shape=outs, in_specs=in_specs, out_specs=[pl.B...  93.9 us
    ppermute x12, waiting for transfers between devices, on_expert(): return lax.ppermute(x, 'expert', pairs)  49.4 us
    all_to_all x5, waiting for transfers between devices, exchange(): return lax.all_to_all(x, ALL, split_axis=0, concat_axis=0, tiled=True)  44.4 us
    all_to_all x5, starting transfers between devices, exchange(): return lax.all_to_all(x, ALL, split_axis=0, concat_axis=0, tiled=True)  36.5 us
    all_to_all x1, blocking collectives, on_device(): lax.all_to_all(small, 'expert', split_axis=0, concat_axis=0, tiled=True)  30.3 us
    ppermute x6, waiting for transfers between devices, from_chip(): return lax.ppermute(x, 'shard', [(i, (i - 2 * dy) % 8) for i in range(8)])  26.5 us
    pallas_call x4, Pallas kernels, grid_call(): pl.pallas_call(kernel, out_shape=outs, grid_spec=pltpu.PrefetchScalarGrid...  26.1 us
    ppermute x6, waiting for transfers between devices, to_chip(): return lax.ppermute(x, 'shard', [(i, (i + 2 * dy) % 8) for i in range(8)])  25.1 us
  transfers between devices with their start and end apart: 46, of which 18 were waited for; matrix products, arithmetic and copies ran while one was open for 7% of the time, Pallas kernels for 26%

profile of v9, /device:TPU:1, one launch (start us, length us, event | category | flops | bytes accessed | tf_op | source)
XLA Modules:
  0.0 459.3 jit_solution(8012468359750309541)
XLA Ops:
  7.2 1.5 collective-permute-start.3
  10.1 2.6 collective-permute-start.1
  17.7 2.0 route_tables.1
  21.0 4.2 pack_rows.1
  25.2 3.9 copy.39
  29.1 1.8 multiply_sine_fusion
  31.0 5.3 %collective-permute-done.1.refs_5_ = bf16[128,2048]{1,0:T(8,128)(2,1)} collective-permute-done((bf16[128,2048]{1,0:T(8,128)(2,1)}, bf16[128,2048]{1,0:T(8,128)(2,1)}, u32[]{:S(2)}, u32[]{:S(2)}) %collective-permute-start.1) | collective-permute-done | bytes 524320 | tf_op jit(solution)/shard_map/ppermute | solution.py:1062
  37.7 9.8 %all-to-all-start.1 = ((bf16[128,88,128]{2,1,0:T(8,128)(2,1)}), bf16[128,88,128]{2,1,0:T(8,128)(2,1)}, u32[]{:S(2)}, u32[]{:S(2)}) async-start(bf16[128,88,128]{2,1,0:T(8,128)(2,1)} %pack_rows.1), calls=%async_computation.1 | async-start | bytes 5767168 | tf_op jit(solution)/shard_map/all_to_all | solution.py:1070
  48.8 9.8 %qkv0123.1 = (bf16[512,256]{1,0:T(8,128)(2,1)}, bf16[512,256]{1,0:T(8,128)(2,1)}, bf16[128,256]{1,0:T(8,128)(2,1)}, bf16[128,256]{1,0:T(8,128)(2,1)}, bf16[128,2...) custom-call(s32[1]{0:T(128)} %bitcast.2.refs_0_, ...), custom_call_target="tpu_custom_call" | custom-call | flops 1 | bytes 1 | tf_op jit(solution)/shard_map/qkv0123/pallas_call | solution.py:61
  58.6 1.4 collective-permute-start.10
  60.0 7.1 %attend.1 = (bf16[512,512]{1,0:T(8,128)(2,1)}, bf16[512,512]{1,0:T(8,128)(2,1)}, f32[8,1024]{1,0:T(8,128)}, bf16[512,1024]{1,0:T(8,128)(2,1)}, bf16[128,1024]{1,...) custom-call(bf16[512,256]{1,0:T(8,128)(2,1)} %get-tuple-element.169.refs_0_, ...), custom_call_target="tpu_custom_call" | custom-call | flops 1 | bytes 6600001 | tf_op jit(solution)/shard_map/attend/pallas_call | solution.py:61
  67.1 2.1 collective-permute-done.9.otr
  70.0 5.6 %out_projection.1 = (bf16[128,2048]{1,0:T(8,128)(2,1)}, bf16[128,2048]{1,0:T(8,128)(2,1)}, bf16[128,2048]{1,0:T(8,128)(2,1)}, bf16[128,2048]{1,0:T(8,128)(2,1)}) custom-call(bf16[512,512]{1,0:T(8,128)(2,1)} %get-tuple-element.182.ot0.refs_8_.refs_17_, bf16[512,512]{1,0:T(8,128)(2,1)} %copy-done.9, bf16[512,2048]{1,0:T(8,128)(2,1)} %refs_10_.1, ...), custom_call_target="tpu_custom_call" | custom-call | flops 1 | bytes 3000001 | tf_op jit(solution)/shard_map/out_projection/pallas_call | solution.py:74
  76.3 2.0 collective-permute-start.12
  79.8 25.1 %collective-permute-done.11.b1 = bf16[128,2048]{1,0:T(8,128)(2,1)S(1)} collective-permute-done((bf16[128,2048]{1,0:T(8,128)(2,1)}, bf16[128,2048]{1,0:T(8,128)(2,1)S(1)}, u32[]{:S(2)}, u32[]{:S(2)}) %collective-permute-start.11) | collective-permute-done | bytes 524320 | tf_op jit(solution)/shard_map/ppermute | solution.py:1066
  105.7 5.6 %router.1 = (f32[128,2048]{1,0:T(8,128)}, bf16[128,2048]{1,0:T(8,128)(2,1)}, f32[128,128]{1,0:T(8,128)}, f32[128,128]{1,0:T(8,128)}, bf16[128,88,128]{2,1,0:T(8,128)(2,1)}) custom-call(bf16[128,2048]{1,0:T(8,128)(2,1)} %get-tuple-element.185.b0, bf16[128,2048]{1,0:T(8,128)(2,1)} %copy-done.14, bf16[128,2048]{1,0:T(8,128)(2,1)} %collective-permute-done.12.b2, ...), custom_call_target="tpu_custom_call" | custom-call | flops 1 | bytes 3600001 | tf_op jit(solution)/shard_map/router/pallas_call | solution.py:61
  111.4 6.5 %all-to-all-start = ((bf16[128,88,128]{2,1,0:T(8,128)(2,1)}), bf16[128,88,128]{2,1,0:T(8,128)(2,1)}, u32[]{:S(2)}, u32[]{:S(2)}) async-start(bf16[128,88,128]{2,1,0:T(8,128)(2,1)} %get-tuple-element.190), calls=%async_computation | async-start | bytes 5767168 | tf_op jit(solution)/shard_map/all_to_all | solution.py:1070
  119.1 7.9 %expert_grad_rows.1 = (bf16[640,2048]{1,0:T(8,128)(2,1)}, f32[640,768]{1,0:T(8,128)}) custom-call(bf16[128,88,128]{2,1,0:T(8,128)(2,1)} %all-to-all-done.1.wire, bf16[768,2048]{1,0:T(8,128)(2,1)} %bitcast.69), custom_call_target="tpu_custom_call" | custom-call | flops 1 | bytes 4800001 | tf_op jit(solution)/shard_map/expert_grad_rows/pallas_call | solution.py:61
  127.0 5.5 %transpose_rows.1.n1t = bf16[2048,1024]{1,0:T(8,128)(2,1)} custom-call(bf16[256,2048]{1,0:T(8,128)(2,1)} %get-tuple-element.195.n0, bf16[256,2048]{1,0:T(8,128)(2,1)} %get-tuple-element.196.n1, bf16[256,2048]{1,0:T(8,128)(2,1)} %get-tuple-element.197.n2, bf16[256,2048]{1,0:T(8,128)(2,1)} %get-tuple-element.198.n3), custom_call_target="tpu_custom_call" | custom-call | flops 1 | bytes 3600001 | tf_op jit(solution)/shard_map/transpose_rows/pallas_call | solution.py:61
  133.1 23.5 %all-to-all-done.wire = bf16[128,88,128]{2,1,0:T(8,128)(2,1)} async-done(((bf16[128,88,128]{2,1,0:T(8,128)(2,1)}), bf16[128,88,128]{2,1,0:T(8,128)(2,1)}, u32[]{:S(2)}, u32[]{:S(2)}) %all-to-all-start) | async-done | bytes 2883616 | tf_op jit(solution)/shard_map/all_to_all | solution.py:1070
  156.6 15.9 %expert_main.1 = (bf16[128,88,128]{2,1,0:T(8,128)(2,1)}, bf16[640,2048]{1,0:T(8,128)(2,1)}, bf16[640,768]{1,0:T(8,128)(2,1)}, bf16[640,768]{1,0:T(8,128)(2,1)}, ...) custom-call(bf16[128,88,128]{2,1,0:T(8,128)(2,1)} %all-to-all-done.wire, bf16[2048,768]{1,0:T(8,128)(2,1)} %bitcast.73, ...), custom_call_target="tpu_custom_call" | custom-call | flops 1 | bytes 10800001 | tf_op jit(solution)/shard_map/expert_main/pallas_call | solution.py:564
  172.5 5.9 %all-to-all-start.2 = ((bf16[128,88,128]{2,1,0:T(8,128)(2,1)}), bf16[128,88,128]{2,1,0:T(8,128)(2,1)}, u32[]{:S(2)}, u32[]{:S(2)}) async-start(bf16[128,88,128]{2,1,0:T(8,128)(2,1)} %get-tuple-element.223), calls=%async_computation.2 | async-start | bytes 5767168 | tf_op jit(solution)/shard_map/all_to_all | solution.py:1070
  180.6 6.5 %expert_out.1 = bf16[128,80,128]{2,1,0:T(8,128)(2,1)} custom-call(bf16[640,768]{1,0:T(8,128)(2,1)} %get-tuple-element.229.act, bf16[768,2048]{1,0:T(8,128)(2,1)} %bitcast.70), custom_call_target="tpu_custom_call" | custom-call | flops 1 | bytes 4200001 | tf_op jit(solution)/shard_map/expert_out/pallas_call | solution.py:61
  187.1 7.5 %fusion.7 = f32[2048,768]{1,0:T(8,128)} fusion(bf16[640,2048]{1,0:T(8,128)(2,1)} %get-tuple-element.230, bf16[640,768]{1,0:T(8,128)(2,1)} %get-tuple-element.231), kind=kOutput, calls=%fused_computation.32 | convolution fusion | flops 2013265920 | bytes 9895936 | tf_op jit(solution)/shard_map/dot_general | solution.py:1174
  194.6 4.6 fusion.8
  199.2 4.5 fusion.9
  203.7 13.4 %all-to-all-done.2.wire = bf16[128,88,128]{2,1,0:T(8,128)(2,1)} async-done(((bf16[128,88,128]{2,1,0:T(8,128)(2,1)}), bf16[128,88,128]{2,1,0:T(8,128)(2,1)}, u32[]{:S(2)}, u32[]{:S(2)}) %all-to-all-start.2) | async-done | bytes 2883616 | tf_op jit(solution)/shard_map/all_to_all | solution.py:1070
  217.1 7.1 %combine_grads.1 = (f32[128,2048]{1,0:T(8,128)}, bf16[128,2048]{1,0:T(8,128)(2,1)}, bf16[4,256,128]{2,1,0:T(8,128)(2,1)}, bf16[4,256,128]{2,1,0:T(8,128)(2,1)}, f32[1,2048]{1,0:T(1,128)}) custom-call(s32[4]{0:T(128)} %pad_add_fusion.where, s32[512]{0:T(512)} %reshape.212.experts, s32[512]{0:T(512)} %reshape.213.slots, f32[512]{0:T(512)} %reshape.211.gate_list, ...), custom_call_target="tpu_custom_call" | custom-call | flops 1 | bytes 4200001 | tf_op jit(solution)/shard_map/combine_grads/pallas_call | solution.py:61
  225.1 1.8 collective-permute-start.15
  226.9 1.4 collective-permute-start.18
  228.3 21.1 %collective-permute-done.17.refs_3_ = bf16[128,2048]{1,0:T(8,128)(2,1)S(1)} collective-permute-done((bf16[128,2048]{1,0:T(8,128)(2,1)}, bf16[128,2048]{1,0:T(8,128)(2,1)S(1)}, u32[]{:S(2)}, u32[]{:S(2)}) %collective-permute-start.17) | collective-permute-done | bytes 524320 | tf_op jit(solution)/shard_map/ppermute | solution.py:1062
  249.4 1.8 collective-permute-start.21
  252.7 1.5 collective-permute-done.20.refs_6_
  255.1 4.8 %all-to-all-start.3 = ((bf16[128,80,128]{2,1,0:T(8,128)(2,1)}), bf16[128,80,128]{2,1,0:T(8,128)(2,1)}, u32[]{:S(2)}, u32[]{:S(2)}) async-start(bf16[128,80,128]{2,1,0:T(8,128)(2,1)} %expert_out.1), calls=%async_computation.3 | async-start | bytes 5242880 | tf_op jit(solution)/shard_map/all_to_all | solution.py:1070
  260.4 8.8 %out_projection_grad.1 = (bf16[4,512,128]{2,1,0:T(8,128)(2,1)}, bf16[4,512,128]{2,1,0:T(8,128)(2,1)}, bf16[4,512,128]{2,1,0:T(8,128)(2,1)}, bf16[4,512,128]{2,1,0:T(8,128)(2,1)}, bf16[512,1024]{1,0:T(8,128)(2,1)}) custom-call(s32[4]{0:T(128)} %pad_add_fusion.where, bf16[128,2048]{1,0:T(8,128)(2,1)} %get-tuple-element.239.refs_0_, ...), custom_call_target="tpu_custom_call" | custom-call | flops 1 | bytes 4200001 | tf_op jit(solution)/shard_map/out_projection_grad/pallas_call | solution.py:93
  269.2 16.9 %attend_grad.1 = (bf16[512,512]{1,0:T(8,128)(2,1)}, bf16[512,512]{1,0:T(8,128)(2,1)}, bf16[256,1024]{1,0:T(8,128)(2,1)}, f32[8,128]{1,0:T(8,128)}, f32[8,128]{1,0:T(8,128)}) custom-call(bf16[512,256]{1,0:T(8,128)(2,1)} %get-tuple-element.204.refs_0_, bf16[512,256]{1,0:T(8,128)(2,1)} %get-tuple-element.205.refs_1_, ...), custom_call_target="tpu_custom_call" | custom-call | flops 1 | bytes 1 | tf_op jit(solution)/shard_map/attend_grad/pallas_call | solution.py:61
  287.4 1.7 collective-permute-done.22.sib
  290.0 7.9 %qkv_weight_grad.1 = (bf16[2048,640]{1,0:T(8,128)(2,1)}, bf16[256,1024]{1,0:T(8,128)(2,1)}) custom-call(s32[4]{0:T(128)} %pad_add_fusion.where, bf16[2048,1024]{1,0:T(8,128)(2,1)} %transpose_rows.1.n1t, bf16[512,512]{1,0:T(8,128)(2,1)} %get-tuple-element.262.dq0, bf16[512,512]{1,0:T(8,128)(2,1)} %get-tuple-element.243.dq1, ...), custom_call_target="tpu_custom_call" | custom-call | flops 1 | bytes 1 | tf_op jit(solution)/shard_map/qkv_weight_grad/pallas_call | solution.py:74
  298.4 2.2 collective-permute-start.24
  302.7 12.1 %collective-permute-done.23.b = bf16[4,512,128]{2,1,0:T(8,128)(2,1)S(1)} collective-permute-done((bf16[4,512,128]{2,1,0:T(8,128)(2,1)}, bf16[4,512,128]{2,1,0:T(8,128)(2,1)S(1)}, u32[]{:S(2)}, u32[]{:S(2)}) %collective-permute-start.23) | collective-permute-done | bytes 524320 | tf_op jit(solution)/shard_map/ppermute | solution.py:1081
  314.8 1.6 collective-permute-done.24.c
  316.4 18.1 %collective-permute-done.25.d = bf16[4,512,128]{2,1,0:T(8,128)(2,1)S(1)} collective-permute-done((bf16[4,512,128]{2,1,0:T(8,128)(2,1)}, bf16[4,512,128]{2,1,0:T(8,128)(2,1)S(1)}, u32[]{:S(2)}, u32[]{:S(2)}) %collective-permute-start.25) | collective-permute-done | bytes 524320 | tf_op jit(solution)/shard_map/ppermute | solution.py:1081
  335.6 8.1 %normed_grad.1 = (bf16[160,2048]{1,0:T(8,128)(2,1)}, bf16[160,2048]{1,0:T(8,128)(2,1)}, bf16[160,2048]{1,0:T(8,128)(2,1)}, bf16[160,2048]{1,0:T(8,128)(2,1)}) custom-call(bf16[512,2048]{1,0:T(8,128)(2,1)} %bitcast.5.refs_10_.wa, bf16[512,2048]{1,0:T(8,128)(2,1)} %collective-permute-done.14.wb, bf16[256,2048]{1,0:T(8,128)(2,1)} %get-tuple-element.261.wkv, ...), custom_call_target="tpu_custom_call" | custom-call | flops 1 | bytes 1 | tf_op jit(solution)/shard_map/normed_grad/pallas_call | solution.py:74
  344.9 1.4 collective-permute-start.35
  346.4 1.6 collective-permute-start.36
  348.0 2.4 add_parts.1
  350.4 1.5 collective-permute-start.26
  351.9 1.7 collective-permute-start.27
  353.7 3.5 collective-permute-done.26.b
  358.5 4.3 collective-permute-done.28.d
  362.8 1.8 add_last.1.a
  364.6 2.6 collective-permute-start.30
  367.2 3.8 collective-permute-done.31.d
  371.9 5.1 %collective-permute-done.29.b = bf16[512,128]{1,0:T(8,128)(2,1)S(1)} collective-permute-done((bf16[512,128]{1,0:T(8,128)(2,1)}, bf16[512,128]{1,0:T(8,128)(2,1)S(1)}, u32[]{:S(2)}, u32[]{:S(2)}) %collective-permute-start.29) | collective-permute-done | bytes 131104 | tf_op jit(solution)/shard_map/ppermute | solution.py:1081
  377.7 2.1 stack_parts.1.c0
  379.8 1.5 collective-permute-start.38
  382.7 4.0 input_grad.1
  386.7 30.3 %all_to_all.30.parts = bf16[16,24,128]{2,1,0:T(8,128)(2,1)} all-to-all(bf16[16,24,128]{2,1,0:T(8,128)(2,1)} %get-tuple-element.279), channel_id=1, replica_groups=mesh['expert'=16,'shard'=8] {'expert'}, dimensions={0} | all-to-all | bytes 196608 | tf_op jit(solution)/shard_map/all_to_all | solution.py:1213
  417.0 2.5 fold_small.1
  419.5 9.5 %all-to-all-start.5 = ((bf16[128,24,128]{2,1,0:T(8,128)(2,1)}), bf16[128,24,128]{2,1,0:T(8,128)(2,1)S(1)}, u32[]{:S(2)}, u32[]{:S(2)}) async-start(bf16[128,24,128]{2,1,0:T(8,128)(2,1)} %fold_small.1), calls=%async_computation.5 | async-start | bytes 1572864 | tf_op jit(solution)/shard_map/all_to_all | solution.py:1070
  429.0 4.5 result.1
  433.5 4.1 place_output_grads.1
  437.6 7.5 %all-to-all-done.5 = bf16[128,24,128]{2,1,0:T(8,128)(2,1)S(1)} async-done(((bf16[128,24,128]{2,1,0:T(8,128)(2,1)}), bf16[128,24,128]{2,1,0:T(8,128)(2,1)S(1)}, u32[]{:S(2)}, u32[]{:S(2)}) %all-to-all-start.5) | async-done | bytes 786464 | tf_op jit(solution)/shard_map/all_to_all | solution.py:1070
  447.6 4.6 widen_grads.1
  (157 shorter events, 35.9 us)
Async XLA Ops:
  7.2 8.4 %copy-start = (s32[1,1024]{1,0:T(1,128)S(1)}, s32[1,1024]{1,0:T(1,128)}, u32[]{:S(2)}) copy-start(s32[1,1024]{1,0:T(1,128)} %param.32) | copy-start | bytes 12292
  7.2 23.7 %collective-permute-start.3 = (bf16[128,2048]{1,0:T(8,128)(2,1)}, bf16[128,2048]{1,0:T(8,128)(2,1)S(1)}, u32[]{:S(2)}, u32[]{:S(2)}) collective-permute-start(bf16[128,2048]{1,0:T(8,128)(2,1)} %x0.3), channel_id=1, source_target_pairs={{0,1},{1,0},{2,3},{3,2},{4,5},{5,4},{6,7},{7,6},{8,9},{9,8},{10,11... | collective-permute-start | bytes 1572872 | tf_op jit(solution)/shard_map/ppermute | solution.py:1058
  8.7 22.2 %collective-permute-start.2 = (bf16[128,2048]{1,0:T(8,128)(2,1)}, bf16[128,2048]{1,0:T(8,128)(2,1)}, u32[]{:S(2)}, u32[]{:S(2)}) collective-permute-start(bf16[128,2048]{1,0:T(8,128)(2,1)} %x0.3), channel_id=1, source_target_pairs={{0,2},{1,3},{2,4},{3,5},{4,6},{5,7},{6,0},{7,1},{8,10},{9,11},{10,... | collective-permute-start | bytes 1572872 | tf_op jit(solution)/shard_map/ppermute | solution.py:1062
  10.1 26.2 %collective-permute-start.1 = (bf16[128,2048]{1,0:T(8,128)(2,1)}, bf16[128,2048]{1,0:T(8,128)(2,1)}, u32[]{:S(2)}, u32[]{:S(2)}) collective-permute-start(bf16[128,2048]{1,0:T(8,128)(2,1)} %x0.3), channel_id=1, source_target_pairs={{0,4},{1,5},{2,6},{3,7},{4,0},{5,1},{6,2},{7,3},{8,12},{9,13},{10,... | collective-permute-start | bytes 1572872 | tf_op jit(solution)/shard_map/ppermute | solution.py:1062
  12.7 23.6 %collective-permute-start = (bf16[128,2048]{1,0:T(8,128)(2,1)}, bf16[128,2048]{1,0:T(8,128)(2,1)}, u32[]{:S(2)}, u32[]{:S(2)}) collective-permute-start(bf16[128,2048]{1,0:T(8,128)(2,1)} %x0.3), channel_id=1, source_target_pairs={{0,6},{1,7},{2,0},{3,1},{4,2},{5,3},{6,4},{7,5},{8,14},{9,15},{10,... | collective-permute-start | bytes 1572872 | tf_op jit(solution)/shard_map/ppermute | solution.py:1062
  13.8 3.9 collective-permute-start.4
  17.7 11.4 %copy-start.22 = (bf16[64,2048]{1,0:T(8,128)(2,1)}, bf16[64,2048]{1,0:T(8,128)(2,1)S(1)}, u32[]{:S(2)}) copy-start(bf16[64,2048]{1,0:T(8,128)(2,1)S(1)} %collective-permute-done.4.refs_12_) | copy-start | bytes 786436
  17.7 13.2 %collective-permute-start.5 = (bf16[64,2048]{1,0:T(8,128)(2,1)}, bf16[64,2048]{1,0:T(8,128)(2,1)}, u32[]{:S(2)}, u32[]{:S(2)}) collective-permute-start(bf16[64,2048]{1,0:T(8,128)(2,1)} %bitcast.79), channel_id=1, source_target_pairs={{0,1},{1,0},{2,3},{3,2},{4,5},{5,4},{6,7},{7,6},{8,9},{9,8},{10,11... | collective-permute-start | bytes 786440 | tf_op jit(solution)/shard_map/ppermute | solution.py:1058
  30.9 6.8 %copy-start.6 = (bf16[128,2048]{1,0:T(8,128)(2,1)}, bf16[128,2048]{1,0:T(8,128)(2,1)S(1)}, u32[]{:S(2)}) copy-start(bf16[128,2048]{1,0:T(8,128)(2,1)S(1)} %collective-permute-done.3.refs_2_) | copy-start | bytes 1572868
  36.3 11.3 %copy-start.29 = (bf16[2048]{0:T(1024)(128)(2,1)S(1)}, bf16[2048]{0:T(1024)(128)(2,1)}, u32[]{:S(2)}) copy-start(bf16[2048]{0:T(1024)(128)(2,1)} %param.19) | copy-start | bytes 12292
  36.3 11.9 %copy-start.31 = (bf16[128]{0:T(256)(128)(2,1)S(1)}, bf16[128]{0:T(256)(128)(2,1)}, u32[]{:S(2)}) copy-start(bf16[128]{0:T(256)(128)(2,1)} %param.24) | copy-start | bytes 772
  36.3 11.9 %copy-start.32 = (bf16[128]{0:T(256)(128)(2,1)S(1)}, bf16[128]{0:T(256)(128)(2,1)}, u32[]{:S(2)}) copy-start(bf16[128]{0:T(256)(128)(2,1)} %param.23) | copy-start | bytes 772
  36.3 12.5 %collective-permute-start.6 = (bf16[128,2048]{1,0:T(8,128)(2,1)}, bf16[128,2048]{1,0:T(8,128)(2,1)}, u32[]{:S(2)}, u32[]{:S(2)}) collective-permute-start(bf16[128,2048]{1,0:T(8,128)(2,1)} %collective-permute-done.refs_3_), channel_id=1, source_target_pairs={{0,1},{1,0},{2,3},{3,2},{4,5},{5,4},{6,7},{7,6},{8,9},{9,8},{10,11... | collective-permute-start | bytes 1572872 | tf_op jit(solution)/shard_map/ppermute | solution.py:1058
  37.2 11.6 %collective-permute-start.7 = (bf16[128,2048]{1,0:T(8,128)(2,1)}, bf16[128,2048]{1,0:T(8,128)(2,1)}, u32[]{:S(2)}, u32[]{:S(2)}) collective-permute-start(bf16[128,2048]{1,0:T(8,128)(2,1)} %collective-permute-done.1.refs_5_), channel_id=1, source_target_pairs={{0,1},{1,0},{2,3},{3,2},{4,5},{5,4},{6,7},{7,6},{8,9},{9,8},{10,11... | collective-permute-start | bytes 1572872 | tf_op jit(solution)/shard_map/ppermute | solution.py:1058
  37.3 11.5 %collective-permute-start.8 = (bf16[128,2048]{1,0:T(8,128)(2,1)}, bf16[128,2048]{1,0:T(8,128)(2,1)}, u32[]{:S(2)}, u32[]{:S(2)}) collective-permute-start(bf16[128,2048]{1,0:T(8,128)(2,1)} %collective-permute-done.2.refs_7_), channel_id=1, source_target_pairs={{0,1},{1,0},{2,3},{3,2},{4,5},{5,4},{6,7},{7,6},{8,9},{9,8},{10,11... | collective-permute-start | bytes 1572872 | tf_op jit(solution)/shard_map/ppermute | solution.py:1058
  37.7 73.6 %all-to-all-start.1 = ((bf16[128,88,128]{2,1,0:T(8,128)(2,1)}), bf16[128,88,128]{2,1,0:T(8,128)(2,1)}, u32[]{:S(2)}, u32[]{:S(2)}) async-start(bf16[128,88,128]{2,1,0:T(8,128)(2,1)} %pack_rows.1), calls=%async_computation.1 | async-start | bytes 5767168 | tf_op jit(solution)/shard_map/all_to_all | solution.py:1070
  58.6 10.6 %collective-permute-start.10 = (bf16[512,2048]{1,0:T(8,128)(2,1)}, bf16[512,2048]{1,0:T(8,128)(2,1)}, u32[]{:S(2)}, u32[]{:S(2)}) collective-permute-start(bf16[512,2048]{1,0:T(8,128)(2,1)} %refs_10_.1), channel_id=1, source_target_pairs={{0,1},{1,0},{2,3},{3,2},{4,5},{5,4},{6,7},{7,6},{8,9},{9,8},{10,11... | collective-permute-start | bytes 6291464 | tf_op jit(solution)/shard_map/ppermute | solution.py:1058
  67.1 2.1 collective-permute-start.9
  70.0 9.2 %copy-start.30 = (bf16[2048]{0:T(1024)(128)(2,1)S(1)}, bf16[2048]{0:T(1024)(128)(2,1)}, u32[]{:S(2)}) copy-start(bf16[2048]{0:T(1024)(128)(2,1)} %param.26) | copy-start | bytes 12292
  75.6 29.3 %collective-permute-start.11 = (bf16[128,2048]{1,0:T(8,128)(2,1)}, bf16[128,2048]{1,0:T(8,128)(2,1)S(1)}, u32[]{:S(2)}, u32[]{:S(2)}) collective-permute-start(bf16[128,2048]{1,0:T(8,128)(2,1)} %get-tuple-element.186), channel_id=1, source_target_pairs={{0,2},{1,3},{2,4},{3,5},{4,6},{5,7},{6,0},{7,1},{8,10},{9,11},{10,... | collective-permute-start | bytes 1572872 | tf_op jit(solution)/shard_map/ppermute | solution.py:1066
  76.3 28.7 %collective-permute-start.12 = (bf16[128,2048]{1,0:T(8,128)(2,1)}, bf16[128,2048]{1,0:T(8,128)(2,1)}, u32[]{:S(2)}, u32[]{:S(2)}) collective-permute-start(bf16[128,2048]{1,0:T(8,128)(2,1)} %get-tuple-element.187), channel_id=1, source_target_pairs={{0,6},{1,7},{2,0},{3,1},{4,2},{5,3},{6,4},{7,5},{8,14},{9,15},{10,... | collective-permute-start | bytes 1572872 | tf_op jit(solution)/shard_map/ppermute | solution.py:1066
  78.3 26.7 %collective-permute-start.13 = (bf16[128,2048]{1,0:T(8,128)(2,1)}, bf16[128,2048]{1,0:T(8,128)(2,1)}, u32[]{:S(2)}, u32[]{:S(2)}) collective-permute-start(bf16[128,2048]{1,0:T(8,128)(2,1)} %get-tuple-element.188), channel_id=1, source_target_pairs={{0,4},{1,5},{2,6},{3,7},{4,0},{5,1},{6,2},{7,3},{8,12},{9,13},{10,... | collective-permute-start | bytes 1572872 | tf_op jit(solution)/shard_map/ppermute | solution.py:1066
  111.4 45.2 %all-to-all-start = ((bf16[128,88,128]{2,1,0:T(8,128)(2,1)}), bf16[128,88,128]{2,1,0:T(8,128)(2,1)}, u32[]{:S(2)}, u32[]{:S(2)}) async-start(bf16[128,88,128]{2,1,0:T(8,128)(2,1)} %get-tuple-element.190), calls=%async_computation | async-start | bytes 5767168 | tf_op jit(solution)/shard_map/all_to_all | solution.py:1070
  117.9 15.3 %collective-permute-start.14 = (bf16[512,2048]{1,0:T(8,128)(2,1)}, bf16[512,2048]{1,0:T(8,128)(2,1)}, u32[]{:S(2)}, u32[]{:S(2)}) collective-permute-start(bf16[512,2048]{1,0:T(8,128)(2,1)} %bitcast.5.refs_10_.wa), channel_id=1, source_target_pairs={{0,1},{1,0},{2,3},{3,2},{4,5},{5,4},{6,7},{7,6},{8,9},{9,8},{10,11... | collective-permute-start | bytes 6291464 | tf_op jit(solution)/shard_map/ppermute | solution.py:1058
  127.0 5.5 %copy-start.21 = (f32[128,128]{1,0:T(8,128)S(1)}, f32[128,128]{1,0:T(8,128)}, u32[]{:S(2)}) copy-start(f32[128,128]{1,0:T(8,128)} %get-tuple-element.202.gates) | copy-start | bytes 196612
  172.5 5.9 %copy-start.3 = (s32[128,128]{1,0:T(8,128)S(1)}, s32[128,128]{1,0:T(8,128)}, u32[]{:S(2)}) copy-start(s32[128,128]{1,0:T(8,128)} %get-tuple-element.189.ids) | copy-start | bytes 196612
  172.5 44.6 %all-to-all-start.2 = ((bf16[128,88,128]{2,1,0:T(8,128)(2,1)}), bf16[128,88,128]{2,1,0:T(8,128)(2,1)}, u32[]{:S(2)}, u32[]{:S(2)}) async-start(bf16[128,88,128]{2,1,0:T(8,128)(2,1)} %get-tuple-element.223), calls=%async_computation.2 | async-start | bytes 5767168 | tf_op jit(solution)/shard_map/all_to_all | solution.py:1070
  187.1 7.5 %copy-start.33 = (bf16[640,2048]{1,0:T(8,128)(2,1)S(1)}, bf16[640,2048]{1,0:T(8,128)(2,1)}, u32[]{:S(2)}) copy-start(bf16[640,2048]{1,0:T(8,128)(2,1)} %get-tuple-element.230) | copy-start | bytes 7864324
  187.1 7.5 %copy-start.34 = (bf16[640,768]{1,0:T(8,128)(2,1)S(1)}, bf16[640,768]{1,0:T(8,128)(2,1)}, u32[]{:S(2)}) copy-start(bf16[640,768]{1,0:T(8,128)(2,1)} %get-tuple-element.232) | copy-start | bytes 2949124
  224.2 25.2 %collective-permute-start.17 = (bf16[128,2048]{1,0:T(8,128)(2,1)}, bf16[128,2048]{1,0:T(8,128)(2,1)S(1)}, u32[]{:S(2)}, u32[]{:S(2)}) collective-permute-start(bf16[128,2048]{1,0:T(8,128)(2,1)} %get-tuple-element.239.refs_0_), channel_id=1, source_target_pairs={{0,2},{1,3},{2,4},{3,5},{4,6},{5,7},{6,0},{7,1},{8,10},{9,11},{10,... | collective-permute-start | bytes 1572872 | tf_op jit(solution)/shard_map/ppermute | solution.py:1062
  224.2 27.0 %collective-permute-start.16 = (bf16[128,2048]{1,0:T(8,128)(2,1)}, bf16[128,2048]{1,0:T(8,128)(2,1)S(1)}, u32[]{:S(2)}, u32[]{:S(2)}) collective-permute-start(bf16[128,2048]{1,0:T(8,128)(2,1)} %get-tuple-element.239.refs_0_), channel_id=1, source_target_pairs={{0,4},{1,5},{2,6},{3,7},{4,0},{5,1},{6,2},{7,3},{8,12},{9,13},{10,... | collective-permute-start | bytes 1572872 | tf_op jit(solution)/shard_map/ppermute | solution.py:1062
  225.1 26.2 %collective-permute-start.15 = (bf16[128,2048]{1,0:T(8,128)(2,1)}, bf16[128,2048]{1,0:T(8,128)(2,1)S(1)}, u32[]{:S(2)}, u32[]{:S(2)}) collective-permute-start(bf16[128,2048]{1,0:T(8,128)(2,1)} %get-tuple-element.239.refs_0_), channel_id=1, source_target_pairs={{0,6},{1,7},{2,0},{3,1},{4,2},{5,3},{6,4},{7,5},{8,14},{9,15},{10,... | collective-permute-start | bytes 1572872 | tf_op jit(solution)/shard_map/ppermute | solution.py:1062
  226.9 24.9 %collective-permute-start.18 = (bf16[128,2048]{1,0:T(8,128)(2,1)}, bf16[128,2048]{1,0:T(8,128)(2,1)S(1)}, u32[]{:S(2)}, u32[]{:S(2)}) collective-permute-start(bf16[128,2048]{1,0:T(8,128)(2,1)} %get-tuple-element.239.refs_0_), channel_id=1, source_target_pairs={{0,1},{1,0},{2,3},{3,2},{4,5},{5,4},{6,7},{7,6},{8,9},{9,8},{10,11... | collective-permute-start | bytes 1572872 | tf_op jit(solution)/shard_map/ppermute | solution.py:1058
  249.4 5.7 %copy-start.15 = (bf16[128,2048]{1,0:T(8,128)(2,1)}, bf16[128,2048]{1,0:T(8,128)(2,1)S(1)}, u32[]{:S(2)}) copy-start(bf16[128,2048]{1,0:T(8,128)(2,1)S(1)} %collective-permute-done.17.refs_3_) | copy-start | bytes 1572868
  249.4 3.3 collective-permute-start.21
  251.2 3.0 collective-permute-start.20
  251.3 3.8 collective-permute-start.19
  255.1 79.4 %all-to-all-start.3 = ((bf16[128,80,128]{2,1,0:T(8,128)(2,1)}), bf16[128,80,128]{2,1,0:T(8,128)(2,1)}, u32[]{:S(2)}, u32[]{:S(2)}) async-start(bf16[128,80,128]{2,1,0:T(8,128)(2,1)} %expert_out.1), calls=%async_computation.3 | async-start | bytes 5242880 | tf_op jit(solution)/shard_map/all_to_all | solution.py:1070
  259.9 177.6 %all-reduce.2.cloned.1.call-start = ((), (), s32[]{:S(2)}) async-start(), calls=%async_computation.6 | async-start | bytes 5242880 | tf_op jit(solution)/shard_map/psum | solution.py:1206
  286.1 3.1 collective-permute-start.22
  297.9 17.0 %collective-permute-start.23 = (bf16[4,512,128]{2,1,0:T(8,128)(2,1)}, bf16[4,512,128]{2,1,0:T(8,128)(2,1)S(1)}, u32[]{:S(2)}, u32[]{:S(2)}) collective-permute-start(bf16[4,512,128]{2,1,0:T(8,128)(2,1)} %get-tuple-element.249), channel_id=1, source_target_pairs={{0,8},{8,16},{16,24},{24,0},{32,40},{40,48},{48,56},{56,32},{64,72... | collective-permute-start | bytes 1572872 | tf_op jit(solution)/shard_map/ppermute | solution.py:1081
  298.4 18.0 %collective-permute-start.24 = (bf16[4,512,128]{2,1,0:T(8,128)(2,1)}, bf16[4,512,128]{2,1,0:T(8,128)(2,1)S(1)}, u32[]{:S(2)}, u32[]{:S(2)}) collective-permute-start(bf16[4,512,128]{2,1,0:T(8,128)(2,1)} %get-tuple-element.250), channel_id=1, source_target_pairs={{0,24},{8,0},{16,8},{24,16},{32,56},{40,32},{48,40},{56,48},{64,88... | collective-permute-start | bytes 1572872 | tf_op jit(solution)/shard_map/ppermute | solution.py:1081
  300.6 33.9 %collective-permute-start.25 = (bf16[4,512,128]{2,1,0:T(8,128)(2,1)}, bf16[4,512,128]{2,1,0:T(8,128)(2,1)S(1)}, u32[]{:S(2)}, u32[]{:S(2)}) collective-permute-start(bf16[4,512,128]{2,1,0:T(8,128)(2,1)} %get-tuple-element.251), channel_id=1, source_target_pairs={{0,16},{8,24},{16,0},{24,8},{32,48},{40,56},{48,32},{56,40},{64,80... | collective-permute-start | bytes 1572872 | tf_op jit(solution)/shard_map/ppermute | solution.py:1081
  301.4 33.1 %collective-permute-start.32 = (bf16[512,512]{1,0:T(8,128)(2,1)S(1)}, bf16[512,512]{1,0:T(8,128)(2,1)S(1)}, u32[]{:S(2)}, u32[]{:S(2)}) collective-permute-start(bf16[512,512]{1,0:T(8,128)(2,1)S(1)} %copy-done.7), channel_id=1, source_target_pairs={{0,1},{1,0},{2,3},{3,2},{4,5},{5,4},{6,7},{7,6},{8,9},{9,8},{10,11... | collective-permute-start | bytes 1572872 | tf_op jit(solution)/shard_map/ppermute | solution.py:1058
  302.6 31.9 %collective-permute-start.33 = (bf16[4,256,128]{2,1,0:T(8,128)(2,1)S(1)}, bf16[4,256,128]{2,1,0:T(8,128)(2,1)S(1)}, u32[]{:S(2)}, u32[]{:S(2)}) collective-permute-start(bf16[4,256,128]{2,1,0:T(8,128)(2,1)S(1)} %copy-done.35), channel_id=1, source_target_pairs={{0,1},{1,0},{2,3},{3,2},{4,5},{5,4},{6,7},{7,6},{8,9},{9,8},{10,11... | collective-permute-start | bytes 786440 | tf_op jit(solution)/shard_map/ppermute | solution.py:1058
  314.8 19.7 %copy-start.11 = (bf16[4,512,128]{2,1,0:T(8,128)(2,1)}, bf16[4,512,128]{2,1,0:T(8,128)(2,1)S(1)}, u32[]{:S(2)}) copy-start(bf16[4,512,128]{2,1,0:T(8,128)(2,1)S(1)} %collective-permute-done.23.b) | copy-start | bytes 1572868
  316.4 18.2 %copy-start.12 = (bf16[4,512,128]{2,1,0:T(8,128)(2,1)}, bf16[4,512,128]{2,1,0:T(8,128)(2,1)S(1)}, u32[]{:S(2)}) copy-start(bf16[4,512,128]{2,1,0:T(8,128)(2,1)S(1)} %collective-permute-done.24.c) | copy-start | bytes 1572868
  343.6 33.3 %collective-permute-start.34 = (bf16[160,2048]{1,0:T(8,128)(2,1)}, bf16[160,2048]{1,0:T(8,128)(2,1)S(1)}, u32[]{:S(2)}, u32[]{:S(2)}) collective-permute-start(bf16[160,2048]{1,0:T(8,128)(2,1)} %get-tuple-element.271), channel_id=1, source_target_pairs={{0,2},{1,3},{2,4},{3,5},{4,6},{5,7},{6,0},{7,1},{8,10},{9,11},{10,... | collective-permute-start | bytes 1966088 | tf_op jit(solution)/shard_map/ppermute | solution.py:1066
  344.9 32.7 %collective-permute-start.35 = (bf16[160,2048]{1,0:T(8,128)(2,1)}, bf16[160,2048]{1,0:T(8,128)(2,1)}, u32[]{:S(2)}, u32[]{:S(2)}) collective-permute-start(bf16[160,2048]{1,0:T(8,128)(2,1)} %get-tuple-element.272), channel_id=1, source_target_pairs={{0,6},{1,7},{2,0},{3,1},{4,2},{5,3},{6,4},{7,5},{8,14},{9,15},{10,... | collective-permute-start | bytes 1966088 | tf_op jit(solution)/shard_map/ppermute | solution.py:1066
  346.4 31.3 %collective-permute-start.36 = (bf16[160,2048]{1,0:T(8,128)(2,1)}, bf16[160,2048]{1,0:T(8,128)(2,1)}, u32[]{:S(2)}, u32[]{:S(2)}) collective-permute-start(bf16[160,2048]{1,0:T(8,128)(2,1)} %get-tuple-element.273), channel_id=1, source_target_pairs={{0,4},{1,5},{2,6},{3,7},{4,0},{5,1},{6,2},{7,3},{8,12},{9,13},{10,... | collective-permute-start | bytes 1966088 | tf_op jit(solution)/shard_map/ppermute | solution.py:1066
  350.4 6.7 %collective-permute-start.26 = (bf16[512,128]{1,0:T(8,128)(2,1)}, bf16[512,128]{1,0:T(8,128)(2,1)S(1)}, u32[]{:S(2)}, u32[]{:S(2)}) collective-permute-start(bf16[512,128]{1,0:T(8,128)(2,1)} %get-tuple-element.257), channel_id=1, source_target_pairs={{0,32},{8,40},{16,48},{24,56},{32,64},{40,72},{48,80},{56,88},{64,... | collective-permute-start | bytes 393224 | tf_op jit(solution)/shard_map/ppermute | solution.py:1081
  351.9 6.6 %collective-permute-start.27 = (bf16[512,128]{1,0:T(8,128)(2,1)}, bf16[512,128]{1,0:T(8,128)(2,1)S(1)}, u32[]{:S(2)}, u32[]{:S(2)}) collective-permute-start(bf16[512,128]{1,0:T(8,128)(2,1)} %get-tuple-element.258), channel_id=1, source_target_pairs={{0,96},{8,104},{16,112},{24,120},{32,0},{40,8},{48,16},{56,24},{64... | collective-permute-start | bytes 393224 | tf_op jit(solution)/shard_map/ppermute | solution.py:1081
  357.1 5.6 %copy-start.24 = (bf16[512,128]{1,0:T(8,128)(2,1)}, bf16[512,128]{1,0:T(8,128)(2,1)S(1)}, u32[]{:S(2)}) copy-start(bf16[512,128]{1,0:T(8,128)(2,1)S(1)} %collective-permute-done.26.b) | copy-start | bytes 393220
  357.1 5.6 %collective-permute-start.28 = (bf16[512,128]{1,0:T(8,128)(2,1)}, bf16[512,128]{1,0:T(8,128)(2,1)}, u32[]{:S(2)}, u32[]{:S(2)}) collective-permute-start(bf16[512,128]{1,0:T(8,128)(2,1)} %get-tuple-element.259), channel_id=1, source_target_pairs={{0,64},{8,72},{16,80},{24,88},{32,96},{40,104},{48,112},{56,120},{... | collective-permute-start | bytes 393224 | tf_op jit(solution)/shard_map/ppermute | solution.py:1081
  364.6 6.3 %collective-permute-start.31 = (bf16[512,128]{1,0:T(8,128)(2,1)}, bf16[512,128]{1,0:T(8,128)(2,1)S(1)}, u32[]{:S(2)}, u32[]{:S(2)}) collective-permute-start(bf16[512,128]{1,0:T(8,128)(2,1)} %add_last.1.a), channel_id=1, source_target_pairs={{0,32},{8,40},{16,48},{24,56},{32,64},{40,72},{48,80},{56,88},{64,... | collective-permute-start | bytes 393224 | tf_op jit(solution)/shard_map/ppermute | solution.py:1081
  364.6 7.3 %collective-permute-start.30 = (bf16[512,128]{1,0:T(8,128)(2,1)}, bf16[512,128]{1,0:T(8,128)(2,1)S(1)}, u32[]{:S(2)}, u32[]{:S(2)}) collective-permute-start(bf16[512,128]{1,0:T(8,128)(2,1)} %add_last.1.a), channel_id=1, source_target_pairs={{0,64},{8,72},{16,80},{24,88},{32,96},{40,104},{48,112},{56,120},{... | collective-permute-start | bytes 393224 | tf_op jit(solution)/shard_map/ppermute | solution.py:1081
  371.0 6.7 %copy-start.26 = (bf16[512,128]{1,0:T(8,128)(2,1)}, bf16[512,128]{1,0:T(8,128)(2,1)S(1)}, u32[]{:S(2)}) copy-start(bf16[512,128]{1,0:T(8,128)(2,1)S(1)} %collective-permute-done.31.d) | copy-start | bytes 393220
  371.0 6.0 %collective-permute-start.29 = (bf16[512,128]{1,0:T(8,128)(2,1)}, bf16[512,128]{1,0:T(8,128)(2,1)S(1)}, u32[]{:S(2)}, u32[]{:S(2)}) collective-permute-start(bf16[512,128]{1,0:T(8,128)(2,1)} %add_last.1.a), channel_id=1, source_target_pairs={{0,96},{8,104},{16,112},{24,120},{32,0},{40,8},{48,16},{56,24},{64... | collective-permute-start | bytes 393224 | tf_op jit(solution)/shard_map/ppermute | solution.py:1081
  371.9 5.8 %copy-start.27 = (bf16[512,128]{1,0:T(8,128)(2,1)}, bf16[512,128]{1,0:T(8,128)(2,1)S(1)}, u32[]{:S(2)}) copy-start(bf16[512,128]{1,0:T(8,128)(2,1)S(1)} %collective-permute-done.30.c) | copy-start | bytes 393220
  379.8 37.2 %collective-permute-start.39 = (bf16[4,512,128]{2,1,0:T(8,128)(2,1)}, bf16[4,512,128]{2,1,0:T(8,128)(2,1)}, u32[]{:S(2)}, u32[]{:S(2)}) collective-permute-start(bf16[4,512,128]{2,1,0:T(8,128)(2,1)} %stack_parts.1.c0), channel_id=1, source_target_pairs={{0,8},{8,16},{16,24},{24,0},{32,40},{40,48},{48,56},{56,32},{64,72... | collective-permute-start | bytes 1572872 | tf_op jit(solution)/shard_map/ppermute | solution.py:1081
  379.8 37.2 %collective-permute-start.38 = (bf16[4,512,128]{2,1,0:T(8,128)(2,1)}, bf16[4,512,128]{2,1,0:T(8,128)(2,1)}, u32[]{:S(2)}, u32[]{:S(2)}) collective-permute-start(bf16[4,512,128]{2,1,0:T(8,128)(2,1)} %stack_parts.1.c0), channel_id=1, source_target_pairs={{0,16},{8,24},{16,0},{24,8},{32,48},{40,56},{48,32},{56,40},{64,80... | collective-permute-start | bytes 1572872 | tf_op jit(solution)/shard_map/ppermute | solution.py:1081
  381.3 35.7 %collective-permute-start.37 = (bf16[4,512,128]{2,1,0:T(8,128)(2,1)}, bf16[4,512,128]{2,1,0:T(8,128)(2,1)}, u32[]{:S(2)}, u32[]{:S(2)}) collective-permute-start(bf16[4,512,128]{2,1,0:T(8,128)(2,1)} %stack_parts.1.c0), channel_id=1, source_target_pairs={{0,24},{8,0},{16,8},{24,16},{32,56},{40,32},{48,40},{56,48},{64,88... | collective-permute-start | bytes 1572872 | tf_op jit(solution)/shard_map/ppermute | solution.py:1081
  419.5 25.6 %all-to-all-start.5 = ((bf16[128,24,128]{2,1,0:T(8,128)(2,1)}), bf16[128,24,128]{2,1,0:T(8,128)(2,1)S(1)}, u32[]{:S(2)}, u32[]{:S(2)}) async-start(bf16[128,24,128]{2,1,0:T(8,128)(2,1)} %fold_small.1), calls=%async_computation.5 | async-start | bytes 1572864 | tf_op jit(solution)/shard_map/all_to_all | solution.py:1070
  445.3 6.9 %copy-start.1 = (s32[1,1024]{1,0:T(1,128)S(1)}, s32[1,1024]{1,0:T(1,128)}, u32[]{:S(2)}) copy-start(s32[1,1024]{1,0:T(1,128)} %param.32) | copy-start | bytes 12292
  (18 other events, 41.8 us)
Sparse Core Ops, SparseCore 0:
  298.0 120.4 all-reduce.1
